TPU v7x, 256 devices: a whole 4x4x8 slice. The times are simulated.
256 devices in a mesh: seq: 64 (over z, y, core), batch: 4 (over x).
Axes of the slice: x: 4, y: 4, z: 8, core: 2. Of those that a mesh axis runs over, the one named last changes fastest.
Arguments:
- windows: bfloat16 [4, 8192, 1536], P('batch', 'seq'), may hold values from -6 to 6
- gain_in: float32 [1536], replicated, may hold values from 0.25 to 1.75
- conv_taps: float32 [5, 1536], replicated, may hold values from -2.5 to 2.5
- gain_attn: float32 [1536], replicated, may hold values from 0.25 to 1.75
- query_weight: bfloat16 [1536, 1024], replicated, may hold values from -6 to 6
- key_weight: bfloat16 [1536, 128], replicated, may hold values from -1 to 1
- value_weight: bfloat16 [1536, 192], replicated, may hold values from -0.15625 to 0.15625
- out_weight: bfloat16 [1536, 1536], replicated, may hold values from -0.15625 to 0.15625
- out_cotangent: bfloat16 [4, 4096, 1536], P('batch', 'seq'), may hold values from -6 to 6
Outputs:
- mixed_out: bfloat16 [4, 4096, 1536], P('batch', 'seq')
- input_grad: bfloat16 [4, 8192, 1536], P('batch', 'seq')
- query_grad: float32 [1536, 1024], P(('seq', 'batch'))
- key_grad: float32 [1536, 128], P(('seq', 'batch'))
- value_grad: float32 [1536, 192], P(('seq', 'batch'))
- out_weight_grad: float32 [1536, 1536], P(('seq', 'batch'))
- conv_grad: float32 [5, 1536], replicated
- gain_in_grad: float32 [1536], replicated
- gain_attn_grad: float32 [1536], replicated
All inputs are finite; a program needn't handle non-finite values.
Results may differ from a plain program's by a relative error of at most 0.014.
Values may be sent and summed in bfloat16 or wider, within the bound.
No kernel may reach another device: no remote copies, remote signals or barrier semaphores. Data moves between devices by JAX's collectives and lax.ppermute only.
A program may use at most 128 MiB of HBM per device.

v0:
```python
import math

import jax
import jax.numpy as jnp
from jax import lax
from jax.sharding import PartitionSpec as P

EPS = 1e-06


def padded_2(block, sides, width):
    for axis, dim in sides:
        count = lax.axis_size(axis)
        forward = [(i, i + 1) for i in range(count - 1)]
        backward = [(target, source) for source, target in forward]
        low = lax.ppermute(
            lax.slice_in_dim(block, block.shape[dim] - width, None, axis=dim), axis, forward
        )
        high = lax.ppermute(lax.slice_in_dim(block, 0, width, axis=dim), axis, backward)
        block = jnp.concatenate([low, block, high], axis=dim)
    return block


def act_norm(rows, gain):
    scale = lax.rsqrt(jnp.mean(rows * rows, axis=-1, keepdims=True) + EPS)
    return jax.nn.gelu(rows * scale * gain, approximate=True)


def plain_norm(rows, gain):
    scale = lax.rsqrt(jnp.mean(rows * rows, axis=-1, keepdims=True) + EPS)
    return rows * scale * gain


def contract_rows(left, right):
    return lax.dot_general(
        left, right, (((0,), (0,)), ((), ())), preferred_element_type=jnp.float32
    )


def contract_cols(left, right):
    return lax.dot_general(
        left, right, (((1,), (1,)), ((), ())), preferred_element_type=jnp.float32
    )


def to_heads(features, heads, width, slots):
    pool = features.shape[0]
    groups = slots // heads
    shaped = features.reshape(groups, pool // groups, heads, width)
    return jnp.transpose(shaped, (2, 0, 1, 3)).reshape(slots, pool // groups, width)


def from_heads(pieces, heads):
    slots, part_rows, width = pieces.shape
    groups = slots // heads
    shaped = pieces.reshape(heads, groups, part_rows, width)
    return jnp.transpose(shaped, (1, 2, 0, 3)).reshape(groups * part_rows, heads * width)


def regroup(matrix, seq_count, batch_count, rows_each):
    pool = matrix.shape[0]
    shaped = matrix.reshape(pool, seq_count, batch_count, rows_each)
    return jnp.transpose(shaped, (2, 0, 1, 3)).reshape(batch_count, pool, seq_count * rows_each)


def shards(
    windows,
    gain_in,
    conv_taps,
    gain_attn,
    query_weight,
    key_weight,
    value_weight,
    out_weight,
    out_cotangent,
):
    seq_count = lax.axis_size("seq")
    batch_count = lax.axis_size("batch")
    xf = windows[0].astype(jnp.float32)
    fine = xf.shape[0]
    width = xf.shape[1]
    taps = conv_taps.shape[0]
    qk = key_weight.shape[1]
    vd = value_weight.shape[1]
    heads = query_weight.shape[1] // qk
    scale = 1.0 / math.sqrt(qk)
    act_b = act_norm(xf, gain_in).astype(jnp.bfloat16)
    padded = padded_2(act_b, (("seq", 0),), 2)
    conv = jnp.zeros((fine, width), jnp.float32)
    for tap in range(taps):
        conv = conv + conv_taps[tap] * padded[tap : tap + fine].astype(jnp.float32)
    hidden = xf + conv
    pooled = (hidden[0::2] + hidden[1::2]) * 0.5
    pool = pooled.shape[0]
    normed = plain_norm(pooled, gain_attn).astype(jnp.bfloat16)
    queries = jnp.dot(normed, query_weight, preferred_element_type=jnp.float32).astype(jnp.bfloat16)
    keys = jnp.dot(normed, key_weight, preferred_element_type=jnp.float32).astype(jnp.bfloat16)
    values = jnp.dot(normed, value_weight, preferred_element_type=jnp.float32).astype(jnp.bfloat16)
    keys_all, values_all = (
        lax.all_gather(keys, "seq", axis=0, tiled=True),
        lax.all_gather(values, "seq", axis=0, tiled=True),
    )
    sent = to_heads(queries, heads, qk, seq_count)
    local_q = lax.all_to_all(sent, "seq", split_axis=0, concat_axis=1, tiled=True).reshape(-1, qk)
    scores = contract_cols(local_q, keys_all) * scale
    peak = jnp.max(scores, axis=-1, keepdims=True)
    expo = jnp.exp(scores - peak)
    weights = expo / jnp.sum(expo, axis=-1, keepdims=True)
    packed = weights.astype(jnp.bfloat16)
    mixed_local = jnp.dot(packed, values_all, preferred_element_type=jnp.float32).astype(
        jnp.bfloat16
    )
    returned = lax.all_to_all(
        mixed_local.reshape(1, -1, vd), "seq", split_axis=1, concat_axis=0, tiled=True
    )
    mixed = from_heads(returned, heads)
    out = pooled + jnp.dot(mixed, out_weight, preferred_element_type=jnp.float32)
    mixed_out = out.astype(jnp.bfloat16)
    grad_y = out_cotangent[0]
    grad_mixed = contract_cols(grad_y, out_weight).astype(jnp.bfloat16)
    grad_local = lax.all_to_all(
        to_heads(grad_mixed, heads, vd, seq_count), "seq", split_axis=0, concat_axis=1, tiled=True
    ).reshape(-1, vd)
    grad_w = contract_cols(grad_local, values_all)
    delta = jnp.sum(weights * grad_w, axis=-1, keepdims=True)
    grad_s = (weights * (grad_w - delta) * scale).astype(jnp.bfloat16)
    grad_q_local = jnp.dot(grad_s, keys_all, preferred_element_type=jnp.float32).astype(
        jnp.bfloat16
    )
    key_terms = jnp.concatenate(
        [contract_rows(grad_s, local_q), contract_rows(packed, grad_local)], axis=1
    )
    key_blocks = lax.all_to_all(
        key_terms.reshape(seq_count, pool, qk + vd).astype(jnp.bfloat16),
        "seq",
        split_axis=0,
        concat_axis=0,
        tiled=True,
    ).astype(jnp.float32)
    key_sums = jnp.sum(key_blocks, axis=0)
    grad_keys = key_sums[:, :qk].astype(jnp.bfloat16)
    grad_values = key_sums[:, qk:].astype(jnp.bfloat16)
    grad_queries = from_heads(
        lax.all_to_all(
            grad_q_local.reshape(1, -1, qk), "seq", split_axis=1, concat_axis=0, tiled=True
        ),
        heads,
    )
    grad_normed = (
        contract_cols(grad_queries, query_weight)
        + contract_cols(grad_keys, key_weight)
        + contract_cols(grad_values, value_weight)
    )
    pull_two = jax.vjp(plain_norm, pooled, gain_attn)[1]
    grad_pool_norm, gain_attn_term = pull_two(grad_normed)
    grad_pool = grad_y.astype(jnp.float32) + grad_pool_norm
    grad_half = (grad_pool * 0.5).astype(jnp.bfloat16)
    grad_hidden = jnp.repeat(grad_half, 2, axis=0)
    padded_grad = padded_2(grad_hidden, (("seq", 0),), 2)
    grad_act = jnp.zeros((fine, width), jnp.float32)
    for tap in range(taps):
        grad_act = grad_act + conv_taps[tap] * padded_grad[4 - tap : 4 - tap + fine].astype(
            jnp.float32
        )
    grad_hidden_f = grad_hidden.astype(jnp.float32)
    conv_term = jnp.stack(
        [
            jnp.sum(grad_hidden_f * padded[tap : tap + fine].astype(jnp.float32), axis=0)
            for tap in range(taps)
        ]
    )
    pull_one = jax.vjp(act_norm, xf, gain_in)[1]
    grad_x_norm, gain_in_term = pull_one(grad_act)
    input_grad = (grad_hidden_f + grad_x_norm).astype(jnp.bfloat16)
    conv_grad, gain_in_grad, gain_attn_grad = lax.psum(
        (conv_term, gain_in_term, gain_attn_term), ("seq", "batch")
    )
    joined = jnp.concatenate([grad_queries, grad_keys, grad_values], axis=1)
    rows_each = width // (seq_count * batch_count)
    norm_parts, mixed_parts = (
        lax.all_to_all(
            regroup(normed, seq_count, batch_count, rows_each),
            "batch",
            split_axis=0,
            concat_axis=1,
            tiled=True,
        ),
        lax.all_to_all(
            regroup(mixed, seq_count, batch_count, rows_each),
            "batch",
            split_axis=0,
            concat_axis=1,
            tiled=True,
        ),
    )
    norm_group = norm_parts.reshape(-1, seq_count * rows_each)
    mixed_group = mixed_parts.reshape(-1, seq_count * rows_each)
    joined_group, grad_group = (
        lax.all_gather(joined, "batch", axis=0, tiled=True),
        lax.all_gather(grad_y, "batch", axis=0, tiled=True),
    )
    sums = lax.psum_scatter(
        jnp.concatenate(
            [contract_rows(norm_group, joined_group), contract_rows(mixed_group, grad_group)],
            axis=1,
        ),
        "seq",
        scatter_dimension=0,
        tiled=True,
    )
    q_cols = query_weight.shape[1]
    query_grad = sums[:, :q_cols]
    key_grad = sums[:, q_cols : q_cols + qk]
    value_grad = sums[:, q_cols + qk : q_cols + qk + vd]
    out_weight_grad = sums[:, q_cols + qk + vd :]
    return (
        mixed_out[None],
        input_grad[None],
        query_grad,
        key_grad,
        value_grad,
        out_weight_grad,
        conv_grad,
        gain_in_grad,
        gain_attn_grad,
    )


def solution(mesh):
    in_specs = (P("batch", "seq", None), P(), P(), P(), P(), P(), P(), P(), P("batch", "seq", None))
    out_specs = (
        P("batch", "seq", None),
        P("batch", "seq", None),
        P(("seq", "batch"), None),
        P(("seq", "batch"), None),
        P(("seq", "batch"), None),
        P(("seq", "batch"), None),
        P(),
        P(),
        P(),
    )
    return jax.shard_map(shards, mesh=mesh, in_specs=in_specs, out_specs=out_specs, check_vma=False)
```

profile of v0, /device:TPU:1, one launch (start us, length us, event | category | flops | bytes accessed | tf_op | source)
XLA Modules:
  0.0 617.9 jit_solution(16824024926236755044)
XLA Ops:
  10.0 4.6 collective-permute-start
  14.6 1.9 collective-permute-start.1
  17.7 1.8 collective-permute-done.1
  20.1 2.4 fusion.17
  22.6 2.7 slice.117
  25.3 2.7 slice.118
  32.5 2.1 convolution_convert_fusion.5
  36.9 13.7 %all-to-all-start = ((bf16[64,8,128]{2,1,0:T(8,128)(2,1)}), bf16[64,8,128]{2,1,0:T(8,128)(2,1)}, u32[]{:S(2)}, u32[]{:S(2)}) async-start(bf16[64,8,128]{2,1,0:T(8,128)(2,1)} %bitcast.172), calls=%async_computation | async-start | bytes 262144 | tf_op jit(solution)/shard_map/all_to_all | solution.py:104
  50.6 4.7 convolution_convert_fusion.2
  55.3 1.9 reshape.168
  58.9 2.8 all-to-all-done
  61.6 8.1 %all-to-all-start.2 = ((bf16[64,8,192]{2,1,0:T(8,128)(2,1)}), bf16[64,8,192]{2,1,0:T(8,128)(2,1)}, u32[]{:S(2)}, u32[]{:S(2)}) async-start(bf16[64,8,192]{2,1,0:T(8,128)(2,1)} %bitcast.170), calls=%async_computation.2 | async-start | bytes 524288 | tf_op jit(solution)/shard_map/all_to_all | solution.py:121
  69.7 44.7 %all-gather.4.cloned.1.call-done = bf16[4096,128]{1,0:T(8,128)(2,1)} async-done(((bf16[64,128]{1,0:T(8,128)(2,1)}), bf16[4096,128]{1,0:T(8,128)(2,1)}) %all-gather.4.cloned.1.call-update) | async-done | bytes 1048592 | tf_op jit(solution)/shard_map/all_gather | solution.py:100
  114.4 2.6 multiply_reduce_fusion.1
  117.0 3.2 copy-done.1
  120.2 2.1 fusion.1
  122.3 70.4 %all-gather.6.cloned.1.call-done = bf16[4096,192]{1,0:T(8,128)(2,1)} async-done(((bf16[64,192]{1,0:T(8,128)(2,1)}), bf16[4096,192]{1,0:T(8,128)(2,1)}) %all-gather.6.cloned.1.call-update) | async-done | bytes 1572880 | tf_op jit(solution)/shard_map/all_gather | solution.py:101
  192.7 12.0 %multiply_reduce_fusion = (f32[512]{0:T(512)S(1)}, f32[512,4096]{1,0:T(8,128)}, f32[512,4096]{1,0:T(8,128)}) fusion(f32[512]{0:T(512)} %fusion.1, f32[512]{0:T(512)S(1)} %get-tuple-element.39, f32[512,4096]{1,0:T(8,128)} %copy-done.1, bf16[4096,192]{1,0:T(8,128)(2,1)} %all-gather.6.cloned.1.call-done, bf16[64,8,192]{2,1,0:T(8,128)(2,1)} %all-to-all-done.2), kind=kOutput, calls=%fused_computation.1 | convolution fusion | flops 815791616 | bytes 26941440 | tf_op jit(solution)/shard_map/dot_general | solution.py:41
  204.8 10.1 %multiply_convert_fusion = bf16[512,4096]{1,0:T(8,128)(2,1)} fusion(f32[512,4096]{1,0:T(8,128)} %get-tuple-element.31, f32[512,4096]{1,0:T(8,128)} %get-tuple-element.41, f32[512]{0:T(512)S(1)} %get-tuple-element.30), kind=kLoop, calls=%fused_computation | loop fusion | flops 8388608 | bytes 20973568 | tf_op jit(solution)/shard_map/convert_element_type | solution.py:126
  214.9 3.4 fusion.13
  219.8 3.0 reduce.18
  224.4 6.2 %fusion.10 = bf16[1,512,192]{1,2,0:T(8,128)(2,1)} fusion(bf16[4096,192]{1,0:T(8,128)(2,1)} %all-gather.6.cloned.1.call-done, f32[512,4096]{1,0:T(8,128)} %get-tuple-element.31), kind=kOutput, calls=%fused_computation.29 | convolution fusion | flops 807501824 | bytes 10158080 | tf_op jit(solution)/shard_map/dot_general | solution.py:110
  230.6 2.1 copy.58
  232.7 3.9 reduce.17
  236.6 1.9 reshape.190
  238.6 6.8 %all-to-all-start.1 = ((bf16[64,2,768]{2,1,0:T(2,128)(2,1)}), bf16[64,2,768]{2,1,0:T(2,128)(2,1)}, u32[]{:S(2)}, u32[]{:S(2)}) async-start(bf16[64,2,768]{2,1,0:T(2,128)(2,1)} %reshape.190), calls=%async_computation.1 | async-start | bytes 393216 | tf_op jit(solution)/shard_map/all_to_all | solution.py:113
  245.4 5.6 convolution_convert_fusion
  251.0 6.3 %all-to-all-done.1 = bf16[64,2,768]{2,1,0:T(2,128)(2,1)} async-done(((bf16[64,2,768]{2,1,0:T(2,128)(2,1)}), bf16[64,2,768]{2,1,0:T(2,128)(2,1)}, u32[]{:S(2)}, u32[]{:S(2)}) %all-to-all-start.1) | async-done | bytes 196640 | tf_op jit(solution)/shard_map/all_to_all | solution.py:113
  257.3 5.2 all-to-all-start.3
  262.5 3.9 convolution_convert_fusion.1
  266.5 2.9 reshape.191
  271.2 3.8 copy.67
  274.9 4.8 reshape_reshape.3
  279.7 1.9 copy.68
  281.7 1.9 copy.69
  283.6 4.0 all-to-all-start.6
  287.6 3.5 pad_maximum_fusion.1
  291.1 4.5 copy.63
  295.6 11.0 %all-to-all-start.4 = ((bf16[64,64,320]{2,1,0:T(8,128)(2,1)}), bf16[64,64,320]{2,1,0:T(8,128)(2,1)}, u32[]{:S(2)}, u32[]{:S(2)}) async-start(bf16[64,64,320]{2,1,0:T(8,128)(2,1)} %bitcast.159), calls=%async_computation.4 | async-start | bytes 6291456 | tf_op jit(solution)/shard_map/all_to_all | solution.py:133
  307.9 14.3 %all-gather = bf16[1,256,1536]{2,1,0:T(8,128)(2,1)} all-gather(bf16[1,64,1536]{2,1,0:T(8,128)(2,1)} %param.17), channel_id=2, replica_groups=mesh['seq'=64,'batch'=4] {'batch'}, dimensions={1}, use_global_device_ids=true | all-gather | bytes 983040 | tf_op jit(solution)/shard_map/all_gather | solution.py:200
  324.0 1.9 reshape.175
  326.0 1.9 copy.65
  327.9 1.9 copy.66
  329.8 2.2 reshape.193
  333.8 1.8 fusion.77
  336.5 1.9 reshape.167
  338.4 4.1 fusion.3
  342.5 2.8 fusion.57
  345.4 33.7 %all-to-all-done.4 = bf16[64,64,320]{2,1,0:T(8,128)(2,1)} async-done(((bf16[64,64,320]{2,1,0:T(8,128)(2,1)}), bf16[64,64,320]{2,1,0:T(8,128)(2,1)}, u32[]{:S(2)}, u32[]{:S(2)}) %all-to-all-start.4) | async-done | bytes 2621472 | tf_op jit(solution)/shard_map/all_to_all | solution.py:133
  379.1 4.5 all-to-all-start.5
  383.6 3.0 reduce.2
  388.1 2.7 multiply_reduce_fusion.3
  391.7 12.2 %all_gather.14 = bf16[256,1344]{1,0:T(8,128)(2,1)} all-gather(bf16[64,1344]{1,0:T(8,128)(2,1)S(1)} %pad_maximum_fusion.5), channel_id=1, replica_groups=mesh['seq'=64,'batch'=4] {'batch'}, dimensions={0}, use_global_device_ids=true | all-gather | bytes 860160 | tf_op jit(solution)/shard_map/all_gather | solution.py:199
  404.5 1.8 fusion.81
  406.5 2.9 pad_maximum_fusion
  412.5 1.9 reshape.174
  415.8 7.1 %collective-permute-start.2 = (bf16[2,1536]{1,0:T(2,128)(2,1)}, bf16[2,1536]{1,0:T(2,128)(2,1)}, u32[]{:S(2)}, u32[]{:S(2)}) collective-permute-start(bf16[2,1536]{1,0:T(2,128)(2,1)} %slice.123), channel_id=1, source_target_pairs={{4,0},{8,4},{12,8},{16,12},{20,16},{24,20},{28,24},{32,28},{36,32}... | collective-permute-start | bytes 18440 | tf_op jit(solution)/shard_map/ppermute | solution.py:19
  423.5 3.2 collective-permute-start.3
  426.7 2.1 broadcast_in_dim.32
  428.8 2.6 broadcast_in_dim.33
  435.4 3.7 fusion.30
  439.7 2.2 fusion.56
  442.7 74.8 %all-reduce.1 = (f32[5,1536]{1,0:T(8,128)}, f32[1536]{0:T(1024)}, f32[1536]{0:T(1024)}) all-reduce(f32[5,1536]{1,0:T(8,128)S(1)} %stack.23, f32[1536]{0:T(1024)} %get-tuple-element.9, f32[1536]{0:T(1024)} %get-tuple-element.15), channel_id=1, replica_groups=mesh['seq'=64,'batch'=4] {'seq','batch'}, use_global_device_ids=true, to_apply=%region_14.0 | all-reduce | flops 10752 | bytes 86016 | tf_op jit(solution)/shard_map/psum | solution.py:175
  517.5 87.6 %all-reduce.4.cloned.1.call-done = f32[384,2880]{1,0:T(8,128)} async-done(((f32[384,2880]{1,0:T(8,128)}), f32[384,2880]{1,0:T(8,128)}) %all-reduce.4.cloned.1.call-update) | async-done | bytes 4423696
  (112 shorter events, 42.1 us)
Async XLA Ops:
  7.2 27.4 %copy-start = (bf16[1536,1024]{1,0:T(8,128)(2,1)S(1)}, bf16[1536,1024]{1,0:T(8,128)(2,1)}, u32[]{:S(2)}) copy-start(bf16[1536,1024]{1,0:T(8,128)(2,1)} %param.13) | copy-start | bytes 9437188
  7.2 22.6 %copy-start.14 = (f32[1536]{0:T(1024)S(1)}, f32[1536]{0:T(1024)}, u32[]{:S(2)}) copy-start(f32[1536]{0:T(1024)} %param.12) | copy-start | bytes 18436
  7.2 107.2 %all-gather.4.cloned.1.call-start = ((), (), s32[]{:S(2)}) async-start(), calls=%async_computation.7 | async-start | bytes 1064960 | tf_op jit(solution)/shard_map/all_gather | solution.py:100
  8.6 11.0 %copy-start.24 = (f32[128]{0:T(128)}, f32[128]{0:T(128)S(1)}, u32[]{:S(2)}) copy-start(f32[128]{0:T(128)S(1)} %fusion.35) | copy-start | bytes 1540
  8.6 11.0 %copy-start.23 = (f32[128]{0:T(128)}, f32[128]{0:T(128)S(1)}, u32[]{:S(2)}) copy-start(f32[128]{0:T(128)S(1)} %fusion.75) | copy-start | bytes 1540
  10.0 9.6 %copy-start.7 = (bf16[128,1536]{1,0:T(8,128)(2,1)}, bf16[128,1536]{1,0:T(8,128)(2,1)S(1)}, u32[]{:S(2)}) copy-start(bf16[128,1536]{1,0:T(8,128)(2,1)S(1)} %fusion.27) | copy-start | bytes 1179652
  10.0 7.7 %collective-permute-start = (bf16[2,1536]{1,0:T(2,128)(2,1)S(1)}, bf16[2,1536]{1,0:T(2,128)(2,1)S(1)}, u32[]{:S(2)}, u32[]{:S(2)}) collective-permute-start(bf16[2,1536]{1,0:T(2,128)(2,1)S(1)} %get-tuple-element.35), channel_id=1, source_target_pairs={{0,4},{4,8},{8,12},{12,16},{16,20},{20,24},{24,28},{28,32},{32,36}... | collective-permute-start | bytes 18440 | tf_op jit(solution)/shard_map/ppermute | solution.py:16
  14.6 4.9 collective-permute-start.1
  17.6 1.9 copy-start.15
  17.6 1.9 copy-start.17
  17.7 1.9 copy-start.18
  17.7 1.9 copy-start.19
  17.7 1.9 copy-start.20
  17.7 1.9 copy-start.21
  19.6 0.6 copy-start.22
  29.2 26.1 %copy-start.25 = (f32[64]{0:T(128)}, f32[64]{0:T(128)S(1)}, u32[]{:S(2)}) copy-start(f32[64]{0:T(128)S(1)} %get-tuple-element.32) | copy-start | bytes 772
  29.2 358.8 %copy-start.3 = (f32[64,1536]{1,0:T(8,128)}, f32[64,1536]{1,0:T(8,128)S(1)}, u32[]{:S(2)}) copy-start(f32[64,1536]{1,0:T(8,128)S(1)} %get-tuple-element.33) | copy-start | bytes 1179652
  29.9 0.7 copy-start.6
  32.4 160.3 %all-gather.6.cloned.1.call-start = ((), (), s32[]{:S(2)}) async-start(), calls=%async_computation.8 | async-start | bytes 2129920 | tf_op jit(solution)/shard_map/all_gather | solution.py:101
  36.9 24.7 %all-to-all-start = ((bf16[64,8,128]{2,1,0:T(8,128)(2,1)}), bf16[64,8,128]{2,1,0:T(8,128)(2,1)}, u32[]{:S(2)}, u32[]{:S(2)}) async-start(bf16[64,8,128]{2,1,0:T(8,128)(2,1)} %bitcast.172), calls=%async_computation | async-start | bytes 262144 | tf_op jit(solution)/shard_map/all_to_all | solution.py:104
  61.6 60.7 %all-to-all-start.2 = ((bf16[64,8,192]{2,1,0:T(8,128)(2,1)}), bf16[64,8,192]{2,1,0:T(8,128)(2,1)}, u32[]{:S(2)}, u32[]{:S(2)}) async-start(bf16[64,8,192]{2,1,0:T(8,128)(2,1)} %bitcast.170), calls=%async_computation.2 | async-start | bytes 524288 | tf_op jit(solution)/shard_map/all_to_all | solution.py:121
  117.0 3.2 copy-start.1
  204.8 10.1 %copy-start.12 = (bf16[4096,128]{1,0:T(8,128)(2,1)S(1)}, bf16[4096,128]{1,0:T(8,128)(2,1)}, u32[]{:S(2)}) copy-start(bf16[4096,128]{1,0:T(8,128)(2,1)} %all-gather.4.cloned.1.call-done) | copy-start | bytes 3145732
  238.6 18.8 %all-to-all-start.1 = ((bf16[64,2,768]{2,1,0:T(2,128)(2,1)}), bf16[64,2,768]{2,1,0:T(2,128)(2,1)}, u32[]{:S(2)}, u32[]{:S(2)}) async-start(bf16[64,2,768]{2,1,0:T(2,128)(2,1)} %reshape.190), calls=%async_computation.1 | async-start | bytes 393216 | tf_op jit(solution)/shard_map/all_to_all | solution.py:113
  257.3 26.2 %all-to-all-start.3 = ((bf16[64,2,512]{2,1,0:T(2,128)(2,1)}), bf16[64,2,512]{2,1,0:T(2,128)(2,1)}, u32[]{:S(2)}, u32[]{:S(2)}) async-start(bf16[64,2,512]{2,1,0:T(2,128)(2,1)} %reshape.192), calls=%async_computation.3 | async-start | bytes 262144 | tf_op jit(solution)/shard_map/all_to_all | solution.py:144
  283.6 12.1 %all-to-all-start.6 = ((bf16[4,64,384]{2,1,0:T(8,128)(2,1)}), bf16[4,64,384]{2,1,0:T(8,128)(2,1)}, u32[]{:S(2)}, u32[]{:S(2)}) async-start(bf16[4,64,384]{2,1,0:T(8,128)(2,1)} %copy.69), calls=%async_computation.6 | async-start | bytes 393216 | tf_op jit(solution)/shard_map/all_to_all | solution.py:188
  295.6 11.0 %copy-start.27 = (u32[256]{0:T(256)S(1)}, u32[256]{0:T(256)}, u32[]{:S(2)}) copy-start(u32[256]{0:T(256)} %constant.39) | copy-start | bytes 3076
  295.6 83.5 %all-to-all-start.4 = ((bf16[64,64,320]{2,1,0:T(8,128)(2,1)}), bf16[64,64,320]{2,1,0:T(8,128)(2,1)}, u32[]{:S(2)}, u32[]{:S(2)}) async-start(bf16[64,64,320]{2,1,0:T(8,128)(2,1)} %bitcast.159), calls=%async_computation.4 | async-start | bytes 6291456 | tf_op jit(solution)/shard_map/all_to_all | solution.py:133
  332.0 3.6 copy-start.10
  338.4 4.1 copy-start.9
  345.4 58.6 %copy-start.26 = (f32[64]{0:T(128)S(1)}, f32[64]{0:T(128)}, u32[]{:S(2)}) copy-start(f32[64]{0:T(128)} %copy-done.25) | copy-start | bytes 772
  379.1 25.4 %all-to-all-start.5 = ((bf16[4,64,384]{2,1,0:T(8,128)(2,1)}), bf16[4,64,384]{2,1,0:T(8,128)(2,1)}, u32[]{:S(2)}, u32[]{:S(2)}) async-start(bf16[4,64,384]{2,1,0:T(8,128)(2,1)} %copy.66), calls=%async_computation.5 | async-start | bytes 393216 | tf_op jit(solution)/shard_map/all_to_all | solution.py:181
  383.6 221.5 %all-reduce.4.cloned.1.call-start = ((), (), s32[]{:S(2)}) async-start(), calls=%async_computation.9 | async-start | bytes 9043968
  404.5 2.0 copy-start.4
  409.4 23.0 %copy-start.2 = (bf16[1,128,1536]{2,1,0:T(8,128)(2,1)S(1)}, bf16[1,128,1536]{2,1,0:T(8,128)(2,1)}, u32[]{:S(2)}) copy-start(bf16[1,128,1536]{2,1,0:T(8,128)(2,1)} %param.9) | copy-start | bytes 1179652
  409.4 23.0 %copy-start.13 = (f32[1536]{0:T(1024)S(1)}, f32[1536]{0:T(1024)}, u32[]{:S(2)}) copy-start(f32[1536]{0:T(1024)} %param.10) | copy-start | bytes 18436
  410.8 0.7 copy-start.11
  411.5 23.9 %copy-start.16 = (f32[1536]{0:T(1024)S(1)}, f32[1536]{0:T(1024)}, u32[]{:S(2)}) copy-start(f32[1536]{0:T(1024)} %copy-done.15) | copy-start | bytes 18436
  415.8 18.9 %collective-permute-start.2 = (bf16[2,1536]{1,0:T(2,128)(2,1)}, bf16[2,1536]{1,0:T(2,128)(2,1)}, u32[]{:S(2)}, u32[]{:S(2)}) collective-permute-start(bf16[2,1536]{1,0:T(2,128)(2,1)} %slice.123), channel_id=1, source_target_pairs={{4,0},{8,4},{12,8},{16,12},{20,16},{24,20},{28,24},{32,28},{36,32}... | collective-permute-start | bytes 18440 | tf_op jit(solution)/shard_map/ppermute | solution.py:19
  423.5 11.8 %collective-permute-start.3 = (bf16[2,1536]{1,0:T(2,128)(2,1)}, bf16[2,1536]{1,0:T(2,128)(2,1)}, u32[]{:S(2)}, u32[]{:S(2)}) collective-permute-start(bf16[2,1536]{1,0:T(2,128)(2,1)} %slice.128), channel_id=1, source_target_pairs={{0,4},{4,8},{8,12},{12,16},{16,20},{20,24},{24,28},{28,32},{32,36}... | collective-permute-start | bytes 18440 | tf_op jit(solution)/shard_map/ppermute | solution.py:16
  431.3 8.4 %copy-start.5 = (bf16[128,1536]{1,0:T(8,128)(2,1)S(1)}, bf16[128,1536]{1,0:T(8,128)(2,1)}, u32[]{:S(2)}) copy-start(bf16[128,1536]{1,0:T(8,128)(2,1)} %reshape.174) | copy-start | bytes 1179652
  431.3 8.4 %copy-start.8 = (bf16[128,1536]{1,0:T(8,128)(2,1)S(1)}, bf16[128,1536]{1,0:T(8,128)(2,1)}, u32[]{:S(2)}) copy-start(bf16[128,1536]{1,0:T(8,128)(2,1)} %copy-done.7) | copy-start | bytes 1179652
Sparse Core Ops, SparseCore 0:
  32.6 81.7 all-gather.3
  117.7 74.9 all-gather.5
  409.5 195.4 all-reduce.3
where the time goes:
time: 626 us; the launch traced here: 618 us
  waiting for transfers between devices  247 us (39%)
  blocking collectives  101 us (16%)
  local copies, waits for them, and re-layouts  78.2 us (12%)
  starting transfers between devices  70.2 us (11%)
  matrix products  58.8 us (9%)
  other arithmetic  46.6 us (7%)
  between operations  15.3 us (2%)
    unnamed x4, waiting for transfers between devices  87.6 us
    psum x1, blocking collectives, shards(): lax.psum((conv_term, gain_in_term, gain_attn_term), ('seq', 'batch'))  74.8 us
    all_gather x1, waiting for transfers between devices, shards(): lax.all_gather(values, 'seq', axis=0, tiled=True)  70.4 us
    all_gather x1, waiting for transfers between devices, shards(): lax.all_gather(keys, 'seq', axis=0, tiled=True)  44.7 us
    all_to_all x1, waiting for transfers between devices, shards(): lax.all_to_all(key_terms.reshape(seq_count, pool, qk + vd).astype(jnp.bfl...  33.7 us
    dot_general x6, matrix products, contract_cols(): lax.dot_general(left, right, (((1,), (1,)), ((), ())), preferred_element_...  25.3 us
    unnamed x66, local copies, waits for them, and re-layouts  19.7 us
    all_gather x1, blocking collectives, shards(): lax.all_gather(grad_y, 'batch', axis=0, tiled=True)  14.3 us
  transfers between devices with their start and end apart: 14, of which 7 were waited for; matrix products, arithmetic and copies ran while one was open for 17% of the time, Pallas kernels for 0%

commit v1 on v0

v1 whole, which is shorter than its diff:
```python
import functools
import math

import jax
import jax.numpy as jnp
from jax import lax
from jax.experimental import pallas as pl
from jax.experimental.pallas import tpu as pltpu
from jax.sharding import Mesh
from jax.sharding import PartitionSpec as P

EPS = 1e-06
F32 = jnp.float32
BF = jnp.bfloat16


def plain_norm(rows, gain):
    scale = lax.rsqrt(jnp.mean(rows * rows, axis=-1, keepdims=True) + EPS)
    return rows * scale * gain


def contract_rows(left, right):
    return lax.dot_general(left, right, (((0,), (0,)), ((), ())), preferred_element_type=F32)


def contract_cols(left, right):
    return lax.dot_general(left, right, (((1,), (1,)), ((), ())), preferred_element_type=F32)


def dot(left, right):
    return jnp.dot(left, right, preferred_element_type=F32)


def swap(block):
    return lax.ppermute(block, "core", [(0, 1), (1, 0)])


def exchange(blocks, axis):
    return lax.all_to_all(blocks, axis, 0, 0, tiled=True)


def copies(block, axis):
    count = lax.axis_size(axis)
    sent = jnp.broadcast_to(block[None], (count,) + block.shape)
    return exchange(sent, axis)


def attention_kernel(scale, heads, q_ref, g_ref, kv0_ref, kv1_ref,
                     mixed_ref, gq_ref, gkv0_ref, gkv1_ref, s_ref, gw_ref):
    rows = q_ref.shape[0]
    qk = q_ref.shape[1] // heads
    vd = g_ref.shape[1] // heads
    q = jnp.concatenate([q_ref[:, h * qk : (h + 1) * qk] for h in range(heads)], axis=0)
    g = jnp.concatenate([g_ref[:, h * vd : (h + 1) * vd] for h in range(heads)], axis=0)
    total = rows * heads
    block = 512
    half = kv0_ref.shape[0]
    per = half // block

    def sweep(body, carry):
        for part, (kv, gkv) in enumerate(((kv0_ref, gkv0_ref), (kv1_ref, gkv1_ref))):
            def step(i, c, part=part, kv=kv, gkv=gkv):
                at = pl.ds(pl.multiple_of(i * block, block), block)
                return body(c, kv, gkv, at, pl.ds(pl.multiple_of(part * half + i * block, block), block))
            carry = lax.fori_loop(0, per, step, carry)
        return carry

    def first(peak, kv, gkv, at, here):
        s = contract_cols(kv[at, :qk], q) * scale
        s_ref[here, :] = s
        return jnp.maximum(peak, jnp.max(s, axis=0, keepdims=True))

    peak = sweep(first, jnp.full((1, total), -jnp.inf, F32))

    def second(carry, kv, gkv, at, here):
        norm, dot_sum, out = carry
        v = kv[at, qk:]
        e = jnp.exp(s_ref[here, :] - peak)
        s_ref[here, :] = e
        gw = contract_cols(v, g)
        gw_ref[here, :] = gw
        return (norm + jnp.sum(e, axis=0, keepdims=True),
                dot_sum + jnp.sum(e * gw, axis=0, keepdims=True),
                out + contract_rows(v, e.astype(BF)))

    zero = jnp.zeros((1, total), F32)
    norm, dot_sum, out = sweep(second, (zero, zero, jnp.zeros((vd, total), F32)))
    inv = 1.0 / norm
    delta = dot_sum * inv
    mixed = jnp.transpose(out * inv).astype(BF)
    for h in range(heads):
        mixed_ref[:, h * vd : (h + 1) * vd] = mixed[h * rows : (h + 1) * rows]

    def third(gq, kv, gkv, at, here):
        w = s_ref[here, :] * inv
        ds = (w * (gw_ref[here, :] - delta) * scale).astype(BF)
        gkv[at, :qk] = dot(ds, q).astype(BF)
        gkv[at, qk:] = dot(w.astype(BF), g).astype(BF)
        return gq + contract_rows(kv[at, :qk], ds)

    gq = jnp.transpose(sweep(third, jnp.zeros((qk, total), F32))).astype(BF)
    for h in range(heads):
        gq_ref[:, h * qk : (h + 1) * qk] = gq[h * rows : (h + 1) * rows]


def attention(q, g, kv0, kv1, heads):
    rows, width = q.shape
    keys = kv0.shape[0] + kv1.shape[0]
    scale = 1.0 / math.sqrt(width // heads)
    return pl.pallas_call(
        functools.partial(attention_kernel, scale, heads),
        out_shape=(
            jax.ShapeDtypeStruct(g.shape, BF),
            jax.ShapeDtypeStruct(q.shape, BF),
            jax.ShapeDtypeStruct(kv0.shape, BF),
            jax.ShapeDtypeStruct(kv1.shape, BF),
        ),
        scratch_shapes=[
            pltpu.VMEM((keys, rows * heads), F32),
            pltpu.VMEM((keys, rows * heads), F32),
        ],
        compiler_params=pltpu.CompilerParams(vmem_limit_bytes=48 * 2**20),
        cost_estimate=pl.CostEstimate(
            flops=2 * keys * rows * (3 * width + 3 * g.shape[1]),
            bytes_accessed=8 * keys * kv0.shape[1],
            transcendentals=keys * rows * heads,
        ),
    )(q, g, kv0, kv1)


def shards(
    windows,
    gain_in,
    conv_taps,
    gain_attn,
    query_weight,
    key_weight,
    value_weight,
    out_weight,
    out_cotangent,
):
    seq = ("z", "y", "core")
    nz, ny, nx = lax.axis_size("z"), lax.axis_size("y"), lax.axis_size("x")
    nc = lax.axis_size("core")
    count = nz * ny * nc
    place = lax.axis_index(seq)
    first_core = lax.axis_index("core") == 0
    x = windows[0]
    fine, width = x.shape
    taps = conv_taps.shape[0]
    qk = key_weight.shape[1]
    vd = value_weight.shape[1]
    q_cols = query_weight.shape[1]
    heads = q_cols // qk
    grad_y = out_cotangent[0]

    up = [(i, i + 1) for i in range(count - 1)]
    down = [(b, a) for a, b in up]
    low = lax.ppermute(x[fine - 2 :], seq, up)
    high = lax.ppermute(x[:2], seq, down)
    xe = jnp.concatenate([low, x, high], axis=0).astype(F32)
    at = lax.broadcasted_iota(jnp.int32, (fine + 4, 1), 0) + place * fine - 2
    inside = (at >= 0) & (at < count * fine)

    def act_of(rows, gain):
        scale = lax.rsqrt(jnp.mean(rows * rows, axis=-1, keepdims=True) + EPS)
        return jax.nn.gelu(rows * scale * gain, approximate=True)

    act = jnp.where(inside, act_of(xe, gain_in), 0.0).astype(BF)
    conv = jnp.zeros((fine, width), F32)
    for tap in range(taps):
        conv = conv + conv_taps[tap] * act[tap : tap + fine].astype(F32)
    hidden = x.astype(F32) + conv
    pooled = (hidden[0::2] + hidden[1::2]) * 0.5
    pool = pooled.shape[0]
    normed = plain_norm(pooled, gain_attn).astype(BF)

    kv = jnp.concatenate([dot(normed, key_weight), dot(normed, value_weight)], axis=1).astype(BF)
    kv_cols = qk + vd
    kv_own = copies(copies(kv, "z").reshape(nz * pool, kv_cols), "y").reshape(-1, kv_cols)
    kv_other = swap(kv_own)
    queries = dot(normed, query_weight).astype(BF)
    grad_mixed = contract_cols(grad_y, out_weight).astype(BF)
    mixed, grad_queries, gkv_own, gkv_other = attention(
        queries, grad_mixed, kv_own, kv_other, heads
    )

    left = jnp.where(first_core, normed, mixed)
    left = jnp.concatenate([left, swap(jnp.where(first_core, mixed, normed))], axis=0)
    left = lax.all_gather(left, "x", axis=0, tiled=True)

    gkv = (gkv_own.astype(F32) + swap(gkv_other).astype(F32)).astype(BF)
    gkv = jnp.sum(exchange(gkv.reshape(ny, -1, kv_cols), "y").astype(F32), axis=0).astype(BF)
    gkv = jnp.sum(exchange(gkv.reshape(nz, pool, kv_cols), "z").astype(F32), axis=0).astype(BF)

    mixed_out = (pooled + dot(mixed, out_weight)).astype(BF)

    grad_normed = (
        contract_cols(grad_queries, query_weight)
        + contract_cols(gkv[:, :qk], key_weight)
        + contract_cols(gkv[:, qk:], value_weight)
    )
    grad_pool_norm, gain_attn_term = jax.vjp(plain_norm, pooled, gain_attn)[1](grad_normed)
    grad_half = ((grad_y.astype(F32) + grad_pool_norm) * 0.5).astype(BF)

    before = lax.ppermute(grad_half[pool - 1 :], seq, up)
    after = lax.ppermute(grad_half[:1], seq, down)
    gh = jnp.repeat(grad_half, 2, axis=0).astype(F32)
    ghe = jnp.repeat(jnp.concatenate([before, grad_half, after], axis=0), 2, axis=0).astype(F32)
    grad_act = jnp.zeros((fine, width), F32)
    for tap in range(taps):
        grad_act = grad_act + conv_taps[tap] * ghe[4 - tap : 4 - tap + fine]
    grad_x, _ = jax.vjp(act_of, x.astype(F32), gain_in)[1](grad_act)
    input_grad = (gh + grad_x).astype(BF)

    conv_term = [jnp.sum(gh * act[tap : tap + fine].astype(F32), axis=0) for tap in range(taps)]
    slope = jax.vjp(lambda g: act_of(xe, g), jnp.broadcast_to(gain_in, xe.shape))[1](
        jnp.where(inside, jnp.ones(xe.shape, F32), 0.0)
    )[0]
    spread = jnp.zeros((fine, width), F32)
    for tap in range(taps):
        spread = spread + conv_taps[tap] * slope[tap : tap + fine]
    small = jnp.stack(conv_term + [jnp.sum(gh * spread, axis=0), gain_attn_term])
    lanes = width // nc
    mine = jnp.where(first_core, small[:, :lanes], small[:, lanes:])
    theirs = jnp.where(first_core, small[:, lanes:], small[:, :lanes])
    mine = mine + swap(theirs)

    cols = width // nx
    tail = small.shape[0] * lanes * 2 // cols
    slots = (tail + 15) // 16 * 16

    def to_wire(value):
        high = lax.reduce_precision(value, 8, 7)
        both = jnp.stack([high, value - high]).astype(BF).reshape(tail, cols)
        return jnp.pad(both, ((0, slots - tail), (0, 0)))

    def from_wire(parts):
        both = jnp.sum(parts[:, :tail].astype(F32), axis=0).reshape(2, small.shape[0], lanes)
        return both[0] + both[1]

    def with_small(blocks, value):
        block = to_wire(value)
        return jnp.concatenate(
            [blocks, jnp.broadcast_to(block[None], (blocks.shape[0],) + block.shape)], axis=1
        )

    q_each, kv_each = q_cols // nx, kv_cols // nx
    joined = jnp.concatenate(
        [
            grad_queries.reshape(pool, nx, q_each),
            gkv.reshape(pool, nx, kv_each),
            jnp.zeros((pool, nx, cols - q_each - kv_each), BF),
        ],
        axis=2,
    ).reshape(pool, width)
    right = jnp.where(first_core, joined, grad_y)
    right = jnp.concatenate([right, swap(jnp.where(first_core, grad_y, joined))], axis=0)
    right = jnp.transpose(right.reshape(nc * pool, nx, cols), (1, 0, 2))
    got = exchange(with_small(right, mine), "x")
    right = got[:, : nc * pool].reshape(-1, cols)
    mine = from_wire(got[:, nc * pool :])

    sums = contract_rows(left, right).astype(BF)
    got = exchange(with_small(sums.reshape(nz, width // nz, cols), mine), "z")
    each = width // nz
    sums = jnp.sum(got[:, :each].astype(F32), axis=0).astype(BF)
    mine = from_wire(got[:, each:])
    got = exchange(with_small(sums.reshape(ny, each // ny, cols), mine), "y")
    each = each // ny
    sums = jnp.sum(got[:, :each].astype(F32), axis=0)
    mine = from_wire(got[:, each:])
    theirs = swap(mine)
    small = jnp.concatenate(
        [jnp.where(first_core, mine, theirs), jnp.where(first_core, theirs, mine)], axis=1
    )
    rows = each // (nc * nx)
    sums = exchange(sums.reshape(nc * nx, rows, cols), ("core", "x")).reshape(nc, nx, rows, cols)

    def columns(part):
        return jnp.transpose(part, (1, 0, 2)).reshape(rows, -1)

    query_grad = columns(sums[0, :, :, :q_each])
    kv_grad = columns(sums[0, :, :, q_each : q_each + kv_each])
    out_weight_grad = columns(sums[1])
    return (
        mixed_out[None],
        input_grad[None],
        query_grad,
        kv_grad[:, :qk],
        kv_grad[:, qk:],
        out_weight_grad,
        small[:taps],
        small[taps],
        small[taps + 1],
    )


def solution(mesh):
    fine = Mesh(mesh.devices.reshape(8, 4, 2, 4), ("z", "y", "core", "x"))
    seq = ("z", "y", "core")
    placed = P("x", seq, None)
    rows = P(("z", "y", "core", "x"), None)
    in_specs = (placed, P(), P(), P(), P(), P(), P(), P(), placed)
    out_specs = (placed, placed, rows, rows, rows, rows, P(), P(), P())
    return jax.shard_map(shards, mesh=fine, in_specs=in_specs, out_specs=out_specs, check_vma=False)
```

time: 626 us -> 328 us (0.52)
  waiting for transfers between devices: 247 us -> 40.9 us
  blocking collectives: 101 us -> 56.2 us
  matrix products: 58.8 us -> 17.3 us
  starting transfers between devices: 70.2 us -> 56.3 us
  Pallas kernels: 0 us -> 12.5 us
    all_gather x2 -> x1, waiting for transfers between devices: 115 us -> 0.01 us  [shards(): left = lax.all_gather(left, 'x', axis=0, tiled=True)]
    unnamed x4 -> x1, waiting for transfers between devices: 87.6 us -> 0.02 us
    psum x1 -> x0, blocking collectives: 74.8 us -> none  [shards(): lax.psum((conv_term, gain_in_term, gain_attn_term), ('seq', 'batch'))]
    all_to_all x0 -> x3, blocking collectives: none -> 56.2 us  [exchange(): return lax.all_to_all(blocks, axis, 0, 0, tiled=True)]
    all_gather x2 -> x0, blocking collectives: 26.6 us -> none  [the longest x1 14.3 us: shards(): lax.all_gather(grad_y, 'batch', axis=0, tiled=True)]
    dot_general x6 -> x4, matrix products: 25.3 us -> 8.93 us  [contract_cols(): lax.dot_general(left, right, (((1,), (1,)), ((), ())), preferred_element_...]
    all_to_all x7 -> x5, starting transfers between devices: 53.3 us -> 39.2 us  [exchange(): return lax.all_to_all(blocks, axis, 0, 0, tiled=True)]
    dot_general x6 -> x4, matrix products: 19.2 us -> 5.84 us  [dot(): return jnp.dot(left, right, preferred_element_type=F32)]
  transfers between devices with their start and end apart: 14 -> 16, of which waited for: 7 -> 8; matrix products, arithmetic and copies ran while one was open for 17% -> 25% of each run, Pallas kernels for 0% -> 0%
where the time goes in v1:
time: 328 us; the launch traced here: 325 us
  local copies, waits for them, and re-layouts  79.3 us (24%)
  starting transfers between devices  56.3 us (17%)
  blocking collectives  56.2 us (17%)
  other arithmetic  47.6 us (15%)
  waiting for transfers between devices  40.9 us (12%)
  matrix products  17.3 us (5%)
  between operations  14.6 us (4%)
  Pallas kernels  12.5 us (4%)
    all_to_all x3, blocking collectives, exchange(): return lax.all_to_all(blocks, axis, 0, 0, tiled=True)  56.2 us
    all_to_all x5, starting transfers between devices, exchange(): return lax.all_to_all(blocks, axis, 0, 0, tiled=True)  39.2 us
    all_to_all x5, waiting for transfers between devices, exchange(): return lax.all_to_all(blocks, axis, 0, 0, tiled=True)  35.2 us
    pallas_call x1, Pallas kernels, attention(): pl.pallas_call(functools.partial(attention_kernel, scale, heads), out_sha...  12.5 us
    dot_general x4, matrix products, contract_cols(): lax.dot_general(left, right, (((1,), (1,)), ((), ())), preferred_element_...  8.93 us
    slice x4, local copies, waits for them, and re-layouts, shards(): grad_act = grad_act + conv_taps[tap] * ghe[4 - tap:4 - tap + fine]  8.56 us
    unnamed x69, local copies, waits for them, and re-layouts  8.4 us
    broadcast_in_dim x4, local copies, waits for them, and re-layouts, shards(): jnp.repeat(jnp.concatenate([before, grad_half, after], axis=0), 2, axis=0)  6.72 us
  transfers between devices with their start and end apart: 16, of which 8 were waited for; matrix products, arithmetic and copies ran while one was open for 25% of the time, Pallas kernels for 0%

profile of v1, /device:TPU:1, one launch (start us, length us, event | category | flops | bytes accessed | tf_op | source)
XLA Modules:
  0.0 324.7 jit_solution(6985416360739297546)
XLA Ops:
  7.2 1.5 slice_bitcast_fusion.2
  8.7 4.6 %collective-permute-start = (bf16[2,1536]{1,0:T(2,128)(2,1)}, bf16[2,1536]{1,0:T(2,128)(2,1)}, u32[]{:S(2)}, u32[]{:S(2)}) collective-permute-start(bf16[2,1536]{1,0:T(2,128)(2,1)} %get-tuple-element.49), channel_id=1, source_target_pairs={{0,4},{4,8},{8,12},{12,16},{16,20},{20,24},{24,28},{28,32},{32,36}... | collective-permute-start | bytes 18440 | tf_op jit(solution)/shard_map/ppermute | solution.py:159
  13.3 2.4 collective-permute-start.1
  16.9 1.6 collective-permute-done.1
  19.8 3.0 fusion.3
  22.8 2.0 fusion.36
  24.8 2.0 slice.212
  26.8 2.7 slice.213
  32.6 19.7 %all_to_all.40 = bf16[8,64,320]{2,1,0:T(8,128)(2,1)} all-to-all(bf16[8,64,320]{2,1,0:T(8,128)(2,1)S(1)} %broadcast_in_dim.88), channel_id=1, replica_groups=mesh['z'=8,'y'=4,'core'=2,'x'=4] {'z'}, dimensions={0} | all-to-all | bytes 655360 | tf_op jit(solution)/shard_map/all_to_all | solution.py:39
  52.3 1.9 copy.70
  55.2 24.2 %all_to_all.41 = bf16[4,512,320]{1,2,0:T(8,128)(2,1)} all-to-all(bf16[4,512,320]{1,2,0:T(8,128)(2,1)S(1)} %broadcast_in_dim.90), channel_id=1, replica_groups=mesh['z'=8,'y'=4,'core'=2,'x'=4] {'y'}, dimensions={0} | all-to-all | bytes 2621440 | tf_op jit(solution)/shard_map/all_to_all | solution.py:39
  79.5 2.6 copy.71
  82.0 2.6 copy.72
  84.6 1.8 collective-permute-start.2
  86.4 4.5 %convolution_convert_fusion.1.g_ref = bf16[64,1536]{1,0:T(8,128)(2,1)} fusion(bf16[1536,1536]{1,0:T(8,128)(2,1)} %param.16, bf16[1,64,1536]{2,1,0:T(8,128)(2,1)S(1)} %copy-done.14), kind=kOutput, calls=%fused_computation.6 | convolution fusion | flops 302088192 | bytes 5111808 | tf_op jit(solution)/shard_map/dot_general | solution.py:27
  92.3 2.5 copy.73.kv1_ref
  94.8 1.4 copy-done.1
  98.1 12.5 %shard_map.160 = (bf16[64,1536]{1,0:T(8,128)(2,1)S(1)}, bf16[64,1024]{1,0:T(8,128)(2,1)S(1)}, bf16[2048,320]{1,0:T(8,128)(2,1)S(1)}, bf16[2048,320]{1,0:T(8,128)(2,1)S(1)}) custom-call(bf16[64,1024]{1,0:T(8,128)(2,1)S(1)} %copy-done.5, bf16[64,1536]{1,0:T(8,128)(2,1)S(1)} %copy-done.4, bf16[2048,320]{1,0:T(8,128)(2,1)S(1)} %bitcast.70, ...), custom_call_target="tpu_custom_call" | custom-call | flops 4026531840 | bytes 10485760 | tf_op jit(solution)/shard_map/pallas_call | solution.py:110
  112.9 2.5 copy.74
  115.4 3.4 %collective-permute-done.3 = bf16[2048,320]{0,1:T(8,128)(2,1)} collective-permute-done((bf16[2048,320]{0,1:T(8,128)(2,1)}, bf16[2048,320]{0,1:T(8,128)(2,1)}, u32[]{:S(2)}, u32[]{:S(2)}) %collective-permute-start.3) | collective-permute-done | bytes 1310752 | tf_op jit(solution)/shard_map/ppermute | solution.py:35
  118.8 2.5 copy.75
  121.3 3.4 %add_convert_fusion = bf16[2048,320]{1,0:T(8,128)(2,1)} fusion(bf16[2048,320]{1,0:T(8,128)(2,1)} %copy.75, bf16[2048,320]{1,0:T(8,128)(2,1)} %copy-done.2), kind=kLoop, calls=%fused_computation | loop fusion | flops 2621440 | bytes 3932160 | tf_op jit(solution)/shard_map/convert_element_type | solution.py:192
  124.8 2.5 copy.76
  127.3 4.3 %all-to-all-start.2 = ((bf16[4,512,320]{1,2,0:T(8,128)(2,1)}), bf16[4,512,320]{1,2,0:T(8,128)(2,1)}, u32[]{:S(2)}, u32[]{:S(2)}) async-start(bf16[4,512,320]{1,2,0:T(8,128)(2,1)} %copy.76), calls=%async_computation.2 | async-start | bytes 2621440 | tf_op jit(solution)/shard_map/all_to_all | solution.py:39
  131.6 17.9 %all-to-all-done.2 = bf16[4,512,320]{1,2,0:T(8,128)(2,1)} async-done(((bf16[4,512,320]{1,2,0:T(8,128)(2,1)}), bf16[4,512,320]{1,2,0:T(8,128)(2,1)}, u32[]{:S(2)}, u32[]{:S(2)}) %all-to-all-start.2) | async-done | bytes 1310752 | tf_op jit(solution)/shard_map/all_to_all | solution.py:39
  149.5 2.3 reduce_sum.202
  151.9 1.9 copy.77
  153.7 4.1 %all-to-all-start.3 = ((bf16[8,64,320]{2,1,0:T(8,128)(2,1)}), bf16[8,64,320]{2,1,0:T(8,128)(2,1)}, u32[]{:S(2)}, u32[]{:S(2)}) async-start(bf16[8,64,320]{2,1,0:T(8,128)(2,1)} %bitcast.75), calls=%async_computation.3 | async-start | bytes 786432 | tf_op jit(solution)/shard_map/all_to_all | solution.py:39
  157.9 1.9 broadcast_select_fusion.1
  162.2 1.8 pad_maximum_fusion.3
  164.0 8.1 %all-to-all-done.3 = bf16[8,64,320]{2,1,0:T(8,128)(2,1)} async-done(((bf16[8,64,320]{2,1,0:T(8,128)(2,1)}), bf16[8,64,320]{2,1,0:T(8,128)(2,1)}, u32[]{:S(2)}, u32[]{:S(2)}) %all-to-all-start.3) | async-done | bytes 327712 | tf_op jit(solution)/shard_map/all_to_all | solution.py:39
  173.9 1.4 fusion.58
  177.4 1.8 multiply_reduce_fusion
  180.5 2.6 convert_element_type.137
  183.1 4.5 %fusion.26 = (f32[1536]{0:T(1024)S(1)}, f32[1536]{0:T(1024)S(1)}, f32[1536]{0:T(1024)S(1)}, f32[1536]{0:T(1024)S(1)}, f32[1536]{0:T(1024)S(1)}, /*index=5*/f32[1536]{0:T(1024)S(1)}) fusion(f32[128,1536]{1,0:T(8,128)} %convert_element_type.137, bf16[132,1536]{1,0:T(8,128)(2,1)} %copy-done.6, f32[132,1536]{1,0:T(8,128)} %get-tuple-element.41, ...), kind=kLoop, calls=%fused_computation.59 | loop fusion | flops 5102592 | bytes 6752256 | tf_op jit(solution)/shard_map/reduce_sum | solution.py:216
  191.8 1.5 stack.52
  195.3 1.8 bitcast_select_fusion.1
  198.5 1.4 convert_element_type.141
  201.8 12.3 %all_to_all.42 = bf16[4,160,384]{2,1,0:T(8,128)(2,1)S(1)} all-to-all(bf16[4,160,384]{2,1,0:T(8,128)(2,1)S(1)} %pad_maximum_fusion.1), channel_id=1, replica_groups=mesh['z'=8,'y'=4,'core'=2,'x'=4] {'x'}, dimensions={0} | all-to-all | bytes 983040 | tf_op jit(solution)/shard_map/all_to_all | solution.py:39
  215.5 1.4 add.215
  218.2 1.4 convert_element_type.144
  219.6 1.4 pad.11
  220.9 1.8 slice.274
  222.7 2.5 convolution_convert_fusion
  226.5 4.3 %all-to-all-start.5 = ((bf16[8,224,384]{2,1,0:T(8,128)(2,1)}), bf16[8,224,384]{2,1,0:T(8,128)(2,1)}, u32[]{:S(2)}, u32[]{:S(2)}) async-start(bf16[8,224,384]{2,1,0:T(8,128)(2,1)} %pad_maximum_fusion), calls=%async_computation.5 | async-start | bytes 2752512 | tf_op jit(solution)/shard_map/all_to_all | solution.py:39
  232.0 3.7 %collective-permute-start.4 = (bf16[1,1536]{1,0:T(2,128)(2,1)S(1)}, bf16[1,1536]{1,0:T(2,128)(2,1)S(1)}, u32[]{:S(2)}, u32[]{:S(2)}) collective-permute-start(bf16[1,1536]{1,0:T(2,128)(2,1)S(1)} %get-tuple-element.51), channel_id=1, source_target_pairs={{0,4},{4,8},{8,12},{12,16},{16,20},{20,24},{24,28},{28,32},{32,36}... | collective-permute-start | bytes 9224 | tf_op jit(solution)/shard_map/ppermute | solution.py:206
  235.7 2.1 collective-permute-start.5
  237.9 4.0 %fusion.2 = bf16[1,64,1536]{2,1,0:T(8,128)(2,1)} fusion(bf16[64,1536]{1,0:T(8,128)(2,1)S(1)} %get-tuple-element.13, bf16[1536,1536]{1,0:T(8,128)(2,1)} %param.16, f32[64,1536]{1,0:T(8,128)} %copy-done.7), kind=kOutput, calls=%fused_computation.7 | convolution fusion | flops 302284800 | bytes 5505024 | tf_op jit(solution)/shard_map/dot_general | solution.py:31
  244.7 2.6 slice.219
  247.3 2.2 broadcast_in_dim.95
  249.5 2.6 slice.222
  253.2 2.6 slice.225
  255.8 2.2 broadcast_in_dim.94
  258.0 2.6 convert_element_type.139
  260.6 4.1 %fusion.41 = (f32[128]{0:T(128)S(1)}, f32[128,1536]{1,0:T(8,128)}) fusion(bf16[1,128,1536]{2,1,0:T(8,128)(2,1)S(1)} %copy-done.10, f32[1536]{0:T(1024)} %param.10, f32[128]{0:T(128)} %fusion.71, f32[128,1536]{1,0:T(8,128)} %slice.225, f32[1536]{0:T(1024)} %copy-done.23, f32[132,1536]{1,0:T(8,128)} %convert_element_type.139, f32[1536]{0:T(1024)} %copy-done.24, ...), kind=kLoop, calls=%fused_computation.74 | loop fusion | flops 6684544 | bytes 5149696 | tf_op jit(solution)/shard_map/transpose(jvp())/reduce_sum | solution.py:167
  264.8 2.2 all-to-all-done.5
  268.6 1.4 add.217
  271.3 1.4 convert_element_type.146
  273.4 1.4 slice_reduce_fusion
  275.6 22.8 %all-to-all-start.6 = ((bf16[4,80,384]{2,1,0:T(8,128)(2,1)}), bf16[4,80,384]{2,1,0:T(8,128)(2,1)}, u32[]{:S(2)}, u32[]{:S(2)}) async-start(bf16[4,80,384]{2,1,0:T(8,128)(2,1)} %pad_maximum_fusion.5), calls=%async_computation.6 | async-start | bytes 491520 | tf_op jit(solution)/shard_map/all_to_all | solution.py:39
  298.4 2.3 fusion.55
  300.7 3.2 all-to-all-done.6
  306.5 3.8 %all-to-all-start.7 = ((f32[8,6,384]{2,1,0:T(8,128)}), f32[8,6,384]{2,1,0:T(8,128)S(1)}, u32[]{:S(2)}, u32[]{:S(2)}) async-start(f32[8,6,384]{2,1,0:T(8,128)} %reshape.253), calls=%async_computation.7 | async-start | bytes 196608 | tf_op jit(solution)/shard_map/all_to_all | solution.py:39
  311.6 3.7 %all-to-all-done.7 = f32[8,6,384]{2,1,0:T(8,128)S(1)} async-done(((f32[8,6,384]{2,1,0:T(8,128)}), f32[8,6,384]{2,1,0:T(8,128)S(1)}, u32[]{:S(2)}, u32[]{:S(2)}) %all-to-all-start.7) | async-done | bytes 73760 | tf_op jit(solution)/shard_map/all_to_all | solution.py:39
  (159 shorter events, 49.2 us)
Async XLA Ops:
  7.2 83.8 %copy-start = (bf16[1536,1024]{1,0:T(8,128)(2,1)S(1)}, bf16[1536,1024]{1,0:T(8,128)(2,1)}, u32[]{:S(2)}) copy-start(bf16[1536,1024]{1,0:T(8,128)(2,1)} %param.13) | copy-start | bytes 9437188
  7.2 15.6 %copy-start.9 = (bf16[1,128,1536]{2,1,0:T(8,128)(2,1)S(1)}, bf16[1,128,1536]{2,1,0:T(8,128)(2,1)}, u32[]{:S(2)}) copy-start(bf16[1,128,1536]{2,1,0:T(8,128)(2,1)} %param.9) | copy-start | bytes 1179652
  8.7 8.2 %collective-permute-start = (bf16[2,1536]{1,0:T(2,128)(2,1)}, bf16[2,1536]{1,0:T(2,128)(2,1)}, u32[]{:S(2)}, u32[]{:S(2)}) collective-permute-start(bf16[2,1536]{1,0:T(2,128)(2,1)} %get-tuple-element.49), channel_id=1, source_target_pairs={{0,4},{4,8},{8,12},{12,16},{16,20},{20,24},{24,28},{28,32},{32,36}... | collective-permute-start | bytes 18440 | tf_op jit(solution)/shard_map/ppermute | solution.py:159
  13.3 5.3 %collective-permute-start.1 = (bf16[2,1536]{1,0:T(2,128)(2,1)}, bf16[2,1536]{1,0:T(2,128)(2,1)}, u32[]{:S(2)}, u32[]{:S(2)}) collective-permute-start(bf16[2,1536]{1,0:T(2,128)(2,1)} %get-tuple-element.50), channel_id=1, source_target_pairs={{4,0},{8,4},{12,8},{16,12},{20,16},{24,20},{28,24},{32,28},{36,32}... | collective-permute-start | bytes 18440 | tf_op jit(solution)/shard_map/ppermute | solution.py:160
  16.9 5.9 %copy-start.20 = (f32[1536]{0:T(1024)}, f32[1536]{0:T(1024)S(1)}, u32[]{:S(2)}) copy-start(f32[1536]{0:T(1024)S(1)} %get-tuple-element.28) | copy-start | bytes 18436
  16.9 7.9 %copy-start.22 = (f32[1536]{0:T(1024)}, f32[1536]{0:T(1024)S(1)}, u32[]{:S(2)}) copy-start(f32[1536]{0:T(1024)S(1)} %get-tuple-element.29) | copy-start | bytes 18436
  16.9 7.9 %copy-start.23 = (f32[1536]{0:T(1024)}, f32[1536]{0:T(1024)S(1)}, u32[]{:S(2)}) copy-start(f32[1536]{0:T(1024)S(1)} %get-tuple-element.30) | copy-start | bytes 18436
  16.9 7.9 %copy-start.24 = (f32[1536]{0:T(1024)}, f32[1536]{0:T(1024)S(1)}, u32[]{:S(2)}) copy-start(f32[1536]{0:T(1024)S(1)} %get-tuple-element.31) | copy-start | bytes 18436
  22.8 2.0 copy-start.6
  24.8 7.1 %copy-start.19 = (f32[1536]{0:T(1024)S(1)}, f32[1536]{0:T(1024)}, u32[]{:S(2)}) copy-start(f32[1536]{0:T(1024)} %param.12) | copy-start | bytes 18436
  29.5 2.5 copy-start.12
  29.6 2.8 copy-start.16
  30.8 21.5 %copy-start.7 = (f32[64,1536]{1,0:T(8,128)}, f32[64,1536]{1,0:T(8,128)S(1)}, u32[]{:S(2)}) copy-start(f32[64,1536]{1,0:T(8,128)S(1)} %get-tuple-element.37) | copy-start | bytes 1179652
  30.8 21.5 %copy-start.30 = (f32[64]{0:T(128)}, f32[64]{0:T(128)S(1)}, u32[]{:S(2)}) copy-start(f32[64]{0:T(128)S(1)} %get-tuple-element.36) | copy-start | bytes 772
  31.4 0.5 copy-start.27
  82.0 4.4 %copy-start.14 = (bf16[1,64,1536]{2,1,0:T(8,128)(2,1)S(1)}, bf16[1,64,1536]{2,1,0:T(8,128)(2,1)}, u32[]{:S(2)}) copy-start(bf16[1,64,1536]{2,1,0:T(8,128)(2,1)} %param.17) | copy-start | bytes 589828
  84.6 7.7 %collective-permute-start.2 = (bf16[2048,320]{0,1:T(8,128)(2,1)}, bf16[2048,320]{0,1:T(8,128)(2,1)}, u32[]{:S(2)}, u32[]{:S(2)}) collective-permute-start(bf16[2048,320]{0,1:T(8,128)(2,1)} %copy.72), channel_id=1, source_target_pairs={{0,4},{4,0},{1,5},{5,1},{2,6},{6,2},{3,7},{7,3},{8,12},{12,8},{9,1... | collective-permute-start | bytes 3932168 | tf_op jit(solution)/shard_map/ppermute | solution.py:35
  94.8 1.4 copy-start.1
  96.3 0.9 copy-start.4
  97.2 0.9 copy-start.5
  110.6 1.2 copy-start.2
  111.7 1.1 copy-start.3
  115.4 3.4 %collective-permute-start.3 = (bf16[2048,320]{0,1:T(8,128)(2,1)}, bf16[2048,320]{0,1:T(8,128)(2,1)}, u32[]{:S(2)}, u32[]{:S(2)}) collective-permute-start(bf16[2048,320]{0,1:T(8,128)(2,1)} %copy.74), channel_id=1, source_target_pairs={{0,4},{4,0},{1,5},{5,1},{2,6},{6,2},{3,7},{7,3},{8,12},{12,8},{9,1... | collective-permute-start | bytes 3932168 | tf_op jit(solution)/shard_map/ppermute | solution.py:35
  127.3 22.2 %all-to-all-start.2 = ((bf16[4,512,320]{1,2,0:T(8,128)(2,1)}), bf16[4,512,320]{1,2,0:T(8,128)(2,1)}, u32[]{:S(2)}, u32[]{:S(2)}) async-start(bf16[4,512,320]{1,2,0:T(8,128)(2,1)} %copy.76), calls=%async_computation.2 | async-start | bytes 2621440 | tf_op jit(solution)/shard_map/all_to_all | solution.py:39
  131.6 26.3 %copy-start.28 = (f32[64]{0:T(128)S(1)}, f32[64]{0:T(128)}, u32[]{:S(2)}) copy-start(f32[64]{0:T(128)} %copy-done.27) | copy-start | bytes 772
  153.7 18.4 %all-to-all-start.3 = ((bf16[8,64,320]{2,1,0:T(8,128)(2,1)}), bf16[8,64,320]{2,1,0:T(8,128)(2,1)}, u32[]{:S(2)}, u32[]{:S(2)}) async-start(bf16[8,64,320]{2,1,0:T(8,128)(2,1)} %bitcast.75), calls=%async_computation.3 | async-start | bytes 786432 | tf_op jit(solution)/shard_map/all_to_all | solution.py:39
  157.8 64.9 %all-gather.2.cloned.1.call-start = ((), (), s32[]{:S(2)}) async-start(), calls=%async_computation.8 | async-start | bytes 1966080 | tf_op jit(solution)/shard_map/all_gather | solution.py:190
  159.8 2.4 collective-permute-start.6
  173.9 2.7 copy-start.17
  173.9 2.7 copy-start.18
  173.9 3.5 %copy-start.8 = (f32[64,1536]{1,0:T(8,128)S(1)}, f32[64,1536]{1,0:T(8,128)}, u32[]{:S(2)}) copy-start(f32[64,1536]{1,0:T(8,128)} %copy-done.7) | copy-start | bytes 1179652
  177.4 1.8 copy-start.31
  177.4 1.8 copy-start.15
  177.4 1.8 copy-start.32
  179.4 3.7 %copy-start.21 = (f32[1536]{0:T(1024)S(1)}, f32[1536]{0:T(1024)}, u32[]{:S(2)}) copy-start(f32[1536]{0:T(1024)} %copy-done.20) | copy-start | bytes 18436
  183.1 8.1 %copy-start.26 = (f32[1536]{0:T(1024)S(1)}, f32[1536]{0:T(1024)}, u32[]{:S(2)}) copy-start(f32[1536]{0:T(1024)} %get-tuple-element.22) | copy-start | bytes 18436
  194.0 3.1 collective-permute-start.8
  197.1 3.5 %collective-permute-start.7 = (bf16[64,1536]{1,0:T(8,128)(2,1)}, bf16[64,1536]{1,0:T(8,128)(2,1)}, u32[]{:S(2)}, u32[]{:S(2)}) collective-permute-start(bf16[64,1536]{1,0:T(8,128)(2,1)} %get-tuple-element.46), channel_id=1, source_target_pairs={{0,4},{4,0},{1,5},{5,1},{2,6},{6,2},{3,7},{7,3},{8,12},{12,8},{9,1... | collective-permute-start | bytes 589832 | tf_op jit(solution)/shard_map/ppermute | solution.py:35
  214.1 0.8 copy-start.13
  222.7 2.5 copy-start.25
  226.5 40.5 %all-to-all-start.5 = ((bf16[8,224,384]{2,1,0:T(8,128)(2,1)}), bf16[8,224,384]{2,1,0:T(8,128)(2,1)}, u32[]{:S(2)}, u32[]{:S(2)}) async-start(bf16[8,224,384]{2,1,0:T(8,128)(2,1)} %pad_maximum_fusion), calls=%async_computation.5 | async-start | bytes 2752512 | tf_op jit(solution)/shard_map/all_to_all | solution.py:39
  232.0 9.9 %collective-permute-start.4 = (bf16[1,1536]{1,0:T(2,128)(2,1)S(1)}, bf16[1,1536]{1,0:T(2,128)(2,1)S(1)}, u32[]{:S(2)}, u32[]{:S(2)}) collective-permute-start(bf16[1,1536]{1,0:T(2,128)(2,1)S(1)} %get-tuple-element.51), channel_id=1, source_target_pairs={{0,4},{4,8},{8,12},{12,16},{16,20},{20,24},{24,28},{28,32},{32,36}... | collective-permute-start | bytes 9224 | tf_op jit(solution)/shard_map/ppermute | solution.py:206
  235.7 6.2 %collective-permute-start.5 = (bf16[1,1536]{1,0:T(2,128)(2,1)S(1)}, bf16[1,1536]{1,0:T(2,128)(2,1)S(1)}, u32[]{:S(2)}, u32[]{:S(2)}) collective-permute-start(bf16[1,1536]{1,0:T(2,128)(2,1)S(1)} %get-tuple-element.52), channel_id=1, source_target_pairs={{4,0},{8,4},{12,8},{16,12},{20,16},{24,20},{28,24},{32,28},{36,32}... | collective-permute-start | bytes 9224 | tf_op jit(solution)/shard_map/ppermute | solution.py:207
  242.0 0.8 copy-start.11
  255.8 4.9 %copy-start.10 = (bf16[1,128,1536]{2,1,0:T(8,128)(2,1)S(1)}, bf16[1,128,1536]{2,1,0:T(8,128)(2,1)}, u32[]{:S(2)}) copy-start(bf16[1,128,1536]{2,1,0:T(8,128)(2,1)} %param.9) | copy-start | bytes 1179652
  260.6 4.1 %copy-start.33 = (f32[128]{0:T(128)S(1)}, f32[128]{0:T(128)}, u32[]{:S(2)}) copy-start(f32[128]{0:T(128)} %get-tuple-element.47) | copy-start | bytes 1540
  264.7 33.6 %copy-start.29 = (f32[128]{0:T(128)S(1)}, f32[128]{0:T(128)}, u32[]{:S(2)}) copy-start(f32[128]{0:T(128)} %fusion.71) | copy-start | bytes 1540
  275.6 28.3 %all-to-all-start.6 = ((bf16[4,80,384]{2,1,0:T(8,128)(2,1)}), bf16[4,80,384]{2,1,0:T(8,128)(2,1)}, u32[]{:S(2)}, u32[]{:S(2)}) async-start(bf16[4,80,384]{2,1,0:T(8,128)(2,1)} %pad_maximum_fusion.5), calls=%async_computation.6 | async-start | bytes 491520 | tf_op jit(solution)/shard_map/all_to_all | solution.py:39
  304.9 5.5 %collective-permute-start.9 = (f32[7,768]{1,0:T(8,128)S(1)}, f32[7,768]{1,0:T(8,128)S(1)}, u32[]{:S(2)}, u32[]{:S(2)}) collective-permute-start(f32[7,768]{1,0:T(8,128)S(1)} %add.219), channel_id=1, source_target_pairs={{0,4},{4,0},{1,5},{5,1},{2,6},{6,2},{3,7},{7,3},{8,12},{12,8},{9,1... | collective-permute-start | bytes 64520 | tf_op jit(solution)/shard_map/ppermute | solution.py:35
  306.5 8.8 %all-to-all-start.7 = ((f32[8,6,384]{2,1,0:T(8,128)}), f32[8,6,384]{2,1,0:T(8,128)S(1)}, u32[]{:S(2)}, u32[]{:S(2)}) async-start(f32[8,6,384]{2,1,0:T(8,128)} %reshape.253), calls=%async_computation.7 | async-start | bytes 196608 | tf_op jit(solution)/shard_map/all_to_all | solution.py:39
Sparse Core Ops, SparseCore 0:
  164.1 28.2 all-gather.1

commit v2 on v1

v2 whole, which is shorter than its diff:
```python
import functools
import math

import jax
import jax.numpy as jnp
from jax import lax
from jax.experimental import pallas as pl
from jax.experimental.pallas import tpu as pltpu
from jax.sharding import Mesh
from jax.sharding import PartitionSpec as P

EPS = 1e-06
F32 = jnp.float32
BF = jnp.bfloat16
CURVE = math.sqrt(2.0 / math.pi)
CUBIC = 0.044715


def contract_rows(left, right):
    return lax.dot_general(left, right, (((0,), (0,)), ((), ())), preferred_element_type=F32)


def contract_cols(left, right):
    return lax.dot_general(left, right, (((1,), (1,)), ((), ())), preferred_element_type=F32)


def dot(left, right):
    return jnp.dot(left, right, preferred_element_type=F32)


def swap(block):
    return lax.ppermute(block, "core", [(0, 1), (1, 0)])


def exchange(blocks, axis):
    return lax.all_to_all(blocks, axis, 0, 0, tiled=True)


def call(kernel, out_shape, scratch, flops, *args):
    sizes = [a.size * a.dtype.itemsize for a in args]
    sizes += [math.prod(o.shape) * o.dtype.itemsize for o in out_shape]
    return pl.pallas_call(
        kernel,
        out_shape=out_shape,
        scratch_shapes=scratch,
        compiler_params=pltpu.CompilerParams(vmem_limit_bytes=48 * 2**20),
        cost_estimate=pl.CostEstimate(flops=flops, bytes_accessed=sum(sizes), transcendentals=0),
    )(*args)


def shape(*dims, dtype=BF):
    return jax.ShapeDtypeStruct(dims, dtype)


def pack(keys, values):
    n = keys.shape[0]
    lanes = keys.shape[1]
    rest = jnp.concatenate([values[: n // 2, lanes:], values[n // 2 :, lanes:]], axis=1)
    return jnp.concatenate([keys, values[:, :lanes], rest], axis=0)


def unpack(packed):
    lanes = packed.shape[1]
    n = packed.shape[0] * 2 // 5
    rest = packed[2 * n :]
    rest = jnp.concatenate([rest[:, : lanes // 2], rest[:, lanes // 2 :]], axis=0)
    return packed[:n], jnp.concatenate([packed[n : 2 * n], rest], axis=1)


def front_kernel(
    inside_ref, x_ref, low_ref, high_ref, gain_in_ref, taps_ref, gain_attn_ref, kw_ref, vw_ref,
    kv_ref, normed_ref, pooled_ref, pairs_ref, spread_ref, act, slope, plain,
):
    fine, width = x_ref.shape
    pool = fine // 2
    taps = taps_ref.shape[0]
    gain = gain_in_ref[...]

    def rows_of(x, keep):
        raw = x * lax.rsqrt(jnp.mean(x * x, axis=-1, keepdims=True) + EPS)
        u = raw * gain
        t = jnp.tanh(CURVE * (u + CUBIC * (u * u * u)))
        a = u * (0.5 * (1.0 + t))
        slant = 0.5 * (1.0 + t) + 0.5 * u * (1.0 - t * t) * (CURVE * (1.0 + 3.0 * CUBIC * u * u))
        g = slant * raw
        if keep is not None:
            a, g = jnp.where(keep, a, 0.0), jnp.where(keep, g, 0.0)
        return a.astype(BF).astype(F32), g

    def put(ref, at, value):
        for c in range(width // 128):
            ref[c, at, :] = value[:, c * 128 : (c + 1) * 128]

    def fill(at, x, keep):
        a, g = rows_of(x, keep)
        put(act, at, a)
        put(slope, at, g)

    fill(slice(0, 2), low_ref[...].astype(F32), inside_ref[0] > 0)
    fill(slice(fine + 2, fine + 4), high_ref[...].astype(F32), inside_ref[1] > 0)
    step = 32
    for i in range(0, fine, step):
        rows = x_ref[i : i + step, :].astype(F32)
        put(plain, slice(i, i + step), rows)
        fill(slice(2 + i, 2 + i + step), rows, None)

    for c in range(width // 128):
        at = slice(c * 128, (c + 1) * 128)
        a = [act[c, pl.ds(m, pool, stride=2), :] for m in range(taps + 1)]
        g = [slope[c, pl.ds(m, pool, stride=2), :] for m in range(taps + 1)]
        conv = jnp.zeros((pool, 128), F32)
        spread = jnp.zeros((pool, 128), F32)
        for k in range(taps):
            pair = a[k] + a[k + 1]
            pairs_ref[k, :, at] = pair
            tap = taps_ref[k : k + 1, at]
            conv = conv + tap * pair
            spread = spread + tap * (g[k] + g[k + 1])
        spread_ref[:, at] = spread
        whole = plain[c, pl.ds(0, pool, stride=2), :] + plain[c, pl.ds(1, pool, stride=2), :]
        pooled_ref[:, at] = 0.5 * (whole + conv)
    pooled = pooled_ref[...]
    scale = lax.rsqrt(jnp.mean(pooled * pooled, axis=-1, keepdims=True) + EPS)
    normed = (pooled * scale * gain_attn_ref[...]).astype(BF)
    normed_ref[...] = normed
    kv = pack(dot(normed, kw_ref[...]), dot(normed, vw_ref[...])).astype(BF)
    for i in range(kv_ref.shape[0]):
        kv_ref[i] = kv


def attention_kernel(scale, heads, q_ref, g_ref, kv0_ref, kv1_ref,
                     mixed_ref, gq_ref, gkv0_ref, gkv1_ref, s_ref, gw_ref, v_ref):
    rows = q_ref.shape[0]
    qk = q_ref.shape[1] // heads
    vd = g_ref.shape[1] // heads
    q = jnp.concatenate([q_ref[:, h * qk : (h + 1) * qk] for h in range(heads)], axis=0)
    g = jnp.concatenate([g_ref[:, h * vd : (h + 1) * vd] for h in range(heads)], axis=0)
    total = rows * heads
    per, pieces, packed, _ = kv0_ref.shape
    each = packed * 2 // 5
    block = pieces * each

    def sweep(body, carry):
        for part, (kv, gkv) in enumerate(((kv0_ref, gkv0_ref), (kv1_ref, gkv1_ref))):
            def step(i, c, part=part, kv=kv, gkv=gkv):
                here = pl.ds(pl.multiple_of((part * per + i) * block, block), block)
                return body(c, kv, gkv, i, here)
            carry = lax.fori_loop(0, per, step, carry)
        return carry

    def keys_of(kv, i):
        return jnp.concatenate([kv[i, j, :each] for j in range(pieces)], axis=0)

    def first(peak, kv, gkv, i, here):
        s = contract_cols(keys_of(kv, i), q) * scale
        s_ref[here, :] = s
        return jnp.maximum(peak, jnp.max(s, axis=0, keepdims=True))

    peak = sweep(first, jnp.full((1, total), -jnp.inf, F32))

    def second(carry, kv, gkv, i, here):
        norm, dot_sum, out = carry
        v = jnp.concatenate([unpack(kv[i, j])[1] for j in range(pieces)], axis=0)
        e = jnp.exp(s_ref[here, :] - peak)
        s_ref[here, :] = e
        gw = contract_cols(v, g)
        gw_ref[here, :] = gw
        return (norm + jnp.sum(e, axis=0, keepdims=True),
                dot_sum + jnp.sum(e * gw, axis=0, keepdims=True),
                out + contract_rows(v, e.astype(BF)))

    zero = jnp.zeros((1, total), F32)
    norm, dot_sum, out = sweep(second, (zero, zero, jnp.zeros((vd, total), F32)))
    inv = 1.0 / norm
    delta = dot_sum * inv
    mixed = jnp.transpose(out * inv).astype(BF)
    for h in range(heads):
        mixed_ref[:, h * vd : (h + 1) * vd] = mixed[h * rows : (h + 1) * rows]

    def third(gq, kv, gkv, i, here):
        w = s_ref[here, :] * inv
        ds = (w * (gw_ref[here, :] - delta) * scale).astype(BF)
        gk = dot(ds, q).astype(BF)
        gv = dot(w.astype(BF), g).astype(BF)
        for j in range(pieces):
            at = slice(j * each, (j + 1) * each)
            gkv[i, j] = pack(gk[at], gv[at])
        return gq + contract_rows(keys_of(kv, i), ds)

    gq = jnp.transpose(sweep(third, jnp.zeros((qk, total), F32))).astype(BF)
    for h in range(heads):
        gq_ref[:, h * qk : (h + 1) * qk] = gq[h * rows : (h + 1) * rows]


def attention(q, g, kv0, kv1, heads):
    rows, width = q.shape
    vd = g.shape[1] // heads
    pieces, packed = kv0.shape[1:3]
    keys = 2 * kv0.shape[0] * pieces * packed * 2 // 5
    scale = 1.0 / math.sqrt(width // heads)
    return call(
        functools.partial(attention_kernel, scale, heads),
        (shape(*g.shape), shape(*q.shape), shape(*kv0.shape), shape(*kv1.shape)),
        [pltpu.VMEM((keys, rows * heads), F32), pltpu.VMEM((keys, rows * heads), F32),
         pltpu.VMEM((8, vd), BF)],
        2 * keys * rows * (3 * width + 3 * g.shape[1]),
        q, g, kv0, kv1,
    )


def back_kernel(gkv_ref, part_ref, kw_ref, vw_ref, pooled_ref, gain_ref, gy_ref, pairs_ref,
                spread_ref, half_ref, small_ref):
    gk, gv = unpack(gkv_ref[...])
    grad = part_ref[...] + contract_cols(gk, kw_ref[...]) + contract_cols(gv, vw_ref[...])
    pooled = pooled_ref[...]
    gain = gain_ref[...]
    scale = lax.rsqrt(jnp.mean(pooled * pooled, axis=-1, keepdims=True) + EPS)
    raw = pooled * scale
    inner = grad * gain
    along = jnp.mean(raw * inner, axis=-1, keepdims=True)
    grad_pool = gy_ref[...].astype(F32) + scale * (inner - raw * along)
    half = (grad_pool * 0.5).astype(BF)
    half_ref[...] = half
    h = half.astype(F32)
    taps = pairs_ref.shape[0]
    for k in range(taps):
        small_ref[k : k + 1, :] = jnp.sum(h * pairs_ref[k], axis=0, keepdims=True)
    small_ref[taps : taps + 1, :] = jnp.sum(h * spread_ref[...], axis=0, keepdims=True)
    small_ref[taps + 1 : taps + 2, :] = jnp.sum(grad * raw, axis=0, keepdims=True)
    small_ref[taps + 2 :, :] = jnp.zeros((small_ref.shape[0] - taps - 2, h.shape[1]), F32)


def input_kernel(x_ref, gain_ref, taps_ref, half_ref, before_ref, after_ref, out_ref, held, acts, twice):
    fine, width = x_ref.shape
    pool = fine // 2
    held[0:8, :] = jnp.broadcast_to(before_ref[...].astype(F32), (8, width))
    held[8 : pool + 8, :] = half_ref[...].astype(F32)
    held[pool + 8 :, :] = jnp.broadcast_to(after_ref[...].astype(F32), (8, width))
    t = [taps_ref[k : k + 1, :] for k in range(5)]
    left = held[7 : pool + 7, :]
    mid = held[8 : pool + 8, :]
    right = held[9 : pool + 9, :]
    even = t[0] * right + (t[1] + t[2]) * mid + (t[3] + t[4]) * left
    odd = (t[0] + t[1]) * right + (t[2] + t[3]) * mid + t[4] * left
    tiles = [slice(c * 128, (c + 1) * 128) for c in range(width // 128)]
    for c, at in enumerate(tiles):
        acts[c, pl.ds(0, pool, stride=2), :] = even[:, at]
        acts[c, pl.ds(1, pool, stride=2), :] = odd[:, at]
        twice[c, pl.ds(0, pool, stride=2), :] = mid[:, at]
        twice[c, pl.ds(1, pool, stride=2), :] = mid[:, at]
    gain = gain_ref[...]
    step = 32
    for i in range(0, fine, step):
        x = x_ref[i : i + step, :].astype(F32)
        scale = lax.rsqrt(jnp.mean(x * x, axis=-1, keepdims=True) + EPS)
        raw = x * scale
        u = raw * gain
        th = jnp.tanh(CURVE * (u + CUBIC * (u * u * u)))
        slant = 0.5 * (1.0 + th) + 0.5 * u * (1.0 - th * th) * (CURVE * (1.0 + 3.0 * CUBIC * u * u))
        grad = jnp.concatenate([acts[c, i : i + step, :] for c in range(width // 128)], axis=1)
        inner = grad * slant * gain
        along = jnp.mean(raw * inner, axis=-1, keepdims=True)
        through = jnp.concatenate([twice[c, i : i + step, :] for c in range(width // 128)], axis=1)
        out_ref[i : i + step, :] = (through + scale * (inner - raw * along)).astype(BF)


def pick_kernel(first_ref, target_ref, e_ref, m_ref, left_ref, sums_ref):
    keep, width = left_ref.shape[0], e_ref.shape[1]
    rows = lax.broadcasted_iota(jnp.int32, (keep, width), 0)
    hot = (rows == target_ref[...]).astype(F32).astype(BF)

    def work(left, right):
        picked = contract_cols(hot, left[...]).astype(BF)
        left_ref[...] = picked
        sums_ref[...] = dot(picked, right[...]).astype(BF)

    @pl.when(first_ref[0] > 0)
    def _():
        work(e_ref, m_ref)

    @pl.when(first_ref[0] == 0)
    def _():
        work(m_ref, e_ref)


def late_kernel(q_cols, first_ref, left_ref, sums_ref, gkv_ref, small_ref, out_ref):
    parts = [unpack(gkv_ref[i]) for i in range(gkv_ref.shape[0])]
    keys = jnp.concatenate([k for k, _ in parts], axis=0)
    values = jnp.concatenate([v for _, v in parts], axis=0)
    left = left_ref[...]
    late = (dot(left, keys).astype(BF), dot(left, values).astype(BF))
    ny, slots, width = out_ref.shape
    each = left.shape[0] // ny
    small = jnp.concatenate(
        [small_ref[...], jnp.zeros((slots - each - small_ref.shape[0], width), F32)], axis=0
    ).astype(BF)
    first = first_ref[0] > 0
    mid = q_cols + keys.shape[1]
    end = mid + values.shape[1]
    for i in range(ny):
        at = slice(i * each, (i + 1) * each)
        out_ref[i, :each, :] = sums_ref[at, :]
        out_ref[i, each:, :] = small

    @pl.when(first)
    def _():
        for i in range(ny):
            at = slice(i * each, (i + 1) * each)
            out_ref[i, :each, q_cols:mid] = late[0][at]
            out_ref[i, :each, mid:end] = late[1][at]


def turn_kernel(tail, got_ref, out_ref, held):
    ny, slots, width = got_ref.shape
    nz, rows = out_ref.shape[:2]
    each = held.shape[0] - 16
    for c in range(0, width, 512):
        at = slice(c, c + 512)
        total = got_ref[0, :, at].astype(F32)
        for i in range(1, ny):
            total = total + got_ref[i, :, at].astype(F32)
        held[:, at] = total[: each + 16]
    part = each // nz
    small = held[each : each + tail, :]
    for i in range(nz):
        rest = jnp.zeros((rows - part - tail, width), F32)
        out_ref[i] = jnp.concatenate(
            [held[i * part : (i + 1) * part, :], small, rest], axis=0
        ).astype(BF)


def shards(
    windows,
    gain_in,
    conv_taps,
    gain_attn,
    query_weight,
    key_weight,
    value_weight,
    out_weight,
    out_cotangent,
):
    seq = ("z", "y", "core")
    nz, ny, nx, nc = (lax.axis_size(a) for a in ("z", "y", "x", "core"))
    count = nz * ny * nc
    place = lax.axis_index(seq)
    first_core = lax.axis_index("core") == 0
    first = first_core.astype(jnp.int32).reshape(1)
    x = windows[0]
    fine, width = x.shape
    pool = fine // 2
    taps = conv_taps.shape[0]
    qk = key_weight.shape[1]
    vd = value_weight.shape[1]
    q_cols = query_weight.shape[1]
    heads = q_cols // qk
    grad_y = out_cotangent[0]
    gain_in = gain_in.reshape(1, width)
    gain_attn = gain_attn.reshape(1, width)
    packed = pool * (qk + vd) // qk

    up = [(i, i + 1) for i in range(count - 1)]
    down = [(b, a) for a, b in up]
    low = lax.ppermute(x[fine - 2 :], seq, up)
    high = lax.ppermute(x[:2], seq, down)
    inside = jnp.stack([place > 0, place < count - 1]).astype(jnp.int32)
    smem = pl.BlockSpec(memory_space=pltpu.SMEM)
    vmem = pl.BlockSpec(memory_space=pltpu.VMEM)

    def flagged(kernel, out_shape, scratch, flops, flag, *args):
        return pl.pallas_call(
            kernel,
            out_shape=out_shape,
            in_specs=[smem] + [vmem] * len(args),
            scratch_shapes=scratch,
            compiler_params=pltpu.CompilerParams(vmem_limit_bytes=48 * 2**20),
            cost_estimate=pl.CostEstimate(
                flops=flops, bytes_accessed=4 * width * width, transcendentals=0
            ),
        )(flag, *args)

    kv, normed, pooled, pairs, spread = flagged(
        front_kernel,
        (shape(nz, packed, qk), shape(pool, width), shape(pool, width, dtype=F32),
         shape(taps, pool, width, dtype=F32), shape(pool, width, dtype=F32)),
        [pltpu.VMEM((width // 128, n, 128), F32) for n in (fine + 4, fine + 4, fine)],
        2 * pool * width * (qk + vd),
        inside, x, low, high, gain_in, conv_taps, gain_attn, key_weight, value_weight,
    )

    def ours_theirs(ours, theirs):
        return (jnp.where(first_core, ours, theirs),
                swap(jnp.where(first_core, theirs, ours)))

    kv = exchange(kv, "z")
    early = lax.all_gather(
        jnp.concatenate(ours_theirs(normed, grad_y), axis=0), "x", axis=0, tiled=True
    )
    queries = dot(normed, query_weight).astype(BF)
    grad_mixed = contract_cols(grad_y, out_weight).astype(BF)
    kv, queries, grad_mixed = lax.optimization_barrier((kv, queries, grad_mixed))
    kv_own = exchange(jnp.broadcast_to(kv[None], (ny,) + kv.shape), "y")
    kv_other = swap(kv_own)
    mixed, grad_queries, gkv_own, gkv_other = attention(
        queries, grad_mixed, kv_own, kv_other, heads
    )

    gq_wide = jnp.pad(grad_queries, ((0, 0), (0, width - q_cols)))
    later = lax.all_gather(
        jnp.concatenate(ours_theirs(gq_wide, mixed), axis=0), "x", axis=0, tiled=True
    )

    gkv = (gkv_own.astype(F32) + swap(gkv_other).astype(F32)).astype(BF)
    gkv = jnp.sum(exchange(gkv, "y").astype(F32), axis=0).astype(BF)
    gkv = jnp.sum(exchange(gkv, "z").astype(F32), axis=0).astype(BF)
    gkv_group = exchange(
        jnp.broadcast_to(gkv[None], (nx * nc,) + gkv.shape), ("x", "core")
    )

    mixed_out = (pooled + dot(mixed, out_weight)).astype(BF)
    half, small = call(
        back_kernel,
        (shape(pool, width), shape(8, width, dtype=F32)),
        [],
        2 * pool * width * (qk + vd),
        gkv, contract_cols(grad_queries, query_weight), key_weight, value_weight, pooled,
        gain_attn, grad_y, pairs, spread,
    )
    before = lax.ppermute(half[pool - 1 :], seq, up)
    after = lax.ppermute(half[:1], seq, down)
    (input_grad,) = call(
        input_kernel,
        (shape(fine, width),),
        [pltpu.VMEM((pool + 16, width), F32)]
        + [pltpu.VMEM((width // 128, fine, 128), F32) for _ in range(2)],
        fine * width * 40,
        x, gain_in, conv_taps, half, before, after,
    )

    total = small
    for step in range(1, nx):
        total = total + lax.ppermute(small, "x", [(i, (i + step) % nx) for i in range(nx)])

    keep = width // nx
    each = width // (count * nx)
    row = jnp.arange(width, dtype=jnp.int32)
    at_x, at_core = row // each % nx, row // (each * nx) % nc
    at_y, at_z = row // (each * nx * nc) % ny, row // (each * nx * nc * ny)
    target = ((at_y * nz + at_z) * nc + at_core) * each + row % each
    target = jnp.where(at_x == lax.axis_index("x"), target, -1).reshape(1, width)
    left, sums = flagged(
        pick_kernel,
        (shape(keep, nx * nc * pool), shape(keep, width)),
        [],
        4 * keep * width * nx * nc * pool,
        first, target, early, later,
    )
    tail = taps + 2
    (sums,) = flagged(
        functools.partial(late_kernel, q_cols),
        (shape(ny, keep // ny + 16, width),),
        [],
        2 * keep * nx * nc * pool * (qk + vd),
        first, left, sums, gkv_group, total,
    )
    got = exchange(sums, "y")
    part = keep // (ny * nz)
    slots = (part + tail + 7) // 8 * 8
    (sums,) = call(
        functools.partial(turn_kernel, tail),
        (shape(nz, slots, width),),
        [pltpu.VMEM((keep // ny + 16, width), F32)],
        0,
        got,
    )
    sums = jnp.sum(exchange(sums, "z").astype(F32), axis=0)
    small = sums[part : part + tail]
    mine = jnp.where(first_core, sums[:each], sums[each:part])
    theirs = jnp.where(first_core, sums[each:part], sums[:each])
    got = swap(jnp.concatenate([theirs, small], axis=0))
    small = small + got[each:]
    keys_rows = jnp.where(first_core, mine, got[:each])
    out_rows = jnp.where(first_core, got[:each], mine)
    return (
        mixed_out[None],
        input_grad[None],
        keys_rows[:, :q_cols],
        keys_rows[:, q_cols : q_cols + qk],
        keys_rows[:, q_cols + qk : q_cols + qk + vd],
        out_rows,
        small[:taps],
        small[taps],
        small[taps + 1],
    )


def solution(mesh):
    fine = Mesh(mesh.devices.reshape(8, 4, 2, 4), ("z", "y", "core", "x"))
    seq = ("z", "y", "core")
    placed = P("x", seq, None)
    rows = P(("z", "y", "core", "x"), None)
    in_specs = (placed, P(), P(), P(), P(), P(), P(), P(), placed)
    out_specs = (placed, placed, rows, rows, rows, rows, P(), P(), P())
    return jax.shard_map(shards, mesh=fine, in_specs=in_specs, out_specs=out_specs, check_vma=False)
```

time: 328 us -> 246 us (0.75)
  local copies, waits for them, and re-layouts: 79.3 us -> 40.3 us
  other arithmetic: 47.6 us -> 12.2 us
  blocking collectives: 56.2 us -> 40.6 us
  Pallas kernels: 12.5 us -> 22.4 us
  matrix products: 17.3 us -> 11.8 us
  waiting for transfers between devices: 40.9 us -> 46.3 us
    unnamed x69 -> x79, local copies, waits for them, and re-layouts: 8.4 us -> 31.1 us
    reduce_sum x12 -> x3, other arithmetic: 20.7 us -> 4.52 us  [the longest x1 2.34 us: shards(): gkv = jnp.sum(exchange(gkv, 'y').astype(F32), axis=0).astype(BF)]
    all_to_all x3 -> x2, blocking collectives: 56.2 us -> 40.6 us  [exchange(): return lax.all_to_all(blocks, axis, 0, 0, tiled=True)]
    slice x14 -> x7, local copies, waits for them, and re-layouts: 20.2 us -> 4.76 us  [the longest x1 1.36 us: shards(): after = lax.ppermute(half[:1], seq, down)]
    pallas_call x1 -> x7, Pallas kernels: 12.5 us -> 22.4 us  [the longest x4 17.8 us: call(): pl.pallas_call(kernel, out_shape=out_shape, scratch_shapes=scratch, compi...]
    convert_element_type x5 -> x0, local copies, waits for them, and re-layouts: 9.26 us -> none  [the longest x3 4.09 us: to_wire(): both = jnp.stack([high, value - high]).astype(BF).reshape(tail, cols)]
    all_to_all x5, starting transfers between devices: 39.2 us -> 30.7 us  [exchange(): return lax.all_to_all(blocks, axis, 0, 0, tiled=True)]
    broadcast_in_dim x12 -> x2, local copies, waits for them, and re-layouts: 10.8 us -> 3.01 us  [the longest x1 2.25 us: shards(): kv_own = exchange(jnp.broadcast_to(kv[None], (ny,) + kv.shape), 'y')]
  transfers between devices with their start and end apart: 16 -> 19, of which waited for: 8 -> 7; matrix products, arithmetic and copies ran while one was open for 25% -> 12% of each run, Pallas kernels for 0% -> 8%
where the time goes in v2:
time: 246 us; the launch traced here: 244 us
  starting transfers between devices  56.6 us (23%)
  waiting for transfers between devices  46.3 us (19%)
  blocking collectives  40.6 us (17%)
  local copies, waits for them, and re-layouts  40.3 us (16%)
  Pallas kernels  22.4 us (9%)
  between operations  14.4 us (6%)
  other arithmetic  12.2 us (5%)
  matrix products  11.8 us (5%)
    all_to_all x5, waiting for transfers between devices, exchange(): return lax.all_to_all(blocks, axis, 0, 0, tiled=True)  42.8 us
    all_to_all x2, blocking collectives, exchange(): return lax.all_to_all(blocks, axis, 0, 0, tiled=True)  40.6 us
    unnamed x79, local copies, waits for them, and re-layouts  31.1 us
    all_to_all x5, starting transfers between devices, exchange(): return lax.all_to_all(blocks, axis, 0, 0, tiled=True)  30.7 us
    pallas_call x4, Pallas kernels, call(): pl.pallas_call(kernel, out_shape=out_shape, scratch_shapes=scratch, compi...  17.8 us
    ppermute x5, starting transfers between devices, swap(): return lax.ppermute(block, 'core', [(0, 1), (1, 0)])  8.72 us
    dot_general x2, matrix products, contract_cols(): lax.dot_general(left, right, (((1,), (1,)), ((), ())), preferred_element_...  6.41 us
    dot_general x2, matrix products, dot(): return jnp.dot(left, right, preferred_element_type=F32)  5.37 us
  transfers between devices with their start and end apart: 19, of which 7 were waited for; matrix products, arithmetic and copies ran while one was open for 12% of the time, Pallas kernels for 8%

profile of v2, /device:TPU:1, one launch (start us, length us, event | category | flops | bytes accessed | tf_op | source)
XLA Modules:
  0.0 244.4 jit_solution(15694434313010980293)
XLA Ops:
  7.2 0.9 slice_bitcast_fusion
  8.1 4.7 %collective-permute-start = (bf16[2,1536]{1,0:T(2,128)(2,1)S(1)}, bf16[2,1536]{1,0:T(2,128)(2,1)S(1)}, u32[]{:S(2)}, u32[]{:S(2)}) collective-permute-start(bf16[2,1536]{1,0:T(2,128)(2,1)S(1)} %get-tuple-element.46), channel_id=1, source_target_pairs={{0,4},{4,8},{8,12},{12,16},{16,20},{20,24},{24,28},{28,32},{32,36}... | collective-permute-start | bytes 18440 | tf_op jit(solution)/shard_map/ppermute | solution.py:364
  12.9 1.9 collective-permute-start.1
  15.4 2.2 copy.20.vw_ref
  20.2 1.1 copy-done.1
  21.4 1.0 copy-done.7
  22.4 1.0 copy-done.10
  23.4 0.8 copy-done.27
  26.2 2.4 shard_map.160
  28.6 1.3 copy-done.4
  32.1 8.2 %all-to-all-start = ((bf16[8,160,128]{2,1,0:T(8,128)(2,1)}), bf16[8,160,128]{2,1,0:T(8,128)(2,1)}, u32[]{:S(2)}, u32[]{:S(2)}) async-start(bf16[8,160,128]{2,1,0:T(8,128)(2,1)} %copy-done.23), calls=%async_computation | async-start | bytes 655360 | tf_op jit(solution)/shard_map/all_to_all | solution.py:36
  40.3 4.5 %convolution_convert_fusion.g_ref = bf16[64,1536]{1,0:T(8,128)(2,1)} fusion(bf16[1536,1536]{1,0:T(8,128)(2,1)} %param.16, bf16[1,64,1536]{2,1,0:T(8,128)(2,1)S(1)} %copy-done.6), kind=kOutput, calls=%fused_computation.3 | convolution fusion | flops 302088192 | bytes 5111808 | tf_op jit(solution)/shard_map/dot_general | solution.py:24
  44.8 1.3 convolution_convert_fusion.1.q_ref
  46.1 4.5 %all-to-all-done = bf16[8,160,128]{2,1,0:T(8,128)(2,1)} async-done(((bf16[8,160,128]{2,1,0:T(8,128)(2,1)}), bf16[8,160,128]{2,1,0:T(8,128)(2,1)}, u32[]{:S(2)}, u32[]{:S(2)}) %all-to-all-start) | async-done | bytes 327712 | tf_op jit(solution)/shard_map/all_to_all | solution.py:36
  50.6 2.2 broadcast_in_dim.10
  52.8 7.4 %all-to-all-start.1 = ((bf16[4,8,160,128]{3,2,1,0:T(8,128)(2,1)}), bf16[4,8,160,128]{3,2,1,0:T(8,128)(2,1)}, u32[]{:S(2)}, u32[]{:S(2)}) async-start(bf16[4,8,160,128]{3,2,1,0:T(8,128)(2,1)} %broadcast_in_dim.10), calls=%async_computation.1 | async-start | bytes 2621440 | tf_op jit(solution)/shard_map/all_to_all | solution.py:36
  60.2 0.8 broadcast_select_fusion.1
  61.0 2.1 collective-permute-start.6
  63.1 13.2 %all-to-all-done.1.kv0_ref = bf16[4,8,160,128]{3,2,1,0:T(8,128)(2,1)} async-done(((bf16[4,8,160,128]{3,2,1,0:T(8,128)(2,1)}), bf16[4,8,160,128]{3,2,1,0:T(8,128)(2,1)}, u32[]{:S(2)}, u32[]{:S(2)}) %all-to-all-start.1) | async-done | bytes 1310752 | tf_op jit(solution)/shard_map/all_to_all | solution.py:36
  76.3 2.9 %collective-permute-start.2 = (bf16[4,8,160,128]{3,2,1,0:T(8,128)(2,1)}, bf16[4,8,160,128]{3,2,1,0:T(8,128)(2,1)}, u32[]{:S(2)}, u32[]{:S(2)}) collective-permute-start(bf16[4,8,160,128]{3,2,1,0:T(8,128)(2,1)} %all-to-all-done.1.kv0_ref), channel_id=1, source_target_pairs={{0,4},{4,0},{1,5},{5,1},{2,6},{6,2},{3,7},{7,3},{8,12},{12,8},{9,1... | collective-permute-start | bytes 3932168 | tf_op jit(solution)/shard_map/ppermute | solution.py:32
  79.2 1.7 pad_maximum_fusion
  81.0 1.2 collective-permute-done.2.kv1_ref
  82.2 0.9 copy-done.26
  83.1 0.9 copy-done.29
  84.0 13.8 %shard_map.161 = (bf16[64,1536]{1,0:T(8,128)(2,1)S(1)}, bf16[64,1024]{1,0:T(8,128)(2,1)S(1)}, bf16[4,8,160,128]{3,2,1,0:T(8,128)(2,1)S(1)}, bf16[4,8,160,128]{3,2,1,0:T(8,128)(2,1)}) custom-call(bf16[64,1024]{1,0:T(8,128)(2,1)S(1)} %copy-done.29, bf16[64,1536]{1,0:T(8,128)(2,1)S(1)} %copy-done.26, bf16[4,8,160,128]{3,2,1,0:T(8,128)(2,1)} %all-to-all-done.1.kv0_ref, ...), custom_call_target="tpu_custom_call" | custom-call | flops 4026531840 | bytes 5898240 | tf_op jit(solution)/shard_map/pallas_call | solution.py:42
  97.9 1.0 copy-done.15
  100.1 2.1 collective-permute-done.7
  102.2 0.8 pad_maximum_fusion.1
  103.0 2.1 add_convert_fusion
  105.1 20.9 %all_to_all.35 = bf16[4,8,160,128]{3,2,1,0:T(8,128)(2,1)} all-to-all(bf16[4,8,160,128]{3,2,1,0:T(8,128)(2,1)S(1)} %add_convert_fusion), channel_id=1, replica_groups=mesh['z'=8,'y'=4,'core'=2,'x'=4] {'y'}, dimensions={0} | all-to-all | bytes 2621440 | tf_op jit(solution)/shard_map/all_to_all | solution.py:36
  125.9 2.3 reduce_sum.33
  128.3 4.1 %all-to-all-start.3 = ((bf16[8,160,128]{2,1,0:T(8,128)(2,1)}), bf16[8,160,128]{2,1,0:T(8,128)(2,1)}, u32[]{:S(2)}, u32[]{:S(2)}) async-start(bf16[8,160,128]{2,1,0:T(8,128)(2,1)} %reduce_sum.33), calls=%async_computation.3 | async-start | bytes 655360 | tf_op jit(solution)/shard_map/all_to_all | solution.py:36
  132.5 1.9 fusion.14.part_ref
  134.3 9.5 %all-to-all-done.3 = bf16[8,160,128]{2,1,0:T(8,128)(2,1)} async-done(((bf16[8,160,128]{2,1,0:T(8,128)(2,1)}), bf16[8,160,128]{2,1,0:T(8,128)(2,1)}, u32[]{:S(2)}, u32[]{:S(2)}) %all-to-all-start.3) | async-done | bytes 327712 | tf_op jit(solution)/shard_map/all_to_all | solution.py:36
  143.9 1.0 reduce_sum.34.gkv_ref
  144.9 1.1 copy-done.2
  146.0 1.5 copy-done.5
  147.6 1.0 copy-done.9
  148.6 1.0 copy-done.11
  149.6 1.0 copy-done.13
  150.6 1.0 copy-done.20
  151.5 0.9 shard_map.162
  153.2 2.5 %collective-permute-start.10 = (f32[8,1536]{1,0:T(8,128)S(1)}, f32[8,1536]{1,0:T(8,128)}, u32[]{:S(2)}, u32[]{:S(2)}) collective-permute-start(f32[8,1536]{1,0:T(8,128)S(1)} %get-tuple-element.40), channel_id=1, source_target_pairs={{0,3},{1,0},{2,1},{3,2},{4,7},{5,4},{6,5},{7,6},{8,11},{9,8},{10,9... | collective-permute-start | bytes 147464 | tf_op jit(solution)/shard_map/ppermute | solution.py:442
  155.7 1.7 collective-permute-start.9
  157.4 1.4 copy-done.36
  158.8 1.4 copy-done.37
  160.2 1.7 shard_map.164
  162.0 1.0 copy-done.16
  164.5 6.9 %all-to-all-start.4 = ((bf16[8,160,128]{2,1,0:T(8,128)(2,1)}), bf16[8,160,128]{2,1,0:T(8,128)(2,1)S(1)}, u32[]{:S(2)}, u32[]{:S(2)}) async-start(bf16[8,160,128]{2,1,0:T(8,128)(2,1)} %broadcast_in_dim.23), calls=%async_computation.4 | async-start | bytes 655360 | tf_op jit(solution)/shard_map/all_to_all | solution.py:36
  171.4 0.9 add_add_fusion.small_ref
  172.3 6.2 %all-to-all-done.4.gkv_ref = bf16[8,160,128]{2,1,0:T(8,128)(2,1)S(1)} async-done(((bf16[8,160,128]{2,1,0:T(8,128)(2,1)}), bf16[8,160,128]{2,1,0:T(8,128)(2,1)S(1)}, u32[]{:S(2)}, u32[]{:S(2)}) %all-to-all-start.4) | async-done | bytes 327712 | tf_op jit(solution)/shard_map/all_to_all | solution.py:36
  178.6 1.3 copy-done.17
  179.8 1.0 copy-done.22
  181.3 19.7 %all_to_all.36.got_ref = bf16[4,112,1536]{2,1,0:T(8,128)(2,1)S(1)} all-to-all(bf16[4,112,1536]{2,1,0:T(8,128)(2,1)S(1)} %shard_map.165), channel_id=1, replica_groups=mesh['z'=8,'y'=4,'core'=2,'x'=4] {'y'}, dimensions={0} | all-to-all | bytes 2752512 | tf_op jit(solution)/shard_map/all_to_all | solution.py:36
  201.3 0.8 copy-done.3
  202.1 4.2 %all-to-all-start.6 = ((bf16[8,24,1536]{2,1,0:T(8,128)(2,1)}), bf16[8,24,1536]{2,1,0:T(8,128)(2,1)}, u32[]{:S(2)}, u32[]{:S(2)}) async-start(bf16[8,24,1536]{2,1,0:T(8,128)(2,1)} %copy-done.3), calls=%async_computation.6 | async-start | bytes 1179648 | tf_op jit(solution)/shard_map/all_to_all | solution.py:36
  206.3 1.4 fusion.13
  207.7 4.3 %collective-permute-start.4 = (bf16[1,1536]{1,0:T(2,128)(2,1)}, bf16[1,1536]{1,0:T(2,128)(2,1)S(1)}, u32[]{:S(2)}, u32[]{:S(2)}) collective-permute-start(bf16[1,1536]{1,0:T(2,128)(2,1)} %get-tuple-element.52), channel_id=1, source_target_pairs={{0,4},{4,8},{8,12},{12,16},{16,20},{20,24},{24,28},{28,32},{32,36}... | collective-permute-start | bytes 9224 | tf_op jit(solution)/shard_map/ppermute | solution.py:429
  212.0 1.9 collective-permute-start.5
  213.9 9.4 %all-to-all-done.6 = bf16[8,24,1536]{2,1,0:T(8,128)(2,1)} async-done(((bf16[8,24,1536]{2,1,0:T(8,128)(2,1)}), bf16[8,24,1536]{2,1,0:T(8,128)(2,1)}, u32[]{:S(2)}, u32[]{:S(2)}) %all-to-all-start.6) | async-done | bytes 589856 | tf_op jit(solution)/shard_map/all_to_all | solution.py:36
  223.4 1.2 convert_reduce_fusion
  224.6 2.9 %collective-permute-start.11 = (f32[13,1536]{1,0:T(8,128)S(1)}, f32[13,1536]{1,0:T(8,128)S(1)}, u32[]{:S(2)}, u32[]{:S(2)}) collective-permute-start(f32[13,1536]{1,0:T(8,128)S(1)} %pad_maximum_fusion.2), channel_id=1, source_target_pairs={{0,4},{4,0},{1,5},{5,1},{2,6},{6,2},{3,7},{7,3},{8,12},{12,8},{9,1... | collective-permute-start | bytes 239624 | tf_op jit(solution)/shard_map/ppermute | solution.py:32
  227.5 4.1 %fusion.1 = bf16[1,64,1536]{2,1,0:T(8,128)(2,1)} fusion(f32[64,1536]{1,0:T(8,128)S(1)} %copy-done.14, bf16[64,1536]{1,0:T(8,128)(2,1)} %copy-done.18, bf16[1536,1536]{1,0:T(8,128)(2,1)} %param.16), kind=kOutput, calls=%fused_computation.4 | convolution fusion | flops 302186496 | bytes 5505024 | tf_op jit(solution)/shard_map/dot_general | solution.py:28
  231.6 2.9 %shard_map.163 = bf16[128,1536]{1,0:T(8,128)(2,1)} custom-call(bf16[128,1536]{1,0:T(8,128)(2,1)S(1)} %bitcast.26, f32[1,1536]{1,0:T(1,128)S(1)} %reshape.275.gain_in_ref.gain_ref, f32[5,1536]{1,0:T(8,128)S(1)} %copy-done.28, bf16[64,1536]{1,0:T(8,128)(2,1)S(1)} %copy-done.25, bf16[1,1536]{1,0:T(2,128)(2,1)S(1)} %collective-permute-done.4.before_ref, ...), custom_call_target="tpu_custom_call" | custom-call | flops 7864320 | bytes 1026048 | tf_op jit(solution)/shard_map/pallas_call | solution.py:42
  (94 shorter events, 14.9 us)
Async XLA Ops:
  7.2 37.6 %copy-start = (bf16[1536,1024]{1,0:T(8,128)(2,1)S(1)}, bf16[1536,1024]{1,0:T(8,128)(2,1)}, u32[]{:S(2)}) copy-start(bf16[1536,1024]{1,0:T(8,128)(2,1)} %param.13) | copy-start | bytes 9437188
  7.2 33.1 %copy-start.6 = (bf16[1,64,1536]{2,1,0:T(8,128)(2,1)S(1)}, bf16[1,64,1536]{2,1,0:T(8,128)(2,1)}, u32[]{:S(2)}) copy-start(bf16[1,64,1536]{2,1,0:T(8,128)(2,1)} %param.17) | copy-start | bytes 589828
  8.1 10.9 %collective-permute-start = (bf16[2,1536]{1,0:T(2,128)(2,1)S(1)}, bf16[2,1536]{1,0:T(2,128)(2,1)S(1)}, u32[]{:S(2)}, u32[]{:S(2)}) collective-permute-start(bf16[2,1536]{1,0:T(2,128)(2,1)S(1)} %get-tuple-element.46), channel_id=1, source_target_pairs={{0,4},{4,8},{8,12},{12,16},{16,20},{20,24},{24,28},{28,32},{32,36}... | collective-permute-start | bytes 18440 | tf_op jit(solution)/shard_map/ppermute | solution.py:364
  12.9 6.8 %collective-permute-start.1 = (bf16[2,1536]{1,0:T(2,128)(2,1)S(1)}, bf16[2,1536]{1,0:T(2,128)(2,1)S(1)}, u32[]{:S(2)}, u32[]{:S(2)}) collective-permute-start(bf16[2,1536]{1,0:T(2,128)(2,1)S(1)} %get-tuple-element.45), channel_id=1, source_target_pairs={{4,0},{8,4},{12,8},{16,12},{20,16},{24,20},{28,24},{32,28},{36,32}... | collective-permute-start | bytes 18440 | tf_op jit(solution)/shard_map/ppermute | solution.py:365
  19.0 0.6 copy-start.31
  19.6 0.6 copy-start.33
  20.2 1.1 copy-start.1
  21.4 1.0 copy-start.7
  22.4 1.0 copy-start.10
  23.4 0.8 copy-start.27
  24.2 0.7 copy-start.32
  24.9 0.7 copy-start.34
  25.5 0.7 copy-start.35
  28.6 1.3 copy-start.4
  29.8 0.7 copy-start.12
  30.6 0.8 copy-start.19
  31.3 0.7 copy-start.23
  32.1 18.5 %all-to-all-start = ((bf16[8,160,128]{2,1,0:T(8,128)(2,1)}), bf16[8,160,128]{2,1,0:T(8,128)(2,1)}, u32[]{:S(2)}, u32[]{:S(2)}) async-start(bf16[8,160,128]{2,1,0:T(8,128)(2,1)} %copy-done.23), calls=%async_computation | async-start | bytes 655360 | tf_op jit(solution)/shard_map/all_to_all | solution.py:36
  52.8 23.5 %all-to-all-start.1 = ((bf16[4,8,160,128]{3,2,1,0:T(8,128)(2,1)}), bf16[4,8,160,128]{3,2,1,0:T(8,128)(2,1)}, u32[]{:S(2)}, u32[]{:S(2)}) async-start(bf16[4,8,160,128]{3,2,1,0:T(8,128)(2,1)} %broadcast_in_dim.10), calls=%async_computation.1 | async-start | bytes 2621440 | tf_op jit(solution)/shard_map/all_to_all | solution.py:36
  60.2 97.2 %all-gather.3.cloned.1.call-start = ((), (), s32[]{:S(2)}) async-start(), calls=%async_computation.7 | async-start | bytes 1966080 | tf_op jit(solution)/shard_map/all_gather | solution.py:396
  61.0 18.2 %collective-permute-start.6 = (bf16[64,1536]{1,0:T(8,128)(2,1)}, bf16[64,1536]{1,0:T(8,128)(2,1)S(1)}, u32[]{:S(2)}, u32[]{:S(2)}) collective-permute-start(bf16[64,1536]{1,0:T(8,128)(2,1)} %get-tuple-element.44), channel_id=1, source_target_pairs={{0,4},{4,0},{1,5},{5,1},{2,6},{6,2},{3,7},{7,3},{8,12},{12,8},{9,1... | collective-permute-start | bytes 589832 | tf_op jit(solution)/shard_map/ppermute | solution.py:32
  76.3 5.9 %collective-permute-start.2 = (bf16[4,8,160,128]{3,2,1,0:T(8,128)(2,1)}, bf16[4,8,160,128]{3,2,1,0:T(8,128)(2,1)}, u32[]{:S(2)}, u32[]{:S(2)}) collective-permute-start(bf16[4,8,160,128]{3,2,1,0:T(8,128)(2,1)} %all-to-all-done.1.kv0_ref), channel_id=1, source_target_pairs={{0,4},{4,0},{1,5},{5,1},{2,6},{6,2},{3,7},{7,3},{8,12},{12,8},{9,1... | collective-permute-start | bytes 3932168 | tf_op jit(solution)/shard_map/ppermute | solution.py:32
  80.9 76.5 %all-gather.5.cloned.1.call-start = ((), (), s32[]{:S(2)}) async-start(), calls=%async_computation.8 | async-start | bytes 1966080 | tf_op jit(solution)/shard_map/all_gather | solution.py:409
  82.2 0.9 copy-start.26
  83.1 0.9 copy-start.29
  97.8 1.1 copy-start.15
  98.9 0.7 copy-start.18
  98.9 4.1 %collective-permute-start.3 = (bf16[4,8,160,128]{3,2,1,0:T(8,128)(2,1)}, bf16[4,8,160,128]{3,2,1,0:T(8,128)(2,1)}, u32[]{:S(2)}, u32[]{:S(2)}) collective-permute-start(bf16[4,8,160,128]{3,2,1,0:T(8,128)(2,1)} %get-tuple-element.33), channel_id=1, source_target_pairs={{0,4},{4,0},{1,5},{5,1},{2,6},{6,2},{3,7},{7,3},{8,12},{12,8},{9,1... | collective-permute-start | bytes 3932168 | tf_op jit(solution)/shard_map/ppermute | solution.py:32
  99.6 2.6 %collective-permute-start.7 = (bf16[64,1536]{1,0:T(8,128)(2,1)S(1)}, bf16[64,1536]{1,0:T(8,128)(2,1)S(1)}, u32[]{:S(2)}, u32[]{:S(2)}) collective-permute-start(bf16[64,1536]{1,0:T(8,128)(2,1)S(1)} %get-tuple-element.48), channel_id=1, source_target_pairs={{0,4},{4,0},{1,5},{5,1},{2,6},{6,2},{3,7},{7,3},{8,12},{12,8},{9,1... | collective-permute-start | bytes 589832 | tf_op jit(solution)/shard_map/ppermute | solution.py:32
  128.3 15.6 %all-to-all-start.3 = ((bf16[8,160,128]{2,1,0:T(8,128)(2,1)}), bf16[8,160,128]{2,1,0:T(8,128)(2,1)}, u32[]{:S(2)}, u32[]{:S(2)}) async-start(bf16[8,160,128]{2,1,0:T(8,128)(2,1)} %reduce_sum.33), calls=%async_computation.3 | async-start | bytes 655360 | tf_op jit(solution)/shard_map/all_to_all | solution.py:36
  144.9 1.1 copy-start.2
  146.0 1.5 copy-start.5
  147.6 1.0 copy-start.9
  148.6 1.0 copy-start.11
  149.6 1.0 copy-start.13
  150.5 1.0 copy-start.20
  152.5 0.7 copy-start.24
  153.2 8.8 %copy-start.30 = (f32[8,1536]{1,0:T(8,128)}, f32[8,1536]{1,0:T(8,128)S(1)}, u32[]{:S(2)}) copy-start(f32[8,1536]{1,0:T(8,128)S(1)} %get-tuple-element.40) | copy-start | bytes 147460
  153.2 18.3 %collective-permute-start.10 = (f32[8,1536]{1,0:T(8,128)S(1)}, f32[8,1536]{1,0:T(8,128)}, u32[]{:S(2)}, u32[]{:S(2)}) collective-permute-start(f32[8,1536]{1,0:T(8,128)S(1)} %get-tuple-element.40), channel_id=1, source_target_pairs={{0,3},{1,0},{2,1},{3,2},{4,7},{5,4},{6,5},{7,6},{8,11},{9,8},{10,9... | collective-permute-start | bytes 147464 | tf_op jit(solution)/shard_map/ppermute | solution.py:442
  155.7 15.7 %collective-permute-start.8 = (f32[8,1536]{1,0:T(8,128)S(1)}, f32[8,1536]{1,0:T(8,128)}, u32[]{:S(2)}, u32[]{:S(2)}) collective-permute-start(f32[8,1536]{1,0:T(8,128)S(1)} %get-tuple-element.40), channel_id=1, source_target_pairs={{0,1},{1,2},{2,3},{3,0},{4,5},{5,6},{6,7},{7,4},{8,9},{9,10},{10,1... | collective-permute-start | bytes 147464 | tf_op jit(solution)/shard_map/ppermute | solution.py:442
  155.7 15.7 %collective-permute-start.9 = (f32[8,1536]{1,0:T(8,128)S(1)}, f32[8,1536]{1,0:T(8,128)}, u32[]{:S(2)}, u32[]{:S(2)}) collective-permute-start(f32[8,1536]{1,0:T(8,128)S(1)} %get-tuple-element.40), channel_id=1, source_target_pairs={{0,2},{1,3},{2,0},{3,1},{4,6},{5,7},{6,4},{7,5},{8,10},{9,11},{10,... | collective-permute-start | bytes 147464 | tf_op jit(solution)/shard_map/ppermute | solution.py:442
  157.4 1.4 copy-start.36
  158.8 1.4 copy-start.37
  162.0 1.0 copy-start.16
  163.0 0.8 copy-start.21
  164.5 14.0 %all-to-all-start.4 = ((bf16[8,160,128]{2,1,0:T(8,128)(2,1)}), bf16[8,160,128]{2,1,0:T(8,128)(2,1)S(1)}, u32[]{:S(2)}, u32[]{:S(2)}) async-start(bf16[8,160,128]{2,1,0:T(8,128)(2,1)} %broadcast_in_dim.23), calls=%async_computation.4 | async-start | bytes 655360 | tf_op jit(solution)/shard_map/all_to_all | solution.py:36
  178.6 1.3 copy-start.17
  179.8 1.0 copy-start.22
  201.0 26.5 %copy-start.14 = (f32[64,1536]{1,0:T(8,128)S(1)}, f32[64,1536]{1,0:T(8,128)}, u32[]{:S(2)}) copy-start(f32[64,1536]{1,0:T(8,128)} %copy-done.12) | copy-start | bytes 1179652
  201.3 0.8 copy-start.3
  202.1 21.3 %all-to-all-start.6 = ((bf16[8,24,1536]{2,1,0:T(8,128)(2,1)}), bf16[8,24,1536]{2,1,0:T(8,128)(2,1)}, u32[]{:S(2)}, u32[]{:S(2)}) async-start(bf16[8,24,1536]{2,1,0:T(8,128)(2,1)} %copy-done.3), calls=%async_computation.6 | async-start | bytes 1179648 | tf_op jit(solution)/shard_map/all_to_all | solution.py:36
  207.7 23.9 %collective-permute-start.4 = (bf16[1,1536]{1,0:T(2,128)(2,1)}, bf16[1,1536]{1,0:T(2,128)(2,1)S(1)}, u32[]{:S(2)}, u32[]{:S(2)}) collective-permute-start(bf16[1,1536]{1,0:T(2,128)(2,1)} %get-tuple-element.52), channel_id=1, source_target_pairs={{0,4},{4,8},{8,12},{12,16},{16,20},{20,24},{24,28},{28,32},{32,36}... | collective-permute-start | bytes 9224 | tf_op jit(solution)/shard_map/ppermute | solution.py:429
  212.0 19.6 %collective-permute-start.5 = (bf16[1,1536]{1,0:T(2,128)(2,1)}, bf16[1,1536]{1,0:T(2,128)(2,1)}, u32[]{:S(2)}, u32[]{:S(2)}) collective-permute-start(bf16[1,1536]{1,0:T(2,128)(2,1)} %get-tuple-element.51), channel_id=1, source_target_pairs={{4,0},{8,4},{12,8},{16,12},{20,16},{24,20},{28,24},{32,28},{36,32}... | collective-permute-start | bytes 9224 | tf_op jit(solution)/shard_map/ppermute | solution.py:430
  224.6 7.0 %copy-start.8 = (bf16[1,128,1536]{2,1,0:T(8,128)(2,1)S(1)}, bf16[1,128,1536]{2,1,0:T(8,128)(2,1)}, u32[]{:S(2)}) copy-start(bf16[1,128,1536]{2,1,0:T(8,128)(2,1)} %param.9) | copy-start | bytes 1179652
  224.6 7.0 %copy-start.25 = (bf16[64,1536]{1,0:T(8,128)(2,1)S(1)}, bf16[64,1536]{1,0:T(8,128)(2,1)}, u32[]{:S(2)}) copy-start(bf16[64,1536]{1,0:T(8,128)(2,1)} %copy-done.24) | copy-start | bytes 589828
  224.6 7.0 %copy-start.28 = (f32[5,1536]{1,0:T(8,128)S(1)}, f32[5,1536]{1,0:T(8,128)}, u32[]{:S(2)}) copy-start(f32[5,1536]{1,0:T(8,128)} %taps_ref.3) | copy-start | bytes 92164
  224.6 9.9 %collective-permute-start.11 = (f32[13,1536]{1,0:T(8,128)S(1)}, f32[13,1536]{1,0:T(8,128)S(1)}, u32[]{:S(2)}, u32[]{:S(2)}) collective-permute-start(f32[13,1536]{1,0:T(8,128)S(1)} %pad_maximum_fusion.2), channel_id=1, source_target_pairs={{0,4},{4,0},{1,5},{5,1},{2,6},{6,2},{3,7},{7,3},{8,12},{12,8},{9,1... | collective-permute-start | bytes 239624 | tf_op jit(solution)/shard_map/ppermute | solution.py:32
  237.0 0.6 copy-start.38
Sparse Core Ops, SparseCore 0:
  81.1 22.7 all-gather.2
  105.7 29.1 all-gather.4

commit v3 on v2

--- a/solution.py
+++ b/solution.py
@@ -43,7 +43,7 @@
         kernel,
         out_shape=out_shape,
         scratch_shapes=scratch,
-        compiler_params=pltpu.CompilerParams(vmem_limit_bytes=48 * 2**20),
+        compiler_params=pltpu.CompilerParams(vmem_limit_bytes=60 * 2**20),
         cost_estimate=pl.CostEstimate(flops=flops, bytes_accessed=sum(sizes), transcendentals=0),
     )(*args)
 
@@ -68,41 +68,38 @@
 
 
 def front_kernel(
-    inside_ref, x_ref, low_ref, high_ref, gain_in_ref, taps_ref, gain_attn_ref, kw_ref, vw_ref,
+    x_ref, low_ref, high_ref, gain_in_ref, taps_ref, gain_attn_ref, kw_ref, vw_ref,
     kv_ref, normed_ref, pooled_ref, pairs_ref, spread_ref, act, slope, plain,
 ):
     fine, width = x_ref.shape
     pool = fine // 2
     taps = taps_ref.shape[0]
-    gain = gain_in_ref[...]
-
-    def rows_of(x, keep):
+    gain = gain_in_ref[...].reshape(1, width)
+
+    def rows_of(x):
         raw = x * lax.rsqrt(jnp.mean(x * x, axis=-1, keepdims=True) + EPS)
         u = raw * gain
         t = jnp.tanh(CURVE * (u + CUBIC * (u * u * u)))
         a = u * (0.5 * (1.0 + t))
         slant = 0.5 * (1.0 + t) + 0.5 * u * (1.0 - t * t) * (CURVE * (1.0 + 3.0 * CUBIC * u * u))
-        g = slant * raw
-        if keep is not None:
-            a, g = jnp.where(keep, a, 0.0), jnp.where(keep, g, 0.0)
-        return a.astype(BF).astype(F32), g
+        return a.astype(BF).astype(F32), slant * raw
 
     def put(ref, at, value):
         for c in range(width // 128):
             ref[c, at, :] = value[:, c * 128 : (c + 1) * 128]
 
-    def fill(at, x, keep):
-        a, g = rows_of(x, keep)
+    def fill(at, x):
+        a, g = rows_of(x)
         put(act, at, a)
         put(slope, at, g)
 
-    fill(slice(0, 2), low_ref[...].astype(F32), inside_ref[0] > 0)
-    fill(slice(fine + 2, fine + 4), high_ref[...].astype(F32), inside_ref[1] > 0)
+    fill(slice(0, 2), low_ref[...].astype(F32))
+    fill(slice(fine + 2, fine + 4), high_ref[...].astype(F32))
     step = 32
     for i in range(0, fine, step):
         rows = x_ref[i : i + step, :].astype(F32)
         put(plain, slice(i, i + step), rows)
-        fill(slice(2 + i, 2 + i + step), rows, None)
+        fill(slice(2 + i, 2 + i + step), rows)
 
     for c in range(width // 128):
         at = slice(c * 128, (c + 1) * 128)
@@ -121,9 +118,9 @@
         pooled_ref[:, at] = 0.5 * (whole + conv)
     pooled = pooled_ref[...]
     scale = lax.rsqrt(jnp.mean(pooled * pooled, axis=-1, keepdims=True) + EPS)
-    normed = (pooled * scale * gain_attn_ref[...]).astype(BF)
+    normed = (pooled * scale * gain_attn_ref[...].reshape(1, width)).astype(BF)
     normed_ref[...] = normed
-    kv = pack(dot(normed, kw_ref[...]), dot(normed, vw_ref[...])).astype(BF)
+    kv = pack(dot(normed, kw_ref[...]), contract_cols(normed, vw_ref[...])).astype(BF)
     for i in range(kv_ref.shape[0]):
         kv_ref[i] = kv
 
@@ -208,12 +205,28 @@
     )
 
 
-def back_kernel(gkv_ref, part_ref, kw_ref, vw_ref, pooled_ref, gain_ref, gy_ref, pairs_ref,
-                spread_ref, half_ref, small_ref):
-    gk, gv = unpack(gkv_ref[...])
-    grad = part_ref[...] + contract_cols(gk, kw_ref[...]) + contract_cols(gv, vw_ref[...])
+def add_up(ref):
+    total = ref[0].astype(F32)
+    for i in range(1, ref.shape[0]):
+        total = total + ref[i].astype(F32)
+    return total
+
+
+def sum_kernel(parts_ref, out_ref):
+    for j in range(out_ref.shape[0]):
+        total = parts_ref[0, j].astype(F32)
+        for i in range(1, parts_ref.shape[0]):
+            total = total + parts_ref[i, j].astype(F32)
+        out_ref[j] = total.astype(BF)
+
+
+def back_kernel(cores, parts_ref, part_ref, kw_ref, vw_ref, pooled_ref, gain_ref, gy_ref, pairs_ref,
+                spread_ref, half_ref, out_ref, small_ref):
+    gkv = add_up(parts_ref).astype(BF)
+    gk, gv = unpack(gkv)
+    grad = part_ref[...] + contract_cols(gk, kw_ref[...]) + dot(gv, vw_ref[...])
     pooled = pooled_ref[...]
-    gain = gain_ref[...]
+    gain = gain_ref[...].reshape(1, gain_ref.shape[0])
     scale = lax.rsqrt(jnp.mean(pooled * pooled, axis=-1, keepdims=True) + EPS)
     raw = pooled * scale
     inner = grad * gain
@@ -227,7 +240,22 @@
         small_ref[k : k + 1, :] = jnp.sum(h * pairs_ref[k], axis=0, keepdims=True)
     small_ref[taps : taps + 1, :] = jnp.sum(h * spread_ref[...], axis=0, keepdims=True)
     small_ref[taps + 1 : taps + 2, :] = jnp.sum(grad * raw, axis=0, keepdims=True)
-    small_ref[taps + 2 :, :] = jnp.zeros((small_ref.shape[0] - taps - 2, h.shape[1]), F32)
+    tail = taps + 2
+    packed = gkv.shape[0]
+    lanes = gkv.shape[1]
+    tiles = h.shape[1] // (cores * lanes)
+    blank = jnp.zeros((out_ref.shape[1] - packed - tail * tiles, lanes), F32)
+    halves = [
+        jnp.concatenate(
+            [small_ref[:tail, (c * tiles + t) * lanes : (c * tiles + t + 1) * lanes]
+             for t in range(tiles)] + [blank],
+            axis=0,
+        ).astype(BF)
+        for c in range(cores)
+    ]
+    for i in range(out_ref.shape[0]):
+        out_ref[i, :packed] = gkv
+        out_ref[i, packed:] = halves[i % cores]
 
 
 def input_kernel(x_ref, gain_ref, taps_ref, half_ref, before_ref, after_ref, out_ref, held, acts, twice):
@@ -248,7 +276,7 @@
         acts[c, pl.ds(1, pool, stride=2), :] = odd[:, at]
         twice[c, pl.ds(0, pool, stride=2), :] = mid[:, at]
         twice[c, pl.ds(1, pool, stride=2), :] = mid[:, at]
-    gain = gain_ref[...]
+    gain = gain_ref[...].reshape(1, gain_ref.shape[0])
     step = 32
     for i in range(0, fine, step):
         x = x_ref[i : i + step, :].astype(F32)
@@ -283,50 +311,92 @@
         work(m_ref, e_ref)
 
 
-def late_kernel(q_cols, first_ref, left_ref, sums_ref, gkv_ref, small_ref, out_ref):
-    parts = [unpack(gkv_ref[i]) for i in range(gkv_ref.shape[0])]
+def late_kernel(q_cols, first_ref, left_ref, sums_ref, got_ref, out_ref):
+    peers, slots, lanes = got_ref.shape
+    ny = out_ref.shape[0]
+    keep, width = sums_ref.shape
+    each = keep // ny
+    tail = out_ref.shape[1] - each * (width // lanes)
+    packed = slots - tail
+    parts = [unpack(got_ref[i, :packed]) for i in range(peers)]
     keys = jnp.concatenate([k for k, _ in parts], axis=0)
     values = jnp.concatenate([v for _, v in parts], axis=0)
     left = left_ref[...]
-    late = (dot(left, keys).astype(BF), dot(left, values).astype(BF))
-    ny, slots, width = out_ref.shape
-    each = left.shape[0] // ny
-    small = jnp.concatenate(
-        [small_ref[...], jnp.zeros((slots - each - small_ref.shape[0], width), F32)], axis=0
-    ).astype(BF)
+    late = jnp.concatenate([dot(left, keys), dot(left, values)], axis=1).astype(BF)
+    total = got_ref[0, packed:].astype(F32)
+    for i in range(1, peers):
+        total = total + got_ref[i, packed:].astype(F32)
+    small = total.astype(BF)
     first = first_ref[0] > 0
-    mid = q_cols + keys.shape[1]
-    end = mid + values.shape[1]
+    end = q_cols + late.shape[1]
+    for t in range(width // lanes):
+        low, high = t * lanes, (t + 1) * lanes
+        block = sums_ref[:, low:high]
+        if low >= q_cols and low < end:
+            piece = late[:, low - q_cols : min(high, end) - q_cols]
+            if high > end:
+                piece = jnp.concatenate([piece, block[:, end - low :]], axis=1)
+            block = jnp.where(first, piece, block)
+        for i in range(ny):
+            out_ref[i, t * each : (t + 1) * each] = block[i * each : (i + 1) * each]
     for i in range(ny):
-        at = slice(i * each, (i + 1) * each)
-        out_ref[i, :each, :] = sums_ref[at, :]
-        out_ref[i, each:, :] = small
-
-    @pl.when(first)
-    def _():
-        for i in range(ny):
-            at = slice(i * each, (i + 1) * each)
-            out_ref[i, :each, q_cols:mid] = late[0][at]
-            out_ref[i, :each, mid:end] = late[1][at]
-
-
-def turn_kernel(tail, got_ref, out_ref, held):
-    ny, slots, width = got_ref.shape
-    nz, rows = out_ref.shape[:2]
-    each = held.shape[0] - 16
-    for c in range(0, width, 512):
-        at = slice(c, c + 512)
-        total = got_ref[0, :, at].astype(F32)
-        for i in range(1, ny):
-            total = total + got_ref[i, :, at].astype(F32)
-        held[:, at] = total[: each + 16]
+        out_ref[i, each * (width // lanes) :] = small
+
+
+def turn_kernel(tiles, got_ref, out_ref, held):
+    nz, slots, lanes = out_ref.shape
+    held[...] = add_up(got_ref)
+    rows = held.shape[0]
+    tail = (slots * nz - rows) // (nz - 1)
+    each = (rows - tail) // tiles
     part = each // nz
-    small = held[each : each + tail, :]
     for i in range(nz):
-        rest = jnp.zeros((rows - part - tail, width), F32)
-        out_ref[i] = jnp.concatenate(
-            [held[i * part : (i + 1) * part, :], small, rest], axis=0
-        ).astype(BF)
+        pieces = [held[t * each + i * part : t * each + (i + 1) * part] for t in range(tiles)]
+        out_ref[i] = jnp.concatenate(pieces + [held[rows - tail :]], axis=0).astype(BF)
+
+
+def end_kernel(tiles, rows, first_ref, got_ref, mine_ref, theirs_ref, held):
+    held[...] = add_up(got_ref)
+    first = first_ref[0] > 0
+    small = [held[2 * tiles * rows :]]
+    low = [held[2 * t * rows : (2 * t + 1) * rows] for t in range(tiles)]
+    high = [held[(2 * t + 1) * rows : (2 * t + 2) * rows] for t in range(tiles)]
+    low = jnp.concatenate(low + small, axis=0)
+    high = jnp.concatenate(high + small, axis=0)
+    mine_ref[...] = jnp.where(first, low, high)
+    theirs_ref[...] = jnp.where(first, high, low)
+
+
+def last_kernel(tiles, first_ref, mine_ref, got_ref, q_ref, k_ref, v_ref, o_ref, conv_ref, in_ref,
+                attn_ref, held):
+    first = first_ref[0] > 0
+    mine, got = mine_ref[...], got_ref[...]
+    held[0] = jnp.where(first, mine, got)
+    held[1] = jnp.where(first, got, mine)
+    rows, q_cols = q_ref.shape
+    lanes = k_ref.shape[1]
+    for t in range(tiles):
+        at = slice(t * lanes, (t + 1) * lanes)
+        block = held[0, t * rows : (t + 1) * rows]
+        if (t + 1) * lanes <= q_cols:
+            q_ref[:, at] = block
+        elif t * lanes == q_cols:
+            k_ref[...] = block
+        else:
+            start = t * lanes - q_cols - lanes
+            stop = min(start + lanes, v_ref.shape[1])
+            if stop > start:
+                v_ref[:, start:stop] = block[:, : stop - start]
+        o_ref[:, at] = held[1, t * rows : (t + 1) * rows]
+    taps = conv_ref.shape[0]
+    half = tiles // 2
+    for c in range(2):
+        for t in range(half):
+            at = slice((c * half + t) * lanes, (c * half + t + 1) * lanes)
+            row = tiles * rows + t * (taps + 2)
+            conv_ref[:, at] = held[c, row : row + taps]
+            in_ref[at] = held[c, row + taps]
+            attn_ref[at] = held[c, row + taps + 1]
 
 
 def shards(
@@ -343,7 +413,6 @@
     seq = ("z", "y", "core")
     nz, ny, nx, nc = (lax.axis_size(a) for a in ("z", "y", "x", "core"))
     count = nz * ny * nc
-    place = lax.axis_index(seq)
     first_core = lax.axis_index("core") == 0
     first = first_core.astype(jnp.int32).reshape(1)
     x = windows[0]
@@ -355,15 +424,13 @@
     q_cols = query_weight.shape[1]
     heads = q_cols // qk
     grad_y = out_cotangent[0]
-    gain_in = gain_in.reshape(1, width)
-    gain_attn = gain_attn.reshape(1, width)
+    value_weight = value_weight.T
     packed = pool * (qk + vd) // qk
 
     up = [(i, i + 1) for i in range(count - 1)]
     down = [(b, a) for a, b in up]
     low = lax.ppermute(x[fine - 2 :], seq, up)
     high = lax.ppermute(x[:2], seq, down)
-    inside = jnp.stack([place > 0, place < count - 1]).astype(jnp.int32)
     smem = pl.BlockSpec(memory_space=pltpu.SMEM)
     vmem = pl.BlockSpec(memory_space=pltpu.VMEM)
 
@@ -373,19 +440,19 @@
             out_shape=out_shape,
             in_specs=[smem] + [vmem] * len(args),
             scratch_shapes=scratch,
-            compiler_params=pltpu.CompilerParams(vmem_limit_bytes=48 * 2**20),
+            compiler_params=pltpu.CompilerParams(vmem_limit_bytes=60 * 2**20),
             cost_estimate=pl.CostEstimate(
                 flops=flops, bytes_accessed=4 * width * width, transcendentals=0
             ),
         )(flag, *args)
 
-    kv, normed, pooled, pairs, spread = flagged(
+    kv, normed, pooled, pairs, spread = call(
         front_kernel,
         (shape(nz, packed, qk), shape(pool, width), shape(pool, width, dtype=F32),
          shape(taps, pool, width, dtype=F32), shape(pool, width, dtype=F32)),
         [pltpu.VMEM((width // 128, n, 128), F32) for n in (fine + 4, fine + 4, fine)],
         2 * pool * width * (qk + vd),
-        inside, x, low, high, gain_in, conv_taps, gain_attn, key_weight, value_weight,
+        x, low, high, gain_in, conv_taps, gain_attn, key_weight, value_weight,
     )
 
     def ours_theirs(ours, theirs):
@@ -411,35 +478,8 @@
     )
 
     gkv = (gkv_own.astype(F32) + swap(gkv_other).astype(F32)).astype(BF)
-    gkv = jnp.sum(exchange(gkv, "y").astype(F32), axis=0).astype(BF)
-    gkv = jnp.sum(exchange(gkv, "z").astype(F32), axis=0).astype(BF)
-    gkv_group = exchange(
-        jnp.broadcast_to(gkv[None], (nx * nc,) + gkv.shape), ("x", "core")
-    )
-
-    mixed_out = (pooled + dot(mixed, out_weight)).astype(BF)
-    half, small = call(
-        back_kernel,
-        (shape(pool, width), shape(8, width, dtype=F32)),
-        [],
-        2 * pool * width * (qk + vd),
-        gkv, contract_cols(grad_queries, query_weight), key_weight, value_weight, pooled,
-        gain_attn, grad_y, pairs, spread,
-    )
-    before = lax.ppermute(half[pool - 1 :], seq, up)
-    after = lax.ppermute(half[:1], seq, down)
-    (input_grad,) = call(
-        input_kernel,
-        (shape(fine, width),),
-        [pltpu.VMEM((pool + 16, width), F32)]
-        + [pltpu.VMEM((width // 128, fine, 128), F32) for _ in range(2)],
-        fine * width * 40,
-        x, gain_in, conv_taps, half, before, after,
-    )
-
-    total = small
-    for step in range(1, nx):
-        total = total + lax.ppermute(small, "x", [(i, (i + step) % nx) for i in range(nx)])
+    (gkv,) = call(sum_kernel, (shape(nz, packed, qk),), [], 0, exchange(gkv, "y"))
+    gkv = exchange(gkv, "z")
 
     keep = width // nx
     each = width // (count * nx)
@@ -455,43 +495,65 @@
         4 * keep * width * nx * nc * pool,
         first, target, early, later,
     )
+    part = contract_cols(grad_queries, query_weight)
+    gkv, left, sums, part = lax.optimization_barrier((gkv, left, sums, part))
+
     tail = taps + 2
+    tiles = width // qk
+    extra = (tail * tiles // nc + 15) // 16 * 16
+    half, gkv = call(
+        functools.partial(back_kernel, nc),
+        (shape(pool, width), shape(nx * nc, packed + extra, qk)),
+        [pltpu.VMEM((8, width), F32)],
+        2 * pool * width * (qk + vd),
+        gkv, part, key_weight, value_weight, pooled, gain_attn, grad_y, pairs, spread,
+    )
+    before = lax.ppermute(half[pool - 1 :], seq, up)
+    after = lax.ppermute(half[:1], seq, down)
+    got = exchange(gkv, ("x", "core"))
+    (input_grad,) = call(
+        input_kernel,
+        (shape(fine, width),),
+        [pltpu.VMEM((pool + 16, width), F32)]
+        + [pltpu.VMEM((width // 128, fine, 128), F32) for _ in range(2)],
+        fine * width * 40,
+        x, gain_in, conv_taps, half, before, after,
+    )
+    mixed_out = (pooled + dot(mixed, out_weight)).astype(BF)
     (sums,) = flagged(
         functools.partial(late_kernel, q_cols),
-        (shape(ny, keep // ny + 16, width),),
+        (shape(ny, tiles * keep // ny + extra, qk),),
         [],
         2 * keep * nx * nc * pool * (qk + vd),
-        first, left, sums, gkv_group, total,
+        first, left, sums, got,
     )
     got = exchange(sums, "y")
-    part = keep // (ny * nz)
-    slots = (part + tail + 7) // 8 * 8
+    got, mixed_out, input_grad = lax.optimization_barrier((got, mixed_out, input_grad))
     (sums,) = call(
-        functools.partial(turn_kernel, tail),
-        (shape(nz, slots, width),),
-        [pltpu.VMEM((keep // ny + 16, width), F32)],
+        functools.partial(turn_kernel, tiles),
+        (shape(nz, tiles * keep // (ny * nz) + extra, qk),),
+        [pltpu.VMEM((tiles * keep // ny + extra, qk), F32)],
         0,
         got,
     )
-    sums = jnp.sum(exchange(sums, "z").astype(F32), axis=0)
-    small = sums[part : part + tail]
-    mine = jnp.where(first_core, sums[:each], sums[each:part])
-    theirs = jnp.where(first_core, sums[each:part], sums[:each])
-    got = swap(jnp.concatenate([theirs, small], axis=0))
-    small = small + got[each:]
-    keys_rows = jnp.where(first_core, mine, got[:each])
-    out_rows = jnp.where(first_core, got[:each], mine)
-    return (
-        mixed_out[None],
-        input_grad[None],
-        keys_rows[:, :q_cols],
-        keys_rows[:, q_cols : q_cols + qk],
-        keys_rows[:, q_cols + qk : q_cols + qk + vd],
-        out_rows,
-        small[:taps],
-        small[taps],
-        small[taps + 1],
-    )
+    got = exchange(sums, "z")
+    mine, theirs = flagged(
+        functools.partial(end_kernel, tiles, each),
+        (shape(tiles * each + extra, qk, dtype=F32),) * 2,
+        [pltpu.VMEM((2 * tiles * each + extra, qk), F32)],
+        0,
+        first, got,
+    )
+    results = flagged(
+        functools.partial(last_kernel, tiles),
+        tuple(shape(*dims, dtype=F32) for dims in (
+            (each, q_cols), (each, qk), (each, vd), (each, width),
+            (taps, width), (width,), (width,))),
+        [pltpu.VMEM((2, tiles * each + extra, qk), F32)],
+        0,
+        first, mine, swap(theirs),
+    )
+    return mixed_out[None], input_grad[None], *results
 
 
 def solution(mesh):

time: 246 us -> 215 us (0.87)
  local copies, waits for them, and re-layouts: 40.3 us -> 6.48 us
  Pallas kernels: 22.4 us -> 42 us
  starting transfers between devices: 56.6 us -> 44.2 us
  blocking collectives: 40.6 us -> 33 us
  waiting for transfers between devices: 46.3 us -> 52.7 us
  other arithmetic: 12.2 us -> 8.09 us
    unnamed x79 -> x20, local copies, waits for them, and re-layouts: 31.1 us -> 2.56 us
    pallas_call x4 -> x6, Pallas kernels: 17.8 us -> 30.6 us  [call(): pl.pallas_call(kernel, out_shape=out_shape, scratch_shapes=scratch, compi...]
    all_to_all x2, blocking collectives: 40.6 us -> 33 us  [exchange(): return lax.all_to_all(blocks, axis, 0, 0, tiled=True)]
    pallas_call x3 -> x4, Pallas kernels: 4.56 us -> 11.4 us  [flagged(): pl.pallas_call(kernel, out_shape=out_shape, in_specs=[smem] + [vmem] * le...]
    ppermute x5, starting transfers between devices: 8.72 us -> 3.31 us  [swap(): return lax.ppermute(block, 'core', [(0, 1), (1, 0)])]
    reduce_sum x3 -> x0, other arithmetic: 4.52 us -> none  [the longest x1 2.34 us: shards(): gkv = jnp.sum(exchange(gkv, 'y').astype(F32), axis=0).astype(BF)]
    ppermute x3 -> x0, starting transfers between devices: 4.26 us -> none  [shards(): lax.ppermute(small, 'x', [(i, (i + step) % nx) for i in range(nx)])]
    all_to_all x5, waiting for transfers between devices: 42.8 us -> 39.4 us  [exchange(): return lax.all_to_all(blocks, axis, 0, 0, tiled=True)]
  transfers between devices with their start and end apart: 19 -> 16, of which waited for: 7 -> 10; matrix products, arithmetic and copies ran while one was open for 12% -> 10% of each run, Pallas kernels for 8% -> 12%
where the time goes in v3:
time: 215 us; the launch traced here: 213 us
  waiting for transfers between devices  52.7 us (25%)
  starting transfers between devices  44.2 us (21%)
  Pallas kernels  42 us (20%)
  blocking collectives  33 us (15%)
  between operations  14.2 us (7%)
  matrix products  12.8 us (6%)
  other arithmetic  8.09 us (4%)
  local copies, waits for them, and re-layouts  6.48 us (3%)
    all_to_all x5, waiting for transfers between devices, exchange(): return lax.all_to_all(blocks, axis, 0, 0, tiled=True)  39.4 us
    all_to_all x2, blocking collectives, exchange(): return lax.all_to_all(blocks, axis, 0, 0, tiled=True)  33 us
    pallas_call x6, Pallas kernels, call(): pl.pallas_call(kernel, out_shape=out_shape, scratch_shapes=scratch, compi...  30.6 us
    all_to_all x5, starting transfers between devices, exchange(): return lax.all_to_all(blocks, axis, 0, 0, tiled=True)  27.9 us
    pallas_call x4, Pallas kernels, flagged(): pl.pallas_call(kernel, out_shape=out_shape, in_specs=[smem] + [vmem] * le...  11.4 us
    dot_general x2, matrix products, contract_cols(): lax.dot_general(left, right, (((1,), (1,)), ((), ())), preferred_element_...  7.41 us
    dot_general x2, matrix products, dot(): return jnp.dot(left, right, preferred_element_type=F32)  5.39 us
    ppermute x5, waiting for transfers between devices, swap(): return lax.ppermute(block, 'core', [(0, 1), (1, 0)])  5.28 us
  transfers between devices with their start and end apart: 16, of which 10 were waited for; matrix products, arithmetic and copies ran while one was open for 10% of the time, Pallas kernels for 12%

profile of v3, /device:TPU:1, one launch (start us, length us, event | category | flops | bytes accessed | tf_op | source)
XLA Modules:
  0.0 213.4 jit_solution(16055626799211523697)
XLA Ops:
  7.2 0.0 copy-start
  7.2 0.9 slice_bitcast_fusion
  8.1 4.7 %collective-permute-start = (bf16[2,1536]{1,0:T(2,128)(2,1)S(1)}, bf16[2,1536]{1,0:T(2,128)(2,1)S(1)}, u32[]{:S(2)}, u32[]{:S(2)}) collective-permute-start(bf16[2,1536]{1,0:T(2,128)(2,1)S(1)} %get-tuple-element.76), channel_id=1, source_target_pairs={{0,4},{4,8},{8,12},{12,16},{16,20},{20,24},{24,28},{28,32},{32,36}... | collective-permute-start | bytes 18440 | tf_op jit(solution)/shard_map/ppermute | solution.py:432
  12.8 1.9 collective-permute-start.1
  14.8 0.0 collective-permute-done.low_ref
  14.8 0.0 copy-start.6
  14.8 3.0 %collective-permute-done.1.high_ref = bf16[2,1536]{1,0:T(2,128)(2,1)S(1)} collective-permute-done((bf16[2,1536]{1,0:T(2,128)(2,1)S(1)}, bf16[2,1536]{1,0:T(2,128)(2,1)S(1)}, u32[]{:S(2)}, u32[]{:S(2)}) %collective-permute-start.1) | collective-permute-done | bytes 6176 | tf_op jit(solution)/shard_map/ppermute | solution.py:433
  17.8 0.6 copy-done.8
  18.4 4.5 %shard_map.160 = (bf16[8,160,128]{2,1,0:T(8,128)(2,1)}, bf16[64,1536]{1,0:T(8,128)(2,1)}, f32[64,1536]{1,0:T(8,128)}, f32[5,64,1536]{2,1,0:T(8,128)}, f32[64,1536]{1,0:T(8,128)}) custom-call(bf16[128,1536]{1,0:T(8,128)(2,1)} %bitcast.24, bf16[2,1536]{1,0:T(2,128)(2,1)} %copy-done.6, bf16[2,1536]{1,0:T(2,128)(2,1)} %copy-done.8, f32[1536]{0:T(1024)} %gain_ref.3, ...), custom_call_target="tpu_custom_call" | custom-call | flops 62914560 | bytes 4708352 | tf_op jit(solution)/shard_map/pallas_call | solution.py:42
  22.8 8.2 %all-to-all-start = ((bf16[8,160,128]{2,1,0:T(8,128)(2,1)}), bf16[8,160,128]{2,1,0:T(8,128)(2,1)}, u32[]{:S(2)}, u32[]{:S(2)}) async-start(bf16[8,160,128]{2,1,0:T(8,128)(2,1)} %get-tuple-element.41), calls=%async_computation | async-start | bytes 655360 | tf_op jit(solution)/shard_map/all_to_all | solution.py:36
  31.0 4.7 %convolution_convert_fusion.g_ref = bf16[64,1536]{1,0:T(8,128)(2,1)} fusion(bf16[1536,1536]{1,0:T(8,128)(2,1)} %param.16, bf16[1,64,1536]{2,1,0:T(8,128)(2,1)} %param.17), kind=kOutput, calls=%fused_computation.3 | convolution fusion | flops 302088192 | bytes 5111808 | tf_op jit(solution)/shard_map/dot_general | solution.py:24
  35.7 0.0 copy-done
  35.7 1.3 convolution_convert_fusion.1.q_ref
  37.1 4.0 %all-to-all-done = bf16[8,160,128]{2,1,0:T(8,128)(2,1)} async-done(((bf16[8,160,128]{2,1,0:T(8,128)(2,1)}), bf16[8,160,128]{2,1,0:T(8,128)(2,1)}, u32[]{:S(2)}, u32[]{:S(2)}) %all-to-all-start) | async-done | bytes 327712 | tf_op jit(solution)/shard_map/all_to_all | solution.py:36
  41.1 2.2 %broadcast_in_dim.14 = bf16[4,8,160,128]{3,2,1,0:T(8,128)(2,1)} broadcast(bf16[8,160,128]{2,1,0:T(8,128)(2,1)} %all-to-all-done), dimensions={1,2,3} | broadcast | bytes 1638400 | tf_op jit(solution)/shard_map/broadcast_in_dim | solution.py:469
  43.3 7.7 %all-to-all-start.1 = ((bf16[4,8,160,128]{3,2,1,0:T(8,128)(2,1)}), bf16[4,8,160,128]{3,2,1,0:T(8,128)(2,1)}, u32[]{:S(2)}, u32[]{:S(2)}) async-start(bf16[4,8,160,128]{3,2,1,0:T(8,128)(2,1)} %broadcast_in_dim.14), calls=%async_computation.1 | async-start | bytes 2621440 | tf_op jit(solution)/shard_map/all_to_all | solution.py:36
  51.0 1.6 broadcast_select_fusion.1
  52.6 1.0 collective-permute-start.4
  53.6 14.6 %all-to-all-done.1.kv0_ref = bf16[4,8,160,128]{3,2,1,0:T(8,128)(2,1)} async-done(((bf16[4,8,160,128]{3,2,1,0:T(8,128)(2,1)}), bf16[4,8,160,128]{3,2,1,0:T(8,128)(2,1)}, u32[]{:S(2)}, u32[]{:S(2)}) %all-to-all-start.1) | async-done | bytes 1310752 | tf_op jit(solution)/shard_map/all_to_all | solution.py:36
  68.3 1.7 collective-permute-start.2
  70.0 0.0 collective-permute-done.4
  70.0 0.8 pad_maximum_fusion
  70.8 0.0 all-gather.3.cloned.1.call-update
  70.8 0.0 all-gather.5.cloned.1.call-start
  70.8 2.2 %collective-permute-done.2.kv1_ref = bf16[4,8,160,128]{3,2,1,0:T(8,128)(2,1)} collective-permute-done((bf16[4,8,160,128]{3,2,1,0:T(8,128)(2,1)}, bf16[4,8,160,128]{3,2,1,0:T(8,128)(2,1)}, u32[]{:S(2)}, u32[]{:S(2)}) %collective-permute-start.2) | collective-permute-done | bytes 1310752 | tf_op jit(solution)/shard_map/ppermute | solution.py:32
  73.0 14.4 %shard_map.161 = (bf16[64,1536]{1,0:T(8,128)(2,1)}, bf16[64,1024]{1,0:T(8,128)(2,1)}, bf16[4,8,160,128]{3,2,1,0:T(8,128)(2,1)}, bf16[4,8,160,128]{3,2,1,0:T(8,128)(2,1)}) custom-call(bf16[64,1024]{1,0:T(8,128)(2,1)} %convolution_convert_fusion.1.q_ref, bf16[64,1536]{1,0:T(8,128)(2,1)} %convolution_convert_fusion.g_ref, ...), custom_call_target="tpu_custom_call" | custom-call | flops 4026531840 | bytes 5898240 | tf_op jit(solution)/shard_map/pallas_call | solution.py:42
  87.4 0.4 collective-permute-start.3
  87.8 1.1 pad_select_fusion.1
  88.8 0.2 collective-permute-start.5
  89.1 1.7 collective-permute-done.5
  90.7 0.8 pad_maximum_fusion.1
  91.5 0.0 all-gather.5.cloned.1.call-update
  91.5 0.0 collective-permute-done.3
  91.5 3.1 %add_convert_fusion = bf16[4,8,160,128]{3,2,1,0:T(8,128)(2,1)} fusion(bf16[4,8,160,128]{3,2,1,0:T(8,128)(2,1)} %collective-permute-done.3, bf16[4,8,160,128]{3,2,1,0:T(8,128)(2,1)} %get-tuple-element.46), kind=kLoop, calls=%fused_computation | loop fusion | flops 2621440 | bytes 3932160 | tf_op jit(solution)/shard_map/convert_element_type | solution.py:480
  94.7 4.3 %all-to-all-start.2 = ((bf16[4,8,160,128]{3,2,1,0:T(8,128)(2,1)}), bf16[4,8,160,128]{3,2,1,0:T(8,128)(2,1)}, u32[]{:S(2)}, u32[]{:S(2)}) async-start(bf16[4,8,160,128]{3,2,1,0:T(8,128)(2,1)} %add_convert_fusion), calls=%async_computation.2 | async-start | bytes 2621440 | tf_op jit(solution)/shard_map/all_to_all | solution.py:36
  99.0 17.7 %all-to-all-done.2.parts_ref = bf16[4,8,160,128]{3,2,1,0:T(8,128)(2,1)} async-done(((bf16[4,8,160,128]{3,2,1,0:T(8,128)(2,1)}), bf16[4,8,160,128]{3,2,1,0:T(8,128)(2,1)}, u32[]{:S(2)}, u32[]{:S(2)}) %all-to-all-start.2) | async-done | bytes 1310752 | tf_op jit(solution)/shard_map/all_to_all | solution.py:36
  116.7 2.2 %shard_map.162 = bf16[8,160,128]{2,1,0:T(8,128)(2,1)} custom-call(bf16[4,8,160,128]{3,2,1,0:T(8,128)(2,1)} %all-to-all-done.2.parts_ref), custom_call_target="tpu_custom_call" | custom-call | bytes 1638400 | tf_op jit(solution)/shard_map/pallas_call | solution.py:42
  118.9 3.4 %all-to-all-start.3 = ((bf16[8,160,128]{2,1,0:T(8,128)(2,1)}), bf16[8,160,128]{2,1,0:T(8,128)(2,1)S(1)}, u32[]{:S(2)}, u32[]{:S(2)}) async-start(bf16[8,160,128]{2,1,0:T(8,128)(2,1)} %shard_map.162), calls=%async_computation.3 | async-start | bytes 655360 | tf_op jit(solution)/shard_map/all_to_all | solution.py:36
  122.3 0.7 compare_select_fusion.6.target_ref
  123.0 2.7 %fusion.13.part_ref = f32[64,1536]{1,0:T(8,128)} fusion(bf16[64,1024]{1,0:T(8,128)(2,1)} %get-tuple-element.48, bf16[1536,1024]{1,0:T(8,128)(2,1)S(1)} %copy-done), kind=kOutput, calls=%fused_computation.49 | convolution fusion | flops 201326592 | bytes 3670016 | tf_op jit(solution)/shard_map/dot_general | solution.py:24
  125.8 5.0 %shard_map.163 = (bf16[384,512]{1,0:T(8,128)(2,1)}, bf16[384,1536]{1,0:T(8,128)(2,1)}) custom-call(s32[1]{0:T(128)} %bitcast.first_ref, s32[1,1536]{1,0:T(1,128)} %compare_select_fusion.6.target_ref, bf16[512,1536]{1,0:T(8,128)(2,1)} %all-gather.3.cloned.1.call-done.e_ref, bf16[512,1536]{1,0:T(8,128)(2,1)} %all-gather.5.cloned.1.call-done.m_ref), custom_call_target="tpu_custom_call" | custom-call | flops 1207959552 | bytes 9437184 | tf_op jit(solution)/shard_map/pallas_call | solution.py:438
  130.8 3.0 %all-to-all-done.3.parts_ref = bf16[8,160,128]{2,1,0:T(8,128)(2,1)S(1)} async-done(((bf16[8,160,128]{2,1,0:T(8,128)(2,1)}), bf16[8,160,128]{2,1,0:T(8,128)(2,1)S(1)}, u32[]{:S(2)}, u32[]{:S(2)}) %all-to-all-start.3) | async-done | bytes 327712 | tf_op jit(solution)/shard_map/all_to_all | solution.py:36
  133.8 0.7 copy-done.3
  134.5 3.9 %shard_map.164 = (bf16[64,1536]{1,0:T(8,128)(2,1)}, bf16[8,208,128]{2,1,0:T(8,128)(2,1)}) custom-call(bf16[8,160,128]{2,1,0:T(8,128)(2,1)} %copy-done.3, f32[64,1536]{1,0:T(8,128)} %fusion.13.part_ref, bf16[1536,128]{1,0:T(8,128)(2,1)} %kw_ref.3, bf16[192,1536]{1,0:T(8,128)(2,1)} %bitcast.22, f32[64,1536]{1,0:T(8,128)} %get-tuple-element.56.pooled_ref, ...), custom_call_target="tpu_custom_call" | custom-call | flops 62914560 | bytes 5281792 | tf_op jit(solution)/shard_map/pallas_call | solution.py:42
  138.4 15.5 %all_to_all.35.got_ref = bf16[8,208,128]{2,1,0:T(8,128)(2,1)} all-to-all(bf16[8,208,128]{2,1,0:T(8,128)(2,1)} %get-tuple-element.59), channel_id=1, replica_groups=mesh['z'=8,'y'=4,'core'=2,'x'=4] {'x','core'}, dimensions={0} | all-to-all | bytes 851968 | tf_op jit(solution)/shard_map/all_to_all | solution.py:36
  153.9 3.1 %shard_map.165 = bf16[4,1200,128]{2,1,0:T(8,128)(2,1)} custom-call(s32[1]{0:T(128)} %bitcast.first_ref, bf16[384,512]{1,0:T(8,128)(2,1)} %get-tuple-element.52.left_ref, bf16[384,1536]{1,0:T(8,128)(2,1)} %get-tuple-element.53.sums_ref, bf16[8,208,128]{2,1,0:T(8,128)(2,1)} %all_to_all.35.got_ref), custom_call_target="tpu_custom_call" | custom-call | flops 125829120 | bytes 9437184 | tf_op jit(solution)/shard_map/pallas_call | solution.py:438
  157.0 4.3 %all-to-all-start.5 = ((bf16[4,1200,128]{2,1,0:T(8,128)(2,1)}), bf16[4,1200,128]{2,1,0:T(8,128)(2,1)}, u32[]{:S(2)}, u32[]{:S(2)}) async-start(bf16[4,1200,128]{2,1,0:T(8,128)(2,1)} %shard_map.165), calls=%async_computation.5 | async-start | bytes 2457600 | tf_op jit(solution)/shard_map/all_to_all | solution.py:36
  161.3 0.8 fusion.12
  162.1 4.4 %collective-permute-start.6 = (bf16[1,1536]{1,0:T(2,128)(2,1)S(1)}, bf16[1,1536]{1,0:T(2,128)(2,1)S(1)}, u32[]{:S(2)}, u32[]{:S(2)}) collective-permute-start(bf16[1,1536]{1,0:T(2,128)(2,1)S(1)} %get-tuple-element.80), channel_id=1, source_target_pairs={{0,4},{4,8},{8,12},{12,16},{16,20},{20,24},{24,28},{28,32},{32,36}... | collective-permute-start | bytes 9224 | tf_op jit(solution)/shard_map/ppermute | solution.py:511
  166.5 1.9 collective-permute-start.7
  168.4 0.0 copy-done.2
  168.4 4.1 %fusion = bf16[64,1536]{1,0:T(8,128)(2,1)} fusion(f32[64,1536]{1,0:T(8,128)S(1)} %copy-done.2, bf16[64,1536]{1,0:T(8,128)(2,1)} %get-tuple-element.49, bf16[1536,1536]{1,0:T(8,128)(2,1)} %param.16), kind=kOutput, calls=%fused_computation.2 | convolution fusion | flops 302186496 | bytes 5505024 | tf_op jit(solution)/shard_map/dot_general | solution.py:28
  172.5 1.8 collective-permute-done.6.before_ref
  174.3 3.3 %collective-permute-done.7.after_ref = bf16[1,1536]{1,0:T(2,128)(2,1)S(1)} collective-permute-done((bf16[1,1536]{1,0:T(2,128)(2,1)S(1)}, bf16[1,1536]{1,0:T(2,128)(2,1)S(1)}, u32[]{:S(2)}, u32[]{:S(2)}) %collective-permute-start.7) | collective-permute-done | bytes 3104 | tf_op jit(solution)/shard_map/ppermute | solution.py:512
  177.5 0.6 copy-done.9
  178.1 3.3 %shard_map.166 = bf16[128,1536]{1,0:T(8,128)(2,1)} custom-call(bf16[128,1536]{1,0:T(8,128)(2,1)} %bitcast.25, f32[1536]{0:T(1024)} %gain_ref.3, f32[5,1536]{1,0:T(8,128)} %taps_ref.3, bf16[64,1536]{1,0:T(8,128)(2,1)} %get-tuple-element.60.half_ref, bf16[1,1536]{1,0:T(2,128)(2,1)} %copy-done.7, bf16[1,1536]{1,0:T(2,128)(2,1)} %copy-done.9), custom_call_target="tpu_custom_call" | custom-call | flops 7864320 | bytes 1026048 | tf_op jit(solution)/shard_map/pallas_call | solution.py:42
  181.4 0.0 all-to-all-done.5.got_ref
  181.4 2.3 %shard_map.167 = bf16[8,192,128]{2,1,0:T(8,128)(2,1)} custom-call(bf16[4,1200,128]{2,1,0:T(8,128)(2,1)} %all-to-all-done.5.got_ref), custom_call_target="tpu_custom_call" | custom-call | bytes 1622016 | tf_op jit(solution)/shard_map/pallas_call | solution.py:42
  183.8 17.5 %all_to_all.36.got_ref = bf16[8,192,128]{2,1,0:T(8,128)(2,1)} all-to-all(bf16[8,192,128]{2,1,0:T(8,128)(2,1)} %shard_map.167), channel_id=1, replica_groups=mesh['z'=8,'y'=4,'core'=2,'x'=4] {'z'}, dimensions={0} | all-to-all | bytes 786432 | tf_op jit(solution)/shard_map/all_to_all | solution.py:36
  201.2 1.7 shard_map.168
  202.9 0.0 collective-permute-start.8
  202.9 1.5 collective-permute-done.8.got_ref
  204.4 0.6 copy-done.5
  205.0 1.5 shard_map.169
  (15 shorter events, 0.0 us)
Async XLA Ops:
  7.2 28.6 %copy-start = (bf16[1536,1024]{1,0:T(8,128)(2,1)S(1)}, bf16[1536,1024]{1,0:T(8,128)(2,1)}, u32[]{:S(2)}) copy-start(bf16[1536,1024]{1,0:T(8,128)(2,1)} %param.13) | copy-start | bytes 9437188
  8.1 6.7 %collective-permute-start = (bf16[2,1536]{1,0:T(2,128)(2,1)S(1)}, bf16[2,1536]{1,0:T(2,128)(2,1)S(1)}, u32[]{:S(2)}, u32[]{:S(2)}) collective-permute-start(bf16[2,1536]{1,0:T(2,128)(2,1)S(1)} %get-tuple-element.76), channel_id=1, source_target_pairs={{0,4},{4,8},{8,12},{12,16},{16,20},{20,24},{24,28},{28,32},{32,36}... | collective-permute-start | bytes 18440 | tf_op jit(solution)/shard_map/ppermute | solution.py:432
  12.8 4.9 %collective-permute-start.1 = (bf16[2,1536]{1,0:T(2,128)(2,1)S(1)}, bf16[2,1536]{1,0:T(2,128)(2,1)S(1)}, u32[]{:S(2)}, u32[]{:S(2)}) collective-permute-start(bf16[2,1536]{1,0:T(2,128)(2,1)S(1)} %get-tuple-element.75), channel_id=1, source_target_pairs={{4,0},{8,4},{12,8},{16,12},{20,16},{24,20},{28,24},{32,28},{36,32}... | collective-permute-start | bytes 18440 | tf_op jit(solution)/shard_map/ppermute | solution.py:433
  14.8 3.0 %copy-start.6 = (bf16[2,1536]{1,0:T(2,128)(2,1)}, bf16[2,1536]{1,0:T(2,128)(2,1)S(1)}, u32[]{:S(2)}) copy-start(bf16[2,1536]{1,0:T(2,128)(2,1)S(1)} %collective-permute-done.low_ref) | copy-start | bytes 18436
  17.8 0.6 copy-start.8
  22.8 18.2 %all-to-all-start = ((bf16[8,160,128]{2,1,0:T(8,128)(2,1)}), bf16[8,160,128]{2,1,0:T(8,128)(2,1)}, u32[]{:S(2)}, u32[]{:S(2)}) async-start(bf16[8,160,128]{2,1,0:T(8,128)(2,1)} %get-tuple-element.41), calls=%async_computation | async-start | bytes 655360 | tf_op jit(solution)/shard_map/all_to_all | solution.py:36
  31.0 4.7 %copy-start.4 = (bf16[64,1536]{1,0:T(8,128)(2,1)S(1)}, bf16[64,1536]{1,0:T(8,128)(2,1)}, u32[]{:S(2)}) copy-start(bf16[64,1536]{1,0:T(8,128)(2,1)} %get-tuple-element.42) | copy-start | bytes 589828
  37.1 13.9 %copy-start.1 = (bf16[1,64,1536]{2,1,0:T(8,128)(2,1)S(1)}, bf16[1,64,1536]{2,1,0:T(8,128)(2,1)}, u32[]{:S(2)}) copy-start(bf16[1,64,1536]{2,1,0:T(8,128)(2,1)} %param.17) | copy-start | bytes 589828
  43.3 24.9 %all-to-all-start.1 = ((bf16[4,8,160,128]{3,2,1,0:T(8,128)(2,1)}), bf16[4,8,160,128]{3,2,1,0:T(8,128)(2,1)}, u32[]{:S(2)}, u32[]{:S(2)}) async-start(bf16[4,8,160,128]{3,2,1,0:T(8,128)(2,1)} %broadcast_in_dim.14), calls=%async_computation.1 | async-start | bytes 2621440 | tf_op jit(solution)/shard_map/all_to_all | solution.py:36
  51.0 74.8 %all-gather.3.cloned.1.call-start = ((), (), s32[]{:S(2)}) async-start(), calls=%async_computation.7 | async-start | bytes 1966080 | tf_op jit(solution)/shard_map/all_gather | solution.py:463
  52.6 17.4 %collective-permute-start.4 = (bf16[64,1536]{1,0:T(8,128)(2,1)}, bf16[64,1536]{1,0:T(8,128)(2,1)S(1)}, u32[]{:S(2)}, u32[]{:S(2)}) collective-permute-start(bf16[64,1536]{1,0:T(8,128)(2,1)} %get-tuple-element.74), channel_id=1, source_target_pairs={{0,4},{4,0},{1,5},{5,1},{2,6},{6,2},{3,7},{7,3},{8,12},{12,8},{9,1... | collective-permute-start | bytes 589832 | tf_op jit(solution)/shard_map/ppermute | solution.py:32
  68.3 4.7 %collective-permute-start.2 = (bf16[4,8,160,128]{3,2,1,0:T(8,128)(2,1)}, bf16[4,8,160,128]{3,2,1,0:T(8,128)(2,1)}, u32[]{:S(2)}, u32[]{:S(2)}) collective-permute-start(bf16[4,8,160,128]{3,2,1,0:T(8,128)(2,1)} %all-to-all-done.1.kv0_ref), channel_id=1, source_target_pairs={{0,4},{4,0},{1,5},{5,1},{2,6},{6,2},{3,7},{7,3},{8,12},{12,8},{9,1... | collective-permute-start | bytes 3932168 | tf_op jit(solution)/shard_map/ppermute | solution.py:32
  70.8 55.0 %all-gather.5.cloned.1.call-start = ((), (), s32[]{:S(2)}) async-start(), calls=%async_computation.8 | async-start | bytes 1966080 | tf_op jit(solution)/shard_map/all_gather | solution.py:476
  87.4 4.1 %collective-permute-start.3 = (bf16[4,8,160,128]{3,2,1,0:T(8,128)(2,1)}, bf16[4,8,160,128]{3,2,1,0:T(8,128)(2,1)}, u32[]{:S(2)}, u32[]{:S(2)}) collective-permute-start(bf16[4,8,160,128]{3,2,1,0:T(8,128)(2,1)} %get-tuple-element.47), channel_id=1, source_target_pairs={{0,4},{4,0},{1,5},{5,1},{2,6},{6,2},{3,7},{7,3},{8,12},{12,8},{9,1... | collective-permute-start | bytes 3932168 | tf_op jit(solution)/shard_map/ppermute | solution.py:32
  88.8 1.9 collective-permute-start.5
  94.7 22.0 %all-to-all-start.2 = ((bf16[4,8,160,128]{3,2,1,0:T(8,128)(2,1)}), bf16[4,8,160,128]{3,2,1,0:T(8,128)(2,1)}, u32[]{:S(2)}, u32[]{:S(2)}) async-start(bf16[4,8,160,128]{3,2,1,0:T(8,128)(2,1)} %add_convert_fusion), calls=%async_computation.2 | async-start | bytes 2621440 | tf_op jit(solution)/shard_map/all_to_all | solution.py:36
  118.9 14.9 %all-to-all-start.3 = ((bf16[8,160,128]{2,1,0:T(8,128)(2,1)}), bf16[8,160,128]{2,1,0:T(8,128)(2,1)S(1)}, u32[]{:S(2)}, u32[]{:S(2)}) async-start(bf16[8,160,128]{2,1,0:T(8,128)(2,1)} %shard_map.162), calls=%async_computation.3 | async-start | bytes 655360 | tf_op jit(solution)/shard_map/all_to_all | solution.py:36
  133.8 0.7 copy-start.3
  153.9 14.5 %copy-start.2 = (f32[64,1536]{1,0:T(8,128)S(1)}, f32[64,1536]{1,0:T(8,128)}, u32[]{:S(2)}) copy-start(f32[64,1536]{1,0:T(8,128)} %get-tuple-element.56.pooled_ref) | copy-start | bytes 1179652
  157.0 24.4 %all-to-all-start.5 = ((bf16[4,1200,128]{2,1,0:T(8,128)(2,1)}), bf16[4,1200,128]{2,1,0:T(8,128)(2,1)}, u32[]{:S(2)}, u32[]{:S(2)}) async-start(bf16[4,1200,128]{2,1,0:T(8,128)(2,1)} %shard_map.165), calls=%async_computation.5 | async-start | bytes 2457600 | tf_op jit(solution)/shard_map/all_to_all | solution.py:36
  162.1 12.2 %collective-permute-start.6 = (bf16[1,1536]{1,0:T(2,128)(2,1)S(1)}, bf16[1,1536]{1,0:T(2,128)(2,1)S(1)}, u32[]{:S(2)}, u32[]{:S(2)}) collective-permute-start(bf16[1,1536]{1,0:T(2,128)(2,1)S(1)} %get-tuple-element.80), channel_id=1, source_target_pairs={{0,4},{4,8},{8,12},{12,16},{16,20},{20,24},{24,28},{28,32},{32,36}... | collective-permute-start | bytes 9224 | tf_op jit(solution)/shard_map/ppermute | solution.py:511
  166.5 11.0 %collective-permute-start.7 = (bf16[1,1536]{1,0:T(2,128)(2,1)S(1)}, bf16[1,1536]{1,0:T(2,128)(2,1)S(1)}, u32[]{:S(2)}, u32[]{:S(2)}) collective-permute-start(bf16[1,1536]{1,0:T(2,128)(2,1)S(1)} %get-tuple-element.79), channel_id=1, source_target_pairs={{4,0},{8,4},{12,8},{16,12},{20,16},{24,20},{28,24},{32,28},{36,32}... | collective-permute-start | bytes 9224 | tf_op jit(solution)/shard_map/ppermute | solution.py:512
  174.3 3.3 %copy-start.7 = (bf16[1,1536]{1,0:T(2,128)(2,1)}, bf16[1,1536]{1,0:T(2,128)(2,1)S(1)}, u32[]{:S(2)}) copy-start(bf16[1,1536]{1,0:T(2,128)(2,1)S(1)} %collective-permute-done.6.before_ref) | copy-start | bytes 9220
  177.5 0.6 copy-start.9
  202.9 1.5 collective-permute-start.8
  204.4 0.6 copy-start.5
Sparse Core Ops, SparseCore 0:
  70.9 22.8 all-gather.2
  95.5 29.1 all-gather.4

commit v4 on v3

--- a/solution.py
+++ b/solution.py
@@ -30,6 +30,11 @@
 
 def swap(block):
     return lax.ppermute(block, "core", [(0, 1), (1, 0)])
+
+
+def shift(block, axis, step):
+    count = lax.axis_size(axis)
+    return lax.ppermute(block, axis, [(i, (i + step) % count) for i in range(count)])
 
 
 def exchange(blocks, axis):
@@ -125,84 +130,128 @@
         kv_ref[i] = kv
 
 
-def attention_kernel(scale, heads, q_ref, g_ref, kv0_ref, kv1_ref,
-                     mixed_ref, gq_ref, gkv0_ref, gkv1_ref, s_ref, gw_ref, v_ref):
+def attention_kernel(scale, heads, group, unroll, place_ref, q_ref, g_ref, *refs):
+    ins = refs[:10]
+    mixed_ref, gq_ref, own_ref, others_ref = refs[10:14]
+    kv_ref, gkv_ref, s_ref, gw_ref, in_sem, out_sem = refs[14:]
+    ny, nz, packed, _ = own_ref.shape
+    half = nz // 2
+    slots = [(i * nz, nz) for i in range(ny - 1)]
+    slots += [((ny - 1) * nz, half), ((ny - 1) * nz + half, half)]
+    slots += [(ny * nz + at, size) for at, size in slots]
+    loads = [
+        pltpu.make_async_copy(ref, kv_ref.at[at : at + size], in_sem.at[k])
+        for k, (ref, (at, size)) in enumerate(zip(ins, slots))
+    ]
+    for load in loads:
+        load.start()
     rows = q_ref.shape[0]
     qk = q_ref.shape[1] // heads
     vd = g_ref.shape[1] // heads
     q = jnp.concatenate([q_ref[:, h * qk : (h + 1) * qk] for h in range(heads)], axis=0)
     g = jnp.concatenate([g_ref[:, h * vd : (h + 1) * vd] for h in range(heads)], axis=0)
     total = rows * heads
-    per, pieces, packed, _ = kv0_ref.shape
     each = packed * 2 // 5
-    block = pieces * each
-
-    def sweep(body, carry):
-        for part, (kv, gkv) in enumerate(((kv0_ref, gkv0_ref), (kv1_ref, gkv1_ref))):
-            def step(i, c, part=part, kv=kv, gkv=gkv):
-                here = pl.ds(pl.multiple_of((part * per + i) * block, block), block)
-                return body(c, kv, gkv, i, here)
-            carry = lax.fori_loop(0, per, step, carry)
-        return carry
-
-    def keys_of(kv, i):
-        return jnp.concatenate([kv[i, j, :each] for j in range(pieces)], axis=0)
-
-    def first(peak, kv, gkv, i, here):
-        s = contract_cols(keys_of(kv, i), q) * scale
-        s_ref[here, :] = s
+    block = group * each
+    blocks = kv_ref.shape[0] // group
+    def part(i, low, high):
+        return jnp.concatenate([kv_ref[i * group + j, low:high] for j in range(group)], axis=0)
+
+    def here(i):
+        return pl.ds(pl.multiple_of(i * block, block), block)
+
+    def first(i, peak):
+        s = contract_cols(part(i, 0, each), q) * scale
+        s_ref[here(i), :] = s
         return jnp.maximum(peak, jnp.max(s, axis=0, keepdims=True))
 
-    peak = sweep(first, jnp.full((1, total), -jnp.inf, F32))
-
-    def second(carry, kv, gkv, i, here):
+    def second(i, carry):
         norm, dot_sum, out = carry
-        v = jnp.concatenate([unpack(kv[i, j])[1] for j in range(pieces)], axis=0)
-        e = jnp.exp(s_ref[here, :] - peak)
-        s_ref[here, :] = e
+        v = jnp.concatenate([unpack(kv_ref[i * group + j])[1] for j in range(group)], axis=0)
+        e = jnp.exp(s_ref[here(i), :] - peak)
+        s_ref[here(i), :] = e
         gw = contract_cols(v, g)
-        gw_ref[here, :] = gw
+        gw_ref[here(i), :] = gw
         return (norm + jnp.sum(e, axis=0, keepdims=True),
                 dot_sum + jnp.sum(e * gw, axis=0, keepdims=True),
                 out + contract_rows(v, e.astype(BF)))
 
+    peak = jnp.full((1, total), -jnp.inf, F32)
+    for c in range(2):
+        for load in loads[c * len(loads) // 2 : (c + 1) * len(loads) // 2]:
+            load.wait()
+        peak = lax.fori_loop(c * blocks // 2, (c + 1) * blocks // 2, first, peak, unroll=unroll)
     zero = jnp.zeros((1, total), F32)
-    norm, dot_sum, out = sweep(second, (zero, zero, jnp.zeros((vd, total), F32)))
+    norm, dot_sum, out = lax.fori_loop(
+        0, blocks, second, (zero, zero, jnp.zeros((vd, total), F32)), unroll=unroll
+    )
     inv = 1.0 / norm
     delta = dot_sum * inv
     mixed = jnp.transpose(out * inv).astype(BF)
     for h in range(heads):
         mixed_ref[:, h * vd : (h + 1) * vd] = mixed[h * rows : (h + 1) * rows]
 
-    def third(gq, kv, gkv, i, here):
-        w = s_ref[here, :] * inv
-        ds = (w * (gw_ref[here, :] - delta) * scale).astype(BF)
+    def third(i, gq):
+        w = s_ref[here(i), :] * inv
+        ds = (w * (gw_ref[here(i), :] - delta) * scale).astype(BF)
         gk = dot(ds, q).astype(BF)
         gv = dot(w.astype(BF), g).astype(BF)
-        for j in range(pieces):
+        for j in range(group):
             at = slice(j * each, (j + 1) * each)
-            gkv[i, j] = pack(gk[at], gv[at])
-        return gq + contract_rows(keys_of(kv, i), ds)
-
-    gq = jnp.transpose(sweep(third, jnp.zeros((qk, total), F32))).astype(BF)
+            gkv_ref[i * group + j] = pack(gk[at], gv[at])
+        return gq + contract_rows(part(i, 0, each), ds)
+
+    place = place_ref[0]
+    stores = []
+    for c, ref in enumerate((own_ref, others_ref)):
+        for i, back in enumerate((0, 1, ny - 1, 2)):
+            to = lax.rem(place + ny - back, ny)
+            at = pl.ds((c * ny + i) * nz, nz)
+            stores.append(
+                pltpu.make_async_copy(gkv_ref.at[at], ref.at[to], out_sem.at[c * ny + i])
+            )
+    gq = lax.fori_loop(blocks // 2, blocks, third, jnp.zeros((qk, total), F32), unroll=unroll)
+    for store in stores[ny:]:
+        store.start()
+    gq = lax.fori_loop(0, blocks // 2, third, gq, unroll=unroll)
+    for store in stores[:ny]:
+        store.start()
+    gq = jnp.transpose(gq).astype(BF)
     for h in range(heads):
         gq_ref[:, h * qk : (h + 1) * qk] = gq[h * rows : (h + 1) * rows]
-
-
-def attention(q, g, kv0, kv1, heads):
+    for store in stores:
+        store.wait()
+
+
+def attention(q, g, pieces, ny, place, heads, group=32, unroll=1):
     rows, width = q.shape
-    vd = g.shape[1] // heads
-    pieces, packed = kv0.shape[1:3]
-    keys = 2 * kv0.shape[0] * pieces * packed * 2 // 5
+    nz, packed, lanes = pieces[0].shape
+    count = 2 * ny * nz
+    keys = count * packed * 2 // 5
     scale = 1.0 / math.sqrt(width // heads)
-    return call(
-        functools.partial(attention_kernel, scale, heads),
-        (shape(*g.shape), shape(*q.shape), shape(*kv0.shape), shape(*kv1.shape)),
-        [pltpu.VMEM((keys, rows * heads), F32), pltpu.VMEM((keys, rows * heads), F32),
-         pltpu.VMEM((8, vd), BF)],
-        2 * keys * rows * (3 * width + 3 * g.shape[1]),
-        q, g, kv0, kv1,
-    )
+    smem, vmem, anywhere = (
+        pl.BlockSpec(memory_space=m) for m in (pltpu.SMEM, pltpu.VMEM, pl.ANY)
+    )
+    return pl.pallas_call(
+        functools.partial(attention_kernel, scale, heads, group, unroll),
+        out_shape=(shape(*g.shape), shape(*q.shape)) + (shape(ny, nz, packed, lanes),) * 2,
+        in_specs=[smem] + [vmem] * 2 + [anywhere] * len(pieces),
+        out_specs=(vmem,) * 2 + (anywhere,) * 2,
+        scratch_shapes=[
+            pltpu.VMEM((count, packed, lanes), BF),
+            pltpu.VMEM((count, packed, lanes), BF),
+            pltpu.VMEM((keys, rows * heads), F32),
+            pltpu.VMEM((keys, rows * heads), F32),
+            pltpu.SemaphoreType.DMA((len(pieces),)),
+            pltpu.SemaphoreType.DMA((2 * ny,)),
+        ],
+        compiler_params=pltpu.CompilerParams(vmem_limit_bytes=60 * 2**20),
+        cost_estimate=pl.CostEstimate(
+            flops=2 * keys * rows * (3 * width + 3 * g.shape[1]),
+            bytes_accessed=4 * count * packed * lanes,
+            transcendentals=keys * rows * heads,
+        ),
+    )(place, q, g, *pieces)
 
 
 def add_up(ref):
@@ -292,15 +341,22 @@
         out_ref[i : i + step, :] = (through + scale * (inner - raw * along)).astype(BF)
 
 
-def pick_kernel(first_ref, target_ref, e_ref, m_ref, left_ref, sums_ref):
+def pick_kernel(first_ref, target_ref, e_ref, m_ref, left_ref, *sums_refs):
     keep, width = left_ref.shape[0], e_ref.shape[1]
     rows = lax.broadcasted_iota(jnp.int32, (keep, width), 0)
     hot = (rows == target_ref[...]).astype(F32).astype(BF)
+    each = keep // len(sums_refs)
+    lanes = sums_refs[0].shape[1]
 
     def work(left, right):
         picked = contract_cols(hot, left[...]).astype(BF)
         left_ref[...] = picked
-        sums_ref[...] = dot(picked, right[...]).astype(BF)
+        sums = dot(picked, right[...]).astype(BF)
+        for i, ref in enumerate(sums_refs):
+            for t in range(width // lanes):
+                ref[t * each : (t + 1) * each] = sums[
+                    i * each : (i + 1) * each, t * lanes : (t + 1) * lanes
+                ]
 
     @pl.when(first_ref[0] > 0)
     def _():
@@ -311,68 +367,61 @@
         work(m_ref, e_ref)
 
 
-def late_kernel(q_cols, first_ref, left_ref, sums_ref, got_ref, out_ref):
+def late_kernel(left_ref, got_ref, *out_refs):
     peers, slots, lanes = got_ref.shape
-    ny = out_ref.shape[0]
-    keep, width = sums_ref.shape
-    each = keep // ny
-    tail = out_ref.shape[1] - each * (width // lanes)
+    each = left_ref.shape[0] // len(out_refs)
+    tail = out_refs[0].shape[0] - each * 5 // 2
     packed = slots - tail
     parts = [unpack(got_ref[i, :packed]) for i in range(peers)]
     keys = jnp.concatenate([k for k, _ in parts], axis=0)
     values = jnp.concatenate([v for _, v in parts], axis=0)
     left = left_ref[...]
-    late = jnp.concatenate([dot(left, keys), dot(left, values)], axis=1).astype(BF)
-    total = got_ref[0, packed:].astype(F32)
+    keys, values = dot(left, keys), dot(left, values)
+    small = got_ref[0, packed:].astype(F32)
     for i in range(1, peers):
-        total = total + got_ref[i, packed:].astype(F32)
-    small = total.astype(BF)
+        small = small + got_ref[i, packed:].astype(F32)
+    small = small.astype(BF)
+    for i, ref in enumerate(out_refs):
+        at = slice(i * each, (i + 1) * each)
+        ref[: each * 5 // 2] = pack(keys[at], values[at]).astype(BF)
+        ref[each * 5 // 2 :] = small
+
+
+def turn_kernel(count, q_cols, first_ref, *refs):
+    early, late, out_ref, held = refs[:count], refs[count : 2 * count], refs[-2], refs[-1]
+    peers, slots, lanes = out_ref.shape
+    rows = early[0].shape[0]
+    held[:rows] = sum((ref[...].astype(F32) for ref in early[1:]), early[0][...].astype(F32))
+    total = sum((ref[...].astype(F32) for ref in late[1:]), late[0][...].astype(F32))
+    tail = total.shape[0] - (held.shape[0] - rows)
+    held[rows:] = total[: held.shape[0] - rows]
+    small = total[held.shape[0] - rows :]
+    each = (held.shape[0] - rows) * 2 // 5
+    tiles = rows // each
     first = first_ref[0] > 0
-    end = q_cols + late.shape[1]
-    for t in range(width // lanes):
-        low, high = t * lanes, (t + 1) * lanes
-        block = sums_ref[:, low:high]
-        if low >= q_cols and low < end:
-            piece = late[:, low - q_cols : min(high, end) - q_cols]
-            if high > end:
-                piece = jnp.concatenate([piece, block[:, end - low :]], axis=1)
-            block = jnp.where(first, piece, block)
-        for i in range(ny):
-            out_ref[i, t * each : (t + 1) * each] = block[i * each : (i + 1) * each]
-    for i in range(ny):
-        out_ref[i, each * (width // lanes) :] = small
-
-
-def turn_kernel(tiles, got_ref, out_ref, held):
-    nz, slots, lanes = out_ref.shape
-    held[...] = add_up(got_ref)
-    rows = held.shape[0]
-    tail = (slots * nz - rows) // (nz - 1)
-    each = (rows - tail) // tiles
-    part = each // nz
-    for i in range(nz):
+    keys, values = unpack(held[rows:])
+    late = jnp.concatenate([keys, values], axis=1)
+    low = q_cols // lanes
+    for t in range(low, -(-(q_cols + late.shape[1]) // lanes)):
+        piece = late[:, (t - low) * lanes : (t - low + 1) * lanes]
+        at = slice(t * each, (t + 1) * each)
+        if piece.shape[1] < lanes:
+            piece = jnp.concatenate([piece, jnp.zeros((each, lanes - piece.shape[1]), F32)], axis=1)
+        held[at] = jnp.where(first, piece, held[at])
+    part = each // peers
+    blank = jnp.zeros((slots - tiles * part - tail, lanes), F32)
+    for i in range(peers):
         pieces = [held[t * each + i * part : t * each + (i + 1) * part] for t in range(tiles)]
-        out_ref[i] = jnp.concatenate(pieces + [held[rows - tail :]], axis=0).astype(BF)
-
-
-def end_kernel(tiles, rows, first_ref, got_ref, mine_ref, theirs_ref, held):
-    held[...] = add_up(got_ref)
-    first = first_ref[0] > 0
-    small = [held[2 * tiles * rows :]]
-    low = [held[2 * t * rows : (2 * t + 1) * rows] for t in range(tiles)]
-    high = [held[(2 * t + 1) * rows : (2 * t + 2) * rows] for t in range(tiles)]
-    low = jnp.concatenate(low + small, axis=0)
-    high = jnp.concatenate(high + small, axis=0)
-    mine_ref[...] = jnp.where(first, low, high)
-    theirs_ref[...] = jnp.where(first, high, low)
-
-
-def last_kernel(tiles, first_ref, mine_ref, got_ref, q_ref, k_ref, v_ref, o_ref, conv_ref, in_ref,
-                attn_ref, held):
-    first = first_ref[0] > 0
-    mine, got = mine_ref[...], got_ref[...]
-    held[0] = jnp.where(first, mine, got)
-    held[1] = jnp.where(first, got, mine)
+        out_ref[i] = jnp.concatenate(pieces + [small, blank], axis=0).astype(BF)
+
+
+def last_kernel(tiles, got_ref, q_ref, k_ref, v_ref, o_ref, conv_ref, in_ref, attn_ref, held):
+    cores = held.shape[0]
+    for c in range(cores):
+        total = got_ref[c].astype(F32)
+        for i in range(c + cores, got_ref.shape[0], cores):
+            total = total + got_ref[i].astype(F32)
+        held[c] = total
     rows, q_cols = q_ref.shape
     lanes = k_ref.shape[1]
     for t in range(tiles):
@@ -389,8 +438,8 @@
                 v_ref[:, start:stop] = block[:, : stop - start]
         o_ref[:, at] = held[1, t * rows : (t + 1) * rows]
     taps = conv_ref.shape[0]
-    half = tiles // 2
-    for c in range(2):
+    half = tiles // cores
+    for c in range(cores):
         for t in range(half):
             at = slice((c * half + t) * lanes, (c * half + t + 1) * lanes)
             row = tiles * rows + t * (taps + 2)
@@ -466,10 +515,14 @@
     queries = dot(normed, query_weight).astype(BF)
     grad_mixed = contract_cols(grad_y, out_weight).astype(BF)
     kv, queries, grad_mixed = lax.optimization_barrier((kv, queries, grad_mixed))
-    kv_own = exchange(jnp.broadcast_to(kv[None], (ny,) + kv.shape), "y")
-    kv_other = swap(kv_own)
-    mixed, grad_queries, gkv_own, gkv_other = attention(
-        queries, grad_mixed, kv_own, kv_other, heads
+    half = nz // 2
+    before, after = shift(kv, "y", 1), shift(kv, "y", ny - 1)
+    pieces = [kv, before, after,
+              shift(before[:half], "y", 1), shift(after[half:], "y", ny - 1)]
+    pieces += [swap(piece) for piece in pieces]
+    at_y = lax.axis_index("y").astype(jnp.int32).reshape(1)
+    mixed, grad_queries, gkv, others = attention(
+        queries, grad_mixed, pieces, ny, at_y, heads
     )
 
     gq_wide = jnp.pad(grad_queries, ((0, 0), (0, width - q_cols)))
@@ -477,8 +530,8 @@
         jnp.concatenate(ours_theirs(gq_wide, mixed), axis=0), "x", axis=0, tiled=True
     )
 
-    gkv = (gkv_own.astype(F32) + swap(gkv_other).astype(F32)).astype(BF)
-    (gkv,) = call(sum_kernel, (shape(nz, packed, qk),), [], 0, exchange(gkv, "y"))
+    gkv = (gkv.astype(F32) + swap(others).astype(F32)).astype(BF)
+    (gkv,) = call(sum_kernel, (shape(*kv.shape),), [], 0, exchange(gkv, "y"))
     gkv = exchange(gkv, "z")
 
     keep = width // nx
@@ -486,20 +539,22 @@
     row = jnp.arange(width, dtype=jnp.int32)
     at_x, at_core = row // each % nx, row // (each * nx) % nc
     at_y, at_z = row // (each * nx * nc) % ny, row // (each * nx * nc * ny)
+    at_y = (at_y - lax.axis_index("y") + ny) % ny
     target = ((at_y * nz + at_z) * nc + at_core) * each + row % each
     target = jnp.where(at_x == lax.axis_index("x"), target, -1).reshape(1, width)
-    left, sums = flagged(
+    tiles = width // qk
+    left, *sums = flagged(
         pick_kernel,
-        (shape(keep, nx * nc * pool), shape(keep, width)),
+        (shape(keep, nx * nc * pool),) + (shape(tiles * keep // ny, qk),) * ny,
         [],
         4 * keep * width * nx * nc * pool,
         first, target, early, later,
     )
     part = contract_cols(grad_queries, query_weight)
     gkv, left, sums, part = lax.optimization_barrier((gkv, left, sums, part))
+    sums = [sums[0]] + [shift(sums[i], "y", i) for i in range(1, ny)]
 
     tail = taps + 2
-    tiles = width // qk
     extra = (tail * tiles // nc + 15) // 16 * 16
     half, gkv = call(
         functools.partial(back_kernel, nc),
@@ -520,38 +575,32 @@
         x, gain_in, conv_taps, half, before, after,
     )
     mixed_out = (pooled + dot(mixed, out_weight)).astype(BF)
-    (sums,) = flagged(
-        functools.partial(late_kernel, q_cols),
-        (shape(ny, tiles * keep // ny + extra, qk),),
+    late = call(
+        late_kernel,
+        (shape(keep // ny * 5 // 2 + extra, qk),) * ny,
         [],
         2 * keep * nx * nc * pool * (qk + vd),
-        first, left, sums, got,
-    )
-    got = exchange(sums, "y")
-    got, mixed_out, input_grad = lax.optimization_barrier((got, mixed_out, input_grad))
-    (sums,) = call(
-        functools.partial(turn_kernel, tiles),
-        (shape(nz, tiles * keep // (ny * nz) + extra, qk),),
-        [pltpu.VMEM((tiles * keep // ny + extra, qk), F32)],
+        left, got,
+    )
+    late = [late[0]] + [shift(late[i], "y", i) for i in range(1, ny)]
+    (sums,) = flagged(
+        functools.partial(turn_kernel, ny, q_cols),
+        (shape(nz * nc, (tiles * each + extra + 15) // 16 * 16, qk),),
+        [pltpu.VMEM((tiles * keep // ny + keep // ny * 5 // 2, qk), F32)],
         0,
-        got,
-    )
-    got = exchange(sums, "z")
-    mine, theirs = flagged(
-        functools.partial(end_kernel, tiles, each),
-        (shape(tiles * each + extra, qk, dtype=F32),) * 2,
-        [pltpu.VMEM((2 * tiles * each + extra, qk), F32)],
-        0,
-        first, got,
-    )
-    results = flagged(
+        first, *sums, *late,
+    )
+    got, mixed_out, input_grad = lax.optimization_barrier(
+        (exchange(sums, ("z", "core")), mixed_out, input_grad)
+    )
+    results = call(
         functools.partial(last_kernel, tiles),
         tuple(shape(*dims, dtype=F32) for dims in (
             (each, q_cols), (each, qk), (each, vd), (each, width),
             (taps, width), (width,), (width,))),
-        [pltpu.VMEM((2, tiles * each + extra, qk), F32)],
+        [pltpu.VMEM((nc,) + got.shape[1:], F32)],
         0,
-        first, mine, swap(theirs),
+        got,
     )
     return mixed_out[None], input_grad[None], *results
 

time: 215 us -> 196 us (0.912)
  blocking collectives: 33 us -> 0 us
  starting transfers between devices: 44.2 us -> 62.9 us
  Pallas kernels: 42 us -> 36.2 us
    all_to_all x2 -> x0, blocking collectives: 33 us -> none  [exchange(): return lax.all_to_all(blocks, axis, 0, 0, tiled=True)]
    ppermute x0 -> x10, waiting for transfers between devices: none -> 13 us  [shift(): lax.ppermute(block, axis, [(i, (i + step) % count) for i in range(count)])]
    pallas_call x6, Pallas kernels: 30.6 us -> 17.9 us  [call(): pl.pallas_call(kernel, out_shape=out_shape, scratch_shapes=scratch, compi...]
    ppermute x0 -> x10, starting transfers between devices: none -> 12.6 us  [shift(): lax.ppermute(block, axis, [(i, (i + step) % count) for i in range(count)])]
    pallas_call x0 -> x1, Pallas kernels: none -> 11.1 us  [attention(): pl.pallas_call(functools.partial(attention_kernel, scale, heads, group, u...]
    all_to_all x5, starting transfers between devices: 27.9 us -> 32.8 us  [exchange(): return lax.all_to_all(blocks, axis, 0, 0, tiled=True)]
    all_to_all x5, waiting for transfers between devices: 39.4 us -> 35.1 us  [exchange(): return lax.all_to_all(blocks, axis, 0, 0, tiled=True)]
    pallas_call x4 -> x2, Pallas kernels: 11.4 us -> 7.3 us  [flagged(): pl.pallas_call(kernel, out_shape=out_shape, in_specs=[smem] + [vmem] * le...]
  transfers between devices with their start and end apart: 16 -> 29, of which waited for: 10 -> 15; matrix products, arithmetic and copies ran while one was open for 10% -> 11% of each run, Pallas kernels for 12% -> 12%
where the time goes in v4:
time: 196 us; the launch traced here: 195 us
  starting transfers between devices  62.9 us (32%)
  waiting for transfers between devices  54.2 us (28%)
  Pallas kernels  36.2 us (18%)
  between operations  14.2 us (7%)
  matrix products  12.7 us (6%)
  other arithmetic  9.2 us (5%)
  local copies, waits for them, and re-layouts  5.81 us (3%)
    all_to_all x5, waiting for transfers between devices, exchange(): return lax.all_to_all(blocks, axis, 0, 0, tiled=True)  35.1 us
    all_to_all x5, starting transfers between devices, exchange(): return lax.all_to_all(blocks, axis, 0, 0, tiled=True)  32.8 us
    pallas_call x6, Pallas kernels, call(): pl.pallas_call(kernel, out_shape=out_shape, scratch_shapes=scratch, compi...  17.9 us
    ppermute x10, waiting for transfers between devices, shift(): lax.ppermute(block, axis, [(i, (i + step) % count) for i in range(count)])  13 us
    ppermute x10, starting transfers between devices, shift(): lax.ppermute(block, axis, [(i, (i + step) % count) for i in range(count)])  12.6 us
    pallas_call x1, Pallas kernels, attention(): pl.pallas_call(functools.partial(attention_kernel, scale, heads, group, u...  11.1 us
    dot_general x2, matrix products, contract_cols(): lax.dot_general(left, right, (((1,), (1,)), ((), ())), preferred_element_...  7.34 us
    pallas_call x2, Pallas kernels, flagged(): pl.pallas_call(kernel, out_shape=out_shape, in_specs=[smem] + [vmem] * le...  7.3 us
  transfers between devices with their start and end apart: 29, of which 15 were waited for; matrix products, arithmetic and copies ran while one was open for 11% of the time, Pallas kernels for 12%

profile of v4, /device:TPU:1, one launch (start us, length us, event | category | flops | bytes accessed | tf_op | source)
XLA Modules:
  0.0 195.4 jit_solution(14449713732402426099)
XLA Ops:
  7.2 0.9 slice_bitcast_fusion
  8.1 4.7 %collective-permute-start = (bf16[2,1536]{1,0:T(2,128)(2,1)S(1)}, bf16[2,1536]{1,0:T(2,128)(2,1)S(1)}, u32[]{:S(2)}, u32[]{:S(2)}) collective-permute-start(bf16[2,1536]{1,0:T(2,128)(2,1)S(1)} %get-tuple-element.92), channel_id=1, source_target_pairs={{0,4},{4,8},{8,12},{12,16},{16,20},{20,24},{24,28},{28,32},{32,36}... | collective-permute-start | bytes 18440 | tf_op jit(solution)/shard_map/ppermute | solution.py:481
  12.9 1.9 collective-permute-start.1
  14.8 3.0 %collective-permute-done.1.high_ref = bf16[2,1536]{1,0:T(2,128)(2,1)S(1)} collective-permute-done((bf16[2,1536]{1,0:T(2,128)(2,1)S(1)}, bf16[2,1536]{1,0:T(2,128)(2,1)S(1)}, u32[]{:S(2)}, u32[]{:S(2)}) %collective-permute-start.1) | collective-permute-done | bytes 6176 | tf_op jit(solution)/shard_map/ppermute | solution.py:482
  17.8 0.6 copy-done.10
  18.4 4.5 %shard_map.160 = (bf16[8,160,128]{2,1,0:T(8,128)(2,1)}, bf16[64,1536]{1,0:T(8,128)(2,1)}, f32[64,1536]{1,0:T(8,128)}, f32[5,64,1536]{2,1,0:T(8,128)}, f32[64,1536]{1,0:T(8,128)}) custom-call(bf16[128,1536]{1,0:T(8,128)(2,1)} %bitcast.25, bf16[2,1536]{1,0:T(2,128)(2,1)} %copy-done.9, bf16[2,1536]{1,0:T(2,128)(2,1)} %copy-done.10, f32[1536]{0:T(1024)} %gain_ref.3, ...), custom_call_target="tpu_custom_call" | custom-call | flops 62914560 | bytes 4708352 | tf_op jit(solution)/shard_map/pallas_call | solution.py:47
  22.9 1.7 broadcast_select_fusion.1
  24.6 10.4 %all-to-all-start = ((bf16[8,160,128]{2,1,0:T(8,128)(2,1)}), bf16[8,160,128]{2,1,0:T(8,128)(2,1)}, u32[]{:S(2)}, u32[]{:S(2)}) async-start(bf16[8,160,128]{2,1,0:T(8,128)(2,1)} %get-tuple-element.49), calls=%async_computation | async-start | bytes 655360 | tf_op jit(solution)/shard_map/all_to_all | solution.py:41
  35.1 1.7 pad_maximum_fusion
  36.9 4.6 %convolution_convert_fusion.g_ref = bf16[64,1536]{1,0:T(8,128)(2,1)} fusion(bf16[1536,1536]{1,0:T(8,128)(2,1)} %param.16, bf16[1,64,1536]{2,1,0:T(8,128)(2,1)S(1)} %copy-done.1), kind=kOutput, calls=%fused_computation.3 | convolution fusion | flops 302088192 | bytes 5111808 | tf_op jit(solution)/shard_map/dot_general | solution.py:24
  41.5 1.3 convolution_convert_fusion.1.q_ref
  42.8 6.1 %all-to-all-done.refs_0_ = bf16[8,160,128]{2,1,0:T(8,128)(2,1)} async-done(((bf16[8,160,128]{2,1,0:T(8,128)(2,1)}), bf16[8,160,128]{2,1,0:T(8,128)(2,1)}, u32[]{:S(2)}, u32[]{:S(2)}) %all-to-all-start) | async-done | bytes 327712 | tf_op jit(solution)/shard_map/all_to_all | solution.py:41
  48.9 2.7 %collective-permute-start.3 = (bf16[8,160,128]{2,1,0:T(8,128)(2,1)}, bf16[8,160,128]{2,1,0:T(8,128)(2,1)}, u32[]{:S(2)}, u32[]{:S(2)}) collective-permute-start(bf16[8,160,128]{2,1,0:T(8,128)(2,1)} %all-to-all-done.refs_0_), channel_id=1, source_target_pairs={{0,24},{8,0},{16,8},{24,16},{1,25},{9,1},{17,9},{25,17},{2,26},{10... | collective-permute-start | bytes 983048 | tf_op jit(solution)/shard_map/ppermute | solution.py:37
  51.6 1.0 collective-permute-start.6
  52.6 6.6 %collective-permute-done.2.refs_1_ = bf16[8,160,128]{2,1,0:T(8,128)(2,1)S(1)} collective-permute-done((bf16[8,160,128]{2,1,0:T(8,128)(2,1)}, bf16[8,160,128]{2,1,0:T(8,128)(2,1)S(1)}, u32[]{:S(2)}, u32[]{:S(2)}) %collective-permute-start.2) | collective-permute-done | bytes 327712 | tf_op jit(solution)/shard_map/ppermute | solution.py:37
  59.3 1.3 collective-permute-start.7
  60.6 0.9 slice.33
  61.7 2.9 %collective-permute-start.5 = (bf16[4,160,128]{2,1,0:T(8,128)(2,1)S(1)}, bf16[4,160,128]{2,1,0:T(8,128)(2,1)}, u32[]{:S(2)}, u32[]{:S(2)}) collective-permute-start(bf16[4,160,128]{2,1,0:T(8,128)(2,1)S(1)} %slice.33), channel_id=1, source_target_pairs={{0,24},{8,0},{16,8},{24,16},{1,25},{9,1},{17,9},{25,17},{2,26},{10... | collective-permute-start | bytes 491528 | tf_op jit(solution)/shard_map/ppermute | solution.py:37
  64.6 0.5 collective-permute-done.4.refs_3_
  65.1 2.1 %collective-permute-start.9 = (bf16[4,160,128]{2,1,0:T(8,128)(2,1)}, bf16[4,160,128]{2,1,0:T(8,128)(2,1)}, u32[]{:S(2)}, u32[]{:S(2)}) collective-permute-start(bf16[4,160,128]{2,1,0:T(8,128)(2,1)} %collective-permute-done.4.refs_3_), channel_id=1, source_target_pairs={{0,4},{4,0},{1,5},{5,1},{2,6},{6,2},{3,7},{7,3},{8,12},{12,8},{9,1... | collective-permute-start | bytes 491528 | tf_op jit(solution)/shard_map/ppermute | solution.py:32
  67.2 0.5 collective-permute-done.5.refs_4_
  67.8 1.3 collective-permute-start.10
  69.0 1.3 collective-permute-done.10.refs_9_
  70.4 11.1 %shard_map.161 = (bf16[64,1536]{1,0:T(8,128)(2,1)}, bf16[64,1024]{1,0:T(8,128)(2,1)}, bf16[4,8,160,128]{3,2,1,0:T(8,128)(2,1)}, bf16[4,8,160,128]{3,2,1,0:T(8,128)(2,1)}) custom-call(s32[1]{0:T(128)} %bitcast.1.place_ref, bf16[64,1024]{1,0:T(8,128)(2,1)} %convolution_convert_fusion.1.q_ref, bf16[64,1536]{1,0:T(8,128)(2,1)} %convolution_convert_fusion.g_ref, ...), custom_call_target="tpu_custom_call" | custom-call | flops 4026531840 | bytes 5242880 | tf_op jit(solution)/shard_map/pallas_call | solution.py:235
  81.5 0.5 collective-permute-start.11
  82.0 1.1 pad_select_fusion.1
  83.0 0.2 collective-permute-start.13
  83.2 1.7 collective-permute-done.13
  84.9 0.8 pad_maximum_fusion.1
  85.7 3.2 %add_convert_fusion = bf16[4,8,160,128]{3,2,1,0:T(8,128)(2,1)} fusion(bf16[4,8,160,128]{3,2,1,0:T(8,128)(2,1)} %collective-permute-done.11, bf16[4,8,160,128]{3,2,1,0:T(8,128)(2,1)} %get-tuple-element.54), kind=kLoop, calls=%fused_computation | loop fusion | flops 2621440 | bytes 3932160 | tf_op jit(solution)/shard_map/convert_element_type | solution.py:533
  88.9 4.8 %all-to-all-start.1 = ((bf16[4,8,160,128]{3,2,1,0:T(8,128)(2,1)}), bf16[4,8,160,128]{3,2,1,0:T(8,128)(2,1)}, u32[]{:S(2)}, u32[]{:S(2)}) async-start(bf16[4,8,160,128]{3,2,1,0:T(8,128)(2,1)} %add_convert_fusion), calls=%async_computation.1 | async-start | bytes 2621440 | tf_op jit(solution)/shard_map/all_to_all | solution.py:41
  93.7 17.5 %all-to-all-done.1.parts_ref = bf16[4,8,160,128]{3,2,1,0:T(8,128)(2,1)} async-done(((bf16[4,8,160,128]{3,2,1,0:T(8,128)(2,1)}), bf16[4,8,160,128]{3,2,1,0:T(8,128)(2,1)}, u32[]{:S(2)}, u32[]{:S(2)}) %all-to-all-start.1) | async-done | bytes 1310752 | tf_op jit(solution)/shard_map/all_to_all | solution.py:41
  111.1 2.2 %shard_map.162 = bf16[8,160,128]{2,1,0:T(8,128)(2,1)} custom-call(bf16[4,8,160,128]{3,2,1,0:T(8,128)(2,1)} %all-to-all-done.1.parts_ref), custom_call_target="tpu_custom_call" | custom-call | bytes 1638400 | tf_op jit(solution)/shard_map/pallas_call | solution.py:47
  113.3 3.4 %all-to-all-start.2 = ((bf16[8,160,128]{2,1,0:T(8,128)(2,1)}), bf16[8,160,128]{2,1,0:T(8,128)(2,1)S(1)}, u32[]{:S(2)}, u32[]{:S(2)}) async-start(bf16[8,160,128]{2,1,0:T(8,128)(2,1)} %shard_map.162), calls=%async_computation.2 | async-start | bytes 655360 | tf_op jit(solution)/shard_map/all_to_all | solution.py:41
  116.8 0.7 compare_select_fusion.8.target_ref
  117.5 2.7 %fusion.16.part_ref = f32[64,1536]{1,0:T(8,128)} fusion(bf16[64,1024]{1,0:T(8,128)(2,1)} %get-tuple-element.56, bf16[1536,1024]{1,0:T(8,128)(2,1)S(1)} %copy-done), kind=kOutput, calls=%fused_computation.55 | convolution fusion | flops 201326592 | bytes 3670016 | tf_op jit(solution)/shard_map/dot_general | solution.py:24
  120.3 4.8 %shard_map.163 = (bf16[384,512]{1,0:T(8,128)(2,1)}, bf16[1152,128]{1,0:T(8,128)(2,1)}, bf16[1152,128]{1,0:T(8,128)(2,1)}, bf16[1152,128]{1,0:T(8,128)(2,1)}, bf16[1152,128]{1,0:T(8,128)(2,1)}) custom-call(s32[1]{0:T(128)} %bitcast.first_ref, s32[1,1536]{1,0:T(1,128)} %compare_select_fusion.8.target_ref, ...), custom_call_target="tpu_custom_call" | custom-call | flops 1207959552 | bytes 9437184 | tf_op jit(solution)/shard_map/pallas_call | solution.py:487
  125.1 2.7 %all-to-all-done.2.parts_ref = bf16[8,160,128]{2,1,0:T(8,128)(2,1)S(1)} async-done(((bf16[8,160,128]{2,1,0:T(8,128)(2,1)}), bf16[8,160,128]{2,1,0:T(8,128)(2,1)S(1)}, u32[]{:S(2)}, u32[]{:S(2)}) %all-to-all-start.2) | async-done | bytes 327712 | tf_op jit(solution)/shard_map/all_to_all | solution.py:41
  127.8 0.7 copy-done.3
  128.6 3.9 %shard_map.164 = (bf16[64,1536]{1,0:T(8,128)(2,1)}, bf16[8,208,128]{2,1,0:T(8,128)(2,1)}) custom-call(bf16[8,160,128]{2,1,0:T(8,128)(2,1)} %copy-done.3, f32[64,1536]{1,0:T(8,128)} %fusion.16.part_ref, bf16[1536,128]{1,0:T(8,128)(2,1)} %kw_ref.3, bf16[192,1536]{1,0:T(8,128)(2,1)} %bitcast.23, f32[64,1536]{1,0:T(8,128)} %get-tuple-element.70.pooled_ref, ...), custom_call_target="tpu_custom_call" | custom-call | flops 62914560 | bytes 5281792 | tf_op jit(solution)/shard_map/pallas_call | solution.py:47
  132.4 7.5 %all-to-all-start.3 = ((bf16[8,208,128]{2,1,0:T(8,128)(2,1)}), bf16[8,208,128]{2,1,0:T(8,128)(2,1)}, u32[]{:S(2)}, u32[]{:S(2)}) async-start(bf16[8,208,128]{2,1,0:T(8,128)(2,1)} %get-tuple-element.73), calls=%async_computation.3 | async-start | bytes 851968 | tf_op jit(solution)/shard_map/all_to_all | solution.py:41
  139.9 1.0 collective-permute-start.14
  141.0 1.0 collective-permute-start.15
  142.0 1.4 collective-permute-start.16
  143.4 5.1 %all-to-all-done.3.got_ref = bf16[8,208,128]{2,1,0:T(8,128)(2,1)} async-done(((bf16[8,208,128]{2,1,0:T(8,128)(2,1)}), bf16[8,208,128]{2,1,0:T(8,128)(2,1)}, u32[]{:S(2)}, u32[]{:S(2)}) %all-to-all-start.3) | async-done | bytes 426016 | tf_op jit(solution)/shard_map/all_to_all | solution.py:41
  148.5 2.2 %shard_map.165 = (bf16[288,128]{1,0:T(8,128)(2,1)}, bf16[288,128]{1,0:T(8,128)(2,1)}, bf16[288,128]{1,0:T(8,128)(2,1)}, bf16[288,128]{1,0:T(8,128)(2,1)}) custom-call(bf16[384,512]{1,0:T(8,128)(2,1)} %get-tuple-element.67.left_ref, bf16[8,208,128]{2,1,0:T(8,128)(2,1)} %all-to-all-done.3.got_ref), custom_call_target="tpu_custom_call" | custom-call | flops 125829120 | bytes 1114112 | tf_op jit(solution)/shard_map/pallas_call | solution.py:47
  150.7 1.0 collective-permute-start.17
  151.8 1.0 collective-permute-start.18
  152.8 1.4 collective-permute-start.19
  154.2 1.4 collective-permute-done.15.refs_2_
  155.6 1.0 collective-permute-done.16.refs_3_
  156.6 2.8 %collective-permute-done.17.refs_5_ = bf16[288,128]{1,0:T(8,128)(2,1)S(1)} collective-permute-done((bf16[288,128]{1,0:T(8,128)(2,1)}, bf16[288,128]{1,0:T(8,128)(2,1)S(1)}, u32[]{:S(2)}, u32[]{:S(2)}) %collective-permute-start.17) | collective-permute-done | bytes 73760 | tf_op jit(solution)/shard_map/ppermute | solution.py:37
  159.5 0.5 copy-done.6
  160.2 2.5 %shard_map.166 = bf16[16,128,128]{2,1,0:T(8,128)(2,1)} custom-call(s32[1]{0:T(128)} %bitcast.first_ref, bf16[1152,128]{1,0:T(8,128)(2,1)} %get-tuple-element.63.refs_0_, bf16[1152,128]{1,0:T(8,128)(2,1)} %collective-permute-done.14.refs_1_, bf16[1152,128]{1,0:T(8,128)(2,1)} %collective-permute-done.15.refs_2_, ...), custom_call_target="tpu_custom_call" | custom-call | bytes 9437184 | tf_op jit(solution)/shard_map/pallas_call | solution.py:487
  162.6 6.7 %all-to-all-start.4 = ((bf16[16,128,128]{2,1,0:T(8,128)(2,1)}), bf16[16,128,128]{2,1,0:T(8,128)(2,1)}, u32[]{:S(2)}, u32[]{:S(2)}) async-start(bf16[16,128,128]{2,1,0:T(8,128)(2,1)} %shard_map.166), calls=%async_computation.4 | async-start | bytes 1048576 | tf_op jit(solution)/shard_map/all_to_all | solution.py:41
  169.3 0.8 fusion.15
  170.1 1.9 collective-permute-start.20
  172.0 2.4 %collective-permute-start.21 = (bf16[1,1536]{1,0:T(2,128)(2,1)S(1)}, bf16[1,1536]{1,0:T(2,128)(2,1)S(1)}, u32[]{:S(2)}, u32[]{:S(2)}) collective-permute-start(bf16[1,1536]{1,0:T(2,128)(2,1)S(1)} %get-tuple-element.95), channel_id=1, source_target_pairs={{4,0},{8,4},{12,8},{16,12},{20,16},{24,20},{28,24},{32,28},{36,32}... | collective-permute-start | bytes 9224 | tf_op jit(solution)/shard_map/ppermute | solution.py:567
  174.4 4.1 %fusion = bf16[64,1536]{1,0:T(8,128)(2,1)} fusion(f32[64,1536]{1,0:T(8,128)S(1)} %copy-done.2, bf16[64,1536]{1,0:T(8,128)(2,1)} %get-tuple-element.57, bf16[1536,1536]{1,0:T(8,128)(2,1)} %param.16), kind=kOutput, calls=%fused_computation.2 | convolution fusion | flops 302186496 | bytes 5505024 | tf_op jit(solution)/shard_map/dot_general | solution.py:28
  178.5 0.6 copy-done.11
  179.1 0.6 copy-done.12
  179.7 3.3 %shard_map.167 = bf16[128,1536]{1,0:T(8,128)(2,1)} custom-call(bf16[128,1536]{1,0:T(8,128)(2,1)} %bitcast.26, f32[1536]{0:T(1024)} %gain_ref.3, f32[5,1536]{1,0:T(8,128)} %taps_ref.3, bf16[64,1536]{1,0:T(8,128)(2,1)} %get-tuple-element.78.half_ref, bf16[1,1536]{1,0:T(2,128)(2,1)} %copy-done.11, bf16[1,1536]{1,0:T(2,128)(2,1)} %copy-done.12), custom_call_target="tpu_custom_call" | custom-call | flops 7864320 | bytes 1026048 | tf_op jit(solution)/shard_map/pallas_call | solution.py:47
  183.0 3.8 %all-to-all-done.4.got_ref = bf16[16,128,128]{2,1,0:T(8,128)(2,1)} async-done(((bf16[16,128,128]{2,1,0:T(8,128)(2,1)}), bf16[16,128,128]{2,1,0:T(8,128)(2,1)}, u32[]{:S(2)}, u32[]{:S(2)}) %all-to-all-start.4) | async-done | bytes 524320 | tf_op jit(solution)/shard_map/all_to_all | solution.py:41
  186.8 1.7 shard_map.168
  (45 shorter events, 0.6 us)
Async XLA Ops:
  7.2 34.3 %copy-start = (bf16[1536,1024]{1,0:T(8,128)(2,1)S(1)}, bf16[1536,1024]{1,0:T(8,128)(2,1)}, u32[]{:S(2)}) copy-start(bf16[1536,1024]{1,0:T(8,128)(2,1)} %param.13) | copy-start | bytes 9437188
  7.2 29.7 %copy-start.1 = (bf16[1,64,1536]{2,1,0:T(8,128)(2,1)S(1)}, bf16[1,64,1536]{2,1,0:T(8,128)(2,1)}, u32[]{:S(2)}) copy-start(bf16[1,64,1536]{2,1,0:T(8,128)(2,1)} %param.17) | copy-start | bytes 589828
  8.1 6.7 %collective-permute-start = (bf16[2,1536]{1,0:T(2,128)(2,1)S(1)}, bf16[2,1536]{1,0:T(2,128)(2,1)S(1)}, u32[]{:S(2)}, u32[]{:S(2)}) collective-permute-start(bf16[2,1536]{1,0:T(2,128)(2,1)S(1)} %get-tuple-element.92), channel_id=1, source_target_pairs={{0,4},{4,8},{8,12},{12,16},{16,20},{20,24},{24,28},{28,32},{32,36}... | collective-permute-start | bytes 18440 | tf_op jit(solution)/shard_map/ppermute | solution.py:481
  12.9 4.9 %collective-permute-start.1 = (bf16[2,1536]{1,0:T(2,128)(2,1)S(1)}, bf16[2,1536]{1,0:T(2,128)(2,1)S(1)}, u32[]{:S(2)}, u32[]{:S(2)}) collective-permute-start(bf16[2,1536]{1,0:T(2,128)(2,1)S(1)} %get-tuple-element.91), channel_id=1, source_target_pairs={{4,0},{8,4},{12,8},{16,12},{20,16},{24,20},{28,24},{32,28},{36,32}... | collective-permute-start | bytes 18440 | tf_op jit(solution)/shard_map/ppermute | solution.py:482
  14.8 3.0 %copy-start.9 = (bf16[2,1536]{1,0:T(2,128)(2,1)}, bf16[2,1536]{1,0:T(2,128)(2,1)S(1)}, u32[]{:S(2)}) copy-start(bf16[2,1536]{1,0:T(2,128)(2,1)S(1)} %collective-permute-done.low_ref) | copy-start | bytes 18436
  17.8 0.6 copy-start.10
  24.6 10.4 %collective-permute-start.12 = (bf16[64,1536]{1,0:T(8,128)(2,1)}, bf16[64,1536]{1,0:T(8,128)(2,1)}, u32[]{:S(2)}, u32[]{:S(2)}) collective-permute-start(bf16[64,1536]{1,0:T(8,128)(2,1)} %get-tuple-element.90), channel_id=1, source_target_pairs={{0,4},{4,0},{1,5},{5,1},{2,6},{6,2},{3,7},{7,3},{8,12},{12,8},{9,1... | collective-permute-start | bytes 589832 | tf_op jit(solution)/shard_map/ppermute | solution.py:32
  24.6 24.2 %all-to-all-start = ((bf16[8,160,128]{2,1,0:T(8,128)(2,1)}), bf16[8,160,128]{2,1,0:T(8,128)(2,1)}, u32[]{:S(2)}, u32[]{:S(2)}) async-start(bf16[8,160,128]{2,1,0:T(8,128)(2,1)} %get-tuple-element.49), calls=%async_computation | async-start | bytes 655360 | tf_op jit(solution)/shard_map/all_to_all | solution.py:41
  35.0 85.2 %all-gather.3.cloned.1.call-start = ((), (), s32[]{:S(2)}) async-start(), calls=%async_computation.5 | async-start | bytes 1966080 | tf_op jit(solution)/shard_map/all_gather | solution.py:512
  36.8 4.7 %copy-start.4 = (bf16[64,1536]{1,0:T(8,128)(2,1)S(1)}, bf16[64,1536]{1,0:T(8,128)(2,1)}, u32[]{:S(2)}) copy-start(bf16[64,1536]{1,0:T(8,128)(2,1)} %get-tuple-element.50) | copy-start | bytes 589828
  36.8 83.4 %all-gather.5.cloned.1.call-start = ((), (), s32[]{:S(2)}) async-start(), calls=%async_computation.6 | async-start | bytes 1966080 | tf_op jit(solution)/shard_map/all_gather | solution.py:529
  48.9 10.3 %collective-permute-start.2 = (bf16[8,160,128]{2,1,0:T(8,128)(2,1)}, bf16[8,160,128]{2,1,0:T(8,128)(2,1)S(1)}, u32[]{:S(2)}, u32[]{:S(2)}) collective-permute-start(bf16[8,160,128]{2,1,0:T(8,128)(2,1)} %all-to-all-done.refs_0_), channel_id=1, source_target_pairs={{0,8},{8,16},{16,24},{24,0},{1,9},{9,17},{17,25},{25,1},{2,10},{10... | collective-permute-start | bytes 983048 | tf_op jit(solution)/shard_map/ppermute | solution.py:37
  48.9 11.7 %collective-permute-start.3 = (bf16[8,160,128]{2,1,0:T(8,128)(2,1)}, bf16[8,160,128]{2,1,0:T(8,128)(2,1)}, u32[]{:S(2)}, u32[]{:S(2)}) collective-permute-start(bf16[8,160,128]{2,1,0:T(8,128)(2,1)} %all-to-all-done.refs_0_), channel_id=1, source_target_pairs={{0,24},{8,0},{16,8},{24,16},{1,25},{9,1},{17,9},{25,17},{2,26},{10... | collective-permute-start | bytes 983048 | tf_op jit(solution)/shard_map/ppermute | solution.py:37
  51.6 17.5 %collective-permute-start.6 = (bf16[8,160,128]{2,1,0:T(8,128)(2,1)}, bf16[8,160,128]{2,1,0:T(8,128)(2,1)}, u32[]{:S(2)}, u32[]{:S(2)}) collective-permute-start(bf16[8,160,128]{2,1,0:T(8,128)(2,1)} %all-to-all-done.refs_0_), channel_id=1, source_target_pairs={{0,4},{4,0},{1,5},{5,1},{2,6},{6,2},{3,7},{7,3},{8,12},{12,8},{9,1... | collective-permute-start | bytes 983048 | tf_op jit(solution)/shard_map/ppermute | solution.py:32
  59.2 11.2 %copy-start.5 = (bf16[8,160,128]{2,1,0:T(8,128)(2,1)}, bf16[8,160,128]{2,1,0:T(8,128)(2,1)S(1)}, u32[]{:S(2)}) copy-start(bf16[8,160,128]{2,1,0:T(8,128)(2,1)S(1)} %collective-permute-done.2.refs_1_) | copy-start | bytes 983044
  59.2 5.9 %collective-permute-start.4 = (bf16[4,160,128]{2,1,0:T(8,128)(2,1)S(1)}, bf16[4,160,128]{2,1,0:T(8,128)(2,1)}, u32[]{:S(2)}, u32[]{:S(2)}) collective-permute-start(bf16[4,160,128]{2,1,0:T(8,128)(2,1)S(1)} %slice.32), channel_id=1, source_target_pairs={{0,8},{8,16},{16,24},{24,0},{1,9},{9,17},{17,25},{25,1},{2,10},{10... | collective-permute-start | bytes 491528 | tf_op jit(solution)/shard_map/ppermute | solution.py:37
  59.3 9.7 %collective-permute-start.7 = (bf16[8,160,128]{2,1,0:T(8,128)(2,1)S(1)}, bf16[8,160,128]{2,1,0:T(8,128)(2,1)}, u32[]{:S(2)}, u32[]{:S(2)}) collective-permute-start(bf16[8,160,128]{2,1,0:T(8,128)(2,1)S(1)} %collective-permute-done.2.refs_1_), channel_id=1, source_target_pairs={{0,4},{4,0},{1,5},{5,1},{2,6},{6,2},{3,7},{7,3},{8,12},{12,8},{9,1... | collective-permute-start | bytes 983048 | tf_op jit(solution)/shard_map/ppermute | solution.py:32
  61.6 7.5 %collective-permute-start.8 = (bf16[8,160,128]{2,1,0:T(8,128)(2,1)}, bf16[8,160,128]{2,1,0:T(8,128)(2,1)}, u32[]{:S(2)}, u32[]{:S(2)}) collective-permute-start(bf16[8,160,128]{2,1,0:T(8,128)(2,1)} %collective-permute-done.3.refs_2_), channel_id=1, source_target_pairs={{0,4},{4,0},{1,5},{5,1},{2,6},{6,2},{3,7},{7,3},{8,12},{12,8},{9,1... | collective-permute-start | bytes 983048 | tf_op jit(solution)/shard_map/ppermute | solution.py:32
  61.7 6.1 %collective-permute-start.5 = (bf16[4,160,128]{2,1,0:T(8,128)(2,1)S(1)}, bf16[4,160,128]{2,1,0:T(8,128)(2,1)}, u32[]{:S(2)}, u32[]{:S(2)}) collective-permute-start(bf16[4,160,128]{2,1,0:T(8,128)(2,1)S(1)} %slice.33), channel_id=1, source_target_pairs={{0,24},{8,0},{16,8},{24,16},{1,25},{9,1},{17,9},{25,17},{2,26},{10... | collective-permute-start | bytes 491528 | tf_op jit(solution)/shard_map/ppermute | solution.py:37
  65.1 3.9 %collective-permute-start.9 = (bf16[4,160,128]{2,1,0:T(8,128)(2,1)}, bf16[4,160,128]{2,1,0:T(8,128)(2,1)}, u32[]{:S(2)}, u32[]{:S(2)}) collective-permute-start(bf16[4,160,128]{2,1,0:T(8,128)(2,1)} %collective-permute-done.4.refs_3_), channel_id=1, source_target_pairs={{0,4},{4,0},{1,5},{5,1},{2,6},{6,2},{3,7},{7,3},{8,12},{12,8},{9,1... | collective-permute-start | bytes 491528 | tf_op jit(solution)/shard_map/ppermute | solution.py:32
  67.8 2.6 %collective-permute-start.10 = (bf16[4,160,128]{2,1,0:T(8,128)(2,1)}, bf16[4,160,128]{2,1,0:T(8,128)(2,1)}, u32[]{:S(2)}, u32[]{:S(2)}) collective-permute-start(bf16[4,160,128]{2,1,0:T(8,128)(2,1)} %collective-permute-done.5.refs_4_), channel_id=1, source_target_pairs={{0,4},{4,0},{1,5},{5,1},{2,6},{6,2},{3,7},{7,3},{8,12},{12,8},{9,1... | collective-permute-start | bytes 491528 | tf_op jit(solution)/shard_map/ppermute | solution.py:32
  81.5 4.2 %collective-permute-start.11 = (bf16[4,8,160,128]{3,2,1,0:T(8,128)(2,1)}, bf16[4,8,160,128]{3,2,1,0:T(8,128)(2,1)}, u32[]{:S(2)}, u32[]{:S(2)}) collective-permute-start(bf16[4,8,160,128]{3,2,1,0:T(8,128)(2,1)} %get-tuple-element.55), channel_id=1, source_target_pairs={{0,4},{4,0},{1,5},{5,1},{2,6},{6,2},{3,7},{7,3},{8,12},{12,8},{9,1... | collective-permute-start | bytes 3932168 | tf_op jit(solution)/shard_map/ppermute | solution.py:32
  83.0 1.9 collective-permute-start.13
  88.9 22.3 %all-to-all-start.1 = ((bf16[4,8,160,128]{3,2,1,0:T(8,128)(2,1)}), bf16[4,8,160,128]{3,2,1,0:T(8,128)(2,1)}, u32[]{:S(2)}, u32[]{:S(2)}) async-start(bf16[4,8,160,128]{3,2,1,0:T(8,128)(2,1)} %add_convert_fusion), calls=%async_computation.1 | async-start | bytes 2621440 | tf_op jit(solution)/shard_map/all_to_all | solution.py:41
  113.3 14.5 %all-to-all-start.2 = ((bf16[8,160,128]{2,1,0:T(8,128)(2,1)}), bf16[8,160,128]{2,1,0:T(8,128)(2,1)S(1)}, u32[]{:S(2)}, u32[]{:S(2)}) async-start(bf16[8,160,128]{2,1,0:T(8,128)(2,1)} %shard_map.162), calls=%async_computation.2 | async-start | bytes 655360 | tf_op jit(solution)/shard_map/all_to_all | solution.py:41
  127.8 0.7 copy-start.3
  132.4 42.0 %copy-start.2 = (f32[64,1536]{1,0:T(8,128)S(1)}, f32[64,1536]{1,0:T(8,128)}, u32[]{:S(2)}) copy-start(f32[64,1536]{1,0:T(8,128)} %get-tuple-element.70.pooled_ref) | copy-start | bytes 1179652
  132.4 16.0 %all-to-all-start.3 = ((bf16[8,208,128]{2,1,0:T(8,128)(2,1)}), bf16[8,208,128]{2,1,0:T(8,128)(2,1)}, u32[]{:S(2)}, u32[]{:S(2)}) async-start(bf16[8,208,128]{2,1,0:T(8,128)(2,1)} %get-tuple-element.73), calls=%async_computation.3 | async-start | bytes 851968 | tf_op jit(solution)/shard_map/all_to_all | solution.py:41
  139.9 12.9 %collective-permute-start.14 = (bf16[1152,128]{1,0:T(8,128)(2,1)}, bf16[1152,128]{1,0:T(8,128)(2,1)}, u32[]{:S(2)}, u32[]{:S(2)}) collective-permute-start(bf16[1152,128]{1,0:T(8,128)(2,1)} %get-tuple-element.64), channel_id=1, source_target_pairs={{0,8},{8,16},{16,24},{24,0},{1,9},{9,17},{17,25},{25,1},{2,10},{10... | collective-permute-start | bytes 884744 | tf_op jit(solution)/shard_map/ppermute | solution.py:37
  141.0 14.6 %collective-permute-start.15 = (bf16[1152,128]{1,0:T(8,128)(2,1)}, bf16[1152,128]{1,0:T(8,128)(2,1)}, u32[]{:S(2)}, u32[]{:S(2)}) collective-permute-start(bf16[1152,128]{1,0:T(8,128)(2,1)} %get-tuple-element.65), channel_id=1, source_target_pairs={{0,16},{8,24},{16,0},{24,8},{1,17},{9,25},{17,1},{25,9},{2,18},{10... | collective-permute-start | bytes 884744 | tf_op jit(solution)/shard_map/ppermute | solution.py:37
  142.0 14.6 %collective-permute-start.16 = (bf16[1152,128]{1,0:T(8,128)(2,1)}, bf16[1152,128]{1,0:T(8,128)(2,1)}, u32[]{:S(2)}, u32[]{:S(2)}) collective-permute-start(bf16[1152,128]{1,0:T(8,128)(2,1)} %get-tuple-element.66), channel_id=1, source_target_pairs={{0,24},{8,0},{16,8},{24,16},{1,25},{9,1},{17,9},{25,17},{2,26},{10... | collective-permute-start | bytes 884744 | tf_op jit(solution)/shard_map/ppermute | solution.py:37
  150.7 8.7 %collective-permute-start.17 = (bf16[288,128]{1,0:T(8,128)(2,1)}, bf16[288,128]{1,0:T(8,128)(2,1)S(1)}, u32[]{:S(2)}, u32[]{:S(2)}) collective-permute-start(bf16[288,128]{1,0:T(8,128)(2,1)} %get-tuple-element.75), channel_id=1, source_target_pairs={{0,8},{8,16},{16,24},{24,0},{1,9},{9,17},{17,25},{25,1},{2,10},{10... | collective-permute-start | bytes 221192 | tf_op jit(solution)/shard_map/ppermute | solution.py:37
  151.8 7.7 %collective-permute-start.18 = (bf16[288,128]{1,0:T(8,128)(2,1)}, bf16[288,128]{1,0:T(8,128)(2,1)S(1)}, u32[]{:S(2)}, u32[]{:S(2)}) collective-permute-start(bf16[288,128]{1,0:T(8,128)(2,1)} %get-tuple-element.76), channel_id=1, source_target_pairs={{0,16},{8,24},{16,0},{24,8},{1,17},{9,25},{17,1},{25,9},{2,18},{10... | collective-permute-start | bytes 221192 | tf_op jit(solution)/shard_map/ppermute | solution.py:37
  152.8 6.7 %collective-permute-start.19 = (bf16[288,128]{1,0:T(8,128)(2,1)}, bf16[288,128]{1,0:T(8,128)(2,1)S(1)}, u32[]{:S(2)}, u32[]{:S(2)}) collective-permute-start(bf16[288,128]{1,0:T(8,128)(2,1)} %get-tuple-element.77), channel_id=1, source_target_pairs={{0,24},{8,0},{16,8},{24,16},{1,25},{9,1},{17,9},{25,17},{2,26},{10... | collective-permute-start | bytes 221192 | tf_op jit(solution)/shard_map/ppermute | solution.py:37
  159.4 0.6 copy-start.6
  159.4 0.7 copy-start.7
  159.5 0.6 copy-start.8
  162.6 24.2 %all-to-all-start.4 = ((bf16[16,128,128]{2,1,0:T(8,128)(2,1)}), bf16[16,128,128]{2,1,0:T(8,128)(2,1)}, u32[]{:S(2)}, u32[]{:S(2)}) async-start(bf16[16,128,128]{2,1,0:T(8,128)(2,1)} %shard_map.166), calls=%async_computation.4 | async-start | bytes 1048576 | tf_op jit(solution)/shard_map/all_to_all | solution.py:41
  170.1 8.4 %collective-permute-start.20 = (bf16[1,1536]{1,0:T(2,128)(2,1)S(1)}, bf16[1,1536]{1,0:T(2,128)(2,1)S(1)}, u32[]{:S(2)}, u32[]{:S(2)}) collective-permute-start(bf16[1,1536]{1,0:T(2,128)(2,1)S(1)} %get-tuple-element.96), channel_id=1, source_target_pairs={{0,4},{4,8},{8,12},{12,16},{16,20},{20,24},{24,28},{28,32},{32,36}... | collective-permute-start | bytes 9224 | tf_op jit(solution)/shard_map/ppermute | solution.py:566
  172.0 6.5 %collective-permute-start.21 = (bf16[1,1536]{1,0:T(2,128)(2,1)S(1)}, bf16[1,1536]{1,0:T(2,128)(2,1)S(1)}, u32[]{:S(2)}, u32[]{:S(2)}) collective-permute-start(bf16[1,1536]{1,0:T(2,128)(2,1)S(1)} %get-tuple-element.95), channel_id=1, source_target_pairs={{4,0},{8,4},{12,8},{16,12},{20,16},{24,20},{28,24},{32,28},{36,32}... | collective-permute-start | bytes 9224 | tf_op jit(solution)/shard_map/ppermute | solution.py:567
  178.5 0.6 copy-start.11
  179.1 0.6 copy-start.12
Sparse Core Ops, SparseCore 0:
  37.6 30.4 all-gather.2
  85.8 25.6 all-gather.4

commit v5 on v4

--- a/solution.py
+++ b/solution.py
@@ -72,31 +72,33 @@
     return packed[:n], jnp.concatenate([packed[n : 2 * n], rest], axis=1)
 
 
+def put(ref, at, value):
+    for c in range(ref.shape[0]):
+        ref[c, at, :] = value[:, c * 128 : (c + 1) * 128]
+
+
+def scaled(x, gain):
+    raw = x * lax.rsqrt(jnp.mean(x * x, axis=-1, keepdims=True) + EPS)
+    u = raw * gain
+    return raw, u, jnp.tanh(CURVE * (u + CUBIC * (u * u * u)))
+
+
+def slant(u, t):
+    return 0.5 * (1.0 + t) + 0.5 * u * (1.0 - t * t) * (CURVE * (1.0 + 3.0 * CUBIC * u * u))
+
+
 def front_kernel(
     x_ref, low_ref, high_ref, gain_in_ref, taps_ref, gain_attn_ref, kw_ref, vw_ref,
-    kv_ref, normed_ref, pooled_ref, pairs_ref, spread_ref, act, slope, plain,
+    kv_ref, normed_ref, pooled_ref, act, plain,
 ):
     fine, width = x_ref.shape
     pool = fine // 2
     taps = taps_ref.shape[0]
     gain = gain_in_ref[...].reshape(1, width)
 
-    def rows_of(x):
-        raw = x * lax.rsqrt(jnp.mean(x * x, axis=-1, keepdims=True) + EPS)
-        u = raw * gain
-        t = jnp.tanh(CURVE * (u + CUBIC * (u * u * u)))
-        a = u * (0.5 * (1.0 + t))
-        slant = 0.5 * (1.0 + t) + 0.5 * u * (1.0 - t * t) * (CURVE * (1.0 + 3.0 * CUBIC * u * u))
-        return a.astype(BF).astype(F32), slant * raw
-
-    def put(ref, at, value):
-        for c in range(width // 128):
-            ref[c, at, :] = value[:, c * 128 : (c + 1) * 128]
-
     def fill(at, x):
-        a, g = rows_of(x)
-        put(act, at, a)
-        put(slope, at, g)
+        _, u, t = scaled(x, gain)
+        put(act, at, (u * (0.5 * (1.0 + t))).astype(BF).astype(F32))
 
     fill(slice(0, 2), low_ref[...].astype(F32))
     fill(slice(fine + 2, fine + 4), high_ref[...].astype(F32))
@@ -109,18 +111,10 @@
     for c in range(width // 128):
         at = slice(c * 128, (c + 1) * 128)
         a = [act[c, pl.ds(m, pool, stride=2), :] for m in range(taps + 1)]
-        g = [slope[c, pl.ds(m, pool, stride=2), :] for m in range(taps + 1)]
-        conv = jnp.zeros((pool, 128), F32)
-        spread = jnp.zeros((pool, 128), F32)
+        whole = plain[c, pl.ds(0, pool, stride=2), :] + plain[c, pl.ds(1, pool, stride=2), :]
         for k in range(taps):
-            pair = a[k] + a[k + 1]
-            pairs_ref[k, :, at] = pair
-            tap = taps_ref[k : k + 1, at]
-            conv = conv + tap * pair
-            spread = spread + tap * (g[k] + g[k + 1])
-        spread_ref[:, at] = spread
-        whole = plain[c, pl.ds(0, pool, stride=2), :] + plain[c, pl.ds(1, pool, stride=2), :]
-        pooled_ref[:, at] = 0.5 * (whole + conv)
+            whole = whole + taps_ref[k : k + 1, at] * (a[k] + a[k + 1])
+        pooled_ref[:, at] = 0.5 * whole
     pooled = pooled_ref[...]
     scale = lax.rsqrt(jnp.mean(pooled * pooled, axis=-1, keepdims=True) + EPS)
     normed = (pooled * scale * gain_attn_ref[...].reshape(1, width)).astype(BF)
@@ -130,10 +124,37 @@
         kv_ref[i] = kv
 
 
+def side_kernel(x_ref, low_ref, high_ref, gain_in_ref, taps_ref, pairs_ref, spread_ref, act, slope):
+    fine, width = x_ref.shape
+    pool = fine // 2
+    taps = taps_ref.shape[0]
+    gain = gain_in_ref[...].reshape(1, width)
+
+    def fill(at, x):
+        raw, u, t = scaled(x, gain)
+        put(act, at, (u * (0.5 * (1.0 + t))).astype(BF).astype(F32))
+        put(slope, at, slant(u, t) * raw)
+
+    fill(slice(0, 2), low_ref[...].astype(F32))
+    fill(slice(fine + 2, fine + 4), high_ref[...].astype(F32))
+    step = 32
+    for i in range(0, fine, step):
+        fill(slice(2 + i, 2 + i + step), x_ref[i : i + step, :].astype(F32))
+    for c in range(width // 128):
+        at = slice(c * 128, (c + 1) * 128)
+        a = [act[c, pl.ds(m, pool, stride=2), :] for m in range(taps + 1)]
+        g = [slope[c, pl.ds(m, pool, stride=2), :] for m in range(taps + 1)]
+        spread = jnp.zeros((pool, 128), F32)
+        for k in range(taps):
+            pairs_ref[k, :, at] = a[k] + a[k + 1]
+            spread = spread + taps_ref[k : k + 1, at] * (g[k] + g[k + 1])
+        spread_ref[:, at] = spread
+
+
 def attention_kernel(scale, heads, group, unroll, place_ref, q_ref, g_ref, *refs):
     ins = refs[:10]
-    mixed_ref, gq_ref, own_ref, others_ref = refs[10:14]
-    kv_ref, gkv_ref, s_ref, gw_ref, in_sem, out_sem = refs[14:]
+    mixed_ref, gq_ref, keep_ref, send_ref, own_ref, others_ref = refs[10:16]
+    kv_ref, gkv_ref, s_ref, gw_ref, in_sem, out_sem = refs[16:]
     ny, nz, packed, _ = own_ref.shape
     half = nz // 2
     slots = [(i * nz, nz) for i in range(ny - 1)]
@@ -219,6 +240,11 @@
     gq = jnp.transpose(gq).astype(BF)
     for h in range(heads):
         gq_ref[:, h * qk : (h + 1) * qk] = gq[h * rows : (h + 1) * rows]
+    blank = jnp.zeros((rows, mixed_ref.shape[1] - gq_ref.shape[1]), BF)
+    mixed, gq = mixed_ref[...], jnp.concatenate([gq_ref[...], blank], axis=1)
+    first = place_ref[1] > 0
+    keep_ref[...] = jnp.where(first, gq, mixed)
+    send_ref[...] = jnp.where(first, mixed, gq)
     for store in stores:
         store.wait()
 
@@ -234,9 +260,10 @@
     )
     return pl.pallas_call(
         functools.partial(attention_kernel, scale, heads, group, unroll),
-        out_shape=(shape(*g.shape), shape(*q.shape)) + (shape(ny, nz, packed, lanes),) * 2,
+        out_shape=(shape(*g.shape), shape(*q.shape), shape(*g.shape), shape(*g.shape))
+        + (shape(ny, nz, packed, lanes),) * 2,
         in_specs=[smem] + [vmem] * 2 + [anywhere] * len(pieces),
-        out_specs=(vmem,) * 2 + (anywhere,) * 2,
+        out_specs=(vmem,) * 4 + (anywhere,) * 2,
         scratch_shapes=[
             pltpu.VMEM((count, packed, lanes), BF),
             pltpu.VMEM((count, packed, lanes), BF),
@@ -259,6 +286,26 @@
     for i in range(1, ref.shape[0]):
         total = total + ref[i].astype(F32)
     return total
+
+
+def both_kernel(own_ref, got_ref, out_ref):
+    for j in range(own_ref.shape[1]):
+        out_ref[0, j] = (own_ref[0, j].astype(F32) + got_ref[0, j].astype(F32)).astype(BF)
+
+
+def both(own, got):
+    spec = pl.BlockSpec((1,) + own.shape[1:], lambda i: (i, 0, 0, 0))
+    return pl.pallas_call(
+        both_kernel,
+        grid=(own.shape[0],),
+        out_shape=shape(*own.shape),
+        in_specs=[spec, spec],
+        out_specs=spec,
+        compiler_params=pltpu.CompilerParams(vmem_limit_bytes=60 * 2**20),
+        cost_estimate=pl.CostEstimate(
+            flops=own.size, bytes_accessed=6 * own.size, transcendentals=0
+        ),
+    )(own, got)
 
 
 def sum_kernel(parts_ref, out_ref):
@@ -330,12 +377,9 @@
     for i in range(0, fine, step):
         x = x_ref[i : i + step, :].astype(F32)
         scale = lax.rsqrt(jnp.mean(x * x, axis=-1, keepdims=True) + EPS)
-        raw = x * scale
-        u = raw * gain
-        th = jnp.tanh(CURVE * (u + CUBIC * (u * u * u)))
-        slant = 0.5 * (1.0 + th) + 0.5 * u * (1.0 - th * th) * (CURVE * (1.0 + 3.0 * CUBIC * u * u))
+        raw, u, th = scaled(x, gain)
         grad = jnp.concatenate([acts[c, i : i + step, :] for c in range(width // 128)], axis=1)
-        inner = grad * slant * gain
+        inner = grad * slant(u, th) * gain
         along = jnp.mean(raw * inner, axis=-1, keepdims=True)
         through = jnp.concatenate([twice[c, i : i + step, :] for c in range(width // 128)], axis=1)
         out_ref[i : i + step, :] = (through + scale * (inner - raw * along)).astype(BF)
@@ -495,13 +539,19 @@
             ),
         )(flag, *args)
 
-    kv, normed, pooled, pairs, spread = call(
+    kv, normed, pooled = call(
         front_kernel,
-        (shape(nz, packed, qk), shape(pool, width), shape(pool, width, dtype=F32),
-         shape(taps, pool, width, dtype=F32), shape(pool, width, dtype=F32)),
-        [pltpu.VMEM((width // 128, n, 128), F32) for n in (fine + 4, fine + 4, fine)],
+        (shape(nz, packed, qk), shape(pool, width), shape(pool, width, dtype=F32)),
+        [pltpu.VMEM((width // 128, n, 128), F32) for n in (fine + 4, fine)],
         2 * pool * width * (qk + vd),
         x, low, high, gain_in, conv_taps, gain_attn, key_weight, value_weight,
+    )
+    pairs, spread = call(
+        side_kernel,
+        (shape(taps, pool, width, dtype=F32), shape(pool, width, dtype=F32)),
+        [pltpu.VMEM((width // 128, fine + 4, 128), F32)] * 2,
+        fine * width * 40,
+        x, low, high, gain_in, conv_taps,
     )
 
     def ours_theirs(ours, theirs):
@@ -509,29 +559,31 @@
                 swap(jnp.where(first_core, theirs, ours)))
 
     kv = exchange(kv, "z")
-    early = lax.all_gather(
-        jnp.concatenate(ours_theirs(normed, grad_y), axis=0), "x", axis=0, tiled=True
-    )
+    normed, cotangent = lax.optimization_barrier((normed, grad_y))
     queries = dot(normed, query_weight).astype(BF)
-    grad_mixed = contract_cols(grad_y, out_weight).astype(BF)
-    kv, queries, grad_mixed = lax.optimization_barrier((kv, queries, grad_mixed))
+    grad_mixed = contract_cols(cotangent, out_weight).astype(BF)
+    normed, queries = lax.optimization_barrier((normed, queries))
+    keep, got = ours_theirs(normed, grad_y)
+    kv, queries, grad_mixed, keep, got = lax.optimization_barrier(
+        (kv, queries, grad_mixed, keep, got)
+    )
+    early = lax.all_gather(jnp.concatenate([keep, got], axis=0), "x", axis=0, tiled=True)
+
     half = nz // 2
     before, after = shift(kv, "y", 1), shift(kv, "y", ny - 1)
     pieces = [kv, before, after,
               shift(before[:half], "y", 1), shift(after[half:], "y", ny - 1)]
     pieces += [swap(piece) for piece in pieces]
-    at_y = lax.axis_index("y").astype(jnp.int32).reshape(1)
-    mixed, grad_queries, gkv, others = attention(
-        queries, grad_mixed, pieces, ny, at_y, heads
-    )
-
-    gq_wide = jnp.pad(grad_queries, ((0, 0), (0, width - q_cols)))
-    later = lax.all_gather(
-        jnp.concatenate(ours_theirs(gq_wide, mixed), axis=0), "x", axis=0, tiled=True
-    )
-
-    gkv = (gkv.astype(F32) + swap(others).astype(F32)).astype(BF)
-    (gkv,) = call(sum_kernel, (shape(*kv.shape),), [], 0, exchange(gkv, "y"))
+    here = jnp.stack([lax.axis_index("y"), first_core.astype(jnp.int32)])
+    mixed, grad_queries, keep, send, gkv, others = attention(
+        queries, grad_mixed, pieces, ny, here, heads
+    )
+
+    later = lax.all_gather(jnp.concatenate([keep, swap(send)], axis=0), "x", axis=0, tiled=True)
+
+    gkv = both(gkv, swap(others))
+    gkv, pairs, spread = lax.optimization_barrier((exchange(gkv, "y"), pairs, spread))
+    (gkv,) = call(sum_kernel, (shape(*kv.shape),), [], 0, gkv)
     gkv = exchange(gkv, "z")
 
     keep = width // nx
@@ -551,8 +603,8 @@
         first, target, early, later,
     )
     part = contract_cols(grad_queries, query_weight)
-    gkv, left, sums, part = lax.optimization_barrier((gkv, left, sums, part))
     sums = [sums[0]] + [shift(sums[i], "y", i) for i in range(1, ny)]
+    gkv, left, part = lax.optimization_barrier((gkv, left, part))
 
     tail = taps + 2
     extra = (tail * tiles // nc + 15) // 16 * 16
@@ -563,9 +615,9 @@
         2 * pool * width * (qk + vd),
         gkv, part, key_weight, value_weight, pooled, gain_attn, grad_y, pairs, spread,
     )
+    got = exchange(gkv, ("x", "core"))
     before = lax.ppermute(half[pool - 1 :], seq, up)
     after = lax.ppermute(half[:1], seq, down)
-    got = exchange(gkv, ("x", "core"))
     (input_grad,) = call(
         input_kernel,
         (shape(fine, width),),

time: 196 us -> 196 us (level)
  waiting for transfers between devices: 54.2 us -> 46.3 us
  Pallas kernels: 36.2 us -> 43.7 us
  other arithmetic: 9.2 us -> 5.69 us
  starting transfers between devices: 62.9 us -> 65.6 us
    all_to_all x5, waiting for transfers between devices: 35.1 us -> 27.2 us  [exchange(): return lax.all_to_all(blocks, axis, 0, 0, tiled=True)]
    pallas_call x0 -> x1, Pallas kernels: none -> 3.82 us  [both(): pl.pallas_call(both_kernel, grid=(own.shape[0],), out_shape=shape(*own.sh...]
    convert_element_type x1 -> x0, other arithmetic: 3.18 us -> none  [shards(): gkv = (gkv.astype(F32) + swap(others).astype(F32)).astype(BF)]
    ppermute x8, starting transfers between devices: 6.5 us -> 9.65 us  [swap(): return lax.ppermute(block, 'core', [(0, 1), (1, 0)])]
    pallas_call x6 -> x7, Pallas kernels: 17.9 us -> 20.6 us  [call(): pl.pallas_call(kernel, out_shape=out_shape, scratch_shapes=scratch, compi...]
    all_to_all x5, starting transfers between devices: 32.8 us -> 30.1 us  [exchange(): return lax.all_to_all(blocks, axis, 0, 0, tiled=True)]
    ppermute x10, starting transfers between devices: 12.6 us -> 14.8 us  [shift(): lax.ppermute(block, axis, [(i, (i + step) % count) for i in range(count)])]
  transfers between devices with their start and end apart: 29 -> 29, of which waited for: 15 -> 14; matrix products, arithmetic and copies ran while one was open for 11% -> 9% of each run, Pallas kernels for 12% -> 17%
where the time goes in v5:
time: 196 us; the launch traced here: 195 us
  starting transfers between devices  65.6 us (33%)
  waiting for transfers between devices  46.3 us (24%)
  Pallas kernels  43.7 us (22%)
  between operations  14.2 us (7%)
  matrix products  13.6 us (7%)
  local copies, waits for them, and re-layouts  5.78 us (3%)
  other arithmetic  5.69 us (3%)
    all_to_all x5, starting transfers between devices, exchange(): return lax.all_to_all(blocks, axis, 0, 0, tiled=True)  30.1 us
    all_to_all x5, waiting for transfers between devices, exchange(): return lax.all_to_all(blocks, axis, 0, 0, tiled=True)  27.2 us
    pallas_call x7, Pallas kernels, call(): pl.pallas_call(kernel, out_shape=out_shape, scratch_shapes=scratch, compi...  20.6 us
    ppermute x10, starting transfers between devices, shift(): lax.ppermute(block, axis, [(i, (i + step) % count) for i in range(count)])  14.8 us
    ppermute x10, waiting for transfers between devices, shift(): lax.ppermute(block, axis, [(i, (i + step) % count) for i in range(count)])  12.3 us
    pallas_call x1, Pallas kernels, attention(): pl.pallas_call(functools.partial(attention_kernel, scale, heads, group, u...  11.8 us
    ppermute x8, starting transfers between devices, swap(): return lax.ppermute(block, 'core', [(0, 1), (1, 0)])  9.65 us
    pallas_call x2, Pallas kernels, flagged(): pl.pallas_call(kernel, out_shape=out_shape, in_specs=[smem] + [vmem] * le...  7.49 us
  transfers between devices with their start and end apart: 29, of which 14 were waited for; matrix products, arithmetic and copies ran while one was open for 9% of the time, Pallas kernels for 17%

profile of v5, /device:TPU:1, one launch (start us, length us, event | category | flops | bytes accessed | tf_op | source)
XLA Modules:
  0.0 194.9 jit_solution(2640178550959030492)
XLA Ops:
  7.2 0.9 slice_bitcast_fusion
  8.1 4.7 %collective-permute-start = (bf16[2,1536]{1,0:T(2,128)(2,1)S(1)}, bf16[2,1536]{1,0:T(2,128)(2,1)S(1)}, u32[]{:S(2)}, u32[]{:S(2)}) collective-permute-start(bf16[2,1536]{1,0:T(2,128)(2,1)S(1)} %get-tuple-element.106), channel_id=1, source_target_pairs={{0,4},{4,8},{8,12},{12,16},{16,20},{20,24},{24,28},{28,32},{32,36}... | collective-permute-start | bytes 18440 | tf_op jit(solution)/shard_map/ppermute | solution.py:525
  12.9 1.9 collective-permute-start.1
  14.8 3.0 %collective-permute-done.1.high_ref = bf16[2,1536]{1,0:T(2,128)(2,1)S(1)} collective-permute-done((bf16[2,1536]{1,0:T(2,128)(2,1)S(1)}, bf16[2,1536]{1,0:T(2,128)(2,1)S(1)}, u32[]{:S(2)}, u32[]{:S(2)}) %collective-permute-start.1) | collective-permute-done | bytes 6176 | tf_op jit(solution)/shard_map/ppermute | solution.py:526
  17.8 0.6 copy-done.9
  18.4 3.4 %shard_map.160 = (bf16[8,160,128]{2,1,0:T(8,128)(2,1)}, bf16[64,1536]{1,0:T(8,128)(2,1)}, f32[64,1536]{1,0:T(8,128)}) custom-call(bf16[128,1536]{1,0:T(8,128)(2,1)} %bitcast.21, bf16[2,1536]{1,0:T(2,128)(2,1)} %copy-done.8, bf16[2,1536]{1,0:T(2,128)(2,1)} %copy-done.9, f32[1536]{0:T(1024)} %gain_ref.3, f32[5,1536]{1,0:T(8,128)} %taps_ref.5, f32[1536]{0:T(1024)} %gain_ref.2, ...), custom_call_target="tpu_custom_call" | custom-call | flops 62914560 | bytes 2349056 | tf_op jit(solution)/shard_map/pallas_call | solution.py:47
  21.8 2.2 %convolution_convert_fusion.1.q_ref = bf16[64,1024]{1,0:T(8,128)(2,1)} fusion(bf16[64,1536]{1,0:T(8,128)(2,1)} %get-tuple-element.61, bf16[1536,1024]{1,0:T(8,128)(2,1)S(1)} %copy-done), kind=kOutput, calls=%fused_computation.3 | convolution fusion | flops 201392128 | bytes 3473408 | tf_op jit(solution)/shard_map/dot_general | solution.py:28
  24.1 8.2 %all-to-all-start = ((bf16[8,160,128]{2,1,0:T(8,128)(2,1)}), bf16[8,160,128]{2,1,0:T(8,128)(2,1)}, u32[]{:S(2)}, u32[]{:S(2)}) async-start(bf16[8,160,128]{2,1,0:T(8,128)(2,1)} %get-tuple-element.56), calls=%async_computation | async-start | bytes 655360 | tf_op jit(solution)/shard_map/all_to_all | solution.py:41
  32.3 1.0 broadcast_select_fusion
  33.3 2.5 %collective-permute-start.2 = (bf16[64,1536]{1,0:T(8,128)(2,1)S(1)}, bf16[64,1536]{1,0:T(8,128)(2,1)}, u32[]{:S(2)}, u32[]{:S(2)}) collective-permute-start(bf16[64,1536]{1,0:T(8,128)(2,1)S(1)} %get-tuple-element.103), channel_id=1, source_target_pairs={{0,4},{4,0},{1,5},{5,1},{2,6},{6,2},{3,7},{7,3},{8,12},{12,8},{9,1... | collective-permute-start | bytes 589832 | tf_op jit(solution)/shard_map/ppermute | solution.py:32
  35.8 4.5 %convolution_convert_fusion.g_ref = bf16[64,1536]{1,0:T(8,128)(2,1)} fusion(bf16[64,1536]{1,0:T(8,128)(2,1)S(1)} %bitcast.27, bf16[1536,1536]{1,0:T(8,128)(2,1)} %param.16), kind=kOutput, calls=%fused_computation.2 | convolution fusion | flops 302088192 | bytes 5111808 | tf_op jit(solution)/shard_map/dot_general | solution.py:24
  40.4 2.0 %all-to-all-done.refs_0_ = bf16[8,160,128]{2,1,0:T(8,128)(2,1)} async-done(((bf16[8,160,128]{2,1,0:T(8,128)(2,1)}), bf16[8,160,128]{2,1,0:T(8,128)(2,1)}, u32[]{:S(2)}, u32[]{:S(2)}) %all-to-all-start) | async-done | bytes 327712 | tf_op jit(solution)/shard_map/all_to_all | solution.py:41
  42.3 1.7 pad_maximum_fusion
  44.1 4.8 %collective-permute-start.3 = (bf16[8,160,128]{2,1,0:T(8,128)(2,1)}, bf16[8,160,128]{2,1,0:T(8,128)(2,1)S(1)}, u32[]{:S(2)}, u32[]{:S(2)}) collective-permute-start(bf16[8,160,128]{2,1,0:T(8,128)(2,1)} %all-to-all-done.refs_0_), channel_id=1, source_target_pairs={{0,8},{8,16},{16,24},{24,0},{1,9},{9,17},{17,25},{25,1},{2,10},{10... | collective-permute-start | bytes 983048 | tf_op jit(solution)/shard_map/ppermute | solution.py:37
  48.9 1.3 collective-permute-start.4
  50.2 1.5 collective-permute-start.7
  51.7 5.3 %collective-permute-done.3.refs_1_ = bf16[8,160,128]{2,1,0:T(8,128)(2,1)S(1)} collective-permute-done((bf16[8,160,128]{2,1,0:T(8,128)(2,1)}, bf16[8,160,128]{2,1,0:T(8,128)(2,1)S(1)}, u32[]{:S(2)}, u32[]{:S(2)}) %collective-permute-start.3) | collective-permute-done | bytes 327712 | tf_op jit(solution)/shard_map/ppermute | solution.py:37
  57.1 1.2 collective-permute-start.5
  58.2 0.9 slice.33
  59.2 2.0 %collective-permute-start.6 = (bf16[4,160,128]{2,1,0:T(8,128)(2,1)S(1)}, bf16[4,160,128]{2,1,0:T(8,128)(2,1)}, u32[]{:S(2)}, u32[]{:S(2)}) collective-permute-start(bf16[4,160,128]{2,1,0:T(8,128)(2,1)S(1)} %slice.33), channel_id=1, source_target_pairs={{0,24},{8,0},{16,8},{24,16},{1,25},{9,1},{17,9},{25,17},{2,26},{10... | collective-permute-start | bytes 491528 | tf_op jit(solution)/shard_map/ppermute | solution.py:37
  61.2 2.2 %collective-permute-start.8 = (bf16[8,160,128]{2,1,0:T(8,128)(2,1)S(1)}, bf16[8,160,128]{2,1,0:T(8,128)(2,1)}, u32[]{:S(2)}, u32[]{:S(2)}) collective-permute-start(bf16[8,160,128]{2,1,0:T(8,128)(2,1)S(1)} %collective-permute-done.3.refs_1_), channel_id=1, source_target_pairs={{0,4},{4,0},{1,5},{5,1},{2,6},{6,2},{3,7},{7,3},{8,12},{12,8},{9,1... | collective-permute-start | bytes 983048 | tf_op jit(solution)/shard_map/ppermute | solution.py:32
  63.3 2.4 %collective-permute-start.10 = (bf16[4,160,128]{2,1,0:T(8,128)(2,1)}, bf16[4,160,128]{2,1,0:T(8,128)(2,1)}, u32[]{:S(2)}, u32[]{:S(2)}) collective-permute-start(bf16[4,160,128]{2,1,0:T(8,128)(2,1)} %collective-permute-done.5.refs_3_), channel_id=1, source_target_pairs={{0,4},{4,0},{1,5},{5,1},{2,6},{6,2},{3,7},{7,3},{8,12},{12,8},{9,1... | collective-permute-start | bytes 491528 | tf_op jit(solution)/shard_map/ppermute | solution.py:32
  65.7 0.4 collective-permute-start.11
  66.2 0.6 pad_add_fusion.place_ref
  67.1 0.5 collective-permute-done.11.refs_9_
  67.6 11.8 %shard_map.161 = (bf16[64,1536]{1,0:T(8,128)(2,1)}, bf16[64,1024]{1,0:T(8,128)(2,1)}, bf16[64,1536]{1,0:T(8,128)(2,1)}, bf16[64,1536]{1,0:T(8,128)(2,1)}, bf16[4...) custom-call(s32[2]{0:T(128)} %pad_add_fusion.place_ref, bf16[64,1024]{1,0:T(8,128)(2,1)} %convolution_convert_fusion.1.q_ref, ...), custom_call_target="tpu_custom_call" | custom-call | flops 4026531840 | bytes 5242880 | tf_op jit(solution)/shard_map/pallas_call | solution.py:261
  79.4 0.5 collective-permute-start.16
  80.0 3.0 %collective-permute-done.12 = bf16[64,1536]{1,0:T(8,128)(2,1)S(1)} collective-permute-done((bf16[64,1536]{1,0:T(8,128)(2,1)}, bf16[64,1536]{1,0:T(8,128)(2,1)S(1)}, u32[]{:S(2)}, u32[]{:S(2)}) %collective-permute-start.12) | collective-permute-done | bytes 196640 | tf_op jit(solution)/shard_map/ppermute | solution.py:32
  83.0 1.7 pad_maximum_fusion.1
  84.8 3.8 %shard_map.163 = bf16[4,8,160,128]{3,2,1,0:T(8,128)(2,1)} custom-call(bf16[4,8,160,128]{3,2,1,0:T(8,128)(2,1)} %get-tuple-element.73.own_ref, bf16[4,8,160,128]{3,2,1,0:T(8,128)(2,1)} %collective-permute-done.16.got_ref), custom_call_target="tpu_custom_call" | custom-call | flops 655360 | bytes 3932160 | tf_op jit(solution)/shard_map/pallas_call | solution.py:298
  88.6 4.7 %all-to-all-start.1 = ((bf16[4,8,160,128]{3,2,1,0:T(8,128)(2,1)}), bf16[4,8,160,128]{3,2,1,0:T(8,128)(2,1)}, u32[]{:S(2)}, u32[]{:S(2)}) async-start(bf16[4,8,160,128]{3,2,1,0:T(8,128)(2,1)} %shard_map.163), calls=%async_computation.1 | async-start | bytes 2621440 | tf_op jit(solution)/shard_map/all_to_all | solution.py:41
  93.3 3.8 %shard_map.164 = (f32[5,64,1536]{2,1,0:T(8,128)}, f32[64,1536]{1,0:T(8,128)}) custom-call(bf16[128,1536]{1,0:T(8,128)(2,1)} %bitcast.22, bf16[2,1536]{1,0:T(2,128)(2,1)} %copy-done.8, bf16[2,1536]{1,0:T(2,128)(2,1)} %copy-done.9, f32[1536]{0:T(1024)} %gain_ref.3, f32[5,1536]{1,0:T(8,128)} %taps_ref.5), custom_call_target="tpu_custom_call" | custom-call | flops 7864320 | bytes 2801664 | tf_op jit(solution)/shard_map/pallas_call | solution.py:47
  97.1 13.8 %all-to-all-done.1.parts_ref = bf16[4,8,160,128]{3,2,1,0:T(8,128)(2,1)} async-done(((bf16[4,8,160,128]{3,2,1,0:T(8,128)(2,1)}), bf16[4,8,160,128]{3,2,1,0:T(8,128)(2,1)}, u32[]{:S(2)}, u32[]{:S(2)}) %all-to-all-start.1) | async-done | bytes 1310752 | tf_op jit(solution)/shard_map/all_to_all | solution.py:41
  110.9 2.2 %shard_map.165 = bf16[8,160,128]{2,1,0:T(8,128)(2,1)} custom-call(bf16[4,8,160,128]{3,2,1,0:T(8,128)(2,1)} %all-to-all-done.1.parts_ref), custom_call_target="tpu_custom_call" | custom-call | bytes 1638400 | tf_op jit(solution)/shard_map/pallas_call | solution.py:47
  113.1 3.4 %all-to-all-start.2 = ((bf16[8,160,128]{2,1,0:T(8,128)(2,1)}), bf16[8,160,128]{2,1,0:T(8,128)(2,1)S(1)}, u32[]{:S(2)}, u32[]{:S(2)}) async-start(bf16[8,160,128]{2,1,0:T(8,128)(2,1)} %shard_map.165), calls=%async_computation.2 | async-start | bytes 655360 | tf_op jit(solution)/shard_map/all_to_all | solution.py:41
  116.5 0.7 compare_select_fusion.8.target_ref
  117.2 2.7 %fusion.15.part_ref = f32[64,1536]{1,0:T(8,128)} fusion(bf16[64,1024]{1,0:T(8,128)(2,1)} %get-tuple-element.79, bf16[1536,1024]{1,0:T(8,128)(2,1)S(1)} %copy-done), kind=kOutput, calls=%fused_computation.52 | convolution fusion | flops 201326592 | bytes 3670016 | tf_op jit(solution)/shard_map/dot_general | solution.py:24
  120.0 5.0 %shard_map.162 = (bf16[384,512]{1,0:T(8,128)(2,1)}, bf16[1152,128]{1,0:T(8,128)(2,1)}, bf16[1152,128]{1,0:T(8,128)(2,1)}, bf16[1152,128]{1,0:T(8,128)(2,1)}, bf16[1152,128]{1,0:T(8,128)(2,1)}) custom-call(s32[1]{0:T(128)} %bitcast.first_ref, s32[1,1536]{1,0:T(1,128)} %compare_select_fusion.8.target_ref, ...), custom_call_target="tpu_custom_call" | custom-call | flops 1207959552 | bytes 9437184 | tf_op jit(solution)/shard_map/pallas_call | solution.py:531
  125.0 2.6 %all-to-all-done.2.parts_ref = bf16[8,160,128]{2,1,0:T(8,128)(2,1)S(1)} async-done(((bf16[8,160,128]{2,1,0:T(8,128)(2,1)}), bf16[8,160,128]{2,1,0:T(8,128)(2,1)S(1)}, u32[]{:S(2)}, u32[]{:S(2)}) %all-to-all-start.2) | async-done | bytes 327712 | tf_op jit(solution)/shard_map/all_to_all | solution.py:41
  127.6 0.7 copy-done.3
  128.3 3.9 %shard_map.166 = (bf16[64,1536]{1,0:T(8,128)(2,1)}, bf16[8,208,128]{2,1,0:T(8,128)(2,1)}) custom-call(bf16[8,160,128]{2,1,0:T(8,128)(2,1)} %copy-done.3, f32[64,1536]{1,0:T(8,128)} %fusion.15.part_ref, bf16[1536,128]{1,0:T(8,128)(2,1)} %kw_ref.3, bf16[192,1536]{1,0:T(8,128)(2,1)} %bitcast.25, f32[64,1536]{1,0:T(8,128)} %get-tuple-element.83.pooled_ref, ...), custom_call_target="tpu_custom_call" | custom-call | flops 62914560 | bytes 5281792 | tf_op jit(solution)/shard_map/pallas_call | solution.py:47
  132.2 7.4 %all-to-all-start.3 = ((bf16[8,208,128]{2,1,0:T(8,128)(2,1)}), bf16[8,208,128]{2,1,0:T(8,128)(2,1)}, u32[]{:S(2)}, u32[]{:S(2)}) async-start(bf16[8,208,128]{2,1,0:T(8,128)(2,1)} %get-tuple-element.86), calls=%async_computation.3 | async-start | bytes 851968 | tf_op jit(solution)/shard_map/all_to_all | solution.py:41
  139.6 1.1 collective-permute-start.13
  140.7 1.0 collective-permute-start.14
  141.7 1.4 collective-permute-start.15
  143.1 5.1 %all-to-all-done.3.got_ref = bf16[8,208,128]{2,1,0:T(8,128)(2,1)} async-done(((bf16[8,208,128]{2,1,0:T(8,128)(2,1)}), bf16[8,208,128]{2,1,0:T(8,128)(2,1)}, u32[]{:S(2)}, u32[]{:S(2)}) %all-to-all-start.3) | async-done | bytes 426016 | tf_op jit(solution)/shard_map/all_to_all | solution.py:41
  148.1 2.3 %shard_map.167 = (bf16[288,128]{1,0:T(8,128)(2,1)}, bf16[288,128]{1,0:T(8,128)(2,1)}, bf16[288,128]{1,0:T(8,128)(2,1)}, bf16[288,128]{1,0:T(8,128)(2,1)}) custom-call(bf16[384,512]{1,0:T(8,128)(2,1)} %get-tuple-element.80.left_ref, bf16[8,208,128]{2,1,0:T(8,128)(2,1)} %all-to-all-done.3.got_ref), custom_call_target="tpu_custom_call" | custom-call | flops 125829120 | bytes 1114112 | tf_op jit(solution)/shard_map/pallas_call | solution.py:47
  150.4 1.1 collective-permute-start.17
  151.5 1.0 collective-permute-start.18
  152.5 3.3 %collective-permute-done.13.refs_1_ = bf16[1152,128]{1,0:T(8,128)(2,1)} collective-permute-done((bf16[1152,128]{1,0:T(8,128)(2,1)}, bf16[1152,128]{1,0:T(8,128)(2,1)}, u32[]{:S(2)}, u32[]{:S(2)}) %collective-permute-start.13) | collective-permute-done | bytes 294944 | tf_op jit(solution)/shard_map/ppermute | solution.py:37
  155.8 0.6 collective-permute-done.15.refs_3_
  156.4 2.8 %collective-permute-done.17.refs_5_ = bf16[288,128]{1,0:T(8,128)(2,1)S(1)} collective-permute-done((bf16[288,128]{1,0:T(8,128)(2,1)}, bf16[288,128]{1,0:T(8,128)(2,1)S(1)}, u32[]{:S(2)}, u32[]{:S(2)}) %collective-permute-start.17) | collective-permute-done | bytes 73760 | tf_op jit(solution)/shard_map/ppermute | solution.py:37
  159.1 0.4 collective-permute-done.19.refs_7_
  160.1 2.4 %shard_map.168 = bf16[16,128,128]{2,1,0:T(8,128)(2,1)} custom-call(s32[1]{0:T(128)} %bitcast.first_ref, bf16[1152,128]{1,0:T(8,128)(2,1)} %get-tuple-element.69.refs_0_, bf16[1152,128]{1,0:T(8,128)(2,1)} %collective-permute-done.13.refs_1_, bf16[1152,128]{1,0:T(8,128)(2,1)} %collective-permute-done.14.refs_2_, ...), custom_call_target="tpu_custom_call" | custom-call | bytes 9437184 | tf_op jit(solution)/shard_map/pallas_call | solution.py:531
  162.6 6.3 %all-to-all-start.4 = ((bf16[16,128,128]{2,1,0:T(8,128)(2,1)}), bf16[16,128,128]{2,1,0:T(8,128)(2,1)}, u32[]{:S(2)}, u32[]{:S(2)}) async-start(bf16[16,128,128]{2,1,0:T(8,128)(2,1)} %shard_map.168), calls=%async_computation.4 | async-start | bytes 1048576 | tf_op jit(solution)/shard_map/all_to_all | solution.py:41
  168.9 0.8 fusion.14
  169.7 1.9 collective-permute-start.20
  171.6 2.4 %collective-permute-start.21 = (bf16[1,1536]{1,0:T(2,128)(2,1)S(1)}, bf16[1,1536]{1,0:T(2,128)(2,1)S(1)}, u32[]{:S(2)}, u32[]{:S(2)}) collective-permute-start(bf16[1,1536]{1,0:T(2,128)(2,1)S(1)} %get-tuple-element.107), channel_id=1, source_target_pairs={{4,0},{8,4},{12,8},{16,12},{20,16},{24,20},{28,24},{32,28},{36,32}... | collective-permute-start | bytes 9224 | tf_op jit(solution)/shard_map/ppermute | solution.py:620
  174.0 4.1 %fusion = bf16[64,1536]{1,0:T(8,128)(2,1)} fusion(f32[64,1536]{1,0:T(8,128)S(1)} %copy-done.2, bf16[64,1536]{1,0:T(8,128)(2,1)} %get-tuple-element.91, bf16[1536,1536]{1,0:T(8,128)(2,1)} %param.16), kind=kOutput, calls=%fused_computation.1 | convolution fusion | flops 302186496 | bytes 5505024 | tf_op jit(solution)/shard_map/dot_general | solution.py:28
  178.1 0.6 copy-done.10
  178.7 0.6 copy-done.11
  179.3 3.3 %shard_map.169 = bf16[128,1536]{1,0:T(8,128)(2,1)} custom-call(bf16[128,1536]{1,0:T(8,128)(2,1)} %bitcast.23, f32[1536]{0:T(1024)} %gain_ref.3, f32[5,1536]{1,0:T(8,128)} %taps_ref.5, bf16[64,1536]{1,0:T(8,128)(2,1)} %get-tuple-element.92.half_ref, bf16[1,1536]{1,0:T(2,128)(2,1)} %copy-done.10, bf16[1,1536]{1,0:T(2,128)(2,1)} %copy-done.11), custom_call_target="tpu_custom_call" | custom-call | flops 7864320 | bytes 1026048 | tf_op jit(solution)/shard_map/pallas_call | solution.py:47
  182.6 3.8 %all-to-all-done.4.got_ref = bf16[16,128,128]{2,1,0:T(8,128)(2,1)} async-done(((bf16[16,128,128]{2,1,0:T(8,128)(2,1)}), bf16[16,128,128]{2,1,0:T(8,128)(2,1)}, u32[]{:S(2)}, u32[]{:S(2)}) %all-to-all-start.4) | async-done | bytes 524320 | tf_op jit(solution)/shard_map/all_to_all | solution.py:41
  186.4 1.7 shard_map.170
  (44 shorter events, 1.3 us)
Async XLA Ops:
  7.2 14.7 %copy-start = (bf16[1536,1024]{1,0:T(8,128)(2,1)S(1)}, bf16[1536,1024]{1,0:T(8,128)(2,1)}, u32[]{:S(2)}) copy-start(bf16[1536,1024]{1,0:T(8,128)(2,1)} %param.13) | copy-start | bytes 9437188
  7.2 25.1 %copy-start.1 = (bf16[1,64,1536]{2,1,0:T(8,128)(2,1)S(1)}, bf16[1,64,1536]{2,1,0:T(8,128)(2,1)}, u32[]{:S(2)}) copy-start(bf16[1,64,1536]{2,1,0:T(8,128)(2,1)} %param.17) | copy-start | bytes 589828
  8.1 6.7 %collective-permute-start = (bf16[2,1536]{1,0:T(2,128)(2,1)S(1)}, bf16[2,1536]{1,0:T(2,128)(2,1)S(1)}, u32[]{:S(2)}, u32[]{:S(2)}) collective-permute-start(bf16[2,1536]{1,0:T(2,128)(2,1)S(1)} %get-tuple-element.106), channel_id=1, source_target_pairs={{0,4},{4,8},{8,12},{12,16},{16,20},{20,24},{24,28},{28,32},{32,36}... | collective-permute-start | bytes 18440 | tf_op jit(solution)/shard_map/ppermute | solution.py:525
  12.9 4.9 %collective-permute-start.1 = (bf16[2,1536]{1,0:T(2,128)(2,1)S(1)}, bf16[2,1536]{1,0:T(2,128)(2,1)S(1)}, u32[]{:S(2)}, u32[]{:S(2)}) collective-permute-start(bf16[2,1536]{1,0:T(2,128)(2,1)S(1)} %get-tuple-element.105), channel_id=1, source_target_pairs={{4,0},{8,4},{12,8},{16,12},{20,16},{24,20},{28,24},{32,28},{36,32}... | collective-permute-start | bytes 18440 | tf_op jit(solution)/shard_map/ppermute | solution.py:526
  14.8 3.0 %copy-start.8 = (bf16[2,1536]{1,0:T(2,128)(2,1)}, bf16[2,1536]{1,0:T(2,128)(2,1)S(1)}, u32[]{:S(2)}) copy-start(bf16[2,1536]{1,0:T(2,128)(2,1)S(1)} %collective-permute-done.low_ref) | copy-start | bytes 18436
  17.8 0.6 copy-start.9
  24.1 18.2 %all-to-all-start = ((bf16[8,160,128]{2,1,0:T(8,128)(2,1)}), bf16[8,160,128]{2,1,0:T(8,128)(2,1)}, u32[]{:S(2)}, u32[]{:S(2)}) async-start(bf16[8,160,128]{2,1,0:T(8,128)(2,1)} %get-tuple-element.56), calls=%async_computation | async-start | bytes 655360 | tf_op jit(solution)/shard_map/all_to_all | solution.py:41
  32.3 87.7 %all-gather.3.cloned.1.call-start = ((), (), s32[]{:S(2)}) async-start(), calls=%async_computation.5 | async-start | bytes 1966080 | tf_op jit(solution)/shard_map/all_gather | solution.py:570
  33.3 7.1 %collective-permute-start.2 = (bf16[64,1536]{1,0:T(8,128)(2,1)S(1)}, bf16[64,1536]{1,0:T(8,128)(2,1)}, u32[]{:S(2)}, u32[]{:S(2)}) collective-permute-start(bf16[64,1536]{1,0:T(8,128)(2,1)S(1)} %get-tuple-element.103), channel_id=1, source_target_pairs={{0,4},{4,0},{1,5},{5,1},{2,6},{6,2},{3,7},{7,3},{8,12},{12,8},{9,1... | collective-permute-start | bytes 589832 | tf_op jit(solution)/shard_map/ppermute | solution.py:32
  44.1 75.9 %all-gather.5.cloned.1.call-start = ((), (), s32[]{:S(2)}) async-start(), calls=%async_computation.6 | async-start | bytes 1966080 | tf_op jit(solution)/shard_map/all_gather | solution.py:582
  44.1 12.9 %collective-permute-start.3 = (bf16[8,160,128]{2,1,0:T(8,128)(2,1)}, bf16[8,160,128]{2,1,0:T(8,128)(2,1)S(1)}, u32[]{:S(2)}, u32[]{:S(2)}) collective-permute-start(bf16[8,160,128]{2,1,0:T(8,128)(2,1)} %all-to-all-done.refs_0_), channel_id=1, source_target_pairs={{0,8},{8,16},{16,24},{24,0},{1,9},{9,17},{17,25},{25,1},{2,10},{10... | collective-permute-start | bytes 983048 | tf_op jit(solution)/shard_map/ppermute | solution.py:37
  48.9 9.3 %collective-permute-start.4 = (bf16[8,160,128]{2,1,0:T(8,128)(2,1)}, bf16[8,160,128]{2,1,0:T(8,128)(2,1)}, u32[]{:S(2)}, u32[]{:S(2)}) collective-permute-start(bf16[8,160,128]{2,1,0:T(8,128)(2,1)} %all-to-all-done.refs_0_), channel_id=1, source_target_pairs={{0,24},{8,0},{16,8},{24,16},{1,25},{9,1},{17,9},{25,17},{2,26},{10... | collective-permute-start | bytes 983048 | tf_op jit(solution)/shard_map/ppermute | solution.py:37
  50.2 16.6 %collective-permute-start.7 = (bf16[8,160,128]{2,1,0:T(8,128)(2,1)}, bf16[8,160,128]{2,1,0:T(8,128)(2,1)}, u32[]{:S(2)}, u32[]{:S(2)}) collective-permute-start(bf16[8,160,128]{2,1,0:T(8,128)(2,1)} %all-to-all-done.refs_0_), channel_id=1, source_target_pairs={{0,4},{4,0},{1,5},{5,1},{2,6},{6,2},{3,7},{7,3},{8,12},{12,8},{9,1... | collective-permute-start | bytes 983048 | tf_op jit(solution)/shard_map/ppermute | solution.py:32
  57.0 10.5 %copy-start.4 = (bf16[8,160,128]{2,1,0:T(8,128)(2,1)}, bf16[8,160,128]{2,1,0:T(8,128)(2,1)S(1)}, u32[]{:S(2)}) copy-start(bf16[8,160,128]{2,1,0:T(8,128)(2,1)S(1)} %collective-permute-done.3.refs_1_) | copy-start | bytes 983044
  57.1 6.3 %collective-permute-start.5 = (bf16[4,160,128]{2,1,0:T(8,128)(2,1)S(1)}, bf16[4,160,128]{2,1,0:T(8,128)(2,1)}, u32[]{:S(2)}, u32[]{:S(2)}) collective-permute-start(bf16[4,160,128]{2,1,0:T(8,128)(2,1)S(1)} %slice.32), channel_id=1, source_target_pairs={{0,8},{8,16},{16,24},{24,0},{1,9},{9,17},{17,25},{25,1},{2,10},{10... | collective-permute-start | bytes 491528 | tf_op jit(solution)/shard_map/ppermute | solution.py:37
  59.2 6.6 %collective-permute-start.6 = (bf16[4,160,128]{2,1,0:T(8,128)(2,1)S(1)}, bf16[4,160,128]{2,1,0:T(8,128)(2,1)}, u32[]{:S(2)}, u32[]{:S(2)}) collective-permute-start(bf16[4,160,128]{2,1,0:T(8,128)(2,1)S(1)} %slice.33), channel_id=1, source_target_pairs={{0,24},{8,0},{16,8},{24,16},{1,25},{9,1},{17,9},{25,17},{2,26},{10... | collective-permute-start | bytes 491528 | tf_op jit(solution)/shard_map/ppermute | solution.py:37
  61.2 6.4 %collective-permute-start.8 = (bf16[8,160,128]{2,1,0:T(8,128)(2,1)S(1)}, bf16[8,160,128]{2,1,0:T(8,128)(2,1)}, u32[]{:S(2)}, u32[]{:S(2)}) collective-permute-start(bf16[8,160,128]{2,1,0:T(8,128)(2,1)S(1)} %collective-permute-done.3.refs_1_), channel_id=1, source_target_pairs={{0,4},{4,0},{1,5},{5,1},{2,6},{6,2},{3,7},{7,3},{8,12},{12,8},{9,1... | collective-permute-start | bytes 983048 | tf_op jit(solution)/shard_map/ppermute | solution.py:32
  63.3 4.2 %collective-permute-start.9 = (bf16[8,160,128]{2,1,0:T(8,128)(2,1)}, bf16[8,160,128]{2,1,0:T(8,128)(2,1)}, u32[]{:S(2)}, u32[]{:S(2)}) collective-permute-start(bf16[8,160,128]{2,1,0:T(8,128)(2,1)} %collective-permute-done.4.refs_2_), channel_id=1, source_target_pairs={{0,4},{4,0},{1,5},{5,1},{2,6},{6,2},{3,7},{7,3},{8,12},{12,8},{9,1... | collective-permute-start | bytes 983048 | tf_op jit(solution)/shard_map/ppermute | solution.py:32
  63.3 3.8 %collective-permute-start.10 = (bf16[4,160,128]{2,1,0:T(8,128)(2,1)}, bf16[4,160,128]{2,1,0:T(8,128)(2,1)}, u32[]{:S(2)}, u32[]{:S(2)}) collective-permute-start(bf16[4,160,128]{2,1,0:T(8,128)(2,1)} %collective-permute-done.5.refs_3_), channel_id=1, source_target_pairs={{0,4},{4,0},{1,5},{5,1},{2,6},{6,2},{3,7},{7,3},{8,12},{12,8},{9,1... | collective-permute-start | bytes 491528 | tf_op jit(solution)/shard_map/ppermute | solution.py:32
  65.7 1.8 collective-permute-start.11
  79.4 5.3 %collective-permute-start.16 = (bf16[4,8,160,128]{3,2,1,0:T(8,128)(2,1)}, bf16[4,8,160,128]{3,2,1,0:T(8,128)(2,1)}, u32[]{:S(2)}, u32[]{:S(2)}) collective-permute-start(bf16[4,8,160,128]{3,2,1,0:T(8,128)(2,1)} %get-tuple-element.74), channel_id=1, source_target_pairs={{0,4},{4,0},{1,5},{5,1},{2,6},{6,2},{3,7},{7,3},{8,12},{12,8},{9,1... | collective-permute-start | bytes 3932168 | tf_op jit(solution)/shard_map/ppermute | solution.py:32
  79.9 3.2 %collective-permute-start.12 = (bf16[64,1536]{1,0:T(8,128)(2,1)}, bf16[64,1536]{1,0:T(8,128)(2,1)S(1)}, u32[]{:S(2)}, u32[]{:S(2)}) collective-permute-start(bf16[64,1536]{1,0:T(8,128)(2,1)} %get-tuple-element.68), channel_id=1, source_target_pairs={{0,4},{4,0},{1,5},{5,1},{2,6},{6,2},{3,7},{7,3},{8,12},{12,8},{9,1... | collective-permute-start | bytes 589832 | tf_op jit(solution)/shard_map/ppermute | solution.py:32
  88.6 22.3 %all-to-all-start.1 = ((bf16[4,8,160,128]{3,2,1,0:T(8,128)(2,1)}), bf16[4,8,160,128]{3,2,1,0:T(8,128)(2,1)}, u32[]{:S(2)}, u32[]{:S(2)}) async-start(bf16[4,8,160,128]{3,2,1,0:T(8,128)(2,1)} %shard_map.163), calls=%async_computation.1 | async-start | bytes 2621440 | tf_op jit(solution)/shard_map/all_to_all | solution.py:41
  113.1 14.5 %all-to-all-start.2 = ((bf16[8,160,128]{2,1,0:T(8,128)(2,1)}), bf16[8,160,128]{2,1,0:T(8,128)(2,1)S(1)}, u32[]{:S(2)}, u32[]{:S(2)}) async-start(bf16[8,160,128]{2,1,0:T(8,128)(2,1)} %shard_map.165), calls=%async_computation.2 | async-start | bytes 655360 | tf_op jit(solution)/shard_map/all_to_all | solution.py:41
  127.6 0.7 copy-start.3
  132.2 41.8 %copy-start.2 = (f32[64,1536]{1,0:T(8,128)S(1)}, f32[64,1536]{1,0:T(8,128)}, u32[]{:S(2)}) copy-start(f32[64,1536]{1,0:T(8,128)} %get-tuple-element.83.pooled_ref) | copy-start | bytes 1179652
  132.2 16.0 %all-to-all-start.3 = ((bf16[8,208,128]{2,1,0:T(8,128)(2,1)}), bf16[8,208,128]{2,1,0:T(8,128)(2,1)}, u32[]{:S(2)}, u32[]{:S(2)}) async-start(bf16[8,208,128]{2,1,0:T(8,128)(2,1)} %get-tuple-element.86), calls=%async_computation.3 | async-start | bytes 851968 | tf_op jit(solution)/shard_map/all_to_all | solution.py:41
  139.6 16.2 %collective-permute-start.13 = (bf16[1152,128]{1,0:T(8,128)(2,1)}, bf16[1152,128]{1,0:T(8,128)(2,1)}, u32[]{:S(2)}, u32[]{:S(2)}) collective-permute-start(bf16[1152,128]{1,0:T(8,128)(2,1)} %get-tuple-element.70), channel_id=1, source_target_pairs={{0,8},{8,16},{16,24},{24,0},{1,9},{9,17},{17,25},{25,1},{2,10},{10... | collective-permute-start | bytes 884744 | tf_op jit(solution)/shard_map/ppermute | solution.py:37
  140.7 15.1 %collective-permute-start.14 = (bf16[1152,128]{1,0:T(8,128)(2,1)}, bf16[1152,128]{1,0:T(8,128)(2,1)}, u32[]{:S(2)}, u32[]{:S(2)}) collective-permute-start(bf16[1152,128]{1,0:T(8,128)(2,1)} %get-tuple-element.71), channel_id=1, source_target_pairs={{0,16},{8,24},{16,0},{24,8},{1,17},{9,25},{17,1},{25,9},{2,18},{10... | collective-permute-start | bytes 884744 | tf_op jit(solution)/shard_map/ppermute | solution.py:37
  141.7 14.7 %collective-permute-start.15 = (bf16[1152,128]{1,0:T(8,128)(2,1)}, bf16[1152,128]{1,0:T(8,128)(2,1)}, u32[]{:S(2)}, u32[]{:S(2)}) collective-permute-start(bf16[1152,128]{1,0:T(8,128)(2,1)} %get-tuple-element.72), channel_id=1, source_target_pairs={{0,24},{8,0},{16,8},{24,16},{1,25},{9,1},{17,9},{25,17},{2,26},{10... | collective-permute-start | bytes 884744 | tf_op jit(solution)/shard_map/ppermute | solution.py:37
  150.4 8.7 %collective-permute-start.17 = (bf16[288,128]{1,0:T(8,128)(2,1)}, bf16[288,128]{1,0:T(8,128)(2,1)S(1)}, u32[]{:S(2)}, u32[]{:S(2)}) collective-permute-start(bf16[288,128]{1,0:T(8,128)(2,1)} %get-tuple-element.88), channel_id=1, source_target_pairs={{0,8},{8,16},{16,24},{24,0},{1,9},{9,17},{17,25},{25,1},{2,10},{10... | collective-permute-start | bytes 221192 | tf_op jit(solution)/shard_map/ppermute | solution.py:37
  151.5 7.7 %collective-permute-start.18 = (bf16[288,128]{1,0:T(8,128)(2,1)}, bf16[288,128]{1,0:T(8,128)(2,1)S(1)}, u32[]{:S(2)}, u32[]{:S(2)}) collective-permute-start(bf16[288,128]{1,0:T(8,128)(2,1)} %get-tuple-element.89), channel_id=1, source_target_pairs={{0,16},{8,24},{16,0},{24,8},{1,17},{9,25},{17,1},{25,9},{2,18},{10... | collective-permute-start | bytes 221192 | tf_op jit(solution)/shard_map/ppermute | solution.py:37
  155.8 3.7 %collective-permute-start.19 = (bf16[288,128]{1,0:T(8,128)(2,1)}, bf16[288,128]{1,0:T(8,128)(2,1)S(1)}, u32[]{:S(2)}, u32[]{:S(2)}) collective-permute-start(bf16[288,128]{1,0:T(8,128)(2,1)} %get-tuple-element.90), channel_id=1, source_target_pairs={{0,24},{8,0},{16,8},{24,16},{1,25},{9,1},{17,9},{25,17},{2,26},{10... | collective-permute-start | bytes 221192 | tf_op jit(solution)/shard_map/ppermute | solution.py:37
  159.1 0.6 copy-start.5
  159.1 0.7 copy-start.6
  159.5 0.6 copy-start.7
  162.6 23.8 %all-to-all-start.4 = ((bf16[16,128,128]{2,1,0:T(8,128)(2,1)}), bf16[16,128,128]{2,1,0:T(8,128)(2,1)}, u32[]{:S(2)}, u32[]{:S(2)}) async-start(bf16[16,128,128]{2,1,0:T(8,128)(2,1)} %shard_map.168), calls=%async_computation.4 | async-start | bytes 1048576 | tf_op jit(solution)/shard_map/all_to_all | solution.py:41
  169.7 8.4 %collective-permute-start.20 = (bf16[1,1536]{1,0:T(2,128)(2,1)S(1)}, bf16[1,1536]{1,0:T(2,128)(2,1)S(1)}, u32[]{:S(2)}, u32[]{:S(2)}) collective-permute-start(bf16[1,1536]{1,0:T(2,128)(2,1)S(1)} %get-tuple-element.108), channel_id=1, source_target_pairs={{0,4},{4,8},{8,12},{12,16},{16,20},{20,24},{24,28},{28,32},{32,36}... | collective-permute-start | bytes 9224 | tf_op jit(solution)/shard_map/ppermute | solution.py:619
  171.6 6.5 %collective-permute-start.21 = (bf16[1,1536]{1,0:T(2,128)(2,1)S(1)}, bf16[1,1536]{1,0:T(2,128)(2,1)S(1)}, u32[]{:S(2)}, u32[]{:S(2)}) collective-permute-start(bf16[1,1536]{1,0:T(2,128)(2,1)S(1)} %get-tuple-element.107), channel_id=1, source_target_pairs={{4,0},{8,4},{12,8},{16,12},{20,16},{24,20},{28,24},{32,28},{36,32}... | collective-permute-start | bytes 9224 | tf_op jit(solution)/shard_map/ppermute | solution.py:620
  178.1 0.6 copy-start.10
  178.7 0.6 copy-start.11
Sparse Core Ops, SparseCore 0:
  44.2 28.5 all-gather.2
  84.9 25.7 all-gather.4

commit v6 on v5

--- a/solution.py
+++ b/solution.py
@@ -88,8 +88,8 @@
 
 
 def front_kernel(
-    x_ref, low_ref, high_ref, gain_in_ref, taps_ref, gain_attn_ref, kw_ref, vw_ref,
-    kv_ref, normed_ref, pooled_ref, act, plain,
+    first_ref, x_ref, low_ref, high_ref, gain_in_ref, taps_ref, gain_attn_ref, kw_ref, vw_ref, gy_ref,
+    kv_ref, normed_ref, pooled_ref, keep_ref, send_ref, act, plain,
 ):
     fine, width = x_ref.shape
     pool = fine // 2
@@ -122,6 +122,9 @@
     kv = pack(dot(normed, kw_ref[...]), contract_cols(normed, vw_ref[...])).astype(BF)
     for i in range(kv_ref.shape[0]):
         kv_ref[i] = kv
+    first = first_ref[0] > 0
+    keep_ref[...] = jnp.where(first, normed, gy_ref[...])
+    send_ref[...] = jnp.where(first, gy_ref[...], normed)
 
 
 def side_kernel(x_ref, low_ref, high_ref, gain_in_ref, taps_ref, pairs_ref, spread_ref, act, slope):
@@ -288,26 +291,6 @@
     return total
 
 
-def both_kernel(own_ref, got_ref, out_ref):
-    for j in range(own_ref.shape[1]):
-        out_ref[0, j] = (own_ref[0, j].astype(F32) + got_ref[0, j].astype(F32)).astype(BF)
-
-
-def both(own, got):
-    spec = pl.BlockSpec((1,) + own.shape[1:], lambda i: (i, 0, 0, 0))
-    return pl.pallas_call(
-        both_kernel,
-        grid=(own.shape[0],),
-        out_shape=shape(*own.shape),
-        in_specs=[spec, spec],
-        out_specs=spec,
-        compiler_params=pltpu.CompilerParams(vmem_limit_bytes=60 * 2**20),
-        cost_estimate=pl.CostEstimate(
-            flops=own.size, bytes_accessed=6 * own.size, transcendentals=0
-        ),
-    )(own, got)
-
-
 def sum_kernel(parts_ref, out_ref):
     for j in range(out_ref.shape[0]):
         total = parts_ref[0, j].astype(F32)
@@ -317,7 +300,7 @@
 
 
 def back_kernel(cores, parts_ref, part_ref, kw_ref, vw_ref, pooled_ref, gain_ref, gy_ref, pairs_ref,
-                spread_ref, half_ref, out_ref, small_ref):
+                spread_ref, half_ref, top_ref, bottom_ref, out_ref, small_ref):
     gkv = add_up(parts_ref).astype(BF)
     gk, gv = unpack(gkv)
     grad = part_ref[...] + contract_cols(gk, kw_ref[...]) + dot(gv, vw_ref[...])
@@ -330,6 +313,8 @@
     grad_pool = gy_ref[...].astype(F32) + scale * (inner - raw * along)
     half = (grad_pool * 0.5).astype(BF)
     half_ref[...] = half
+    top_ref[...] = half[:1]
+    bottom_ref[...] = half[half.shape[0] - 1 :]
     h = half.astype(F32)
     taps = pairs_ref.shape[0]
     for k in range(taps):
@@ -539,12 +524,13 @@
             ),
         )(flag, *args)
 
-    kv, normed, pooled = call(
+    kv, normed, pooled, keep, send = flagged(
         front_kernel,
-        (shape(nz, packed, qk), shape(pool, width), shape(pool, width, dtype=F32)),
+        (shape(nz, packed, qk), shape(pool, width), shape(pool, width, dtype=F32),
+         shape(pool, width), shape(pool, width)),
         [pltpu.VMEM((width // 128, n, 128), F32) for n in (fine + 4, fine)],
         2 * pool * width * (qk + vd),
-        x, low, high, gain_in, conv_taps, gain_attn, key_weight, value_weight,
+        first, x, low, high, gain_in, conv_taps, gain_attn, key_weight, value_weight, grad_y,
     )
     pairs, spread = call(
         side_kernel,
@@ -554,16 +540,11 @@
         x, low, high, gain_in, conv_taps,
     )
 
-    def ours_theirs(ours, theirs):
-        return (jnp.where(first_core, ours, theirs),
-                swap(jnp.where(first_core, theirs, ours)))
-
     kv = exchange(kv, "z")
     normed, cotangent = lax.optimization_barrier((normed, grad_y))
     queries = dot(normed, query_weight).astype(BF)
     grad_mixed = contract_cols(cotangent, out_weight).astype(BF)
-    normed, queries = lax.optimization_barrier((normed, queries))
-    keep, got = ours_theirs(normed, grad_y)
+    got = swap(send)
     kv, queries, grad_mixed, keep, got = lax.optimization_barrier(
         (kv, queries, grad_mixed, keep, got)
     )
@@ -581,8 +562,11 @@
 
     later = lax.all_gather(jnp.concatenate([keep, swap(send)], axis=0), "x", axis=0, tiled=True)
 
-    gkv = both(gkv, swap(others))
-    gkv, pairs, spread = lax.optimization_barrier((exchange(gkv, "y"), pairs, spread))
+    gkv = (gkv.astype(F32) + swap(others).astype(F32)).astype(BF)
+    mixed_out = (pooled + dot(mixed, out_weight)).astype(BF)
+    gkv, pairs, spread, mixed_out = lax.optimization_barrier(
+        (exchange(gkv, "y"), pairs, spread, mixed_out)
+    )
     (gkv,) = call(sum_kernel, (shape(*kv.shape),), [], 0, gkv)
     gkv = exchange(gkv, "z")
 
@@ -608,16 +592,16 @@
 
     tail = taps + 2
     extra = (tail * tiles // nc + 15) // 16 * 16
-    half, gkv = call(
+    half, top, bottom, gkv = call(
         functools.partial(back_kernel, nc),
-        (shape(pool, width), shape(nx * nc, packed + extra, qk)),
+        (shape(pool, width), shape(1, width), shape(1, width),
+         shape(nx * nc, packed + extra, qk)),
         [pltpu.VMEM((8, width), F32)],
         2 * pool * width * (qk + vd),
         gkv, part, key_weight, value_weight, pooled, gain_attn, grad_y, pairs, spread,
     )
-    got = exchange(gkv, ("x", "core"))
-    before = lax.ppermute(half[pool - 1 :], seq, up)
-    after = lax.ppermute(half[:1], seq, down)
+    before, after = lax.ppermute(bottom, seq, up), lax.ppermute(top, seq, down)
+    got, before, after = lax.optimization_barrier((exchange(gkv, ("x", "core")), before, after))
     (input_grad,) = call(
         input_kernel,
         (shape(fine, width),),
@@ -626,7 +610,6 @@
         fine * width * 40,
         x, gain_in, conv_taps, half, before, after,
     )
-    mixed_out = (pooled + dot(mixed, out_weight)).astype(BF)
     late = call(
         late_kernel,
         (shape(keep // ny * 5 // 2 + extra, qk),) * ny,
@@ -635,6 +618,7 @@
         left, got,
     )
     late = [late[0]] + [shift(late[i], "y", i) for i in range(1, ny)]
+    late, input_grad = lax.optimization_barrier((late, input_grad))
     (sums,) = flagged(
         functools.partial(turn_kernel, ny, q_cols),
         (shape(nz * nc, (tiles * each + extra + 15) // 16 * 16, qk),),
@@ -642,9 +626,7 @@
         0,
         first, *sums, *late,
     )
-    got, mixed_out, input_grad = lax.optimization_barrier(
-        (exchange(sums, ("z", "core")), mixed_out, input_grad)
-    )
+    got = exchange(sums, ("z", "core"))
     results = call(
         functools.partial(last_kernel, tiles),
         tuple(shape(*dims, dtype=F32) for dims in (

time: 196 us -> 203 us (1.036)
  blocking collectives: 0 us -> 21.8 us
  starting transfers between devices: 65.6 us -> 53.8 us
  Pallas kernels: 43.7 us -> 40 us
  other arithmetic: 5.69 us -> 8.14 us
    all_to_all x0 -> x1, blocking collectives: none -> 21.8 us  [exchange(): return lax.all_to_all(blocks, axis, 0, 0, tiled=True)]
    ppermute x2, waiting for transfers between devices: 0.01 us -> 9.4 us  [the longest x1 6.06 us: shards(): lax.ppermute(bottom, seq, up)]
    all_to_all x5 -> x4, waiting for transfers between devices: 27.2 us -> 20 us  [exchange(): return lax.all_to_all(blocks, axis, 0, 0, tiled=True)]
    ppermute x10, starting transfers between devices: 14.8 us -> 10.4 us  [shift(): lax.ppermute(block, axis, [(i, (i + step) % count) for i in range(count)])]
    all_to_all x5 -> x4, starting transfers between devices: 30.1 us -> 25.9 us  [exchange(): return lax.all_to_all(blocks, axis, 0, 0, tiled=True)]
    pallas_call x1 -> x0, Pallas kernels: 3.82 us -> none  [both(): pl.pallas_call(both_kernel, grid=(own.shape[0],), out_shape=shape(*own.sh...]
    ppermute x8, starting transfers between devices: 9.65 us -> 6.11 us  [swap(): return lax.ppermute(block, 'core', [(0, 1), (1, 0)])]
    pallas_call x2 -> x3, Pallas kernels: 7.49 us -> 10.9 us  [flagged(): pl.pallas_call(kernel, out_shape=out_shape, in_specs=[smem] + [vmem] * le...]
  transfers between devices with their start and end apart: 29 -> 28, of which waited for: 14 -> 13; matrix products, arithmetic and copies ran while one was open for 9% -> 10% of each run, Pallas kernels for 17% -> 14%
where the time goes in v6:
time: 203 us; the launch traced here: 202 us
  starting transfers between devices  53.8 us (27%)
  waiting for transfers between devices  46.5 us (23%)
  Pallas kernels  40 us (20%)
  blocking collectives  21.8 us (11%)
  between operations  14.3 us (7%)
  matrix products  12.8 us (6%)
  other arithmetic  8.14 us (4%)
  local copies, waits for them, and re-layouts  4.85 us (2%)
    all_to_all x4, starting transfers between devices, exchange(): return lax.all_to_all(blocks, axis, 0, 0, tiled=True)  25.9 us
    all_to_all x1, blocking collectives, exchange(): return lax.all_to_all(blocks, axis, 0, 0, tiled=True)  21.8 us
    all_to_all x4, waiting for transfers between devices, exchange(): return lax.all_to_all(blocks, axis, 0, 0, tiled=True)  20 us
    pallas_call x6, Pallas kernels, call(): pl.pallas_call(kernel, out_shape=out_shape, scratch_shapes=scratch, compi...  17.3 us
    pallas_call x1, Pallas kernels, attention(): pl.pallas_call(functools.partial(attention_kernel, scale, heads, group, u...  11.8 us
    pallas_call x3, Pallas kernels, flagged(): pl.pallas_call(kernel, out_shape=out_shape, in_specs=[smem] + [vmem] * le...  10.9 us
    ppermute x10, starting transfers between devices, shift(): lax.ppermute(block, axis, [(i, (i + step) % count) for i in range(count)])  10.4 us
    ppermute x10, waiting for transfers between devices, shift(): lax.ppermute(block, axis, [(i, (i + step) % count) for i in range(count)])  10.3 us
  transfers between devices with their start and end apart: 28, of which 13 were waited for; matrix products, arithmetic and copies ran while one was open for 10% of the time, Pallas kernels for 14%

profile of v6, /device:TPU:1, one launch (start us, length us, event | category | flops | bytes accessed | tf_op | source)
XLA Modules:
  0.0 202.2 jit_solution(444686185652084424)
XLA Ops:
  7.2 0.9 slice_bitcast_fusion
  8.1 4.7 %collective-permute-start = (bf16[2,1536]{1,0:T(2,128)(2,1)S(1)}, bf16[2,1536]{1,0:T(2,128)(2,1)S(1)}, u32[]{:S(2)}, u32[]{:S(2)}) collective-permute-start(bf16[2,1536]{1,0:T(2,128)(2,1)S(1)} %get-tuple-element.120), channel_id=1, source_target_pairs={{0,4},{4,8},{8,12},{12,16},{16,20},{20,24},{24,28},{28,32},{32,36}... | collective-permute-start | bytes 18440 | tf_op jit(solution)/shard_map/ppermute | solution.py:510
  12.8 1.9 collective-permute-start.1
  14.8 3.0 %collective-permute-done.1.high_ref = bf16[2,1536]{1,0:T(2,128)(2,1)S(1)} collective-permute-done((bf16[2,1536]{1,0:T(2,128)(2,1)S(1)}, bf16[2,1536]{1,0:T(2,128)(2,1)S(1)}, u32[]{:S(2)}, u32[]{:S(2)}) %collective-permute-start.1) | collective-permute-done | bytes 6176 | tf_op jit(solution)/shard_map/ppermute | solution.py:511
  17.8 0.6 copy-done.10
  18.4 3.5 %shard_map.160 = (bf16[8,160,128]{2,1,0:T(8,128)(2,1)}, bf16[64,1536]{1,0:T(8,128)(2,1)}, f32[64,1536]{1,0:T(8,128)}, bf16[64,1536]{1,0:T(8,128)(2,1)}, bf16[64,1536]{1,0:T(8,128)(2,1)}) custom-call(s32[1]{0:T(128)} %bitcast.1.first_ref, bf16[128,1536]{1,0:T(8,128)(2,1)} %bitcast.19, bf16[2,1536]{1,0:T(2,128)(2,1)} %copy-done.9, bf16[2,1536]{1,0:T(2,128)(2,1)} %copy-done.10, ...), custom_call_target="tpu_custom_call" | custom-call | flops 62914560 | bytes 9437184 | tf_op jit(solution)/shard_map/pallas_call | solution.py:516
  21.9 10.4 %all-to-all-start = ((bf16[8,160,128]{2,1,0:T(8,128)(2,1)}), bf16[8,160,128]{2,1,0:T(8,128)(2,1)S(1)}, u32[]{:S(2)}, u32[]{:S(2)}) async-start(bf16[8,160,128]{2,1,0:T(8,128)(2,1)} %get-tuple-element.64), calls=%async_computation | async-start | bytes 655360 | tf_op jit(solution)/shard_map/all_to_all | solution.py:41
  32.3 4.7 %convolution_convert_fusion.g_ref = bf16[64,1536]{1,0:T(8,128)(2,1)} fusion(bf16[64,1536]{1,0:T(8,128)(2,1)} %bitcast.25, bf16[1536,1536]{1,0:T(8,128)(2,1)} %param.16), kind=kOutput, calls=%fused_computation.3 | convolution fusion | flops 302088192 | bytes 5111808 | tf_op jit(solution)/shard_map/dot_general | solution.py:24
  37.0 1.3 convolution_convert_fusion.1.q_ref
  38.3 7.7 %all-to-all-done.refs_0_ = bf16[8,160,128]{2,1,0:T(8,128)(2,1)S(1)} async-done(((bf16[8,160,128]{2,1,0:T(8,128)(2,1)}), bf16[8,160,128]{2,1,0:T(8,128)(2,1)S(1)}, u32[]{:S(2)}, u32[]{:S(2)}) %all-to-all-start) | async-done | bytes 327712 | tf_op jit(solution)/shard_map/all_to_all | solution.py:41
  46.0 1.9 pad_maximum_fusion
  48.0 0.1 collective-permute-start.3
  48.1 2.7 %collective-permute-start.4 = (bf16[8,160,128]{2,1,0:T(8,128)(2,1)S(1)}, bf16[8,160,128]{2,1,0:T(8,128)(2,1)}, u32[]{:S(2)}, u32[]{:S(2)}) collective-permute-start(bf16[8,160,128]{2,1,0:T(8,128)(2,1)S(1)} %all-to-all-done.refs_0_), channel_id=1, source_target_pairs={{0,24},{8,0},{16,8},{24,16},{1,25},{9,1},{17,9},{25,17},{2,26},{10... | collective-permute-start | bytes 983048 | tf_op jit(solution)/shard_map/ppermute | solution.py:37
  50.7 1.0 collective-permute-start.7
  51.8 6.4 %collective-permute-done.3.refs_1_ = bf16[8,160,128]{2,1,0:T(8,128)(2,1)} collective-permute-done((bf16[8,160,128]{2,1,0:T(8,128)(2,1)S(1)}, bf16[8,160,128]{2,1,0:T(8,128)(2,1)}, u32[]{:S(2)}, u32[]{:S(2)}) %collective-permute-start.3) | collective-permute-done | bytes 327712 | tf_op jit(solution)/shard_map/ppermute | solution.py:37
  58.2 0.9 slice.24
  59.1 0.1 collective-permute-start.5
  59.2 0.9 slice.25
  60.2 2.7 %collective-permute-start.6 = (bf16[4,160,128]{2,1,0:T(8,128)(2,1)S(1)}, bf16[4,160,128]{2,1,0:T(8,128)(2,1)}, u32[]{:S(2)}, u32[]{:S(2)}) collective-permute-start(bf16[4,160,128]{2,1,0:T(8,128)(2,1)S(1)} %slice.25), channel_id=1, source_target_pairs={{0,24},{8,0},{16,8},{24,16},{1,25},{9,1},{17,9},{25,17},{2,26},{10... | collective-permute-start | bytes 491528 | tf_op jit(solution)/shard_map/ppermute | solution.py:37
  62.9 1.9 collective-permute-start.8
  64.8 0.2 collective-permute-done.5.refs_3_
  65.0 2.2 %collective-permute-start.10 = (bf16[4,160,128]{2,1,0:T(8,128)(2,1)}, bf16[4,160,128]{2,1,0:T(8,128)(2,1)}, u32[]{:S(2)}, u32[]{:S(2)}) collective-permute-start(bf16[4,160,128]{2,1,0:T(8,128)(2,1)} %collective-permute-done.5.refs_3_), channel_id=1, source_target_pairs={{0,4},{4,0},{1,5},{5,1},{2,6},{6,2},{3,7},{7,3},{8,12},{12,8},{9,1... | collective-permute-start | bytes 491528 | tf_op jit(solution)/shard_map/ppermute | solution.py:32
  67.1 0.4 collective-permute-start.11
  67.6 0.6 pad_add_fusion.place_ref
  68.2 0.3 collective-permute-done.10.refs_8_
  68.5 0.5 collective-permute-done.11.refs_9_
  69.0 11.8 %shard_map.161 = (bf16[64,1536]{1,0:T(8,128)(2,1)}, bf16[64,1024]{1,0:T(8,128)(2,1)}, bf16[64,1536]{1,0:T(8,128)(2,1)}, bf16[64,1536]{1,0:T(8,128)(2,1)}, bf16[4...) custom-call(s32[2]{0:T(128)} %pad_add_fusion.place_ref, bf16[64,1024]{1,0:T(8,128)(2,1)} %convolution_convert_fusion.1.q_ref, ...), custom_call_target="tpu_custom_call" | custom-call | flops 4026531840 | bytes 5242880 | tf_op jit(solution)/shard_map/pallas_call | solution.py:264
  80.8 0.4 collective-permute-start.12
  81.3 0.1 collective-permute-start.13
  81.4 3.0 %collective-permute-done.13 = bf16[64,1536]{1,0:T(8,128)(2,1)S(1)} collective-permute-done((bf16[64,1536]{1,0:T(8,128)(2,1)}, bf16[64,1536]{1,0:T(8,128)(2,1)S(1)}, u32[]{:S(2)}, u32[]{:S(2)}) %collective-permute-start.13) | collective-permute-done | bytes 196640 | tf_op jit(solution)/shard_map/ppermute | solution.py:32
  84.4 1.7 pad_maximum_fusion.1
  86.2 3.2 %add_convert_fusion = bf16[4,8,160,128]{3,2,1,0:T(8,128)(2,1)} fusion(bf16[4,8,160,128]{3,2,1,0:T(8,128)(2,1)} %collective-permute-done.12, bf16[4,8,160,128]{3,2,1,0:T(8,128)(2,1)} %get-tuple-element.73), kind=kLoop, calls=%fused_computation | loop fusion | flops 2621440 | bytes 3932160 | tf_op jit(solution)/shard_map/convert_element_type | solution.py:565
  89.4 4.8 %all-to-all-start.1 = ((bf16[4,8,160,128]{3,2,1,0:T(8,128)(2,1)}), bf16[4,8,160,128]{3,2,1,0:T(8,128)(2,1)}, u32[]{:S(2)}, u32[]{:S(2)}) async-start(bf16[4,8,160,128]{3,2,1,0:T(8,128)(2,1)} %add_convert_fusion), calls=%async_computation.1 | async-start | bytes 2621440 | tf_op jit(solution)/shard_map/all_to_all | solution.py:41
  94.1 3.8 %shard_map.162 = (f32[5,64,1536]{2,1,0:T(8,128)}, f32[64,1536]{1,0:T(8,128)}) custom-call(bf16[128,1536]{1,0:T(8,128)(2,1)} %bitcast.20, bf16[2,1536]{1,0:T(2,128)(2,1)} %copy-done.9, bf16[2,1536]{1,0:T(2,128)(2,1)} %copy-done.10, f32[1536]{0:T(1024)} %gain_ref.3, f32[5,1536]{1,0:T(8,128)} %taps_ref.5), custom_call_target="tpu_custom_call" | custom-call | flops 7864320 | bytes 2801664 | tf_op jit(solution)/shard_map/pallas_call | solution.py:47
  97.9 4.1 %fusion = bf16[64,1536]{1,0:T(8,128)(2,1)} fusion(f32[64,1536]{1,0:T(8,128)S(1)} %copy-done.1, bf16[64,1536]{1,0:T(8,128)(2,1)} %get-tuple-element.78, bf16[1536,1536]{1,0:T(8,128)(2,1)} %param.16), kind=kOutput, calls=%fused_computation.2 | convolution fusion | flops 302186496 | bytes 5505024 | tf_op jit(solution)/shard_map/dot_general | solution.py:28
  102.0 9.8 %all-to-all-done.1.parts_ref = bf16[4,8,160,128]{3,2,1,0:T(8,128)(2,1)} async-done(((bf16[4,8,160,128]{3,2,1,0:T(8,128)(2,1)}), bf16[4,8,160,128]{3,2,1,0:T(8,128)(2,1)}, u32[]{:S(2)}, u32[]{:S(2)}) %all-to-all-start.1) | async-done | bytes 1310752 | tf_op jit(solution)/shard_map/all_to_all | solution.py:41
  111.7 2.2 %shard_map.163 = bf16[8,160,128]{2,1,0:T(8,128)(2,1)} custom-call(bf16[4,8,160,128]{3,2,1,0:T(8,128)(2,1)} %all-to-all-done.1.parts_ref), custom_call_target="tpu_custom_call" | custom-call | bytes 1638400 | tf_op jit(solution)/shard_map/pallas_call | solution.py:47
  113.9 3.4 %all-to-all-start.2 = ((bf16[8,160,128]{2,1,0:T(8,128)(2,1)}), bf16[8,160,128]{2,1,0:T(8,128)(2,1)S(1)}, u32[]{:S(2)}, u32[]{:S(2)}) async-start(bf16[8,160,128]{2,1,0:T(8,128)(2,1)} %shard_map.163), calls=%async_computation.2 | async-start | bytes 655360 | tf_op jit(solution)/shard_map/all_to_all | solution.py:41
  117.4 0.7 compare_select_fusion.8.target_ref
  118.1 2.7 %fusion.14.part_ref = f32[64,1536]{1,0:T(8,128)} fusion(bf16[64,1024]{1,0:T(8,128)(2,1)} %get-tuple-element.86, bf16[1536,1024]{1,0:T(8,128)(2,1)S(1)} %copy-done), kind=kOutput, calls=%fused_computation.50 | convolution fusion | flops 201326592 | bytes 3670016 | tf_op jit(solution)/shard_map/dot_general | solution.py:24
  120.8 5.0 %shard_map.164 = (bf16[384,512]{1,0:T(8,128)(2,1)}, bf16[1152,128]{1,0:T(8,128)(2,1)}, bf16[1152,128]{1,0:T(8,128)(2,1)}, bf16[1152,128]{1,0:T(8,128)(2,1)}, bf16[1152,128]{1,0:T(8,128)(2,1)}) custom-call(s32[1]{0:T(128)} %bitcast.1.first_ref, s32[1,1536]{1,0:T(1,128)} %compare_select_fusion.8.target_ref, ...), custom_call_target="tpu_custom_call" | custom-call | flops 1207959552 | bytes 9437184 | tf_op jit(solution)/shard_map/pallas_call | solution.py:516
  125.8 2.6 %all-to-all-done.2.parts_ref = bf16[8,160,128]{2,1,0:T(8,128)(2,1)S(1)} async-done(((bf16[8,160,128]{2,1,0:T(8,128)(2,1)}), bf16[8,160,128]{2,1,0:T(8,128)(2,1)S(1)}, u32[]{:S(2)}, u32[]{:S(2)}) %all-to-all-start.2) | async-done | bytes 327712 | tf_op jit(solution)/shard_map/all_to_all | solution.py:41
  128.4 0.7 copy-done.2
  129.2 4.0 %shard_map.165 = (bf16[64,1536]{1,0:T(8,128)(2,1)}, bf16[1,1536]{1,0:T(2,128)(2,1)}, bf16[1,1536]{1,0:T(2,128)(2,1)}, bf16[8,208,128]{2,1,0:T(8,128)(2,1)}) custom-call(bf16[8,160,128]{2,1,0:T(8,128)(2,1)} %copy-done.2, f32[64,1536]{1,0:T(8,128)} %fusion.14.part_ref, bf16[1536,128]{1,0:T(8,128)(2,1)} %kw_ref.3, bf16[192,1536]{1,0:T(8,128)(2,1)} %bitcast.23, ...), custom_call_target="tpu_custom_call" | custom-call | flops 62914560 | bytes 5287936 | tf_op jit(solution)/shard_map/pallas_call | solution.py:47
  133.1 7.4 %all-to-all-start.3 = ((bf16[8,208,128]{2,1,0:T(8,128)(2,1)}), bf16[8,208,128]{2,1,0:T(8,128)(2,1)}, u32[]{:S(2)}, u32[]{:S(2)}) async-start(bf16[8,208,128]{2,1,0:T(8,128)(2,1)} %get-tuple-element.92), calls=%async_computation.3 | async-start | bytes 851968 | tf_op jit(solution)/shard_map/all_to_all | solution.py:41
  140.5 1.1 collective-permute-start.19
  141.6 1.0 collective-permute-start.20
  142.6 1.4 collective-permute-start.21
  144.0 2.7 %collective-permute-start.14 = (bf16[1,1536]{1,0:T(2,128)(2,1)}, bf16[1,1536]{1,0:T(2,128)(2,1)S(1)}, u32[]{:S(2)}, u32[]{:S(2)}) collective-permute-start(bf16[1,1536]{1,0:T(2,128)(2,1)} %get-tuple-element.93), channel_id=1, source_target_pairs={{0,4},{4,8},{8,12},{12,16},{16,20},{20,24},{24,28},{28,32},{32,36}... | collective-permute-start | bytes 9224 | tf_op jit(solution)/shard_map/ppermute | solution.py:603
  146.7 1.9 collective-permute-start.15
  148.6 6.1 %collective-permute-done.14.before_ref = bf16[1,1536]{1,0:T(2,128)(2,1)S(1)} collective-permute-done((bf16[1,1536]{1,0:T(2,128)(2,1)}, bf16[1,1536]{1,0:T(2,128)(2,1)S(1)}, u32[]{:S(2)}, u32[]{:S(2)}) %collective-permute-start.14) | collective-permute-done | bytes 3104 | tf_op jit(solution)/shard_map/ppermute | solution.py:603
  154.7 3.3 %collective-permute-done.15.after_ref = bf16[1,1536]{1,0:T(2,128)(2,1)S(1)} collective-permute-done((bf16[1,1536]{1,0:T(2,128)(2,1)}, bf16[1,1536]{1,0:T(2,128)(2,1)S(1)}, u32[]{:S(2)}, u32[]{:S(2)}) %collective-permute-start.15) | collective-permute-done | bytes 3104 | tf_op jit(solution)/shard_map/ppermute | solution.py:603
  158.0 2.3 %shard_map.166 = (bf16[288,128]{1,0:T(8,128)(2,1)}, bf16[288,128]{1,0:T(8,128)(2,1)}, bf16[288,128]{1,0:T(8,128)(2,1)}, bf16[288,128]{1,0:T(8,128)(2,1)}) custom-call(bf16[384,512]{1,0:T(8,128)(2,1)} %get-tuple-element.87.left_ref, bf16[8,208,128]{2,1,0:T(8,128)(2,1)} %all-to-all-done.3.got_ref), custom_call_target="tpu_custom_call" | custom-call | flops 125829120 | bytes 1114112 | tf_op jit(solution)/shard_map/pallas_call | solution.py:47
  160.3 0.7 collective-permute-start.16
  161.0 0.7 collective-permute-start.17
  161.7 3.5 %collective-permute-done.16.refs_5_ = bf16[288,128]{1,0:T(8,128)(2,1)S(1)} collective-permute-done((bf16[288,128]{1,0:T(8,128)(2,1)}, bf16[288,128]{1,0:T(8,128)(2,1)S(1)}, u32[]{:S(2)}, u32[]{:S(2)}) %collective-permute-start.16) | collective-permute-done | bytes 73760 | tf_op jit(solution)/shard_map/ppermute | solution.py:37
  165.2 3.3 %shard_map.167 = bf16[128,1536]{1,0:T(8,128)(2,1)} custom-call(bf16[128,1536]{1,0:T(8,128)(2,1)} %bitcast.21, f32[1536]{0:T(1024)} %gain_ref.3, f32[5,1536]{1,0:T(8,128)} %taps_ref.5, bf16[64,1536]{1,0:T(8,128)(2,1)} %get-tuple-element.100.half_ref, bf16[1,1536]{1,0:T(2,128)(2,1)} %copy-done.11, bf16[1,1536]{1,0:T(2,128)(2,1)} %copy-done.12), custom_call_target="tpu_custom_call" | custom-call | flops 7864320 | bytes 1026048 | tf_op jit(solution)/shard_map/pallas_call | solution.py:47
  168.6 0.1 collective-permute-done.18.refs_7_
  168.7 0.5 copy-done.7
  169.2 0.1 copy-done.8
  169.3 0.1 copy-done.4
  169.4 2.5 %shard_map.168 = bf16[16,128,128]{2,1,0:T(8,128)(2,1)} custom-call(s32[1]{0:T(128)} %bitcast.1.first_ref, bf16[1152,128]{1,0:T(8,128)(2,1)} %get-tuple-element.104.refs_0_, bf16[1152,128]{1,0:T(8,128)(2,1)} %copy-done.4, bf16[1152,128]{1,0:T(8,128)(2,1)} %collective-permute-done.20.refs_2_, bf16[1152,128]{1,0:T(8,128)(2,1)} %collective-permute-done.21.refs_3_, ...), custom_call_target="tpu_custom_call" | custom-call | bytes 9437184 | tf_op jit(solution)/shard_map/pallas_call | solution.py:516
  171.8 21.8 %all_to_all.25.got_ref = bf16[16,128,128]{2,1,0:T(8,128)(2,1)} all-to-all(bf16[16,128,128]{2,1,0:T(8,128)(2,1)} %shard_map.168), channel_id=1, replica_groups=mesh['z'=8,'y'=4,'core'=2,'x'=4] {'z','core'}, dimensions={0} | all-to-all | bytes 1048576 | tf_op jit(solution)/shard_map/all_to_all | solution.py:41
  193.6 1.7 shard_map.169
  (43 shorter events, 0.2 us)
Async XLA Ops:
  7.2 29.8 %copy-start = (bf16[1536,1024]{1,0:T(8,128)(2,1)S(1)}, bf16[1536,1024]{1,0:T(8,128)(2,1)}, u32[]{:S(2)}) copy-start(bf16[1536,1024]{1,0:T(8,128)(2,1)} %param.13) | copy-start | bytes 9437188
  8.1 6.7 %collective-permute-start = (bf16[2,1536]{1,0:T(2,128)(2,1)S(1)}, bf16[2,1536]{1,0:T(2,128)(2,1)S(1)}, u32[]{:S(2)}, u32[]{:S(2)}) collective-permute-start(bf16[2,1536]{1,0:T(2,128)(2,1)S(1)} %get-tuple-element.120), channel_id=1, source_target_pairs={{0,4},{4,8},{8,12},{12,16},{16,20},{20,24},{24,28},{28,32},{32,36}... | collective-permute-start | bytes 18440 | tf_op jit(solution)/shard_map/ppermute | solution.py:510
  12.8 4.9 %collective-permute-start.1 = (bf16[2,1536]{1,0:T(2,128)(2,1)S(1)}, bf16[2,1536]{1,0:T(2,128)(2,1)S(1)}, u32[]{:S(2)}, u32[]{:S(2)}) collective-permute-start(bf16[2,1536]{1,0:T(2,128)(2,1)S(1)} %get-tuple-element.119), channel_id=1, source_target_pairs={{4,0},{8,4},{12,8},{16,12},{20,16},{24,20},{28,24},{32,28},{36,32}... | collective-permute-start | bytes 18440 | tf_op jit(solution)/shard_map/ppermute | solution.py:511
  14.8 3.0 %copy-start.9 = (bf16[2,1536]{1,0:T(2,128)(2,1)}, bf16[2,1536]{1,0:T(2,128)(2,1)S(1)}, u32[]{:S(2)}) copy-start(bf16[2,1536]{1,0:T(2,128)(2,1)S(1)} %collective-permute-done.low_ref) | copy-start | bytes 18436
  17.8 0.6 copy-start.10
  21.8 16.5 %collective-permute-start.2 = (bf16[64,1536]{1,0:T(8,128)(2,1)}, bf16[64,1536]{1,0:T(8,128)(2,1)}, u32[]{:S(2)}, u32[]{:S(2)}) collective-permute-start(bf16[64,1536]{1,0:T(8,128)(2,1)} %get-tuple-element.69), channel_id=1, source_target_pairs={{0,4},{4,0},{1,5},{5,1},{2,6},{6,2},{3,7},{7,3},{8,12},{12,8},{9,1... | collective-permute-start | bytes 589832 | tf_op jit(solution)/shard_map/ppermute | solution.py:32
  21.9 24.1 %all-to-all-start = ((bf16[8,160,128]{2,1,0:T(8,128)(2,1)}), bf16[8,160,128]{2,1,0:T(8,128)(2,1)S(1)}, u32[]{:S(2)}, u32[]{:S(2)}) async-start(bf16[8,160,128]{2,1,0:T(8,128)(2,1)} %get-tuple-element.64), calls=%async_computation | async-start | bytes 655360 | tf_op jit(solution)/shard_map/all_to_all | solution.py:41
  32.2 88.6 %all-gather.3.cloned.1.call-start = ((), (), s32[]{:S(2)}) async-start(), calls=%async_computation.5 | async-start | bytes 1966080 | tf_op jit(solution)/shard_map/all_gather | solution.py:551
  32.3 4.7 %copy-start.5 = (bf16[64,1536]{1,0:T(8,128)(2,1)S(1)}, bf16[64,1536]{1,0:T(8,128)(2,1)}, u32[]{:S(2)}) copy-start(bf16[64,1536]{1,0:T(8,128)(2,1)} %get-tuple-element.66) | copy-start | bytes 589828
  46.0 23.0 %copy-start.3 = (bf16[8,160,128]{2,1,0:T(8,128)(2,1)}, bf16[8,160,128]{2,1,0:T(8,128)(2,1)S(1)}, u32[]{:S(2)}) copy-start(bf16[8,160,128]{2,1,0:T(8,128)(2,1)S(1)} %all-to-all-done.refs_0_) | copy-start | bytes 983044
  47.9 72.9 %all-gather.5.cloned.1.call-start = ((), (), s32[]{:S(2)}) async-start(), calls=%async_computation.6 | async-start | bytes 1966080 | tf_op jit(solution)/shard_map/all_gather | solution.py:563
  48.0 10.2 %collective-permute-start.3 = (bf16[8,160,128]{2,1,0:T(8,128)(2,1)S(1)}, bf16[8,160,128]{2,1,0:T(8,128)(2,1)}, u32[]{:S(2)}, u32[]{:S(2)}) collective-permute-start(bf16[8,160,128]{2,1,0:T(8,128)(2,1)S(1)} %all-to-all-done.refs_0_), channel_id=1, source_target_pairs={{0,8},{8,16},{16,24},{24,0},{1,9},{9,17},{17,25},{25,1},{2,10},{10... | collective-permute-start | bytes 983048 | tf_op jit(solution)/shard_map/ppermute | solution.py:37
  48.1 11.1 %collective-permute-start.4 = (bf16[8,160,128]{2,1,0:T(8,128)(2,1)S(1)}, bf16[8,160,128]{2,1,0:T(8,128)(2,1)}, u32[]{:S(2)}, u32[]{:S(2)}) collective-permute-start(bf16[8,160,128]{2,1,0:T(8,128)(2,1)S(1)} %all-to-all-done.refs_0_), channel_id=1, source_target_pairs={{0,24},{8,0},{16,8},{24,16},{1,25},{9,1},{17,9},{25,17},{2,26},{10... | collective-permute-start | bytes 983048 | tf_op jit(solution)/shard_map/ppermute | solution.py:37
  50.7 17.4 %collective-permute-start.7 = (bf16[8,160,128]{2,1,0:T(8,128)(2,1)S(1)}, bf16[8,160,128]{2,1,0:T(8,128)(2,1)}, u32[]{:S(2)}, u32[]{:S(2)}) collective-permute-start(bf16[8,160,128]{2,1,0:T(8,128)(2,1)S(1)} %all-to-all-done.refs_0_), channel_id=1, source_target_pairs={{0,4},{4,0},{1,5},{5,1},{2,6},{6,2},{3,7},{7,3},{8,12},{12,8},{9,1... | collective-permute-start | bytes 983048 | tf_op jit(solution)/shard_map/ppermute | solution.py:32
  59.1 5.9 %collective-permute-start.5 = (bf16[4,160,128]{2,1,0:T(8,128)(2,1)S(1)}, bf16[4,160,128]{2,1,0:T(8,128)(2,1)}, u32[]{:S(2)}, u32[]{:S(2)}) collective-permute-start(bf16[4,160,128]{2,1,0:T(8,128)(2,1)S(1)} %slice.24), channel_id=1, source_target_pairs={{0,8},{8,16},{16,24},{24,0},{1,9},{9,17},{17,25},{25,1},{2,10},{10... | collective-permute-start | bytes 491528 | tf_op jit(solution)/shard_map/ppermute | solution.py:37
  60.2 7.0 %collective-permute-start.6 = (bf16[4,160,128]{2,1,0:T(8,128)(2,1)S(1)}, bf16[4,160,128]{2,1,0:T(8,128)(2,1)}, u32[]{:S(2)}, u32[]{:S(2)}) collective-permute-start(bf16[4,160,128]{2,1,0:T(8,128)(2,1)S(1)} %slice.25), channel_id=1, source_target_pairs={{0,24},{8,0},{16,8},{24,16},{1,25},{9,1},{17,9},{25,17},{2,26},{10... | collective-permute-start | bytes 491528 | tf_op jit(solution)/shard_map/ppermute | solution.py:37
  62.9 6.1 %collective-permute-start.8 = (bf16[8,160,128]{2,1,0:T(8,128)(2,1)}, bf16[8,160,128]{2,1,0:T(8,128)(2,1)}, u32[]{:S(2)}, u32[]{:S(2)}) collective-permute-start(bf16[8,160,128]{2,1,0:T(8,128)(2,1)} %collective-permute-done.3.refs_1_), channel_id=1, source_target_pairs={{0,4},{4,0},{1,5},{5,1},{2,6},{6,2},{3,7},{7,3},{8,12},{12,8},{9,1... | collective-permute-start | bytes 983048 | tf_op jit(solution)/shard_map/ppermute | solution.py:32
  64.8 4.2 %collective-permute-start.9 = (bf16[8,160,128]{2,1,0:T(8,128)(2,1)}, bf16[8,160,128]{2,1,0:T(8,128)(2,1)}, u32[]{:S(2)}, u32[]{:S(2)}) collective-permute-start(bf16[8,160,128]{2,1,0:T(8,128)(2,1)} %collective-permute-done.4.refs_2_), channel_id=1, source_target_pairs={{0,4},{4,0},{1,5},{5,1},{2,6},{6,2},{3,7},{7,3},{8,12},{12,8},{9,1... | collective-permute-start | bytes 983048 | tf_op jit(solution)/shard_map/ppermute | solution.py:32
  65.0 3.5 %collective-permute-start.10 = (bf16[4,160,128]{2,1,0:T(8,128)(2,1)}, bf16[4,160,128]{2,1,0:T(8,128)(2,1)}, u32[]{:S(2)}, u32[]{:S(2)}) collective-permute-start(bf16[4,160,128]{2,1,0:T(8,128)(2,1)} %collective-permute-done.5.refs_3_), channel_id=1, source_target_pairs={{0,4},{4,0},{1,5},{5,1},{2,6},{6,2},{3,7},{7,3},{8,12},{12,8},{9,1... | collective-permute-start | bytes 491528 | tf_op jit(solution)/shard_map/ppermute | solution.py:32
  67.1 1.8 collective-permute-start.11
  80.8 5.3 %collective-permute-start.12 = (bf16[4,8,160,128]{3,2,1,0:T(8,128)(2,1)}, bf16[4,8,160,128]{3,2,1,0:T(8,128)(2,1)}, u32[]{:S(2)}, u32[]{:S(2)}) collective-permute-start(bf16[4,8,160,128]{3,2,1,0:T(8,128)(2,1)} %get-tuple-element.74), channel_id=1, source_target_pairs={{0,4},{4,0},{1,5},{5,1},{2,6},{6,2},{3,7},{7,3},{8,12},{12,8},{9,1... | collective-permute-start | bytes 3932168 | tf_op jit(solution)/shard_map/ppermute | solution.py:32
  81.3 3.2 %collective-permute-start.13 = (bf16[64,1536]{1,0:T(8,128)(2,1)}, bf16[64,1536]{1,0:T(8,128)(2,1)S(1)}, u32[]{:S(2)}, u32[]{:S(2)}) collective-permute-start(bf16[64,1536]{1,0:T(8,128)(2,1)} %get-tuple-element.84), channel_id=1, source_target_pairs={{0,4},{4,0},{1,5},{5,1},{2,6},{6,2},{3,7},{7,3},{8,12},{12,8},{9,1... | collective-permute-start | bytes 589832 | tf_op jit(solution)/shard_map/ppermute | solution.py:32
  86.2 11.8 %copy-start.1 = (f32[64,1536]{1,0:T(8,128)S(1)}, f32[64,1536]{1,0:T(8,128)}, u32[]{:S(2)}) copy-start(f32[64,1536]{1,0:T(8,128)} %get-tuple-element.77.pooled_ref) | copy-start | bytes 1179652
  89.4 22.3 %all-to-all-start.1 = ((bf16[4,8,160,128]{3,2,1,0:T(8,128)(2,1)}), bf16[4,8,160,128]{3,2,1,0:T(8,128)(2,1)}, u32[]{:S(2)}, u32[]{:S(2)}) async-start(bf16[4,8,160,128]{3,2,1,0:T(8,128)(2,1)} %add_convert_fusion), calls=%async_computation.1 | async-start | bytes 2621440 | tf_op jit(solution)/shard_map/all_to_all | solution.py:41
  113.9 14.5 %all-to-all-start.2 = ((bf16[8,160,128]{2,1,0:T(8,128)(2,1)}), bf16[8,160,128]{2,1,0:T(8,128)(2,1)S(1)}, u32[]{:S(2)}, u32[]{:S(2)}) async-start(bf16[8,160,128]{2,1,0:T(8,128)(2,1)} %shard_map.163), calls=%async_computation.2 | async-start | bytes 655360 | tf_op jit(solution)/shard_map/all_to_all | solution.py:41
  128.4 0.7 copy-start.2
  133.1 24.9 %all-to-all-start.3 = ((bf16[8,208,128]{2,1,0:T(8,128)(2,1)}), bf16[8,208,128]{2,1,0:T(8,128)(2,1)}, u32[]{:S(2)}, u32[]{:S(2)}) async-start(bf16[8,208,128]{2,1,0:T(8,128)(2,1)} %get-tuple-element.92), calls=%async_computation.3 | async-start | bytes 851968 | tf_op jit(solution)/shard_map/all_to_all | solution.py:41
  140.5 28.1 %collective-permute-start.19 = (bf16[1152,128]{1,0:T(8,128)(2,1)}, bf16[1152,128]{1,0:T(8,128)(2,1)S(1)}, u32[]{:S(2)}, u32[]{:S(2)}) collective-permute-start(bf16[1152,128]{1,0:T(8,128)(2,1)} %get-tuple-element.105), channel_id=1, source_target_pairs={{0,8},{8,16},{16,24},{24,0},{1,9},{9,17},{17,25},{25,1},{2,10},{10... | collective-permute-start | bytes 884744 | tf_op jit(solution)/shard_map/ppermute | solution.py:37
  141.6 27.1 %collective-permute-start.20 = (bf16[1152,128]{1,0:T(8,128)(2,1)}, bf16[1152,128]{1,0:T(8,128)(2,1)}, u32[]{:S(2)}, u32[]{:S(2)}) collective-permute-start(bf16[1152,128]{1,0:T(8,128)(2,1)} %get-tuple-element.106), channel_id=1, source_target_pairs={{0,16},{8,24},{16,0},{24,8},{1,17},{9,25},{17,1},{25,9},{2,18},{10... | collective-permute-start | bytes 884744 | tf_op jit(solution)/shard_map/ppermute | solution.py:37
  142.6 26.1 %collective-permute-start.21 = (bf16[1152,128]{1,0:T(8,128)(2,1)}, bf16[1152,128]{1,0:T(8,128)(2,1)}, u32[]{:S(2)}, u32[]{:S(2)}) collective-permute-start(bf16[1152,128]{1,0:T(8,128)(2,1)} %get-tuple-element.107), channel_id=1, source_target_pairs={{0,24},{8,0},{16,8},{24,16},{1,25},{9,1},{17,9},{25,17},{2,26},{10... | collective-permute-start | bytes 884744 | tf_op jit(solution)/shard_map/ppermute | solution.py:37
  144.0 10.7 %collective-permute-start.14 = (bf16[1,1536]{1,0:T(2,128)(2,1)}, bf16[1,1536]{1,0:T(2,128)(2,1)S(1)}, u32[]{:S(2)}, u32[]{:S(2)}) collective-permute-start(bf16[1,1536]{1,0:T(2,128)(2,1)} %get-tuple-element.93), channel_id=1, source_target_pairs={{0,4},{4,8},{8,12},{12,16},{16,20},{20,24},{24,28},{28,32},{32,36}... | collective-permute-start | bytes 9224 | tf_op jit(solution)/shard_map/ppermute | solution.py:603
  146.7 11.3 %collective-permute-start.15 = (bf16[1,1536]{1,0:T(2,128)(2,1)}, bf16[1,1536]{1,0:T(2,128)(2,1)S(1)}, u32[]{:S(2)}, u32[]{:S(2)}) collective-permute-start(bf16[1,1536]{1,0:T(2,128)(2,1)} %get-tuple-element.94), channel_id=1, source_target_pairs={{4,0},{8,4},{12,8},{16,12},{20,16},{24,20},{28,24},{32,28},{36,32}... | collective-permute-start | bytes 9224 | tf_op jit(solution)/shard_map/ppermute | solution.py:603
  154.7 10.5 %copy-start.11 = (bf16[1,1536]{1,0:T(2,128)(2,1)}, bf16[1,1536]{1,0:T(2,128)(2,1)S(1)}, u32[]{:S(2)}) copy-start(bf16[1,1536]{1,0:T(2,128)(2,1)S(1)} %collective-permute-done.14.before_ref) | copy-start | bytes 9220
  158.0 7.2 %copy-start.12 = (bf16[1,1536]{1,0:T(2,128)(2,1)}, bf16[1,1536]{1,0:T(2,128)(2,1)S(1)}, u32[]{:S(2)}) copy-start(bf16[1,1536]{1,0:T(2,128)(2,1)S(1)} %collective-permute-done.15.after_ref) | copy-start | bytes 9220
  160.3 4.9 %collective-permute-start.16 = (bf16[288,128]{1,0:T(8,128)(2,1)}, bf16[288,128]{1,0:T(8,128)(2,1)S(1)}, u32[]{:S(2)}, u32[]{:S(2)}) collective-permute-start(bf16[288,128]{1,0:T(8,128)(2,1)} %get-tuple-element.97), channel_id=1, source_target_pairs={{0,8},{8,16},{16,24},{24,0},{1,9},{9,17},{17,25},{25,1},{2,10},{10... | collective-permute-start | bytes 221192 | tf_op jit(solution)/shard_map/ppermute | solution.py:37
  161.0 7.5 %collective-permute-start.17 = (bf16[288,128]{1,0:T(8,128)(2,1)}, bf16[288,128]{1,0:T(8,128)(2,1)S(1)}, u32[]{:S(2)}, u32[]{:S(2)}) collective-permute-start(bf16[288,128]{1,0:T(8,128)(2,1)} %get-tuple-element.98), channel_id=1, source_target_pairs={{0,16},{8,24},{16,0},{24,8},{1,17},{9,25},{17,1},{25,9},{2,18},{10... | collective-permute-start | bytes 221192 | tf_op jit(solution)/shard_map/ppermute | solution.py:37
  165.2 3.4 %copy-start.6 = (bf16[288,128]{1,0:T(8,128)(2,1)}, bf16[288,128]{1,0:T(8,128)(2,1)S(1)}, u32[]{:S(2)}) copy-start(bf16[288,128]{1,0:T(8,128)(2,1)S(1)} %collective-permute-done.16.refs_5_) | copy-start | bytes 221188
  165.2 3.4 %collective-permute-start.18 = (bf16[288,128]{1,0:T(8,128)(2,1)}, bf16[288,128]{1,0:T(8,128)(2,1)S(1)}, u32[]{:S(2)}, u32[]{:S(2)}) collective-permute-start(bf16[288,128]{1,0:T(8,128)(2,1)} %get-tuple-element.99), channel_id=1, source_target_pairs={{0,24},{8,0},{16,8},{24,16},{1,25},{9,1},{17,9},{25,17},{2,26},{10... | collective-permute-start | bytes 221192 | tf_op jit(solution)/shard_map/ppermute | solution.py:37
  168.6 0.6 copy-start.7
  168.6 0.6 copy-start.8
  168.6 0.7 copy-start.4
Sparse Core Ops, SparseCore 0:
  48.1 24.8 all-gather.2
  86.3 25.5 all-gather.4

commit v7 on v6

--- a/solution.py
+++ b/solution.py
@@ -586,6 +586,7 @@
         4 * keep * width * nx * nc * pool,
         first, target, early, later,
     )
+    grad_queries, left = lax.optimization_barrier((grad_queries, left))
     part = contract_cols(grad_queries, query_weight)
     sums = [sums[0]] + [shift(sums[i], "y", i) for i in range(1, ny)]
     gkv, left, part = lax.optimization_barrier((gkv, left, part))
@@ -601,7 +602,8 @@
         gkv, part, key_weight, value_weight, pooled, gain_attn, grad_y, pairs, spread,
     )
     before, after = lax.ppermute(bottom, seq, up), lax.ppermute(top, seq, down)
-    got, before, after = lax.optimization_barrier((exchange(gkv, ("x", "core")), before, after))
+    gkv, *sums[1::2] = lax.optimization_barrier((gkv, *sums[1::2]))
+    got = exchange(gkv, ("x", "core"))
     (input_grad,) = call(
         input_kernel,
         (shape(fine, width),),
@@ -618,7 +620,6 @@
         left, got,
     )
     late = [late[0]] + [shift(late[i], "y", i) for i in range(1, ny)]
-    late, input_grad = lax.optimization_barrier((late, input_grad))
     (sums,) = flagged(
         functools.partial(turn_kernel, ny, q_cols),
         (shape(nz * nc, (tiles * each + extra + 15) // 16 * 16, qk),),
@@ -626,7 +627,7 @@
         0,
         first, *sums, *late,
     )
-    got = exchange(sums, ("z", "core"))
+    got, input_grad = lax.optimization_barrier((exchange(sums, ("z", "core")), input_grad))
     results = call(
         functools.partial(last_kernel, tiles),
         tuple(shape(*dims, dtype=F32) for dims in (

time: 203 us -> 197 us (0.970)
  blocking collectives: 21.8 us -> 0 us
  starting transfers between devices: 53.8 us -> 71.5 us
    all_to_all x1 -> x0, blocking collectives: 21.8 us -> none  [exchange(): return lax.all_to_all(blocks, axis, 0, 0, tiled=True)]
    ppermute x8, starting transfers between devices: 6.11 us -> 13.3 us  [swap(): return lax.ppermute(block, 'core', [(0, 1), (1, 0)])]
    ppermute x1, waiting for transfers between devices: 6.06 us -> 0.01 us  [shards(): lax.ppermute(bottom, seq, up)]
    all_to_all x4 -> x5, waiting for transfers between devices: 20 us -> 25.7 us  [exchange(): return lax.all_to_all(blocks, axis, 0, 0, tiled=True)]
    all_to_all x4 -> x5, starting transfers between devices: 25.9 us -> 31.4 us  [exchange(): return lax.all_to_all(blocks, axis, 0, 0, tiled=True)]
    ppermute x10, starting transfers between devices: 10.4 us -> 15.2 us  [shift(): lax.ppermute(block, axis, [(i, (i + step) % count) for i in range(count)])]
    ppermute x1, starting transfers between devices: 1.92 us -> 5.28 us  [shards(): high = lax.ppermute(x[:2], seq, down)]
    ppermute x1, waiting for transfers between devices: 2.99 us -> 0.01 us  [shards(): high = lax.ppermute(x[:2], seq, down)]
  transfers between devices with their start and end apart: 28 -> 29, of which waited for: 13 -> 13; matrix products, arithmetic and copies ran while one was open for 10% -> 10% of each run, Pallas kernels for 14% -> 16%
where the time goes in v7:
time: 197 us; the launch traced here: 196 us
  starting transfers between devices  71.5 us (36%)
  waiting for transfers between devices  44.9 us (23%)
  Pallas kernels  39.8 us (20%)
  between operations  14.3 us (7%)
  matrix products  11.9 us (6%)
  other arithmetic  8.15 us (4%)
  local copies, waits for them, and re-layouts  5.37 us (3%)
    all_to_all x5, starting transfers between devices, exchange(): return lax.all_to_all(blocks, axis, 0, 0, tiled=True)  31.4 us
    all_to_all x5, waiting for transfers between devices, exchange(): return lax.all_to_all(blocks, axis, 0, 0, tiled=True)  25.7 us
    pallas_call x6, Pallas kernels, call(): pl.pallas_call(kernel, out_shape=out_shape, scratch_shapes=scratch, compi...  17.3 us
    ppermute x10, starting transfers between devices, shift(): lax.ppermute(block, axis, [(i, (i + step) % count) for i in range(count)])  15.2 us
    ppermute x8, starting transfers between devices, swap(): return lax.ppermute(block, 'core', [(0, 1), (1, 0)])  13.3 us
    pallas_call x1, Pallas kernels, attention(): pl.pallas_call(functools.partial(attention_kernel, scale, heads, group, u...  11.8 us
    ppermute x10, waiting for transfers between devices, shift(): lax.ppermute(block, axis, [(i, (i + step) % count) for i in range(count)])  11.3 us
    pallas_call x3, Pallas kernels, flagged(): pl.pallas_call(kernel, out_shape=out_shape, in_specs=[smem] + [vmem] * le...  10.8 us
  transfers between devices with their start and end apart: 29, of which 13 were waited for; matrix products, arithmetic and copies ran while one was open for 10% of the time, Pallas kernels for 16%

profile of v7, /device:TPU:1, one launch (start us, length us, event | category | flops | bytes accessed | tf_op | source)
XLA Modules:
  0.0 195.9 jit_solution(3215716614754904300)
XLA Ops:
  7.2 0.9 slice_bitcast_fusion
  8.1 5.3 %collective-permute-start.1 = (bf16[2,1536]{1,0:T(2,128)(2,1)S(1)}, bf16[2,1536]{1,0:T(2,128)(2,1)S(1)}, u32[]{:S(2)}, u32[]{:S(2)}) collective-permute-start(bf16[2,1536]{1,0:T(2,128)(2,1)S(1)} %get-tuple-element.117), channel_id=1, source_target_pairs={{4,0},{8,4},{12,8},{16,12},{20,16},{24,20},{28,24},{32,28},{36,32}... | collective-permute-start | bytes 18440 | tf_op jit(solution)/shard_map/ppermute | solution.py:511
  13.4 1.9 collective-permute-start
  15.4 1.1 collective-permute-done.low_ref
  16.5 0.6 copy-done.11
  17.1 3.5 %shard_map.160 = (bf16[8,160,128]{2,1,0:T(8,128)(2,1)}, bf16[64,1536]{1,0:T(8,128)(2,1)}, f32[64,1536]{1,0:T(8,128)}, bf16[64,1536]{1,0:T(8,128)(2,1)}, bf16[64,1536]{1,0:T(8,128)(2,1)}) custom-call(s32[1]{0:T(128)} %bitcast.1.first_ref, bf16[128,1536]{1,0:T(8,128)(2,1)} %bitcast.19, bf16[2,1536]{1,0:T(2,128)(2,1)} %copy-done.11, ...), custom_call_target="tpu_custom_call" | custom-call | flops 62914560 | bytes 9437184 | tf_op jit(solution)/shard_map/pallas_call | solution.py:516
  20.5 8.4 %all-to-all-start = ((bf16[8,160,128]{2,1,0:T(8,128)(2,1)}), bf16[8,160,128]{2,1,0:T(8,128)(2,1)S(1)}, u32[]{:S(2)}, u32[]{:S(2)}) async-start(bf16[8,160,128]{2,1,0:T(8,128)(2,1)} %get-tuple-element.63), calls=%async_computation | async-start | bytes 655360 | tf_op jit(solution)/shard_map/all_to_all | solution.py:41
  29.0 5.6 %collective-permute-start.2 = (bf16[64,1536]{1,0:T(8,128)(2,1)}, bf16[64,1536]{1,0:T(8,128)(2,1)}, u32[]{:S(2)}, u32[]{:S(2)}) collective-permute-start(bf16[64,1536]{1,0:T(8,128)(2,1)} %get-tuple-element.68), channel_id=1, source_target_pairs={{0,4},{4,0},{1,5},{5,1},{2,6},{6,2},{3,7},{7,3},{8,12},{12,8},{9,1... | collective-permute-start | bytes 589832 | tf_op jit(solution)/shard_map/ppermute | solution.py:32
  34.6 4.7 %convolution_convert_fusion.g_ref = bf16[64,1536]{1,0:T(8,128)(2,1)} fusion(bf16[64,1536]{1,0:T(8,128)(2,1)} %bitcast.25, bf16[1536,1536]{1,0:T(8,128)(2,1)} %param.16), kind=kOutput, calls=%fused_computation.3 | convolution fusion | flops 302088192 | bytes 5111808 | tf_op jit(solution)/shard_map/dot_general | solution.py:24
  39.3 1.3 convolution_convert_fusion.1.q_ref
  40.6 1.9 pad_maximum_fusion
  42.6 5.8 %collective-permute-start.4 = (bf16[8,160,128]{2,1,0:T(8,128)(2,1)S(1)}, bf16[8,160,128]{2,1,0:T(8,128)(2,1)}, u32[]{:S(2)}, u32[]{:S(2)}) collective-permute-start(bf16[8,160,128]{2,1,0:T(8,128)(2,1)S(1)} %all-to-all-done.refs_0_), channel_id=1, source_target_pairs={{0,24},{8,0},{16,8},{24,16},{1,25},{9,1},{17,9},{25,17},{2,26},{10... | collective-permute-start | bytes 983048 | tf_op jit(solution)/shard_map/ppermute | solution.py:37
  48.4 1.3 collective-permute-start.7
  49.8 5.4 %collective-permute-done.4.refs_2_ = bf16[8,160,128]{2,1,0:T(8,128)(2,1)} collective-permute-done((bf16[8,160,128]{2,1,0:T(8,128)(2,1)S(1)}, bf16[8,160,128]{2,1,0:T(8,128)(2,1)}, u32[]{:S(2)}, u32[]{:S(2)}) %collective-permute-start.4) | collective-permute-done | bytes 327712 | tf_op jit(solution)/shard_map/ppermute | solution.py:37
  55.1 0.9 slice.25
  56.1 3.6 %collective-permute-start.6 = (bf16[4,160,128]{2,1,0:T(8,128)(2,1)S(1)}, bf16[4,160,128]{2,1,0:T(8,128)(2,1)}, u32[]{:S(2)}, u32[]{:S(2)}) collective-permute-start(bf16[4,160,128]{2,1,0:T(8,128)(2,1)S(1)} %slice.25), channel_id=1, source_target_pairs={{0,24},{8,0},{16,8},{24,16},{1,25},{9,1},{17,9},{25,17},{2,26},{10... | collective-permute-start | bytes 491528 | tf_op jit(solution)/shard_map/ppermute | solution.py:37
  59.7 0.9 slice.24
  60.7 1.6 collective-permute-start.9
  62.4 1.7 collective-permute-start.11
  64.1 2.4 %collective-permute-done.5.refs_3_ = bf16[4,160,128]{2,1,0:T(8,128)(2,1)} collective-permute-done((bf16[4,160,128]{2,1,0:T(8,128)(2,1)S(1)}, bf16[4,160,128]{2,1,0:T(8,128)(2,1)}, u32[]{:S(2)}, u32[]{:S(2)}) %collective-permute-start.5) | collective-permute-done | bytes 163872 | tf_op jit(solution)/shard_map/ppermute | solution.py:37
  66.4 2.4 %collective-permute-start.10 = (bf16[4,160,128]{2,1,0:T(8,128)(2,1)}, bf16[4,160,128]{2,1,0:T(8,128)(2,1)}, u32[]{:S(2)}, u32[]{:S(2)}) collective-permute-start(bf16[4,160,128]{2,1,0:T(8,128)(2,1)} %collective-permute-done.5.refs_3_), channel_id=1, source_target_pairs={{0,4},{4,0},{1,5},{5,1},{2,6},{6,2},{3,7},{7,3},{8,12},{12,8},{9,1... | collective-permute-start | bytes 491528 | tf_op jit(solution)/shard_map/ppermute | solution.py:32
  68.8 0.6 pad_add_fusion.place_ref
  69.4 0.8 collective-permute-done.10.refs_8_
  70.2 11.8 %shard_map.161 = (bf16[64,1536]{1,0:T(8,128)(2,1)}, bf16[64,1024]{1,0:T(8,128)(2,1)}, bf16[64,1536]{1,0:T(8,128)(2,1)}, bf16[64,1536]{1,0:T(8,128)(2,1)}, bf16[4...) custom-call(s32[2]{0:T(128)} %pad_add_fusion.place_ref, bf16[64,1024]{1,0:T(8,128)(2,1)} %convolution_convert_fusion.1.q_ref, ...), custom_call_target="tpu_custom_call" | custom-call | flops 4026531840 | bytes 5242880 | tf_op jit(solution)/shard_map/pallas_call | solution.py:264
  82.0 0.4 collective-permute-start.12
  82.4 0.2 collective-permute-start.13
  82.6 3.0 %collective-permute-done.13 = bf16[64,1536]{1,0:T(8,128)(2,1)S(1)} collective-permute-done((bf16[64,1536]{1,0:T(8,128)(2,1)}, bf16[64,1536]{1,0:T(8,128)(2,1)S(1)}, u32[]{:S(2)}, u32[]{:S(2)}) %collective-permute-start.13) | collective-permute-done | bytes 196640 | tf_op jit(solution)/shard_map/ppermute | solution.py:32
  85.6 1.7 pad_maximum_fusion.1
  87.3 3.2 %add_convert_fusion = bf16[4,8,160,128]{3,2,1,0:T(8,128)(2,1)} fusion(bf16[4,8,160,128]{3,2,1,0:T(8,128)(2,1)} %collective-permute-done.12, bf16[4,8,160,128]{3,2,1,0:T(8,128)(2,1)} %get-tuple-element.72), kind=kLoop, calls=%fused_computation | loop fusion | flops 2621440 | bytes 3932160 | tf_op jit(solution)/shard_map/convert_element_type | solution.py:565
  90.5 4.3 %all-to-all-start.1 = ((bf16[4,8,160,128]{3,2,1,0:T(8,128)(2,1)}), bf16[4,8,160,128]{3,2,1,0:T(8,128)(2,1)}, u32[]{:S(2)}, u32[]{:S(2)}) async-start(bf16[4,8,160,128]{3,2,1,0:T(8,128)(2,1)} %add_convert_fusion), calls=%async_computation.1 | async-start | bytes 2621440 | tf_op jit(solution)/shard_map/all_to_all | solution.py:41
  94.9 3.7 %shard_map.162 = (f32[5,64,1536]{2,1,0:T(8,128)}, f32[64,1536]{1,0:T(8,128)}) custom-call(bf16[128,1536]{1,0:T(8,128)(2,1)} %bitcast.20, bf16[2,1536]{1,0:T(2,128)(2,1)} %copy-done.11, bf16[2,1536]{1,0:T(2,128)(2,1)} %copy-done.10, f32[1536]{0:T(1024)} %gain_ref.3, f32[5,1536]{1,0:T(8,128)} %taps_ref.5), custom_call_target="tpu_custom_call" | custom-call | flops 7864320 | bytes 2801664 | tf_op jit(solution)/shard_map/pallas_call | solution.py:47
  98.6 4.1 %fusion = bf16[64,1536]{1,0:T(8,128)(2,1)} fusion(f32[64,1536]{1,0:T(8,128)S(1)} %copy-done.1, bf16[64,1536]{1,0:T(8,128)(2,1)} %get-tuple-element.77, bf16[1536,1536]{1,0:T(8,128)(2,1)} %param.16), kind=kOutput, calls=%fused_computation.2 | convolution fusion | flops 302186496 | bytes 5505024 | tf_op jit(solution)/shard_map/dot_general | solution.py:28
  102.7 9.9 %all-to-all-done.1.parts_ref = bf16[4,8,160,128]{3,2,1,0:T(8,128)(2,1)} async-done(((bf16[4,8,160,128]{3,2,1,0:T(8,128)(2,1)}), bf16[4,8,160,128]{3,2,1,0:T(8,128)(2,1)}, u32[]{:S(2)}, u32[]{:S(2)}) %all-to-all-start.1) | async-done | bytes 1310752 | tf_op jit(solution)/shard_map/all_to_all | solution.py:41
  112.6 2.2 %shard_map.164 = bf16[8,160,128]{2,1,0:T(8,128)(2,1)} custom-call(bf16[4,8,160,128]{3,2,1,0:T(8,128)(2,1)} %all-to-all-done.1.parts_ref), custom_call_target="tpu_custom_call" | custom-call | bytes 1638400 | tf_op jit(solution)/shard_map/pallas_call | solution.py:47
  114.8 3.4 %all-to-all-start.2 = ((bf16[8,160,128]{2,1,0:T(8,128)(2,1)}), bf16[8,160,128]{2,1,0:T(8,128)(2,1)S(1)}, u32[]{:S(2)}, u32[]{:S(2)}) async-start(bf16[8,160,128]{2,1,0:T(8,128)(2,1)} %shard_map.164), calls=%async_computation.2 | async-start | bytes 655360 | tf_op jit(solution)/shard_map/all_to_all | solution.py:41
  118.3 0.7 compare_select_fusion.8.target_ref
  119.0 4.9 %shard_map.163 = (bf16[384,512]{1,0:T(8,128)(2,1)}, bf16[1152,128]{1,0:T(8,128)(2,1)}, bf16[1152,128]{1,0:T(8,128)(2,1)}, bf16[1152,128]{1,0:T(8,128)(2,1)}, bf16[1152,128]{1,0:T(8,128)(2,1)}) custom-call(s32[1]{0:T(128)} %bitcast.1.first_ref, s32[1,1536]{1,0:T(1,128)} %compare_select_fusion.8.target_ref, ...), custom_call_target="tpu_custom_call" | custom-call | flops 1207959552 | bytes 9437184 | tf_op jit(solution)/shard_map/pallas_call | solution.py:516
  123.9 0.3 collective-permute-start.14
  124.2 2.4 %collective-permute-start.15 = (bf16[1152,128]{1,0:T(8,128)(2,1)}, bf16[1152,128]{1,0:T(8,128)(2,1)}, u32[]{:S(2)}, u32[]{:S(2)}) collective-permute-start(bf16[1152,128]{1,0:T(8,128)(2,1)} %get-tuple-element.95), channel_id=1, source_target_pairs={{0,24},{8,0},{16,8},{24,16},{1,25},{9,1},{17,9},{25,17},{2,26},{10... | collective-permute-start | bytes 884744 | tf_op jit(solution)/shard_map/ppermute | solution.py:37
  126.5 1.8 fusion.14.part_ref
  128.4 1.4 all-to-all-done.2.parts_ref
  129.8 0.7 copy-done.2
  130.5 4.0 %shard_map.165 = (bf16[64,1536]{1,0:T(8,128)(2,1)}, bf16[1,1536]{1,0:T(2,128)(2,1)}, bf16[1,1536]{1,0:T(2,128)(2,1)}, bf16[8,208,128]{2,1,0:T(8,128)(2,1)}) custom-call(bf16[8,160,128]{2,1,0:T(8,128)(2,1)} %copy-done.2, f32[64,1536]{1,0:T(8,128)} %fusion.14.part_ref, bf16[1536,128]{1,0:T(8,128)(2,1)} %kw_ref.3, bf16[192,1536]{1,0:T(8,128)(2,1)} %bitcast.23, ...), custom_call_target="tpu_custom_call" | custom-call | flops 62914560 | bytes 5287936 | tf_op jit(solution)/shard_map/pallas_call | solution.py:47
  134.5 7.1 %all-to-all-start.3 = ((bf16[8,208,128]{2,1,0:T(8,128)(2,1)}), bf16[8,208,128]{2,1,0:T(8,128)(2,1)}, u32[]{:S(2)}, u32[]{:S(2)}) async-start(bf16[8,208,128]{2,1,0:T(8,128)(2,1)} %get-tuple-element.100), calls=%async_computation.3 | async-start | bytes 851968 | tf_op jit(solution)/shard_map/all_to_all | solution.py:41
  141.6 0.4 collective-permute-start.16
  142.0 8.1 %all-to-all-done.3.got_ref = bf16[8,208,128]{2,1,0:T(8,128)(2,1)} async-done(((bf16[8,208,128]{2,1,0:T(8,128)(2,1)}), bf16[8,208,128]{2,1,0:T(8,128)(2,1)}, u32[]{:S(2)}, u32[]{:S(2)}) %all-to-all-start.3) | async-done | bytes 426016 | tf_op jit(solution)/shard_map/all_to_all | solution.py:41
  150.2 2.3 %shard_map.166 = (bf16[288,128]{1,0:T(8,128)(2,1)}, bf16[288,128]{1,0:T(8,128)(2,1)}, bf16[288,128]{1,0:T(8,128)(2,1)}, bf16[288,128]{1,0:T(8,128)(2,1)}) custom-call(bf16[384,512]{1,0:T(8,128)(2,1)} %get-tuple-element.99.left_ref, bf16[8,208,128]{2,1,0:T(8,128)(2,1)} %all-to-all-done.3.got_ref), custom_call_target="tpu_custom_call" | custom-call | flops 125829120 | bytes 1114112 | tf_op jit(solution)/shard_map/pallas_call | solution.py:47
  152.4 0.3 collective-permute-start.17
  152.7 1.8 collective-permute-start.18
  154.5 0.6 collective-permute-start.19
  155.1 2.3 %collective-permute-done.17.refs_5_ = bf16[288,128]{1,0:T(8,128)(2,1)S(1)} collective-permute-done((bf16[288,128]{1,0:T(8,128)(2,1)}, bf16[288,128]{1,0:T(8,128)(2,1)S(1)}, u32[]{:S(2)}, u32[]{:S(2)}) %collective-permute-start.17) | collective-permute-done | bytes 73760 | tf_op jit(solution)/shard_map/ppermute | solution.py:37
  157.4 0.9 collective-permute-done.18.refs_6_
  158.3 0.4 collective-permute-done.19.refs_7_
  158.7 0.2 copy-done.8
  158.9 0.4 copy-done.9
  159.4 2.5 %shard_map.167 = bf16[16,128,128]{2,1,0:T(8,128)(2,1)} custom-call(s32[1]{0:T(128)} %bitcast.1.first_ref, bf16[1152,128]{1,0:T(8,128)(2,1)} %get-tuple-element.83.refs_0_, bf16[1152,128]{1,0:T(8,128)(2,1)} %collective-permute-done.14.refs_1_, bf16[1152,128]{1,0:T(8,128)(2,1)} %copy-done.4, bf16[1152,128]{1,0:T(8,128)(2,1)} %collective-permute-done.15.refs_3_, ...), custom_call_target="tpu_custom_call" | custom-call | bytes 9437184 | tf_op jit(solution)/shard_map/pallas_call | solution.py:516
  161.8 8.1 %all-to-all-start.4 = ((bf16[16,128,128]{2,1,0:T(8,128)(2,1)}), bf16[16,128,128]{2,1,0:T(8,128)(2,1)}, u32[]{:S(2)}, u32[]{:S(2)}) async-start(bf16[16,128,128]{2,1,0:T(8,128)(2,1)} %shard_map.167), calls=%async_computation.4 | async-start | bytes 1048576 | tf_op jit(solution)/shard_map/all_to_all | solution.py:41
  169.9 1.9 collective-permute-start.20
  171.8 2.4 %collective-permute-start.21 = (bf16[1,1536]{1,0:T(2,128)(2,1)S(1)}, bf16[1,1536]{1,0:T(2,128)(2,1)S(1)}, u32[]{:S(2)}, u32[]{:S(2)}) collective-permute-start(bf16[1,1536]{1,0:T(2,128)(2,1)S(1)} %copy-done.14), channel_id=1, source_target_pairs={{4,0},{8,4},{12,8},{16,12},{20,16},{24,20},{28,24},{32,28},{36,32}... | collective-permute-start | bytes 9224 | tf_op jit(solution)/shard_map/ppermute | solution.py:604
  174.3 2.9 %collective-permute-done.21.after_ref = bf16[1,1536]{1,0:T(2,128)(2,1)S(1)} collective-permute-done((bf16[1,1536]{1,0:T(2,128)(2,1)S(1)}, bf16[1,1536]{1,0:T(2,128)(2,1)S(1)}, u32[]{:S(2)}, u32[]{:S(2)}) %collective-permute-start.21) | collective-permute-done | bytes 3104 | tf_op jit(solution)/shard_map/ppermute | solution.py:604
  177.2 0.6 copy-done.13
  177.8 3.3 %shard_map.168 = bf16[128,1536]{1,0:T(8,128)(2,1)} custom-call(bf16[128,1536]{1,0:T(8,128)(2,1)} %bitcast.21, f32[1536]{0:T(1024)} %gain_ref.3, f32[5,1536]{1,0:T(8,128)} %taps_ref.5, bf16[64,1536]{1,0:T(8,128)(2,1)} %get-tuple-element.105.half_ref, bf16[1,1536]{1,0:T(2,128)(2,1)} %copy-done.12, bf16[1,1536]{1,0:T(2,128)(2,1)} %copy-done.13), custom_call_target="tpu_custom_call" | custom-call | flops 7864320 | bytes 1026048 | tf_op jit(solution)/shard_map/pallas_call | solution.py:47
  181.1 6.2 %all-to-all-done.4.got_ref = bf16[16,128,128]{2,1,0:T(8,128)(2,1)} async-done(((bf16[16,128,128]{2,1,0:T(8,128)(2,1)}), bf16[16,128,128]{2,1,0:T(8,128)(2,1)}, u32[]{:S(2)}, u32[]{:S(2)}) %all-to-all-start.4) | async-done | bytes 524320 | tf_op jit(solution)/shard_map/all_to_all | solution.py:41
  187.3 1.7 shard_map.169
  (50 shorter events, 0.4 us)
Async XLA Ops:
  7.2 32.1 %copy-start = (bf16[1536,1024]{1,0:T(8,128)(2,1)S(1)}, bf16[1536,1024]{1,0:T(8,128)(2,1)}, u32[]{:S(2)}) copy-start(bf16[1536,1024]{1,0:T(8,128)(2,1)} %param.13) | copy-start | bytes 9437188
  8.1 7.2 %collective-permute-start.1 = (bf16[2,1536]{1,0:T(2,128)(2,1)S(1)}, bf16[2,1536]{1,0:T(2,128)(2,1)S(1)}, u32[]{:S(2)}, u32[]{:S(2)}) collective-permute-start(bf16[2,1536]{1,0:T(2,128)(2,1)S(1)} %get-tuple-element.117), channel_id=1, source_target_pairs={{4,0},{8,4},{12,8},{16,12},{20,16},{24,20},{28,24},{32,28},{36,32}... | collective-permute-start | bytes 18440 | tf_op jit(solution)/shard_map/ppermute | solution.py:511
  13.4 3.1 %collective-permute-start = (bf16[2,1536]{1,0:T(2,128)(2,1)S(1)}, bf16[2,1536]{1,0:T(2,128)(2,1)S(1)}, u32[]{:S(2)}, u32[]{:S(2)}) collective-permute-start(bf16[2,1536]{1,0:T(2,128)(2,1)S(1)} %get-tuple-element.118), channel_id=1, source_target_pairs={{0,4},{4,8},{8,12},{12,16},{16,20},{20,24},{24,28},{28,32},{32,36}... | collective-permute-start | bytes 18440 | tf_op jit(solution)/shard_map/ppermute | solution.py:510
  15.4 1.1 copy-start.10
  16.5 0.6 copy-start.11
  20.5 20.1 %all-to-all-start = ((bf16[8,160,128]{2,1,0:T(8,128)(2,1)}), bf16[8,160,128]{2,1,0:T(8,128)(2,1)S(1)}, u32[]{:S(2)}, u32[]{:S(2)}) async-start(bf16[8,160,128]{2,1,0:T(8,128)(2,1)} %get-tuple-element.63), calls=%async_computation | async-start | bytes 655360 | tf_op jit(solution)/shard_map/all_to_all | solution.py:41
  28.9 90.0 %all-gather.3.cloned.1.call-start = ((), (), s32[]{:S(2)}) async-start(), calls=%async_computation.5 | async-start | bytes 1966080 | tf_op jit(solution)/shard_map/all_gather | solution.py:551
  29.0 10.3 %copy-start.5 = (bf16[64,1536]{1,0:T(8,128)(2,1)S(1)}, bf16[64,1536]{1,0:T(8,128)(2,1)}, u32[]{:S(2)}) copy-start(bf16[64,1536]{1,0:T(8,128)(2,1)} %get-tuple-element.65) | copy-start | bytes 589828
  29.0 11.6 %collective-permute-start.2 = (bf16[64,1536]{1,0:T(8,128)(2,1)}, bf16[64,1536]{1,0:T(8,128)(2,1)}, u32[]{:S(2)}, u32[]{:S(2)}) collective-permute-start(bf16[64,1536]{1,0:T(8,128)(2,1)} %get-tuple-element.68), channel_id=1, source_target_pairs={{0,4},{4,0},{1,5},{5,1},{2,6},{6,2},{3,7},{7,3},{8,12},{12,8},{9,1... | collective-permute-start | bytes 589832 | tf_op jit(solution)/shard_map/ppermute | solution.py:32
  40.6 29.6 %copy-start.3 = (bf16[8,160,128]{2,1,0:T(8,128)(2,1)}, bf16[8,160,128]{2,1,0:T(8,128)(2,1)S(1)}, u32[]{:S(2)}) copy-start(bf16[8,160,128]{2,1,0:T(8,128)(2,1)S(1)} %all-to-all-done.refs_0_) | copy-start | bytes 983044
  42.6 76.4 %all-gather.5.cloned.1.call-start = ((), (), s32[]{:S(2)}) async-start(), calls=%async_computation.6 | async-start | bytes 1966080 | tf_op jit(solution)/shard_map/all_gather | solution.py:563
  42.6 12.5 %collective-permute-start.4 = (bf16[8,160,128]{2,1,0:T(8,128)(2,1)S(1)}, bf16[8,160,128]{2,1,0:T(8,128)(2,1)}, u32[]{:S(2)}, u32[]{:S(2)}) collective-permute-start(bf16[8,160,128]{2,1,0:T(8,128)(2,1)S(1)} %all-to-all-done.refs_0_), channel_id=1, source_target_pairs={{0,24},{8,0},{16,8},{24,16},{1,25},{9,1},{17,9},{25,17},{2,26},{10... | collective-permute-start | bytes 983048 | tf_op jit(solution)/shard_map/ppermute | solution.py:37
  48.4 11.2 %collective-permute-start.3 = (bf16[8,160,128]{2,1,0:T(8,128)(2,1)S(1)}, bf16[8,160,128]{2,1,0:T(8,128)(2,1)}, u32[]{:S(2)}, u32[]{:S(2)}) collective-permute-start(bf16[8,160,128]{2,1,0:T(8,128)(2,1)S(1)} %all-to-all-done.refs_0_), channel_id=1, source_target_pairs={{0,8},{8,16},{16,24},{24,0},{1,9},{9,17},{17,25},{25,1},{2,10},{10... | collective-permute-start | bytes 983048 | tf_op jit(solution)/shard_map/ppermute | solution.py:37
  48.4 21.0 %collective-permute-start.7 = (bf16[8,160,128]{2,1,0:T(8,128)(2,1)S(1)}, bf16[8,160,128]{2,1,0:T(8,128)(2,1)}, u32[]{:S(2)}, u32[]{:S(2)}) collective-permute-start(bf16[8,160,128]{2,1,0:T(8,128)(2,1)S(1)} %all-to-all-done.refs_0_), channel_id=1, source_target_pairs={{0,4},{4,0},{1,5},{5,1},{2,6},{6,2},{3,7},{7,3},{8,12},{12,8},{9,1... | collective-permute-start | bytes 983048 | tf_op jit(solution)/shard_map/ppermute | solution.py:32
  56.1 6.3 %collective-permute-start.6 = (bf16[4,160,128]{2,1,0:T(8,128)(2,1)S(1)}, bf16[4,160,128]{2,1,0:T(8,128)(2,1)}, u32[]{:S(2)}, u32[]{:S(2)}) collective-permute-start(bf16[4,160,128]{2,1,0:T(8,128)(2,1)S(1)} %slice.25), channel_id=1, source_target_pairs={{0,24},{8,0},{16,8},{24,16},{1,25},{9,1},{17,9},{25,17},{2,26},{10... | collective-permute-start | bytes 491528 | tf_op jit(solution)/shard_map/ppermute | solution.py:37
  60.6 5.9 %collective-permute-start.5 = (bf16[4,160,128]{2,1,0:T(8,128)(2,1)S(1)}, bf16[4,160,128]{2,1,0:T(8,128)(2,1)}, u32[]{:S(2)}, u32[]{:S(2)}) collective-permute-start(bf16[4,160,128]{2,1,0:T(8,128)(2,1)S(1)} %slice.24), channel_id=1, source_target_pairs={{0,8},{8,16},{16,24},{24,0},{1,9},{9,17},{17,25},{25,1},{2,10},{10... | collective-permute-start | bytes 491528 | tf_op jit(solution)/shard_map/ppermute | solution.py:37
  60.7 8.7 %collective-permute-start.9 = (bf16[8,160,128]{2,1,0:T(8,128)(2,1)}, bf16[8,160,128]{2,1,0:T(8,128)(2,1)}, u32[]{:S(2)}, u32[]{:S(2)}) collective-permute-start(bf16[8,160,128]{2,1,0:T(8,128)(2,1)} %collective-permute-done.4.refs_2_), channel_id=1, source_target_pairs={{0,4},{4,0},{1,5},{5,1},{2,6},{6,2},{3,7},{7,3},{8,12},{12,8},{9,1... | collective-permute-start | bytes 983048 | tf_op jit(solution)/shard_map/ppermute | solution.py:32
  62.3 7.9 %collective-permute-start.8 = (bf16[8,160,128]{2,1,0:T(8,128)(2,1)}, bf16[8,160,128]{2,1,0:T(8,128)(2,1)}, u32[]{:S(2)}, u32[]{:S(2)}) collective-permute-start(bf16[8,160,128]{2,1,0:T(8,128)(2,1)} %collective-permute-done.3.refs_1_), channel_id=1, source_target_pairs={{0,4},{4,0},{1,5},{5,1},{2,6},{6,2},{3,7},{7,3},{8,12},{12,8},{9,1... | collective-permute-start | bytes 983048 | tf_op jit(solution)/shard_map/ppermute | solution.py:32
  62.4 7.0 %collective-permute-start.11 = (bf16[4,160,128]{2,1,0:T(8,128)(2,1)}, bf16[4,160,128]{2,1,0:T(8,128)(2,1)}, u32[]{:S(2)}, u32[]{:S(2)}) collective-permute-start(bf16[4,160,128]{2,1,0:T(8,128)(2,1)} %collective-permute-done.6.refs_4_), channel_id=1, source_target_pairs={{0,4},{4,0},{1,5},{5,1},{2,6},{6,2},{3,7},{7,3},{8,12},{12,8},{9,1... | collective-permute-start | bytes 491528 | tf_op jit(solution)/shard_map/ppermute | solution.py:32
  66.4 3.7 %collective-permute-start.10 = (bf16[4,160,128]{2,1,0:T(8,128)(2,1)}, bf16[4,160,128]{2,1,0:T(8,128)(2,1)}, u32[]{:S(2)}, u32[]{:S(2)}) collective-permute-start(bf16[4,160,128]{2,1,0:T(8,128)(2,1)} %collective-permute-done.5.refs_3_), channel_id=1, source_target_pairs={{0,4},{4,0},{1,5},{5,1},{2,6},{6,2},{3,7},{7,3},{8,12},{12,8},{9,1... | collective-permute-start | bytes 491528 | tf_op jit(solution)/shard_map/ppermute | solution.py:32
  82.0 5.3 %collective-permute-start.12 = (bf16[4,8,160,128]{3,2,1,0:T(8,128)(2,1)}, bf16[4,8,160,128]{3,2,1,0:T(8,128)(2,1)}, u32[]{:S(2)}, u32[]{:S(2)}) collective-permute-start(bf16[4,8,160,128]{3,2,1,0:T(8,128)(2,1)} %get-tuple-element.73), channel_id=1, source_target_pairs={{0,4},{4,0},{1,5},{5,1},{2,6},{6,2},{3,7},{7,3},{8,12},{12,8},{9,1... | collective-permute-start | bytes 3932168 | tf_op jit(solution)/shard_map/ppermute | solution.py:32
  82.4 3.2 %collective-permute-start.13 = (bf16[64,1536]{1,0:T(8,128)(2,1)}, bf16[64,1536]{1,0:T(8,128)(2,1)S(1)}, u32[]{:S(2)}, u32[]{:S(2)}) collective-permute-start(bf16[64,1536]{1,0:T(8,128)(2,1)} %get-tuple-element.82), channel_id=1, source_target_pairs={{0,4},{4,0},{1,5},{5,1},{2,6},{6,2},{3,7},{7,3},{8,12},{12,8},{9,1... | collective-permute-start | bytes 589832 | tf_op jit(solution)/shard_map/ppermute | solution.py:32
  87.3 11.3 %copy-start.1 = (f32[64,1536]{1,0:T(8,128)S(1)}, f32[64,1536]{1,0:T(8,128)}, u32[]{:S(2)}) copy-start(f32[64,1536]{1,0:T(8,128)} %get-tuple-element.76.pooled_ref) | copy-start | bytes 1179652
  90.5 22.1 %all-to-all-start.1 = ((bf16[4,8,160,128]{3,2,1,0:T(8,128)(2,1)}), bf16[4,8,160,128]{3,2,1,0:T(8,128)(2,1)}, u32[]{:S(2)}, u32[]{:S(2)}) async-start(bf16[4,8,160,128]{3,2,1,0:T(8,128)(2,1)} %add_convert_fusion), calls=%async_computation.1 | async-start | bytes 2621440 | tf_op jit(solution)/shard_map/all_to_all | solution.py:41
  114.8 14.9 %all-to-all-start.2 = ((bf16[8,160,128]{2,1,0:T(8,128)(2,1)}), bf16[8,160,128]{2,1,0:T(8,128)(2,1)S(1)}, u32[]{:S(2)}, u32[]{:S(2)}) async-start(bf16[8,160,128]{2,1,0:T(8,128)(2,1)} %shard_map.164), calls=%async_computation.2 | async-start | bytes 655360 | tf_op jit(solution)/shard_map/all_to_all | solution.py:41
  119.0 7.6 %copy-start.6 = (bf16[64,1024]{1,0:T(8,128)(2,1)S(1)}, bf16[64,1024]{1,0:T(8,128)(2,1)}, u32[]{:S(2)}) copy-start(bf16[64,1024]{1,0:T(8,128)(2,1)} %get-tuple-element.88) | copy-start | bytes 393220
  123.9 10.6 %collective-permute-start.14 = (bf16[1152,128]{1,0:T(8,128)(2,1)}, bf16[1152,128]{1,0:T(8,128)(2,1)}, u32[]{:S(2)}, u32[]{:S(2)}) collective-permute-start(bf16[1152,128]{1,0:T(8,128)(2,1)} %get-tuple-element.94), channel_id=1, source_target_pairs={{0,8},{8,16},{16,24},{24,0},{1,9},{9,17},{17,25},{25,1},{2,10},{10... | collective-permute-start | bytes 884744 | tf_op jit(solution)/shard_map/ppermute | solution.py:37
  124.2 10.3 %collective-permute-start.15 = (bf16[1152,128]{1,0:T(8,128)(2,1)}, bf16[1152,128]{1,0:T(8,128)(2,1)}, u32[]{:S(2)}, u32[]{:S(2)}) collective-permute-start(bf16[1152,128]{1,0:T(8,128)(2,1)} %get-tuple-element.95), channel_id=1, source_target_pairs={{0,24},{8,0},{16,8},{24,16},{1,25},{9,1},{17,9},{25,17},{2,26},{10... | collective-permute-start | bytes 884744 | tf_op jit(solution)/shard_map/ppermute | solution.py:37
  129.8 0.7 copy-start.2
  134.5 35.4 %copy-start.15 = (bf16[1,1536]{1,0:T(2,128)(2,1)S(1)}, bf16[1,1536]{1,0:T(2,128)(2,1)}, u32[]{:S(2)}) copy-start(bf16[1,1536]{1,0:T(2,128)(2,1)} %get-tuple-element.106) | copy-start | bytes 9220
  134.5 37.3 %copy-start.14 = (bf16[1,1536]{1,0:T(2,128)(2,1)S(1)}, bf16[1,1536]{1,0:T(2,128)(2,1)}, u32[]{:S(2)}) copy-start(bf16[1,1536]{1,0:T(2,128)(2,1)} %get-tuple-element.107) | copy-start | bytes 9220
  134.5 15.7 %all-to-all-start.3 = ((bf16[8,208,128]{2,1,0:T(8,128)(2,1)}), bf16[8,208,128]{2,1,0:T(8,128)(2,1)}, u32[]{:S(2)}, u32[]{:S(2)}) async-start(bf16[8,208,128]{2,1,0:T(8,128)(2,1)} %get-tuple-element.100), calls=%async_computation.3 | async-start | bytes 851968 | tf_op jit(solution)/shard_map/all_to_all | solution.py:41
  141.6 13.5 %collective-permute-start.16 = (bf16[1152,128]{1,0:T(8,128)(2,1)}, bf16[1152,128]{1,0:T(8,128)(2,1)S(1)}, u32[]{:S(2)}, u32[]{:S(2)}) collective-permute-start(bf16[1152,128]{1,0:T(8,128)(2,1)} %get-tuple-element.97), channel_id=1, source_target_pairs={{0,16},{8,24},{16,0},{24,8},{1,17},{9,25},{17,1},{25,9},{2,18},{10... | collective-permute-start | bytes 884744 | tf_op jit(solution)/shard_map/ppermute | solution.py:37
  152.4 5.0 %collective-permute-start.17 = (bf16[288,128]{1,0:T(8,128)(2,1)}, bf16[288,128]{1,0:T(8,128)(2,1)S(1)}, u32[]{:S(2)}, u32[]{:S(2)}) collective-permute-start(bf16[288,128]{1,0:T(8,128)(2,1)} %get-tuple-element.102), channel_id=1, source_target_pairs={{0,8},{8,16},{16,24},{24,0},{1,9},{9,17},{17,25},{25,1},{2,10},{10... | collective-permute-start | bytes 221192 | tf_op jit(solution)/shard_map/ppermute | solution.py:37
  152.7 5.6 %collective-permute-start.18 = (bf16[288,128]{1,0:T(8,128)(2,1)}, bf16[288,128]{1,0:T(8,128)(2,1)S(1)}, u32[]{:S(2)}, u32[]{:S(2)}) collective-permute-start(bf16[288,128]{1,0:T(8,128)(2,1)} %get-tuple-element.103), channel_id=1, source_target_pairs={{0,16},{8,24},{16,0},{24,8},{1,17},{9,25},{17,1},{25,9},{2,18},{10... | collective-permute-start | bytes 221192 | tf_op jit(solution)/shard_map/ppermute | solution.py:37
  154.5 4.2 %collective-permute-start.19 = (bf16[288,128]{1,0:T(8,128)(2,1)}, bf16[288,128]{1,0:T(8,128)(2,1)S(1)}, u32[]{:S(2)}, u32[]{:S(2)}) collective-permute-start(bf16[288,128]{1,0:T(8,128)(2,1)} %get-tuple-element.104), channel_id=1, source_target_pairs={{0,24},{8,0},{16,8},{24,16},{1,25},{9,1},{17,9},{25,17},{2,26},{10... | collective-permute-start | bytes 221192 | tf_op jit(solution)/shard_map/ppermute | solution.py:37
  155.1 3.6 %copy-start.4 = (bf16[1152,128]{1,0:T(8,128)(2,1)}, bf16[1152,128]{1,0:T(8,128)(2,1)S(1)}, u32[]{:S(2)}) copy-start(bf16[1152,128]{1,0:T(8,128)(2,1)S(1)} %collective-permute-done.16.refs_2_) | copy-start | bytes 884740
  157.4 1.3 copy-start.7
  158.3 0.6 copy-start.8
  158.7 0.6 copy-start.9
  161.8 25.5 %all-to-all-start.4 = ((bf16[16,128,128]{2,1,0:T(8,128)(2,1)}), bf16[16,128,128]{2,1,0:T(8,128)(2,1)}, u32[]{:S(2)}, u32[]{:S(2)}) async-start(bf16[16,128,128]{2,1,0:T(8,128)(2,1)} %shard_map.167), calls=%async_computation.4 | async-start | bytes 1048576 | tf_op jit(solution)/shard_map/all_to_all | solution.py:41
  169.9 4.4 %collective-permute-start.20 = (bf16[1,1536]{1,0:T(2,128)(2,1)S(1)}, bf16[1,1536]{1,0:T(2,128)(2,1)S(1)}, u32[]{:S(2)}, u32[]{:S(2)}) collective-permute-start(bf16[1,1536]{1,0:T(2,128)(2,1)S(1)} %copy-done.15), channel_id=1, source_target_pairs={{0,4},{4,8},{8,12},{12,16},{16,20},{20,24},{24,28},{28,32},{32,36}... | collective-permute-start | bytes 9224 | tf_op jit(solution)/shard_map/ppermute | solution.py:604
  171.8 5.3 %collective-permute-start.21 = (bf16[1,1536]{1,0:T(2,128)(2,1)S(1)}, bf16[1,1536]{1,0:T(2,128)(2,1)S(1)}, u32[]{:S(2)}, u32[]{:S(2)}) collective-permute-start(bf16[1,1536]{1,0:T(2,128)(2,1)S(1)} %copy-done.14), channel_id=1, source_target_pairs={{4,0},{8,4},{12,8},{16,12},{20,16},{24,20},{28,24},{32,28},{36,32}... | collective-permute-start | bytes 9224 | tf_op jit(solution)/shard_map/ppermute | solution.py:604
  174.3 2.9 %copy-start.12 = (bf16[1,1536]{1,0:T(2,128)(2,1)}, bf16[1,1536]{1,0:T(2,128)(2,1)S(1)}, u32[]{:S(2)}) copy-start(bf16[1,1536]{1,0:T(2,128)(2,1)S(1)} %collective-permute-done.20.before_ref) | copy-start | bytes 9220
  177.2 0.6 copy-start.13
Sparse Core Ops, SparseCore 0:
  42.7 27.9 all-gather.2
  87.4 22.3 all-gather.4

commit v8 on v7

--- a/solution.py
+++ b/solution.py
@@ -291,12 +291,56 @@
     return total
 
 
-def sum_kernel(parts_ref, out_ref):
-    for j in range(out_ref.shape[0]):
-        total = parts_ref[0, j].astype(F32)
-        for i in range(1, parts_ref.shape[0]):
-            total = total + parts_ref[i, j].astype(F32)
-        out_ref[j] = total.astype(BF)
+def add_kernel(chunks, refs_of, *refs):
+    out_ref, held, sums, in_sem, out_sem = refs[-5:]
+    parts = refs_of(refs[:-5])
+    size = out_ref.shape[0] // chunks
+    spans = [pl.ds(k * size, size) for k in range(chunks)]
+    loads = [
+        [pltpu.make_async_copy(part.at[at], held.at[i, at], in_sem.at[i, k])
+         for i, part in enumerate(parts)]
+        for k, at in enumerate(spans)
+    ]
+    stores = [
+        pltpu.make_async_copy(sums.at[at], out_ref.at[at], out_sem.at[k])
+        for k, at in enumerate(spans)
+    ]
+    for load in loads:
+        for copy in load:
+            copy.start()
+    for k, load in enumerate(loads):
+        for copy in load:
+            copy.wait()
+        for j in range(k * size, (k + 1) * size):
+            total = held[0, j].astype(F32)
+            for i in range(1, len(parts)):
+                total = total + held[i, j].astype(F32)
+            sums[j] = total.astype(BF)
+        stores[k].start()
+    for store in stores:
+        store.wait()
+
+
+def add_parts(count, refs_of, out, chunks, *args):
+    anywhere = pl.BlockSpec(memory_space=pl.ANY)
+    return pl.pallas_call(
+        functools.partial(add_kernel, chunks, refs_of),
+        out_shape=out,
+        in_specs=[anywhere] * len(args),
+        out_specs=anywhere,
+        scratch_shapes=[
+            pltpu.VMEM((count,) + out.shape, BF),
+            pltpu.VMEM(out.shape, BF),
+            pltpu.SemaphoreType.DMA((count, chunks)),
+            pltpu.SemaphoreType.DMA((chunks,)),
+        ],
+        compiler_params=pltpu.CompilerParams(vmem_limit_bytes=60 * 2**20),
+        cost_estimate=pl.CostEstimate(
+            flops=count * math.prod(out.shape),
+            bytes_accessed=2 * (count + 1) * math.prod(out.shape),
+            transcendentals=0,
+        ),
+    )(*args)
 
 
 def back_kernel(cores, parts_ref, part_ref, kw_ref, vw_ref, pooled_ref, gain_ref, gy_ref, pairs_ref,
@@ -545,10 +589,9 @@
     queries = dot(normed, query_weight).astype(BF)
     grad_mixed = contract_cols(cotangent, out_weight).astype(BF)
     got = swap(send)
-    kv, queries, grad_mixed, keep, got = lax.optimization_barrier(
-        (kv, queries, grad_mixed, keep, got)
-    )
-    early = lax.all_gather(jnp.concatenate([keep, got], axis=0), "x", axis=0, tiled=True)
+    early = jnp.concatenate([keep, got], axis=0)
+    kv, queries, grad_mixed, early = lax.optimization_barrier((kv, queries, grad_mixed, early))
+    early = lax.all_gather(early, "x", axis=0, tiled=True)
 
     half = nz // 2
     before, after = shift(kv, "y", 1), shift(kv, "y", ny - 1)
@@ -562,12 +605,17 @@
 
     later = lax.all_gather(jnp.concatenate([keep, swap(send)], axis=0), "x", axis=0, tiled=True)
 
-    gkv = (gkv.astype(F32) + swap(others).astype(F32)).astype(BF)
+    flat = (ny * nz, packed, qk)
+    gkv = add_parts(
+        2, list, shape(*flat), 8, gkv.reshape(flat), swap(others).reshape(flat)
+    ).reshape(ny, nz, packed, qk)
     mixed_out = (pooled + dot(mixed, out_weight)).astype(BF)
     gkv, pairs, spread, mixed_out = lax.optimization_barrier(
         (exchange(gkv, "y"), pairs, spread, mixed_out)
     )
-    (gkv,) = call(sum_kernel, (shape(*kv.shape),), [], 0, gkv)
+    gkv = add_parts(
+        ny, lambda refs: [refs[0].at[i] for i in range(ny)], shape(*kv.shape), 4, gkv
+    )
     gkv = exchange(gkv, "z")
 
     keep = width // nx

time: 197 us -> 192 us (0.975)
  starting transfers between devices: 71.5 us -> 63.5 us
  waiting for transfers between devices: 44.9 us -> 48.4 us
  other arithmetic: 8.15 us -> 4.73 us
  Pallas kernels: 39.8 us -> 42.9 us
    ppermute x8, starting transfers between devices: 13.3 us -> 6.11 us  [swap(): return lax.ppermute(block, 'core', [(0, 1), (1, 0)])]
    all_to_all x5, waiting for transfers between devices: 25.7 us -> 30.6 us  [exchange(): return lax.all_to_all(blocks, axis, 0, 0, tiled=True)]
    pallas_call x0 -> x2, Pallas kernels: none -> 4.93 us  [add_parts(): pl.pallas_call(functools.partial(add_kernel, chunks, refs_of), out_shape=...]
    ppermute x1, starting transfers between devices: 5.28 us -> 1.92 us  [shards(): high = lax.ppermute(x[:2], seq, down)]
    convert_element_type x1 -> x0, other arithmetic: 3.2 us -> none  [shards(): gkv = (gkv.astype(F32) + swap(others).astype(F32)).astype(BF)]
    ppermute x10, starting transfers between devices: 15.2 us -> 12.1 us  [shift(): lax.ppermute(block, axis, [(i, (i + step) % count) for i in range(count)])]
    ppermute x1, waiting for transfers between devices: 0.01 us -> 2.99 us  [shards(): high = lax.ppermute(x[:2], seq, down)]
    all_to_all x5, starting transfers between devices: 31.4 us -> 34.3 us  [exchange(): return lax.all_to_all(blocks, axis, 0, 0, tiled=True)]
  transfers between devices with their start and end apart: 29 -> 29, of which waited for: 13 -> 16; matrix products, arithmetic and copies ran while one was open for 10% -> 10% of each run, Pallas kernels for 16% -> 18%
where the time goes in v8:
time: 192 us; the launch traced here: 191 us
  starting transfers between devices  63.5 us (33%)
  waiting for transfers between devices  48.4 us (25%)
  Pallas kernels  42.9 us (22%)
  between operations  14.3 us (7%)
  matrix products  12 us (6%)
  local copies, waits for them, and re-layouts  5.36 us (3%)
  other arithmetic  4.73 us (2%)
    all_to_all x5, starting transfers between devices, exchange(): return lax.all_to_all(blocks, axis, 0, 0, tiled=True)  34.3 us
    all_to_all x5, waiting for transfers between devices, exchange(): return lax.all_to_all(blocks, axis, 0, 0, tiled=True)  30.6 us
    pallas_call x5, Pallas kernels, call(): pl.pallas_call(kernel, out_shape=out_shape, scratch_shapes=scratch, compi...  15.1 us
    ppermute x10, starting transfers between devices, shift(): lax.ppermute(block, axis, [(i, (i + step) % count) for i in range(count)])  12.1 us
    pallas_call x1, Pallas kernels, attention(): pl.pallas_call(functools.partial(attention_kernel, scale, heads, group, u...  11.8 us
    pallas_call x3, Pallas kernels, flagged(): pl.pallas_call(kernel, out_shape=out_shape, in_specs=[smem] + [vmem] * le...  11 us
    ppermute x10, waiting for transfers between devices, shift(): lax.ppermute(block, axis, [(i, (i + step) % count) for i in range(count)])  9.48 us
    dot_general x2, matrix products, contract_cols(): lax.dot_general(left, right, (((1,), (1,)), ((), ())), preferred_element_...  6.56 us
  transfers between devices with their start and end apart: 29, of which 16 were waited for; matrix products, arithmetic and copies ran while one was open for 10% of the time, Pallas kernels for 18%

profile of v8, /device:TPU:1, one launch (start us, length us, event | category | flops | bytes accessed | tf_op | source)
XLA Modules:
  0.0 191.1 jit_solution(14053444620606926891)
XLA Ops:
  7.2 0.9 slice_bitcast_fusion
  8.1 4.7 %collective-permute-start = (bf16[2,1536]{1,0:T(2,128)(2,1)S(1)}, bf16[2,1536]{1,0:T(2,128)(2,1)S(1)}, u32[]{:S(2)}, u32[]{:S(2)}) collective-permute-start(bf16[2,1536]{1,0:T(2,128)(2,1)S(1)} %get-tuple-element.116), channel_id=1, source_target_pairs={{0,4},{4,8},{8,12},{12,16},{16,20},{20,24},{24,28},{28,32},{32,36}... | collective-permute-start | bytes 18440 | tf_op jit(solution)/shard_map/ppermute | solution.py:554
  12.8 1.9 %collective-permute-start.1 = (bf16[2,1536]{1,0:T(2,128)(2,1)S(1)}, bf16[2,1536]{1,0:T(2,128)(2,1)S(1)}, u32[]{:S(2)}, u32[]{:S(2)}) collective-permute-start(bf16[2,1536]{1,0:T(2,128)(2,1)S(1)} %get-tuple-element.115), channel_id=1, source_target_pairs={{4,0},{8,4},{12,8},{16,12},{20,16},{24,20},{28,24},{32,28},{36,32}... | collective-permute-start | bytes 18440 | tf_op jit(solution)/shard_map/ppermute | solution.py:555
  14.8 3.0 %collective-permute-done.1.high_ref = bf16[2,1536]{1,0:T(2,128)(2,1)S(1)} collective-permute-done((bf16[2,1536]{1,0:T(2,128)(2,1)S(1)}, bf16[2,1536]{1,0:T(2,128)(2,1)S(1)}, u32[]{:S(2)}, u32[]{:S(2)}) %collective-permute-start.1) | collective-permute-done | bytes 6176 | tf_op jit(solution)/shard_map/ppermute | solution.py:555
  17.8 0.6 copy-done.12
  18.4 3.5 %shard_map.160 = (bf16[8,160,128]{2,1,0:T(8,128)(2,1)}, bf16[64,1536]{1,0:T(8,128)(2,1)}, f32[64,1536]{1,0:T(8,128)}, bf16[64,1536]{1,0:T(8,128)(2,1)}, bf16[64,1536]{1,0:T(8,128)(2,1)}) custom-call(s32[1]{0:T(128)} %bitcast.1.first_ref, bf16[128,1536]{1,0:T(8,128)(2,1)} %bitcast.23, bf16[2,1536]{1,0:T(2,128)(2,1)} %copy-done.11, ...), custom_call_target="tpu_custom_call" | custom-call | flops 62914560 | bytes 9437184 | tf_op jit(solution)/shard_map/pallas_call | solution.py:560
  21.9 10.4 %all-to-all-start = ((bf16[8,160,128]{2,1,0:T(8,128)(2,1)}), bf16[8,160,128]{2,1,0:T(8,128)(2,1)S(1)}, u32[]{:S(2)}, u32[]{:S(2)}) async-start(bf16[8,160,128]{2,1,0:T(8,128)(2,1)} %get-tuple-element.62), calls=%async_computation | async-start | bytes 655360 | tf_op jit(solution)/shard_map/all_to_all | solution.py:41
  32.3 4.7 %convolution_convert_fusion.g_ref = bf16[64,1536]{1,0:T(8,128)(2,1)} fusion(bf16[64,1536]{1,0:T(8,128)(2,1)} %bitcast.29, bf16[1536,1536]{1,0:T(8,128)(2,1)} %param.16), kind=kOutput, calls=%fused_computation.2 | convolution fusion | flops 302088192 | bytes 5111808 | tf_op jit(solution)/shard_map/dot_general | solution.py:24
  37.0 1.3 convolution_convert_fusion.1.q_ref
  38.3 1.7 pad_maximum_fusion
  40.1 5.9 %all-to-all-done.refs_0_ = bf16[8,160,128]{2,1,0:T(8,128)(2,1)S(1)} async-done(((bf16[8,160,128]{2,1,0:T(8,128)(2,1)}), bf16[8,160,128]{2,1,0:T(8,128)(2,1)S(1)}, u32[]{:S(2)}, u32[]{:S(2)}) %all-to-all-start) | async-done | bytes 327712 | tf_op jit(solution)/shard_map/all_to_all | solution.py:41
  46.2 2.7 %collective-permute-start.4 = (bf16[8,160,128]{2,1,0:T(8,128)(2,1)S(1)}, bf16[8,160,128]{2,1,0:T(8,128)(2,1)}, u32[]{:S(2)}, u32[]{:S(2)}) collective-permute-start(bf16[8,160,128]{2,1,0:T(8,128)(2,1)S(1)} %all-to-all-done.refs_0_), channel_id=1, source_target_pairs={{0,24},{8,0},{16,8},{24,16},{1,25},{9,1},{17,9},{25,17},{2,26},{10... | collective-permute-start | bytes 983048 | tf_op jit(solution)/shard_map/ppermute | solution.py:37
  48.8 1.0 collective-permute-start.7
  49.8 6.4 %collective-permute-done.3.refs_1_ = bf16[8,160,128]{2,1,0:T(8,128)(2,1)} collective-permute-done((bf16[8,160,128]{2,1,0:T(8,128)(2,1)S(1)}, bf16[8,160,128]{2,1,0:T(8,128)(2,1)}, u32[]{:S(2)}, u32[]{:S(2)}) %collective-permute-start.3) | collective-permute-done | bytes 327712 | tf_op jit(solution)/shard_map/ppermute | solution.py:37
  56.3 0.9 slice.24
  57.3 0.9 slice.25
  58.2 2.7 %collective-permute-start.6 = (bf16[4,160,128]{2,1,0:T(8,128)(2,1)S(1)}, bf16[4,160,128]{2,1,0:T(8,128)(2,1)}, u32[]{:S(2)}, u32[]{:S(2)}) collective-permute-start(bf16[4,160,128]{2,1,0:T(8,128)(2,1)S(1)} %slice.25), channel_id=1, source_target_pairs={{0,24},{8,0},{16,8},{24,16},{1,25},{9,1},{17,9},{25,17},{2,26},{10... | collective-permute-start | bytes 491528 | tf_op jit(solution)/shard_map/ppermute | solution.py:37
  61.0 1.9 collective-permute-start.8
  62.8 0.2 collective-permute-done.5.refs_3_
  63.1 2.2 %collective-permute-start.10 = (bf16[4,160,128]{2,1,0:T(8,128)(2,1)}, bf16[4,160,128]{2,1,0:T(8,128)(2,1)}, u32[]{:S(2)}, u32[]{:S(2)}) collective-permute-start(bf16[4,160,128]{2,1,0:T(8,128)(2,1)} %collective-permute-done.5.refs_3_), channel_id=1, source_target_pairs={{0,4},{4,0},{1,5},{5,1},{2,6},{6,2},{3,7},{7,3},{8,12},{12,8},{9,1... | collective-permute-start | bytes 491528 | tf_op jit(solution)/shard_map/ppermute | solution.py:32
  65.2 0.4 collective-permute-start.11
  65.7 0.6 pad_add_fusion.place_ref
  66.3 0.3 collective-permute-done.10.refs_8_
  66.6 0.5 collective-permute-done.11.refs_9_
  67.1 11.8 %shard_map.161 = (bf16[64,1536]{1,0:T(8,128)(2,1)}, bf16[64,1024]{1,0:T(8,128)(2,1)}, bf16[64,1536]{1,0:T(8,128)(2,1)}, bf16[64,1536]{1,0:T(8,128)(2,1)}, bf16[4...) custom-call(s32[2]{0:T(128)} %pad_add_fusion.place_ref, bf16[64,1024]{1,0:T(8,128)(2,1)} %convolution_convert_fusion.1.q_ref, ...), custom_call_target="tpu_custom_call" | custom-call | flops 4026531840 | bytes 5242880 | tf_op jit(solution)/shard_map/pallas_call | solution.py:264
  78.9 0.4 collective-permute-start.13
  79.3 0.1 collective-permute-start.12
  79.5 1.1 collective-permute-done.13
  80.6 1.7 pad_maximum_fusion.1
  82.3 0.4 collective-permute-done.12
  82.7 2.7 %shard_map.162 = bf16[32,160,128]{2,1,0:T(8,128)(2,1)} custom-call(bf16[32,160,128]{2,1,0:T(8,128)(2,1)} %bitcast.31, bf16[32,160,128]{2,1,0:T(8,128)(2,1)} %bitcast.8.refs_1_), custom_call_target="tpu_custom_call" | custom-call | flops 1310720 | bytes 3932160 | tf_op jit(solution)/shard_map/pallas_call | solution.py:326
  85.5 4.8 %all-to-all-start.1 = ((bf16[4,8,160,128]{3,2,1,0:T(8,128)(2,1)}), bf16[4,8,160,128]{3,2,1,0:T(8,128)(2,1)}, u32[]{:S(2)}, u32[]{:S(2)}) async-start(bf16[4,8,160,128]{3,2,1,0:T(8,128)(2,1)} %bitcast.22), calls=%async_computation.1 | async-start | bytes 2621440 | tf_op jit(solution)/shard_map/all_to_all | solution.py:41
  90.2 3.8 %shard_map.163 = (f32[5,64,1536]{2,1,0:T(8,128)}, f32[64,1536]{1,0:T(8,128)}) custom-call(bf16[128,1536]{1,0:T(8,128)(2,1)} %bitcast.24, bf16[2,1536]{1,0:T(2,128)(2,1)} %copy-done.11, bf16[2,1536]{1,0:T(2,128)(2,1)} %copy-done.12, f32[1536]{0:T(1024)} %gain_ref.3, f32[5,1536]{1,0:T(8,128)} %taps_ref.5), custom_call_target="tpu_custom_call" | custom-call | flops 7864320 | bytes 2801664 | tf_op jit(solution)/shard_map/pallas_call | solution.py:47
  94.0 4.1 %fusion = bf16[64,1536]{1,0:T(8,128)(2,1)} fusion(f32[64,1536]{1,0:T(8,128)S(1)} %copy-done.1, bf16[64,1536]{1,0:T(8,128)(2,1)} %get-tuple-element.76, bf16[1536,1536]{1,0:T(8,128)(2,1)} %param.16), kind=kOutput, calls=%fused_computation.1 | convolution fusion | flops 302186496 | bytes 5505024 | tf_op jit(solution)/shard_map/dot_general | solution.py:28
  98.1 9.7 %all-to-all-done.1.refs_0_ = bf16[4,8,160,128]{3,2,1,0:T(8,128)(2,1)} async-done(((bf16[4,8,160,128]{3,2,1,0:T(8,128)(2,1)}), bf16[4,8,160,128]{3,2,1,0:T(8,128)(2,1)}, u32[]{:S(2)}, u32[]{:S(2)}) %all-to-all-start.1) | async-done | bytes 1310752 | tf_op jit(solution)/shard_map/all_to_all | solution.py:41
  107.8 2.2 %shard_map.165 = bf16[8,160,128]{2,1,0:T(8,128)(2,1)} custom-call(bf16[4,8,160,128]{3,2,1,0:T(8,128)(2,1)} %all-to-all-done.1.refs_0_), custom_call_target="tpu_custom_call" | custom-call | flops 655360 | bytes 1638400 | tf_op jit(solution)/shard_map/pallas_call | solution.py:326
  110.0 3.4 %all-to-all-start.2 = ((bf16[8,160,128]{2,1,0:T(8,128)(2,1)}), bf16[8,160,128]{2,1,0:T(8,128)(2,1)S(1)}, u32[]{:S(2)}, u32[]{:S(2)}) async-start(bf16[8,160,128]{2,1,0:T(8,128)(2,1)} %shard_map.165), calls=%async_computation.2 | async-start | bytes 655360 | tf_op jit(solution)/shard_map/all_to_all | solution.py:41
  113.4 0.7 compare_select_fusion.8.target_ref
  114.2 5.1 %shard_map.164 = (bf16[384,512]{1,0:T(8,128)(2,1)}, bf16[1152,128]{1,0:T(8,128)(2,1)}, bf16[1152,128]{1,0:T(8,128)(2,1)}, bf16[1152,128]{1,0:T(8,128)(2,1)}, bf16[1152,128]{1,0:T(8,128)(2,1)}) custom-call(s32[1]{0:T(128)} %bitcast.1.first_ref, s32[1,1536]{1,0:T(1,128)} %compare_select_fusion.8.target_ref, ...), custom_call_target="tpu_custom_call" | custom-call | flops 1207959552 | bytes 9437184 | tf_op jit(solution)/shard_map/pallas_call | solution.py:560
  119.2 1.1 collective-permute-start.14
  120.3 1.6 collective-permute-start.15
  121.9 1.9 fusion.14.part_ref
  123.8 0.7 all-to-all-done.2.parts_ref
  124.5 0.7 copy-done.2
  125.2 4.0 %shard_map.166 = (bf16[64,1536]{1,0:T(8,128)(2,1)}, bf16[1,1536]{1,0:T(2,128)(2,1)}, bf16[1,1536]{1,0:T(2,128)(2,1)}, bf16[8,208,128]{2,1,0:T(8,128)(2,1)}) custom-call(bf16[8,160,128]{2,1,0:T(8,128)(2,1)} %copy-done.2, f32[64,1536]{1,0:T(8,128)} %fusion.14.part_ref, bf16[1536,128]{1,0:T(8,128)(2,1)} %kw_ref.3, bf16[192,1536]{1,0:T(8,128)(2,1)} %bitcast.27, ...), custom_call_target="tpu_custom_call" | custom-call | flops 62914560 | bytes 5287936 | tf_op jit(solution)/shard_map/pallas_call | solution.py:47
  129.2 7.4 %all-to-all-start.3 = ((bf16[8,208,128]{2,1,0:T(8,128)(2,1)}), bf16[8,208,128]{2,1,0:T(8,128)(2,1)}, u32[]{:S(2)}, u32[]{:S(2)}) async-start(bf16[8,208,128]{2,1,0:T(8,128)(2,1)} %get-tuple-element.98), calls=%async_computation.3 | async-start | bytes 851968 | tf_op jit(solution)/shard_map/all_to_all | solution.py:41
  136.6 0.4 collective-permute-start.16
  137.0 8.2 %all-to-all-done.3.got_ref = bf16[8,208,128]{2,1,0:T(8,128)(2,1)} async-done(((bf16[8,208,128]{2,1,0:T(8,128)(2,1)}), bf16[8,208,128]{2,1,0:T(8,128)(2,1)}, u32[]{:S(2)}, u32[]{:S(2)}) %all-to-all-start.3) | async-done | bytes 426016 | tf_op jit(solution)/shard_map/all_to_all | solution.py:41
  145.2 2.3 %shard_map.167 = (bf16[288,128]{1,0:T(8,128)(2,1)}, bf16[288,128]{1,0:T(8,128)(2,1)}, bf16[288,128]{1,0:T(8,128)(2,1)}, bf16[288,128]{1,0:T(8,128)(2,1)}) custom-call(bf16[384,512]{1,0:T(8,128)(2,1)} %get-tuple-element.97.left_ref, bf16[8,208,128]{2,1,0:T(8,128)(2,1)} %all-to-all-done.3.got_ref), custom_call_target="tpu_custom_call" | custom-call | flops 125829120 | bytes 1114112 | tf_op jit(solution)/shard_map/pallas_call | solution.py:47
  147.4 1.1 collective-permute-start.17
  148.5 1.0 collective-permute-start.18
  149.5 1.4 collective-permute-start.19
  150.9 1.2 collective-permute-done.17.refs_5_
  152.1 1.6 collective-permute-done.18.refs_6_
  153.7 0.5 copy-done.9
  154.3 2.4 %shard_map.168 = bf16[16,128,128]{2,1,0:T(8,128)(2,1)} custom-call(s32[1]{0:T(128)} %bitcast.1.first_ref, bf16[1152,128]{1,0:T(8,128)(2,1)} %get-tuple-element.81.refs_0_, bf16[1152,128]{1,0:T(8,128)(2,1)} %collective-permute-done.14.refs_1_, bf16[1152,128]{1,0:T(8,128)(2,1)} %copy-done.4, bf16[1152,128]{1,0:T(8,128)(2,1)} %collective-permute-done.15.refs_3_, ...), custom_call_target="tpu_custom_call" | custom-call | bytes 9437184 | tf_op jit(solution)/shard_map/pallas_call | solution.py:560
  156.8 8.3 %all-to-all-start.4 = ((bf16[16,128,128]{2,1,0:T(8,128)(2,1)}), bf16[16,128,128]{2,1,0:T(8,128)(2,1)}, u32[]{:S(2)}, u32[]{:S(2)}) async-start(bf16[16,128,128]{2,1,0:T(8,128)(2,1)} %shard_map.168), calls=%async_computation.4 | async-start | bytes 1048576 | tf_op jit(solution)/shard_map/all_to_all | solution.py:41
  165.1 2.0 %collective-permute-start.20 = (bf16[1,1536]{1,0:T(2,128)(2,1)S(1)}, bf16[1,1536]{1,0:T(2,128)(2,1)S(1)}, u32[]{:S(2)}, u32[]{:S(2)}) collective-permute-start(bf16[1,1536]{1,0:T(2,128)(2,1)S(1)} %copy-done.16), channel_id=1, source_target_pairs={{0,4},{4,8},{8,12},{12,16},{16,20},{20,24},{24,28},{28,32},{32,36}... | collective-permute-start | bytes 9224 | tf_op jit(solution)/shard_map/ppermute | solution.py:652
  167.1 2.3 %collective-permute-start.21 = (bf16[1,1536]{1,0:T(2,128)(2,1)S(1)}, bf16[1,1536]{1,0:T(2,128)(2,1)S(1)}, u32[]{:S(2)}, u32[]{:S(2)}) collective-permute-start(bf16[1,1536]{1,0:T(2,128)(2,1)S(1)} %copy-done.15), channel_id=1, source_target_pairs={{4,0},{8,4},{12,8},{16,12},{20,16},{24,20},{28,24},{32,28},{36,32}... | collective-permute-start | bytes 9224 | tf_op jit(solution)/shard_map/ppermute | solution.py:652
  169.5 3.0 %collective-permute-done.21.after_ref = bf16[1,1536]{1,0:T(2,128)(2,1)S(1)} collective-permute-done((bf16[1,1536]{1,0:T(2,128)(2,1)S(1)}, bf16[1,1536]{1,0:T(2,128)(2,1)S(1)}, u32[]{:S(2)}, u32[]{:S(2)}) %collective-permute-start.21) | collective-permute-done | bytes 3104 | tf_op jit(solution)/shard_map/ppermute | solution.py:652
  172.4 0.6 copy-done.14
  173.0 3.3 %shard_map.169 = bf16[128,1536]{1,0:T(8,128)(2,1)} custom-call(bf16[128,1536]{1,0:T(8,128)(2,1)} %bitcast.25, f32[1536]{0:T(1024)} %gain_ref.3, f32[5,1536]{1,0:T(8,128)} %taps_ref.5, bf16[64,1536]{1,0:T(8,128)(2,1)} %get-tuple-element.103.half_ref, bf16[1,1536]{1,0:T(2,128)(2,1)} %copy-done.13, bf16[1,1536]{1,0:T(2,128)(2,1)} %copy-done.14), custom_call_target="tpu_custom_call" | custom-call | flops 7864320 | bytes 1026048 | tf_op jit(solution)/shard_map/pallas_call | solution.py:47
  176.3 6.2 %all-to-all-done.4.got_ref = bf16[16,128,128]{2,1,0:T(8,128)(2,1)} async-done(((bf16[16,128,128]{2,1,0:T(8,128)(2,1)}), bf16[16,128,128]{2,1,0:T(8,128)(2,1)}, u32[]{:S(2)}, u32[]{:S(2)}) %all-to-all-start.4) | async-done | bytes 524320 | tf_op jit(solution)/shard_map/all_to_all | solution.py:41
  182.5 1.7 shard_map.170
  (52 shorter events, 0.6 us)
Async XLA Ops:
  7.2 29.8 %copy-start = (bf16[1536,1024]{1,0:T(8,128)(2,1)S(1)}, bf16[1536,1024]{1,0:T(8,128)(2,1)}, u32[]{:S(2)}) copy-start(bf16[1536,1024]{1,0:T(8,128)(2,1)} %param.13) | copy-start | bytes 9437188
  8.1 6.7 %collective-permute-start = (bf16[2,1536]{1,0:T(2,128)(2,1)S(1)}, bf16[2,1536]{1,0:T(2,128)(2,1)S(1)}, u32[]{:S(2)}, u32[]{:S(2)}) collective-permute-start(bf16[2,1536]{1,0:T(2,128)(2,1)S(1)} %get-tuple-element.116), channel_id=1, source_target_pairs={{0,4},{4,8},{8,12},{12,16},{16,20},{20,24},{24,28},{28,32},{32,36}... | collective-permute-start | bytes 18440 | tf_op jit(solution)/shard_map/ppermute | solution.py:554
  12.8 4.9 %collective-permute-start.1 = (bf16[2,1536]{1,0:T(2,128)(2,1)S(1)}, bf16[2,1536]{1,0:T(2,128)(2,1)S(1)}, u32[]{:S(2)}, u32[]{:S(2)}) collective-permute-start(bf16[2,1536]{1,0:T(2,128)(2,1)S(1)} %get-tuple-element.115), channel_id=1, source_target_pairs={{4,0},{8,4},{12,8},{16,12},{20,16},{24,20},{28,24},{32,28},{36,32}... | collective-permute-start | bytes 18440 | tf_op jit(solution)/shard_map/ppermute | solution.py:555
  14.8 3.0 %copy-start.11 = (bf16[2,1536]{1,0:T(2,128)(2,1)}, bf16[2,1536]{1,0:T(2,128)(2,1)S(1)}, u32[]{:S(2)}) copy-start(bf16[2,1536]{1,0:T(2,128)(2,1)S(1)} %collective-permute-done.low_ref) | copy-start | bytes 18436
  17.8 0.6 copy-start.12
  21.8 16.5 %collective-permute-start.2 = (bf16[64,1536]{1,0:T(8,128)(2,1)}, bf16[64,1536]{1,0:T(8,128)(2,1)}, u32[]{:S(2)}, u32[]{:S(2)}) collective-permute-start(bf16[64,1536]{1,0:T(8,128)(2,1)} %get-tuple-element.67), channel_id=1, source_target_pairs={{0,4},{4,0},{1,5},{5,1},{2,6},{6,2},{3,7},{7,3},{8,12},{12,8},{9,1... | collective-permute-start | bytes 589832 | tf_op jit(solution)/shard_map/ppermute | solution.py:32
  21.9 24.1 %all-to-all-start = ((bf16[8,160,128]{2,1,0:T(8,128)(2,1)}), bf16[8,160,128]{2,1,0:T(8,128)(2,1)S(1)}, u32[]{:S(2)}, u32[]{:S(2)}) async-start(bf16[8,160,128]{2,1,0:T(8,128)(2,1)} %get-tuple-element.62), calls=%async_computation | async-start | bytes 655360 | tf_op jit(solution)/shard_map/all_to_all | solution.py:41
  32.2 81.9 %all-gather.3.cloned.1.call-start = ((), (), s32[]{:S(2)}) async-start(), calls=%async_computation.5 | async-start | bytes 1966080 | tf_op jit(solution)/shard_map/all_gather | solution.py:594
  32.3 4.7 %copy-start.6 = (bf16[64,1536]{1,0:T(8,128)(2,1)S(1)}, bf16[64,1536]{1,0:T(8,128)(2,1)}, u32[]{:S(2)}) copy-start(bf16[64,1536]{1,0:T(8,128)(2,1)} %get-tuple-element.64) | copy-start | bytes 589828
  32.3 6.1 %copy-start.5 = (bf16[64,1536]{1,0:T(8,128)(2,1)S(1)}, bf16[64,1536]{1,0:T(8,128)(2,1)}, u32[]{:S(2)}) copy-start(bf16[64,1536]{1,0:T(8,128)(2,1)} %get-tuple-element.66) | copy-start | bytes 589828
  46.0 21.1 %copy-start.3 = (bf16[8,160,128]{2,1,0:T(8,128)(2,1)}, bf16[8,160,128]{2,1,0:T(8,128)(2,1)S(1)}, u32[]{:S(2)}) copy-start(bf16[8,160,128]{2,1,0:T(8,128)(2,1)S(1)} %all-to-all-done.refs_0_) | copy-start | bytes 983044
  46.0 68.1 %all-gather.5.cloned.1.call-start = ((), (), s32[]{:S(2)}) async-start(), calls=%async_computation.6 | async-start | bytes 1966080 | tf_op jit(solution)/shard_map/all_gather | solution.py:606
  46.1 10.2 %collective-permute-start.3 = (bf16[8,160,128]{2,1,0:T(8,128)(2,1)S(1)}, bf16[8,160,128]{2,1,0:T(8,128)(2,1)}, u32[]{:S(2)}, u32[]{:S(2)}) collective-permute-start(bf16[8,160,128]{2,1,0:T(8,128)(2,1)S(1)} %all-to-all-done.refs_0_), channel_id=1, source_target_pairs={{0,8},{8,16},{16,24},{24,0},{1,9},{9,17},{17,25},{25,1},{2,10},{10... | collective-permute-start | bytes 983048 | tf_op jit(solution)/shard_map/ppermute | solution.py:37
  46.2 11.1 %collective-permute-start.4 = (bf16[8,160,128]{2,1,0:T(8,128)(2,1)S(1)}, bf16[8,160,128]{2,1,0:T(8,128)(2,1)}, u32[]{:S(2)}, u32[]{:S(2)}) collective-permute-start(bf16[8,160,128]{2,1,0:T(8,128)(2,1)S(1)} %all-to-all-done.refs_0_), channel_id=1, source_target_pairs={{0,24},{8,0},{16,8},{24,16},{1,25},{9,1},{17,9},{25,17},{2,26},{10... | collective-permute-start | bytes 983048 | tf_op jit(solution)/shard_map/ppermute | solution.py:37
  48.8 17.4 %collective-permute-start.7 = (bf16[8,160,128]{2,1,0:T(8,128)(2,1)S(1)}, bf16[8,160,128]{2,1,0:T(8,128)(2,1)}, u32[]{:S(2)}, u32[]{:S(2)}) collective-permute-start(bf16[8,160,128]{2,1,0:T(8,128)(2,1)S(1)} %all-to-all-done.refs_0_), channel_id=1, source_target_pairs={{0,4},{4,0},{1,5},{5,1},{2,6},{6,2},{3,7},{7,3},{8,12},{12,8},{9,1... | collective-permute-start | bytes 983048 | tf_op jit(solution)/shard_map/ppermute | solution.py:32
  57.2 5.9 %collective-permute-start.5 = (bf16[4,160,128]{2,1,0:T(8,128)(2,1)S(1)}, bf16[4,160,128]{2,1,0:T(8,128)(2,1)}, u32[]{:S(2)}, u32[]{:S(2)}) collective-permute-start(bf16[4,160,128]{2,1,0:T(8,128)(2,1)S(1)} %slice.24), channel_id=1, source_target_pairs={{0,8},{8,16},{16,24},{24,0},{1,9},{9,17},{17,25},{25,1},{2,10},{10... | collective-permute-start | bytes 491528 | tf_op jit(solution)/shard_map/ppermute | solution.py:37
  58.2 7.0 %collective-permute-start.6 = (bf16[4,160,128]{2,1,0:T(8,128)(2,1)S(1)}, bf16[4,160,128]{2,1,0:T(8,128)(2,1)}, u32[]{:S(2)}, u32[]{:S(2)}) collective-permute-start(bf16[4,160,128]{2,1,0:T(8,128)(2,1)S(1)} %slice.25), channel_id=1, source_target_pairs={{0,24},{8,0},{16,8},{24,16},{1,25},{9,1},{17,9},{25,17},{2,26},{10... | collective-permute-start | bytes 491528 | tf_op jit(solution)/shard_map/ppermute | solution.py:37
  61.0 6.1 %collective-permute-start.8 = (bf16[8,160,128]{2,1,0:T(8,128)(2,1)}, bf16[8,160,128]{2,1,0:T(8,128)(2,1)}, u32[]{:S(2)}, u32[]{:S(2)}) collective-permute-start(bf16[8,160,128]{2,1,0:T(8,128)(2,1)} %collective-permute-done.3.refs_1_), channel_id=1, source_target_pairs={{0,4},{4,0},{1,5},{5,1},{2,6},{6,2},{3,7},{7,3},{8,12},{12,8},{9,1... | collective-permute-start | bytes 983048 | tf_op jit(solution)/shard_map/ppermute | solution.py:32
  62.8 4.2 %collective-permute-start.9 = (bf16[8,160,128]{2,1,0:T(8,128)(2,1)}, bf16[8,160,128]{2,1,0:T(8,128)(2,1)}, u32[]{:S(2)}, u32[]{:S(2)}) collective-permute-start(bf16[8,160,128]{2,1,0:T(8,128)(2,1)} %collective-permute-done.4.refs_2_), channel_id=1, source_target_pairs={{0,4},{4,0},{1,5},{5,1},{2,6},{6,2},{3,7},{7,3},{8,12},{12,8},{9,1... | collective-permute-start | bytes 983048 | tf_op jit(solution)/shard_map/ppermute | solution.py:32
  63.1 3.5 %collective-permute-start.10 = (bf16[4,160,128]{2,1,0:T(8,128)(2,1)}, bf16[4,160,128]{2,1,0:T(8,128)(2,1)}, u32[]{:S(2)}, u32[]{:S(2)}) collective-permute-start(bf16[4,160,128]{2,1,0:T(8,128)(2,1)} %collective-permute-done.5.refs_3_), channel_id=1, source_target_pairs={{0,4},{4,0},{1,5},{5,1},{2,6},{6,2},{3,7},{7,3},{8,12},{12,8},{9,1... | collective-permute-start | bytes 491528 | tf_op jit(solution)/shard_map/ppermute | solution.py:32
  65.2 1.8 collective-permute-start.11
  78.9 1.7 collective-permute-start.13
  79.3 3.4 %collective-permute-start.12 = (bf16[4,8,160,128]{3,2,1,0:T(8,128)(2,1)}, bf16[4,8,160,128]{3,2,1,0:T(8,128)(2,1)}, u32[]{:S(2)}, u32[]{:S(2)}) collective-permute-start(bf16[4,8,160,128]{3,2,1,0:T(8,128)(2,1)} %get-tuple-element.72), channel_id=1, source_target_pairs={{0,4},{4,0},{1,5},{5,1},{2,6},{6,2},{3,7},{7,3},{8,12},{12,8},{9,1... | collective-permute-start | bytes 3932168 | tf_op jit(solution)/shard_map/ppermute | solution.py:32
  82.7 11.3 %copy-start.1 = (f32[64,1536]{1,0:T(8,128)S(1)}, f32[64,1536]{1,0:T(8,128)}, u32[]{:S(2)}) copy-start(f32[64,1536]{1,0:T(8,128)} %get-tuple-element.75.pooled_ref) | copy-start | bytes 1179652
  85.5 22.3 %all-to-all-start.1 = ((bf16[4,8,160,128]{3,2,1,0:T(8,128)(2,1)}), bf16[4,8,160,128]{3,2,1,0:T(8,128)(2,1)}, u32[]{:S(2)}, u32[]{:S(2)}) async-start(bf16[4,8,160,128]{3,2,1,0:T(8,128)(2,1)} %bitcast.22), calls=%async_computation.1 | async-start | bytes 2621440 | tf_op jit(solution)/shard_map/all_to_all | solution.py:41
  110.0 14.5 %all-to-all-start.2 = ((bf16[8,160,128]{2,1,0:T(8,128)(2,1)}), bf16[8,160,128]{2,1,0:T(8,128)(2,1)S(1)}, u32[]{:S(2)}, u32[]{:S(2)}) async-start(bf16[8,160,128]{2,1,0:T(8,128)(2,1)} %shard_map.165), calls=%async_computation.2 | async-start | bytes 655360 | tf_op jit(solution)/shard_map/all_to_all | solution.py:41
  114.2 7.8 %copy-start.7 = (bf16[64,1024]{1,0:T(8,128)(2,1)S(1)}, bf16[64,1024]{1,0:T(8,128)(2,1)}, u32[]{:S(2)}) copy-start(bf16[64,1024]{1,0:T(8,128)(2,1)} %get-tuple-element.86) | copy-start | bytes 393220
  119.2 10.0 %collective-permute-start.14 = (bf16[1152,128]{1,0:T(8,128)(2,1)}, bf16[1152,128]{1,0:T(8,128)(2,1)}, u32[]{:S(2)}, u32[]{:S(2)}) collective-permute-start(bf16[1152,128]{1,0:T(8,128)(2,1)} %get-tuple-element.92), channel_id=1, source_target_pairs={{0,8},{8,16},{16,24},{24,0},{1,9},{9,17},{17,25},{25,1},{2,10},{10... | collective-permute-start | bytes 884744 | tf_op jit(solution)/shard_map/ppermute | solution.py:37
  120.3 8.9 %collective-permute-start.15 = (bf16[1152,128]{1,0:T(8,128)(2,1)}, bf16[1152,128]{1,0:T(8,128)(2,1)}, u32[]{:S(2)}, u32[]{:S(2)}) collective-permute-start(bf16[1152,128]{1,0:T(8,128)(2,1)} %get-tuple-element.93), channel_id=1, source_target_pairs={{0,24},{8,0},{16,8},{24,16},{1,25},{9,1},{17,9},{25,17},{2,26},{10... | collective-permute-start | bytes 884744 | tf_op jit(solution)/shard_map/ppermute | solution.py:37
  124.5 0.7 copy-start.2
  129.2 35.9 %copy-start.16 = (bf16[1,1536]{1,0:T(2,128)(2,1)S(1)}, bf16[1,1536]{1,0:T(2,128)(2,1)}, u32[]{:S(2)}) copy-start(bf16[1,1536]{1,0:T(2,128)(2,1)} %get-tuple-element.104) | copy-start | bytes 9220
  129.2 37.9 %copy-start.15 = (bf16[1,1536]{1,0:T(2,128)(2,1)S(1)}, bf16[1,1536]{1,0:T(2,128)(2,1)}, u32[]{:S(2)}) copy-start(bf16[1,1536]{1,0:T(2,128)(2,1)} %get-tuple-element.105) | copy-start | bytes 9220
  129.2 15.9 %all-to-all-start.3 = ((bf16[8,208,128]{2,1,0:T(8,128)(2,1)}), bf16[8,208,128]{2,1,0:T(8,128)(2,1)}, u32[]{:S(2)}, u32[]{:S(2)}) async-start(bf16[8,208,128]{2,1,0:T(8,128)(2,1)} %get-tuple-element.98), calls=%async_computation.3 | async-start | bytes 851968 | tf_op jit(solution)/shard_map/all_to_all | solution.py:41
  136.6 14.3 %collective-permute-start.16 = (bf16[1152,128]{1,0:T(8,128)(2,1)}, bf16[1152,128]{1,0:T(8,128)(2,1)S(1)}, u32[]{:S(2)}, u32[]{:S(2)}) collective-permute-start(bf16[1152,128]{1,0:T(8,128)(2,1)} %get-tuple-element.95), channel_id=1, source_target_pairs={{0,16},{8,24},{16,0},{24,8},{1,17},{9,25},{17,1},{25,9},{2,18},{10... | collective-permute-start | bytes 884744 | tf_op jit(solution)/shard_map/ppermute | solution.py:37
  147.4 4.6 %collective-permute-start.17 = (bf16[288,128]{1,0:T(8,128)(2,1)}, bf16[288,128]{1,0:T(8,128)(2,1)S(1)}, u32[]{:S(2)}, u32[]{:S(2)}) collective-permute-start(bf16[288,128]{1,0:T(8,128)(2,1)} %get-tuple-element.100), channel_id=1, source_target_pairs={{0,8},{8,16},{16,24},{24,0},{1,9},{9,17},{17,25},{25,1},{2,10},{10... | collective-permute-start | bytes 221192 | tf_op jit(solution)/shard_map/ppermute | solution.py:37
  148.5 5.1 %collective-permute-start.18 = (bf16[288,128]{1,0:T(8,128)(2,1)}, bf16[288,128]{1,0:T(8,128)(2,1)S(1)}, u32[]{:S(2)}, u32[]{:S(2)}) collective-permute-start(bf16[288,128]{1,0:T(8,128)(2,1)} %get-tuple-element.101), channel_id=1, source_target_pairs={{0,16},{8,24},{16,0},{24,8},{1,17},{9,25},{17,1},{25,9},{2,18},{10... | collective-permute-start | bytes 221192 | tf_op jit(solution)/shard_map/ppermute | solution.py:37
  149.5 4.2 %collective-permute-start.19 = (bf16[288,128]{1,0:T(8,128)(2,1)}, bf16[288,128]{1,0:T(8,128)(2,1)S(1)}, u32[]{:S(2)}, u32[]{:S(2)}) collective-permute-start(bf16[288,128]{1,0:T(8,128)(2,1)} %get-tuple-element.102), channel_id=1, source_target_pairs={{0,24},{8,0},{16,8},{24,16},{1,25},{9,1},{17,9},{25,17},{2,26},{10... | collective-permute-start | bytes 221192 | tf_op jit(solution)/shard_map/ppermute | solution.py:37
  150.9 2.8 %copy-start.4 = (bf16[1152,128]{1,0:T(8,128)(2,1)}, bf16[1152,128]{1,0:T(8,128)(2,1)S(1)}, u32[]{:S(2)}) copy-start(bf16[1152,128]{1,0:T(8,128)(2,1)S(1)} %collective-permute-done.16.refs_2_) | copy-start | bytes 884740
  152.1 1.7 copy-start.8
  153.6 0.6 copy-start.9
  153.7 0.6 copy-start.10
  156.8 25.7 %all-to-all-start.4 = ((bf16[16,128,128]{2,1,0:T(8,128)(2,1)}), bf16[16,128,128]{2,1,0:T(8,128)(2,1)}, u32[]{:S(2)}, u32[]{:S(2)}) async-start(bf16[16,128,128]{2,1,0:T(8,128)(2,1)} %shard_map.168), calls=%async_computation.4 | async-start | bytes 1048576 | tf_op jit(solution)/shard_map/all_to_all | solution.py:41
  165.1 4.4 %collective-permute-start.20 = (bf16[1,1536]{1,0:T(2,128)(2,1)S(1)}, bf16[1,1536]{1,0:T(2,128)(2,1)S(1)}, u32[]{:S(2)}, u32[]{:S(2)}) collective-permute-start(bf16[1,1536]{1,0:T(2,128)(2,1)S(1)} %copy-done.16), channel_id=1, source_target_pairs={{0,4},{4,8},{8,12},{12,16},{16,20},{20,24},{24,28},{28,32},{32,36}... | collective-permute-start | bytes 9224 | tf_op jit(solution)/shard_map/ppermute | solution.py:652
  167.1 5.3 %collective-permute-start.21 = (bf16[1,1536]{1,0:T(2,128)(2,1)S(1)}, bf16[1,1536]{1,0:T(2,128)(2,1)S(1)}, u32[]{:S(2)}, u32[]{:S(2)}) collective-permute-start(bf16[1,1536]{1,0:T(2,128)(2,1)S(1)} %copy-done.15), channel_id=1, source_target_pairs={{4,0},{8,4},{12,8},{16,12},{20,16},{24,20},{28,24},{32,28},{36,32}... | collective-permute-start | bytes 9224 | tf_op jit(solution)/shard_map/ppermute | solution.py:652
  169.4 3.0 %copy-start.13 = (bf16[1,1536]{1,0:T(2,128)(2,1)}, bf16[1,1536]{1,0:T(2,128)(2,1)S(1)}, u32[]{:S(2)}) copy-start(bf16[1,1536]{1,0:T(2,128)(2,1)S(1)} %collective-permute-done.20.before_ref) | copy-start | bytes 9220
  172.4 0.6 copy-start.14
Sparse Core Ops, SparseCore 0:
  46.1 24.8 all-gather.2
  82.5 25.6 all-gather.4

commit v9 on v8

--- a/solution.py
+++ b/solution.py
@@ -343,8 +343,15 @@
     )(*args)
 
 
-def back_kernel(cores, parts_ref, part_ref, kw_ref, vw_ref, pooled_ref, gain_ref, gy_ref, pairs_ref,
-                spread_ref, half_ref, top_ref, bottom_ref, out_ref, small_ref):
+def back_kernel(cores, parts_ref, part_ref, kw_ref, vw_ref, pooled_ref, gain_ref, gy_ref,
+                pairs_hbm, spread_hbm, half_ref, top_ref, bottom_ref, out_ref, small_ref,
+                pairs_ref, spread_ref, sem):
+    loads = [
+        pltpu.make_async_copy(pairs_hbm, pairs_ref, sem.at[0]),
+        pltpu.make_async_copy(spread_hbm, spread_ref, sem.at[1]),
+    ]
+    for load in loads:
+        load.start()
     gkv = add_up(parts_ref).astype(BF)
     gk, gv = unpack(gkv)
     grad = part_ref[...] + contract_cols(gk, kw_ref[...]) + dot(gv, vw_ref[...])
@@ -360,6 +367,8 @@
     top_ref[...] = half[:1]
     bottom_ref[...] = half[half.shape[0] - 1 :]
     h = half.astype(F32)
+    for load in loads:
+        load.wait()
     taps = pairs_ref.shape[0]
     for k in range(taps):
         small_ref[k : k + 1, :] = jnp.sum(h * pairs_ref[k], axis=0, keepdims=True)
@@ -572,14 +581,14 @@
         front_kernel,
         (shape(nz, packed, qk), shape(pool, width), shape(pool, width, dtype=F32),
          shape(pool, width), shape(pool, width)),
-        [pltpu.VMEM((width // 128, n, 128), F32) for n in (fine + 4, fine)],
+        [pltpu.VMEM((width // 128, fine + 8, 128), F32)] * 2,
         2 * pool * width * (qk + vd),
         first, x, low, high, gain_in, conv_taps, gain_attn, key_weight, value_weight, grad_y,
     )
     pairs, spread = call(
         side_kernel,
         (shape(taps, pool, width, dtype=F32), shape(pool, width, dtype=F32)),
-        [pltpu.VMEM((width // 128, fine + 4, 128), F32)] * 2,
+        [pltpu.VMEM((width // 128, fine + 8, 128), F32)] * 2,
         fine * width * 40,
         x, low, high, gain_in, conv_taps,
     )
@@ -641,14 +650,23 @@
 
     tail = taps + 2
     extra = (tail * tiles // nc + 15) // 16 * 16
-    half, top, bottom, gkv = call(
+    anywhere = pl.BlockSpec(memory_space=pl.ANY)
+    half, top, bottom, gkv = pl.pallas_call(
         functools.partial(back_kernel, nc),
-        (shape(pool, width), shape(1, width), shape(1, width),
-         shape(nx * nc, packed + extra, qk)),
-        [pltpu.VMEM((8, width), F32)],
-        2 * pool * width * (qk + vd),
-        gkv, part, key_weight, value_weight, pooled, gain_attn, grad_y, pairs, spread,
-    )
+        out_shape=(shape(pool, width), shape(1, width), shape(1, width),
+                   shape(nx * nc, packed + extra, qk)),
+        in_specs=[vmem] * 7 + [anywhere] * 2,
+        scratch_shapes=[
+            pltpu.VMEM((8, width), F32),
+            pltpu.VMEM(pairs.shape, F32),
+            pltpu.VMEM(spread.shape, F32),
+            pltpu.SemaphoreType.DMA((2,)),
+        ],
+        compiler_params=pltpu.CompilerParams(vmem_limit_bytes=60 * 2**20),
+        cost_estimate=pl.CostEstimate(
+            flops=2 * pool * width * (qk + vd), bytes_accessed=4 * width * width, transcendentals=0
+        ),
+    )(gkv, part, key_weight, value_weight, pooled, gain_attn, grad_y, pairs, spread)
     before, after = lax.ppermute(bottom, seq, up), lax.ppermute(top, seq, down)
     gkv, *sums[1::2] = lax.optimization_barrier((gkv, *sums[1::2]))
     got = exchange(gkv, ("x", "core"))
@@ -656,7 +674,7 @@
         input_kernel,
         (shape(fine, width),),
         [pltpu.VMEM((pool + 16, width), F32)]
-        + [pltpu.VMEM((width // 128, fine, 128), F32) for _ in range(2)],
+        + [pltpu.VMEM((width // 128, fine + 8, 128), F32)] * 2,
         fine * width * 40,
         x, gain_in, conv_taps, half, before, after,
     )

time: 192 us -> 192 us (level)
    pallas_call x0 -> x1, Pallas kernels: none -> 4.36 us  [shards(): pl.pallas_call(functools.partial(back_kernel, nc), out_shape=(shape(pool,...]
    pallas_call x5 -> x4, Pallas kernels: 15.1 us -> 11.1 us  [call(): pl.pallas_call(kernel, out_shape=out_shape, scratch_shapes=scratch, compi...]
  transfers between devices with their start and end apart: 29 -> 29, of which waited for: 16 -> 16; matrix products, arithmetic and copies ran while one was open for 10% -> 10% of each run, Pallas kernels for 18% -> 19%
where the time goes in v9:
time: 192 us; the launch traced here: 191 us
  starting transfers between devices  63.1 us (33%)
  waiting for transfers between devices  48.4 us (25%)
  Pallas kernels  43.2 us (22%)
  between operations  14.3 us (7%)
  matrix products  11.9 us (6%)
  local copies, waits for them, and re-layouts  5.37 us (3%)
  other arithmetic  4.73 us (2%)
    all_to_all x5, starting transfers between devices, exchange(): return lax.all_to_all(blocks, axis, 0, 0, tiled=True)  33.9 us
    all_to_all x5, waiting for transfers between devices, exchange(): return lax.all_to_all(blocks, axis, 0, 0, tiled=True)  30.3 us
    ppermute x10, starting transfers between devices, shift(): lax.ppermute(block, axis, [(i, (i + step) % count) for i in range(count)])  12.1 us
    pallas_call x1, Pallas kernels, attention(): pl.pallas_call(functools.partial(attention_kernel, scale, heads, group, u...  11.8 us
    pallas_call x4, Pallas kernels, call(): pl.pallas_call(kernel, out_shape=out_shape, scratch_shapes=scratch, compi...  11.1 us
    pallas_call x3, Pallas kernels, flagged(): pl.pallas_call(kernel, out_shape=out_shape, in_specs=[smem] + [vmem] * le...  11 us
    ppermute x10, waiting for transfers between devices, shift(): lax.ppermute(block, axis, [(i, (i + step) % count) for i in range(count)])  9.48 us
    dot_general x2, matrix products, contract_cols(): lax.dot_general(left, right, (((1,), (1,)), ((), ())), preferred_element_...  6.55 us
  transfers between devices with their start and end apart: 29, of which 16 were waited for; matrix products, arithmetic and copies ran while one was open for 10% of the time, Pallas kernels for 19%

profile of v9, /device:TPU:1, one launch (start us, length us, event | category | flops | bytes accessed | tf_op | source)
XLA Modules:
  0.0 191.1 jit_solution(2747037854057169885)
XLA Ops:
  7.2 0.9 slice_bitcast_fusion
  8.1 4.7 %collective-permute-start = (bf16[2,1536]{1,0:T(2,128)(2,1)S(1)}, bf16[2,1536]{1,0:T(2,128)(2,1)S(1)}, u32[]{:S(2)}, u32[]{:S(2)}) collective-permute-start(bf16[2,1536]{1,0:T(2,128)(2,1)S(1)} %get-tuple-element.116), channel_id=1, source_target_pairs={{0,4},{4,8},{8,12},{12,16},{16,20},{20,24},{24,28},{28,32},{32,36}... | collective-permute-start | bytes 18440 | tf_op jit(solution)/shard_map/ppermute | solution.py:563
  12.8 1.9 %collective-permute-start.1 = (bf16[2,1536]{1,0:T(2,128)(2,1)S(1)}, bf16[2,1536]{1,0:T(2,128)(2,1)S(1)}, u32[]{:S(2)}, u32[]{:S(2)}) collective-permute-start(bf16[2,1536]{1,0:T(2,128)(2,1)S(1)} %get-tuple-element.115), channel_id=1, source_target_pairs={{4,0},{8,4},{12,8},{16,12},{20,16},{24,20},{28,24},{32,28},{36,32}... | collective-permute-start | bytes 18440 | tf_op jit(solution)/shard_map/ppermute | solution.py:564
  14.8 3.0 %collective-permute-done.1.high_ref = bf16[2,1536]{1,0:T(2,128)(2,1)S(1)} collective-permute-done((bf16[2,1536]{1,0:T(2,128)(2,1)S(1)}, bf16[2,1536]{1,0:T(2,128)(2,1)S(1)}, u32[]{:S(2)}, u32[]{:S(2)}) %collective-permute-start.1) | collective-permute-done | bytes 6176 | tf_op jit(solution)/shard_map/ppermute | solution.py:564
  17.8 0.6 copy-done.12
  18.4 3.4 %shard_map.160 = (bf16[8,160,128]{2,1,0:T(8,128)(2,1)}, bf16[64,1536]{1,0:T(8,128)(2,1)}, f32[64,1536]{1,0:T(8,128)}, bf16[64,1536]{1,0:T(8,128)(2,1)}, bf16[64,1536]{1,0:T(8,128)(2,1)}) custom-call(s32[1]{0:T(128)} %bitcast.1.first_ref, bf16[128,1536]{1,0:T(8,128)(2,1)} %bitcast.23, bf16[2,1536]{1,0:T(2,128)(2,1)} %copy-done.11, ...), custom_call_target="tpu_custom_call" | custom-call | flops 62914560 | bytes 9437184 | tf_op jit(solution)/shard_map/pallas_call | solution.py:569
  21.8 10.4 %all-to-all-start = ((bf16[8,160,128]{2,1,0:T(8,128)(2,1)}), bf16[8,160,128]{2,1,0:T(8,128)(2,1)S(1)}, u32[]{:S(2)}, u32[]{:S(2)}) async-start(bf16[8,160,128]{2,1,0:T(8,128)(2,1)} %get-tuple-element.62), calls=%async_computation | async-start | bytes 655360 | tf_op jit(solution)/shard_map/all_to_all | solution.py:41
  32.3 4.7 %convolution_convert_fusion.g_ref = bf16[64,1536]{1,0:T(8,128)(2,1)} fusion(bf16[64,1536]{1,0:T(8,128)(2,1)} %bitcast.29, bf16[1536,1536]{1,0:T(8,128)(2,1)} %param.16), kind=kOutput, calls=%fused_computation.2 | convolution fusion | flops 302088192 | bytes 5111808 | tf_op jit(solution)/shard_map/dot_general | solution.py:24
  37.0 1.3 convolution_convert_fusion.1.q_ref
  38.3 1.7 pad_maximum_fusion
  40.0 5.9 %all-to-all-done.refs_0_ = bf16[8,160,128]{2,1,0:T(8,128)(2,1)S(1)} async-done(((bf16[8,160,128]{2,1,0:T(8,128)(2,1)}), bf16[8,160,128]{2,1,0:T(8,128)(2,1)S(1)}, u32[]{:S(2)}, u32[]{:S(2)}) %all-to-all-start) | async-done | bytes 327712 | tf_op jit(solution)/shard_map/all_to_all | solution.py:41
  46.1 2.7 %collective-permute-start.4 = (bf16[8,160,128]{2,1,0:T(8,128)(2,1)S(1)}, bf16[8,160,128]{2,1,0:T(8,128)(2,1)}, u32[]{:S(2)}, u32[]{:S(2)}) collective-permute-start(bf16[8,160,128]{2,1,0:T(8,128)(2,1)S(1)} %all-to-all-done.refs_0_), channel_id=1, source_target_pairs={{0,24},{8,0},{16,8},{24,16},{1,25},{9,1},{17,9},{25,17},{2,26},{10... | collective-permute-start | bytes 983048 | tf_op jit(solution)/shard_map/ppermute | solution.py:37
  48.8 1.0 collective-permute-start.7
  49.8 6.4 %collective-permute-done.3.refs_1_ = bf16[8,160,128]{2,1,0:T(8,128)(2,1)} collective-permute-done((bf16[8,160,128]{2,1,0:T(8,128)(2,1)S(1)}, bf16[8,160,128]{2,1,0:T(8,128)(2,1)}, u32[]{:S(2)}, u32[]{:S(2)}) %collective-permute-start.3) | collective-permute-done | bytes 327712 | tf_op jit(solution)/shard_map/ppermute | solution.py:37
  56.2 0.9 slice.24
  57.3 0.9 slice.25
  58.2 2.7 %collective-permute-start.6 = (bf16[4,160,128]{2,1,0:T(8,128)(2,1)S(1)}, bf16[4,160,128]{2,1,0:T(8,128)(2,1)}, u32[]{:S(2)}, u32[]{:S(2)}) collective-permute-start(bf16[4,160,128]{2,1,0:T(8,128)(2,1)S(1)} %slice.25), channel_id=1, source_target_pairs={{0,24},{8,0},{16,8},{24,16},{1,25},{9,1},{17,9},{25,17},{2,26},{10... | collective-permute-start | bytes 491528 | tf_op jit(solution)/shard_map/ppermute | solution.py:37
  60.9 1.9 collective-permute-start.8
  62.8 0.2 collective-permute-done.5.refs_3_
  63.0 2.2 %collective-permute-start.10 = (bf16[4,160,128]{2,1,0:T(8,128)(2,1)}, bf16[4,160,128]{2,1,0:T(8,128)(2,1)}, u32[]{:S(2)}, u32[]{:S(2)}) collective-permute-start(bf16[4,160,128]{2,1,0:T(8,128)(2,1)} %collective-permute-done.5.refs_3_), channel_id=1, source_target_pairs={{0,4},{4,0},{1,5},{5,1},{2,6},{6,2},{3,7},{7,3},{8,12},{12,8},{9,1... | collective-permute-start | bytes 491528 | tf_op jit(solution)/shard_map/ppermute | solution.py:32
  65.2 0.4 collective-permute-start.11
  65.6 0.6 pad_add_fusion.place_ref
  66.2 0.3 collective-permute-done.10.refs_8_
  66.6 0.5 collective-permute-done.11.refs_9_
  67.0 11.8 %shard_map.161 = (bf16[64,1536]{1,0:T(8,128)(2,1)}, bf16[64,1024]{1,0:T(8,128)(2,1)}, bf16[64,1536]{1,0:T(8,128)(2,1)}, bf16[64,1536]{1,0:T(8,128)(2,1)}, bf16[4...) custom-call(s32[2]{0:T(128)} %pad_add_fusion.place_ref, bf16[64,1024]{1,0:T(8,128)(2,1)} %convolution_convert_fusion.1.q_ref, ...), custom_call_target="tpu_custom_call" | custom-call | flops 4026531840 | bytes 5242880 | tf_op jit(solution)/shard_map/pallas_call | solution.py:264
  78.9 0.4 collective-permute-start.13
  79.3 0.2 collective-permute-start.12
  79.5 1.1 collective-permute-done.13
  80.6 1.7 pad_maximum_fusion.1
  82.3 0.3 collective-permute-done.12
  82.7 2.7 %shard_map.162 = bf16[32,160,128]{2,1,0:T(8,128)(2,1)} custom-call(bf16[32,160,128]{2,1,0:T(8,128)(2,1)} %bitcast.31, bf16[32,160,128]{2,1,0:T(8,128)(2,1)} %bitcast.8.refs_1_), custom_call_target="tpu_custom_call" | custom-call | flops 1310720 | bytes 3932160 | tf_op jit(solution)/shard_map/pallas_call | solution.py:326
  85.4 4.8 %all-to-all-start.1 = ((bf16[4,8,160,128]{3,2,1,0:T(8,128)(2,1)}), bf16[4,8,160,128]{3,2,1,0:T(8,128)(2,1)}, u32[]{:S(2)}, u32[]{:S(2)}) async-start(bf16[4,8,160,128]{3,2,1,0:T(8,128)(2,1)} %bitcast.22), calls=%async_computation.1 | async-start | bytes 2621440 | tf_op jit(solution)/shard_map/all_to_all | solution.py:41
  90.2 3.8 %shard_map.163 = (f32[5,64,1536]{2,1,0:T(8,128)}, f32[64,1536]{1,0:T(8,128)}) custom-call(bf16[128,1536]{1,0:T(8,128)(2,1)} %bitcast.24, bf16[2,1536]{1,0:T(2,128)(2,1)} %copy-done.11, bf16[2,1536]{1,0:T(2,128)(2,1)} %copy-done.12, f32[1536]{0:T(1024)} %gain_ref.3, f32[5,1536]{1,0:T(8,128)} %taps_ref.5), custom_call_target="tpu_custom_call" | custom-call | flops 7864320 | bytes 2801664 | tf_op jit(solution)/shard_map/pallas_call | solution.py:47
  94.0 4.1 %fusion = bf16[64,1536]{1,0:T(8,128)(2,1)} fusion(f32[64,1536]{1,0:T(8,128)S(1)} %copy-done.1, bf16[64,1536]{1,0:T(8,128)(2,1)} %get-tuple-element.76, bf16[1536,1536]{1,0:T(8,128)(2,1)} %param.16), kind=kOutput, calls=%fused_computation.1 | convolution fusion | flops 302186496 | bytes 5505024 | tf_op jit(solution)/shard_map/dot_general | solution.py:28
  98.1 9.7 %all-to-all-done.1.refs_0_ = bf16[4,8,160,128]{3,2,1,0:T(8,128)(2,1)} async-done(((bf16[4,8,160,128]{3,2,1,0:T(8,128)(2,1)}), bf16[4,8,160,128]{3,2,1,0:T(8,128)(2,1)}, u32[]{:S(2)}, u32[]{:S(2)}) %all-to-all-start.1) | async-done | bytes 1310752 | tf_op jit(solution)/shard_map/all_to_all | solution.py:41
  107.8 2.2 %shard_map.165 = bf16[8,160,128]{2,1,0:T(8,128)(2,1)} custom-call(bf16[4,8,160,128]{3,2,1,0:T(8,128)(2,1)} %all-to-all-done.1.refs_0_), custom_call_target="tpu_custom_call" | custom-call | flops 655360 | bytes 1638400 | tf_op jit(solution)/shard_map/pallas_call | solution.py:326
  110.0 3.4 %all-to-all-start.2 = ((bf16[8,160,128]{2,1,0:T(8,128)(2,1)}), bf16[8,160,128]{2,1,0:T(8,128)(2,1)S(1)}, u32[]{:S(2)}, u32[]{:S(2)}) async-start(bf16[8,160,128]{2,1,0:T(8,128)(2,1)} %shard_map.165), calls=%async_computation.2 | async-start | bytes 655360 | tf_op jit(solution)/shard_map/all_to_all | solution.py:41
  113.4 0.7 compare_select_fusion.8.target_ref
  114.1 5.1 %shard_map.164 = (bf16[384,512]{1,0:T(8,128)(2,1)}, bf16[1152,128]{1,0:T(8,128)(2,1)}, bf16[1152,128]{1,0:T(8,128)(2,1)}, bf16[1152,128]{1,0:T(8,128)(2,1)}, bf16[1152,128]{1,0:T(8,128)(2,1)}) custom-call(s32[1]{0:T(128)} %bitcast.1.first_ref, s32[1,1536]{1,0:T(1,128)} %compare_select_fusion.8.target_ref, ...), custom_call_target="tpu_custom_call" | custom-call | flops 1207959552 | bytes 9437184 | tf_op jit(solution)/shard_map/pallas_call | solution.py:569
  119.2 1.1 collective-permute-start.14
  120.3 1.6 collective-permute-start.15
  121.9 1.9 fusion.14.part_ref
  123.8 0.7 all-to-all-done.2.parts_ref
  124.5 0.7 copy-done.2
  125.2 4.4 %shard_map.166 = (bf16[64,1536]{1,0:T(8,128)(2,1)}, bf16[1,1536]{1,0:T(2,128)(2,1)}, bf16[1,1536]{1,0:T(2,128)(2,1)}, bf16[8,208,128]{2,1,0:T(8,128)(2,1)}) custom-call(bf16[8,160,128]{2,1,0:T(8,128)(2,1)} %copy-done.2, f32[64,1536]{1,0:T(8,128)} %fusion.14.part_ref, bf16[1536,128]{1,0:T(8,128)(2,1)} %kw_ref.3, bf16[192,1536]{1,0:T(8,128)(2,1)} %bitcast.27, ...), custom_call_target="tpu_custom_call" | custom-call | flops 62914560 | bytes 9437184 | tf_op jit(solution)/shard_map/pallas_call | solution.py:654
  129.6 7.4 %all-to-all-start.3 = ((bf16[8,208,128]{2,1,0:T(8,128)(2,1)}), bf16[8,208,128]{2,1,0:T(8,128)(2,1)}, u32[]{:S(2)}, u32[]{:S(2)}) async-start(bf16[8,208,128]{2,1,0:T(8,128)(2,1)} %get-tuple-element.98), calls=%async_computation.3 | async-start | bytes 851968 | tf_op jit(solution)/shard_map/all_to_all | solution.py:41
  137.0 0.4 collective-permute-start.16
  137.4 8.2 %all-to-all-done.3.got_ref = bf16[8,208,128]{2,1,0:T(8,128)(2,1)} async-done(((bf16[8,208,128]{2,1,0:T(8,128)(2,1)}), bf16[8,208,128]{2,1,0:T(8,128)(2,1)}, u32[]{:S(2)}, u32[]{:S(2)}) %all-to-all-start.3) | async-done | bytes 426016 | tf_op jit(solution)/shard_map/all_to_all | solution.py:41
  145.5 2.3 %shard_map.167 = (bf16[288,128]{1,0:T(8,128)(2,1)}, bf16[288,128]{1,0:T(8,128)(2,1)}, bf16[288,128]{1,0:T(8,128)(2,1)}, bf16[288,128]{1,0:T(8,128)(2,1)}) custom-call(bf16[384,512]{1,0:T(8,128)(2,1)} %get-tuple-element.97.left_ref, bf16[8,208,128]{2,1,0:T(8,128)(2,1)} %all-to-all-done.3.got_ref), custom_call_target="tpu_custom_call" | custom-call | flops 125829120 | bytes 1114112 | tf_op jit(solution)/shard_map/pallas_call | solution.py:47
  147.8 1.1 collective-permute-start.17
  148.9 1.0 collective-permute-start.18
  149.9 1.4 collective-permute-start.19
  151.3 1.2 collective-permute-done.17.refs_5_
  152.4 1.6 collective-permute-done.18.refs_6_
  154.1 0.5 copy-done.9
  154.7 2.4 %shard_map.168 = bf16[16,128,128]{2,1,0:T(8,128)(2,1)} custom-call(s32[1]{0:T(128)} %bitcast.1.first_ref, bf16[1152,128]{1,0:T(8,128)(2,1)} %get-tuple-element.81.refs_0_, bf16[1152,128]{1,0:T(8,128)(2,1)} %collective-permute-done.14.refs_1_, bf16[1152,128]{1,0:T(8,128)(2,1)} %copy-done.4, bf16[1152,128]{1,0:T(8,128)(2,1)} %collective-permute-done.15.refs_3_, ...), custom_call_target="tpu_custom_call" | custom-call | bytes 9437184 | tf_op jit(solution)/shard_map/pallas_call | solution.py:569
  157.2 7.9 %all-to-all-start.4 = ((bf16[16,128,128]{2,1,0:T(8,128)(2,1)}), bf16[16,128,128]{2,1,0:T(8,128)(2,1)}, u32[]{:S(2)}, u32[]{:S(2)}) async-start(bf16[16,128,128]{2,1,0:T(8,128)(2,1)} %shard_map.168), calls=%async_computation.4 | async-start | bytes 1048576 | tf_op jit(solution)/shard_map/all_to_all | solution.py:41
  165.1 2.4 %collective-permute-start.20 = (bf16[1,1536]{1,0:T(2,128)(2,1)S(1)}, bf16[1,1536]{1,0:T(2,128)(2,1)S(1)}, u32[]{:S(2)}, u32[]{:S(2)}) collective-permute-start(bf16[1,1536]{1,0:T(2,128)(2,1)S(1)} %copy-done.16), channel_id=1, source_target_pairs={{0,4},{4,8},{8,12},{12,16},{16,20},{20,24},{24,28},{28,32},{32,36}... | collective-permute-start | bytes 9224 | tf_op jit(solution)/shard_map/ppermute | solution.py:670
  167.5 1.9 %collective-permute-start.21 = (bf16[1,1536]{1,0:T(2,128)(2,1)S(1)}, bf16[1,1536]{1,0:T(2,128)(2,1)S(1)}, u32[]{:S(2)}, u32[]{:S(2)}) collective-permute-start(bf16[1,1536]{1,0:T(2,128)(2,1)S(1)} %copy-done.15), channel_id=1, source_target_pairs={{4,0},{8,4},{12,8},{16,12},{20,16},{24,20},{28,24},{32,28},{36,32}... | collective-permute-start | bytes 9224 | tf_op jit(solution)/shard_map/ppermute | solution.py:670
  169.4 3.4 %collective-permute-done.21.after_ref = bf16[1,1536]{1,0:T(2,128)(2,1)S(1)} collective-permute-done((bf16[1,1536]{1,0:T(2,128)(2,1)S(1)}, bf16[1,1536]{1,0:T(2,128)(2,1)S(1)}, u32[]{:S(2)}, u32[]{:S(2)}) %collective-permute-start.21) | collective-permute-done | bytes 3104 | tf_op jit(solution)/shard_map/ppermute | solution.py:670
  172.8 0.6 copy-done.14
  173.4 3.3 %shard_map.169 = bf16[128,1536]{1,0:T(8,128)(2,1)} custom-call(bf16[128,1536]{1,0:T(8,128)(2,1)} %bitcast.25, f32[1536]{0:T(1024)} %gain_ref.3, f32[5,1536]{1,0:T(8,128)} %taps_ref.5, bf16[64,1536]{1,0:T(8,128)(2,1)} %get-tuple-element.103.half_ref, bf16[1,1536]{1,0:T(2,128)(2,1)} %copy-done.13, bf16[1,1536]{1,0:T(2,128)(2,1)} %copy-done.14), custom_call_target="tpu_custom_call" | custom-call | flops 7864320 | bytes 1026048 | tf_op jit(solution)/shard_map/pallas_call | solution.py:47
  176.7 5.8 %all-to-all-done.4.got_ref = bf16[16,128,128]{2,1,0:T(8,128)(2,1)} async-done(((bf16[16,128,128]{2,1,0:T(8,128)(2,1)}), bf16[16,128,128]{2,1,0:T(8,128)(2,1)}, u32[]{:S(2)}, u32[]{:S(2)}) %all-to-all-start.4) | async-done | bytes 524320 | tf_op jit(solution)/shard_map/all_to_all | solution.py:41
  182.5 1.7 shard_map.170
  (52 shorter events, 0.6 us)
Async XLA Ops:
  7.2 29.8 %copy-start = (bf16[1536,1024]{1,0:T(8,128)(2,1)S(1)}, bf16[1536,1024]{1,0:T(8,128)(2,1)}, u32[]{:S(2)}) copy-start(bf16[1536,1024]{1,0:T(8,128)(2,1)} %param.13) | copy-start | bytes 9437188
  8.1 6.7 %collective-permute-start = (bf16[2,1536]{1,0:T(2,128)(2,1)S(1)}, bf16[2,1536]{1,0:T(2,128)(2,1)S(1)}, u32[]{:S(2)}, u32[]{:S(2)}) collective-permute-start(bf16[2,1536]{1,0:T(2,128)(2,1)S(1)} %get-tuple-element.116), channel_id=1, source_target_pairs={{0,4},{4,8},{8,12},{12,16},{16,20},{20,24},{24,28},{28,32},{32,36}... | collective-permute-start | bytes 18440 | tf_op jit(solution)/shard_map/ppermute | solution.py:563
  12.8 4.9 %collective-permute-start.1 = (bf16[2,1536]{1,0:T(2,128)(2,1)S(1)}, bf16[2,1536]{1,0:T(2,128)(2,1)S(1)}, u32[]{:S(2)}, u32[]{:S(2)}) collective-permute-start(bf16[2,1536]{1,0:T(2,128)(2,1)S(1)} %get-tuple-element.115), channel_id=1, source_target_pairs={{4,0},{8,4},{12,8},{16,12},{20,16},{24,20},{28,24},{32,28},{36,32}... | collective-permute-start | bytes 18440 | tf_op jit(solution)/shard_map/ppermute | solution.py:564
  14.8 3.0 %copy-start.11 = (bf16[2,1536]{1,0:T(2,128)(2,1)}, bf16[2,1536]{1,0:T(2,128)(2,1)S(1)}, u32[]{:S(2)}) copy-start(bf16[2,1536]{1,0:T(2,128)(2,1)S(1)} %collective-permute-done.low_ref) | copy-start | bytes 18436
  17.8 0.6 copy-start.12
  21.8 16.5 %collective-permute-start.2 = (bf16[64,1536]{1,0:T(8,128)(2,1)}, bf16[64,1536]{1,0:T(8,128)(2,1)}, u32[]{:S(2)}, u32[]{:S(2)}) collective-permute-start(bf16[64,1536]{1,0:T(8,128)(2,1)} %get-tuple-element.67), channel_id=1, source_target_pairs={{0,4},{4,0},{1,5},{5,1},{2,6},{6,2},{3,7},{7,3},{8,12},{12,8},{9,1... | collective-permute-start | bytes 589832 | tf_op jit(solution)/shard_map/ppermute | solution.py:32
  21.8 24.1 %all-to-all-start = ((bf16[8,160,128]{2,1,0:T(8,128)(2,1)}), bf16[8,160,128]{2,1,0:T(8,128)(2,1)S(1)}, u32[]{:S(2)}, u32[]{:S(2)}) async-start(bf16[8,160,128]{2,1,0:T(8,128)(2,1)} %get-tuple-element.62), calls=%async_computation | async-start | bytes 655360 | tf_op jit(solution)/shard_map/all_to_all | solution.py:41
  32.2 82.0 %all-gather.3.cloned.1.call-start = ((), (), s32[]{:S(2)}) async-start(), calls=%async_computation.5 | async-start | bytes 1966080 | tf_op jit(solution)/shard_map/all_gather | solution.py:603
  32.2 4.7 %copy-start.6 = (bf16[64,1536]{1,0:T(8,128)(2,1)S(1)}, bf16[64,1536]{1,0:T(8,128)(2,1)}, u32[]{:S(2)}) copy-start(bf16[64,1536]{1,0:T(8,128)(2,1)} %get-tuple-element.64) | copy-start | bytes 589828
  32.2 6.1 %copy-start.5 = (bf16[64,1536]{1,0:T(8,128)(2,1)S(1)}, bf16[64,1536]{1,0:T(8,128)(2,1)}, u32[]{:S(2)}) copy-start(bf16[64,1536]{1,0:T(8,128)(2,1)} %get-tuple-element.66) | copy-start | bytes 589828
  46.0 21.1 %copy-start.3 = (bf16[8,160,128]{2,1,0:T(8,128)(2,1)}, bf16[8,160,128]{2,1,0:T(8,128)(2,1)S(1)}, u32[]{:S(2)}) copy-start(bf16[8,160,128]{2,1,0:T(8,128)(2,1)S(1)} %all-to-all-done.refs_0_) | copy-start | bytes 983044
  46.0 68.2 %all-gather.5.cloned.1.call-start = ((), (), s32[]{:S(2)}) async-start(), calls=%async_computation.6 | async-start | bytes 1966080 | tf_op jit(solution)/shard_map/all_gather | solution.py:615
  46.0 10.2 %collective-permute-start.3 = (bf16[8,160,128]{2,1,0:T(8,128)(2,1)S(1)}, bf16[8,160,128]{2,1,0:T(8,128)(2,1)}, u32[]{:S(2)}, u32[]{:S(2)}) collective-permute-start(bf16[8,160,128]{2,1,0:T(8,128)(2,1)S(1)} %all-to-all-done.refs_0_), channel_id=1, source_target_pairs={{0,8},{8,16},{16,24},{24,0},{1,9},{9,17},{17,25},{25,1},{2,10},{10... | collective-permute-start | bytes 983048 | tf_op jit(solution)/shard_map/ppermute | solution.py:37
  46.1 11.1 %collective-permute-start.4 = (bf16[8,160,128]{2,1,0:T(8,128)(2,1)S(1)}, bf16[8,160,128]{2,1,0:T(8,128)(2,1)}, u32[]{:S(2)}, u32[]{:S(2)}) collective-permute-start(bf16[8,160,128]{2,1,0:T(8,128)(2,1)S(1)} %all-to-all-done.refs_0_), channel_id=1, source_target_pairs={{0,24},{8,0},{16,8},{24,16},{1,25},{9,1},{17,9},{25,17},{2,26},{10... | collective-permute-start | bytes 983048 | tf_op jit(solution)/shard_map/ppermute | solution.py:37
  48.8 17.4 %collective-permute-start.7 = (bf16[8,160,128]{2,1,0:T(8,128)(2,1)S(1)}, bf16[8,160,128]{2,1,0:T(8,128)(2,1)}, u32[]{:S(2)}, u32[]{:S(2)}) collective-permute-start(bf16[8,160,128]{2,1,0:T(8,128)(2,1)S(1)} %all-to-all-done.refs_0_), channel_id=1, source_target_pairs={{0,4},{4,0},{1,5},{5,1},{2,6},{6,2},{3,7},{7,3},{8,12},{12,8},{9,1... | collective-permute-start | bytes 983048 | tf_op jit(solution)/shard_map/ppermute | solution.py:32
  57.2 5.9 %collective-permute-start.5 = (bf16[4,160,128]{2,1,0:T(8,128)(2,1)S(1)}, bf16[4,160,128]{2,1,0:T(8,128)(2,1)}, u32[]{:S(2)}, u32[]{:S(2)}) collective-permute-start(bf16[4,160,128]{2,1,0:T(8,128)(2,1)S(1)} %slice.24), channel_id=1, source_target_pairs={{0,8},{8,16},{16,24},{24,0},{1,9},{9,17},{17,25},{25,1},{2,10},{10... | collective-permute-start | bytes 491528 | tf_op jit(solution)/shard_map/ppermute | solution.py:37
  58.2 7.0 %collective-permute-start.6 = (bf16[4,160,128]{2,1,0:T(8,128)(2,1)S(1)}, bf16[4,160,128]{2,1,0:T(8,128)(2,1)}, u32[]{:S(2)}, u32[]{:S(2)}) collective-permute-start(bf16[4,160,128]{2,1,0:T(8,128)(2,1)S(1)} %slice.25), channel_id=1, source_target_pairs={{0,24},{8,0},{16,8},{24,16},{1,25},{9,1},{17,9},{25,17},{2,26},{10... | collective-permute-start | bytes 491528 | tf_op jit(solution)/shard_map/ppermute | solution.py:37
  60.9 6.1 %collective-permute-start.8 = (bf16[8,160,128]{2,1,0:T(8,128)(2,1)}, bf16[8,160,128]{2,1,0:T(8,128)(2,1)}, u32[]{:S(2)}, u32[]{:S(2)}) collective-permute-start(bf16[8,160,128]{2,1,0:T(8,128)(2,1)} %collective-permute-done.3.refs_1_), channel_id=1, source_target_pairs={{0,4},{4,0},{1,5},{5,1},{2,6},{6,2},{3,7},{7,3},{8,12},{12,8},{9,1... | collective-permute-start | bytes 983048 | tf_op jit(solution)/shard_map/ppermute | solution.py:32
  62.8 4.2 %collective-permute-start.9 = (bf16[8,160,128]{2,1,0:T(8,128)(2,1)}, bf16[8,160,128]{2,1,0:T(8,128)(2,1)}, u32[]{:S(2)}, u32[]{:S(2)}) collective-permute-start(bf16[8,160,128]{2,1,0:T(8,128)(2,1)} %collective-permute-done.4.refs_2_), channel_id=1, source_target_pairs={{0,4},{4,0},{1,5},{5,1},{2,6},{6,2},{3,7},{7,3},{8,12},{12,8},{9,1... | collective-permute-start | bytes 983048 | tf_op jit(solution)/shard_map/ppermute | solution.py:32
  63.0 3.5 %collective-permute-start.10 = (bf16[4,160,128]{2,1,0:T(8,128)(2,1)}, bf16[4,160,128]{2,1,0:T(8,128)(2,1)}, u32[]{:S(2)}, u32[]{:S(2)}) collective-permute-start(bf16[4,160,128]{2,1,0:T(8,128)(2,1)} %collective-permute-done.5.refs_3_), channel_id=1, source_target_pairs={{0,4},{4,0},{1,5},{5,1},{2,6},{6,2},{3,7},{7,3},{8,12},{12,8},{9,1... | collective-permute-start | bytes 491528 | tf_op jit(solution)/shard_map/ppermute | solution.py:32
  65.2 1.8 collective-permute-start.11
  78.9 1.7 collective-permute-start.13
  79.3 3.4 %collective-permute-start.12 = (bf16[4,8,160,128]{3,2,1,0:T(8,128)(2,1)}, bf16[4,8,160,128]{3,2,1,0:T(8,128)(2,1)}, u32[]{:S(2)}, u32[]{:S(2)}) collective-permute-start(bf16[4,8,160,128]{3,2,1,0:T(8,128)(2,1)} %get-tuple-element.72), channel_id=1, source_target_pairs={{0,4},{4,0},{1,5},{5,1},{2,6},{6,2},{3,7},{7,3},{8,12},{12,8},{9,1... | collective-permute-start | bytes 3932168 | tf_op jit(solution)/shard_map/ppermute | solution.py:32
  82.7 11.3 %copy-start.1 = (f32[64,1536]{1,0:T(8,128)S(1)}, f32[64,1536]{1,0:T(8,128)}, u32[]{:S(2)}) copy-start(f32[64,1536]{1,0:T(8,128)} %get-tuple-element.75.pooled_ref) | copy-start | bytes 1179652
  85.4 22.3 %all-to-all-start.1 = ((bf16[4,8,160,128]{3,2,1,0:T(8,128)(2,1)}), bf16[4,8,160,128]{3,2,1,0:T(8,128)(2,1)}, u32[]{:S(2)}, u32[]{:S(2)}) async-start(bf16[4,8,160,128]{3,2,1,0:T(8,128)(2,1)} %bitcast.22), calls=%async_computation.1 | async-start | bytes 2621440 | tf_op jit(solution)/shard_map/all_to_all | solution.py:41
  110.0 14.5 %all-to-all-start.2 = ((bf16[8,160,128]{2,1,0:T(8,128)(2,1)}), bf16[8,160,128]{2,1,0:T(8,128)(2,1)S(1)}, u32[]{:S(2)}, u32[]{:S(2)}) async-start(bf16[8,160,128]{2,1,0:T(8,128)(2,1)} %shard_map.165), calls=%async_computation.2 | async-start | bytes 655360 | tf_op jit(solution)/shard_map/all_to_all | solution.py:41
  114.1 7.8 %copy-start.7 = (bf16[64,1024]{1,0:T(8,128)(2,1)S(1)}, bf16[64,1024]{1,0:T(8,128)(2,1)}, u32[]{:S(2)}) copy-start(bf16[64,1024]{1,0:T(8,128)(2,1)} %get-tuple-element.86) | copy-start | bytes 393220
  119.2 10.3 %collective-permute-start.14 = (bf16[1152,128]{1,0:T(8,128)(2,1)}, bf16[1152,128]{1,0:T(8,128)(2,1)}, u32[]{:S(2)}, u32[]{:S(2)}) collective-permute-start(bf16[1152,128]{1,0:T(8,128)(2,1)} %get-tuple-element.92), channel_id=1, source_target_pairs={{0,8},{8,16},{16,24},{24,0},{1,9},{9,17},{17,25},{25,1},{2,10},{10... | collective-permute-start | bytes 884744 | tf_op jit(solution)/shard_map/ppermute | solution.py:37
  120.3 9.3 %collective-permute-start.15 = (bf16[1152,128]{1,0:T(8,128)(2,1)}, bf16[1152,128]{1,0:T(8,128)(2,1)}, u32[]{:S(2)}, u32[]{:S(2)}) collective-permute-start(bf16[1152,128]{1,0:T(8,128)(2,1)} %get-tuple-element.93), channel_id=1, source_target_pairs={{0,24},{8,0},{16,8},{24,16},{1,25},{9,1},{17,9},{25,17},{2,26},{10... | collective-permute-start | bytes 884744 | tf_op jit(solution)/shard_map/ppermute | solution.py:37
  124.5 0.7 copy-start.2
  129.6 35.5 %copy-start.16 = (bf16[1,1536]{1,0:T(2,128)(2,1)S(1)}, bf16[1,1536]{1,0:T(2,128)(2,1)}, u32[]{:S(2)}) copy-start(bf16[1,1536]{1,0:T(2,128)(2,1)} %get-tuple-element.104) | copy-start | bytes 9220
  129.6 37.9 %copy-start.15 = (bf16[1,1536]{1,0:T(2,128)(2,1)S(1)}, bf16[1,1536]{1,0:T(2,128)(2,1)}, u32[]{:S(2)}) copy-start(bf16[1,1536]{1,0:T(2,128)(2,1)} %get-tuple-element.105) | copy-start | bytes 9220
  129.6 15.9 %all-to-all-start.3 = ((bf16[8,208,128]{2,1,0:T(8,128)(2,1)}), bf16[8,208,128]{2,1,0:T(8,128)(2,1)}, u32[]{:S(2)}, u32[]{:S(2)}) async-start(bf16[8,208,128]{2,1,0:T(8,128)(2,1)} %get-tuple-element.98), calls=%async_computation.3 | async-start | bytes 851968 | tf_op jit(solution)/shard_map/all_to_all | solution.py:41
  137.0 14.3 %collective-permute-start.16 = (bf16[1152,128]{1,0:T(8,128)(2,1)}, bf16[1152,128]{1,0:T(8,128)(2,1)S(1)}, u32[]{:S(2)}, u32[]{:S(2)}) collective-permute-start(bf16[1152,128]{1,0:T(8,128)(2,1)} %get-tuple-element.95), channel_id=1, source_target_pairs={{0,16},{8,24},{16,0},{24,8},{1,17},{9,25},{17,1},{25,9},{2,18},{10... | collective-permute-start | bytes 884744 | tf_op jit(solution)/shard_map/ppermute | solution.py:37
  147.8 4.6 %collective-permute-start.17 = (bf16[288,128]{1,0:T(8,128)(2,1)}, bf16[288,128]{1,0:T(8,128)(2,1)S(1)}, u32[]{:S(2)}, u32[]{:S(2)}) collective-permute-start(bf16[288,128]{1,0:T(8,128)(2,1)} %get-tuple-element.100), channel_id=1, source_target_pairs={{0,8},{8,16},{16,24},{24,0},{1,9},{9,17},{17,25},{25,1},{2,10},{10... | collective-permute-start | bytes 221192 | tf_op jit(solution)/shard_map/ppermute | solution.py:37
  148.9 5.1 %collective-permute-start.18 = (bf16[288,128]{1,0:T(8,128)(2,1)}, bf16[288,128]{1,0:T(8,128)(2,1)S(1)}, u32[]{:S(2)}, u32[]{:S(2)}) collective-permute-start(bf16[288,128]{1,0:T(8,128)(2,1)} %get-tuple-element.101), channel_id=1, source_target_pairs={{0,16},{8,24},{16,0},{24,8},{1,17},{9,25},{17,1},{25,9},{2,18},{10... | collective-permute-start | bytes 221192 | tf_op jit(solution)/shard_map/ppermute | solution.py:37
  149.9 4.2 %collective-permute-start.19 = (bf16[288,128]{1,0:T(8,128)(2,1)}, bf16[288,128]{1,0:T(8,128)(2,1)S(1)}, u32[]{:S(2)}, u32[]{:S(2)}) collective-permute-start(bf16[288,128]{1,0:T(8,128)(2,1)} %get-tuple-element.102), channel_id=1, source_target_pairs={{0,24},{8,0},{16,8},{24,16},{1,25},{9,1},{17,9},{25,17},{2,26},{10... | collective-permute-start | bytes 221192 | tf_op jit(solution)/shard_map/ppermute | solution.py:37
  151.3 2.8 %copy-start.4 = (bf16[1152,128]{1,0:T(8,128)(2,1)}, bf16[1152,128]{1,0:T(8,128)(2,1)S(1)}, u32[]{:S(2)}) copy-start(bf16[1152,128]{1,0:T(8,128)(2,1)S(1)} %collective-permute-done.16.refs_2_) | copy-start | bytes 884740
  152.4 1.7 copy-start.8
  154.0 0.6 copy-start.9
  154.1 0.6 copy-start.10
  157.2 25.3 %all-to-all-start.4 = ((bf16[16,128,128]{2,1,0:T(8,128)(2,1)}), bf16[16,128,128]{2,1,0:T(8,128)(2,1)}, u32[]{:S(2)}, u32[]{:S(2)}) async-start(bf16[16,128,128]{2,1,0:T(8,128)(2,1)} %shard_map.168), calls=%async_computation.4 | async-start | bytes 1048576 | tf_op jit(solution)/shard_map/all_to_all | solution.py:41
  165.1 4.4 %collective-permute-start.20 = (bf16[1,1536]{1,0:T(2,128)(2,1)S(1)}, bf16[1,1536]{1,0:T(2,128)(2,1)S(1)}, u32[]{:S(2)}, u32[]{:S(2)}) collective-permute-start(bf16[1,1536]{1,0:T(2,128)(2,1)S(1)} %copy-done.16), channel_id=1, source_target_pairs={{0,4},{4,8},{8,12},{12,16},{16,20},{20,24},{24,28},{28,32},{32,36}... | collective-permute-start | bytes 9224 | tf_op jit(solution)/shard_map/ppermute | solution.py:670
  167.5 5.3 %collective-permute-start.21 = (bf16[1,1536]{1,0:T(2,128)(2,1)S(1)}, bf16[1,1536]{1,0:T(2,128)(2,1)S(1)}, u32[]{:S(2)}, u32[]{:S(2)}) collective-permute-start(bf16[1,1536]{1,0:T(2,128)(2,1)S(1)} %copy-done.15), channel_id=1, source_target_pairs={{4,0},{8,4},{12,8},{16,12},{20,16},{24,20},{28,24},{32,28},{36,32}... | collective-permute-start | bytes 9224 | tf_op jit(solution)/shard_map/ppermute | solution.py:670
  169.4 3.4 %copy-start.13 = (bf16[1,1536]{1,0:T(2,128)(2,1)}, bf16[1,1536]{1,0:T(2,128)(2,1)S(1)}, u32[]{:S(2)}) copy-start(bf16[1,1536]{1,0:T(2,128)(2,1)S(1)} %collective-permute-done.20.before_ref) | copy-start | bytes 9220
  172.8 0.6 copy-start.14
Sparse Core Ops, SparseCore 0:
  46.1 24.8 all-gather.2
  82.5 25.6 all-gather.4

commit v10 on v9

--- a/solution.py
+++ b/solution.py
@@ -155,14 +155,11 @@
 
 
 def attention_kernel(scale, heads, group, unroll, place_ref, q_ref, g_ref, *refs):
-    ins = refs[:10]
-    mixed_ref, gq_ref, keep_ref, send_ref, own_ref, others_ref = refs[10:16]
-    kv_ref, gkv_ref, s_ref, gw_ref, in_sem, out_sem = refs[16:]
+    ins = refs[:8]
+    mixed_ref, gq_ref, keep_ref, send_ref, own_ref, others_ref = refs[8:14]
+    kv_ref, gkv_ref, s_ref, gw_ref, in_sem, out_sem = refs[14:]
     ny, nz, packed, _ = own_ref.shape
-    half = nz // 2
-    slots = [(i * nz, nz) for i in range(ny - 1)]
-    slots += [((ny - 1) * nz, half), ((ny - 1) * nz + half, half)]
-    slots += [(ny * nz + at, size) for at, size in slots]
+    slots = [(i * nz, nz) for i in range(2 * ny)]
     loads = [
         pltpu.make_async_copy(ref, kv_ref.at[at : at + size], in_sem.at[k])
         for k, (ref, (at, size)) in enumerate(zip(ins, slots))
@@ -228,7 +225,8 @@
     place = place_ref[0]
     stores = []
     for c, ref in enumerate((own_ref, others_ref)):
-        for i, back in enumerate((0, 1, ny - 1, 2)):
+        ahead = jnp.where(place_ref[1] > 0, 1 + c * (ny - 2), ny - 1 - c * (ny - 2))
+        for i, back in enumerate((0, ahead, ny - ahead, 2)):
             to = lax.rem(place + ny - back, ny)
             at = pl.ds((c * ny + i) * nz, nz)
             stores.append(
@@ -602,10 +600,15 @@
     kv, queries, grad_mixed, early = lax.optimization_barrier((kv, queries, grad_mixed, early))
     early = lax.all_gather(early, "x", axis=0, tiled=True)
 
-    half = nz // 2
-    before, after = shift(kv, "y", 1), shift(kv, "y", ny - 1)
-    pieces = [kv, before, after,
-              shift(before[:half], "y", 1), shift(after[half:], "y", ny - 1)]
+    def around(block, step):
+        pairs = [
+            (y * nc + c, (y + (step if c == 0 else -step)) % ny * nc + c)
+            for y in range(ny) for c in range(nc)
+        ]
+        return lax.ppermute(block, ("y", "core"), pairs)
+
+    near = around(kv, 1)
+    pieces = [kv, near, around(kv, -1), around(near, 1)]
     pieces += [swap(piece) for piece in pieces]
     here = jnp.stack([lax.axis_index("y"), first_core.astype(jnp.int32)])
     mixed, grad_queries, keep, send, gkv, others = attention(

time: 192 us -> 193 us (level)
  waiting for transfers between devices: 48.4 us -> 54.1 us
  starting transfers between devices: 63.1 us -> 60 us
    ppermute x0 -> x3, waiting for transfers between devices: none -> 10.5 us  [around(): return lax.ppermute(block, ('y', 'core'), pairs)]
    ppermute x10 -> x6, starting transfers between devices: 12.1 us -> 5.74 us  [shift(): lax.ppermute(block, axis, [(i, (i + step) % count) for i in range(count)])]
    ppermute x10 -> x6, waiting for transfers between devices: 9.48 us -> 3.6 us  [shift(): lax.ppermute(block, axis, [(i, (i + step) % count) for i in range(count)])]
    ppermute x0 -> x3, starting transfers between devices: none -> 3.71 us  [around(): return lax.ppermute(block, ('y', 'core'), pairs)]
    ppermute x8 -> x7, starting transfers between devices: 6.11 us -> 6.62 us  [swap(): return lax.ppermute(block, 'core', [(0, 1), (1, 0)])]
  transfers between devices with their start and end apart: 29 -> 27, of which waited for: 16 -> 16; matrix products, arithmetic and copies ran while one was open for 10% -> 9% of each run, Pallas kernels for 19% -> 19%
where the time goes in v10:
time: 193 us; the launch traced here: 192 us
  starting transfers between devices  60 us (31%)
  waiting for transfers between devices  54.1 us (28%)
  Pallas kernels  43.1 us (22%)
  between operations  14.3 us (7%)
  matrix products  12 us (6%)
  other arithmetic  4.74 us (2%)
  local copies, waits for them, and re-layouts  3.51 us (2%)
    all_to_all x5, starting transfers between devices, exchange(): return lax.all_to_all(blocks, axis, 0, 0, tiled=True)  32.9 us
    all_to_all x5, waiting for transfers between devices, exchange(): return lax.all_to_all(blocks, axis, 0, 0, tiled=True)  31.5 us
    pallas_call x1, Pallas kernels, attention(): pl.pallas_call(functools.partial(attention_kernel, scale, heads, group, u...  11.8 us
    pallas_call x4, Pallas kernels, call(): pl.pallas_call(kernel, out_shape=out_shape, scratch_shapes=scratch, compi...  11.1 us
    pallas_call x3, Pallas kernels, flagged(): pl.pallas_call(kernel, out_shape=out_shape, in_specs=[smem] + [vmem] * le...  11 us
    ppermute x3, waiting for transfers between devices, around(): return lax.ppermute(block, ('y', 'core'), pairs)  10.5 us
    ppermute x7, starting transfers between devices, swap(): return lax.ppermute(block, 'core', [(0, 1), (1, 0)])  6.62 us
    dot_general x2, matrix products, contract_cols(): lax.dot_general(left, right, (((1,), (1,)), ((), ())), preferred_element_...  6.55 us
  transfers between devices with their start and end apart: 27, of which 16 were waited for; matrix products, arithmetic and copies ran while one was open for 9% of the time, Pallas kernels for 19%

profile of v10, /device:TPU:1, one launch (start us, length us, event | category | flops | bytes accessed | tf_op | source)
XLA Modules:
  0.0 191.7 jit_solution(1599222424359785465)
XLA Ops:
  7.2 0.9 slice_bitcast_fusion
  8.1 4.7 %collective-permute-start = (bf16[2,1536]{1,0:T(2,128)(2,1)S(1)}, bf16[2,1536]{1,0:T(2,128)(2,1)S(1)}, u32[]{:S(2)}, u32[]{:S(2)}) collective-permute-start(bf16[2,1536]{1,0:T(2,128)(2,1)S(1)} %get-tuple-element.116), channel_id=1, source_target_pairs={{0,4},{4,8},{8,12},{12,16},{16,20},{20,24},{24,28},{28,32},{32,36}... | collective-permute-start | bytes 18440 | tf_op jit(solution)/shard_map/ppermute | solution.py:561
  12.8 1.9 %collective-permute-start.1 = (bf16[2,1536]{1,0:T(2,128)(2,1)S(1)}, bf16[2,1536]{1,0:T(2,128)(2,1)S(1)}, u32[]{:S(2)}, u32[]{:S(2)}) collective-permute-start(bf16[2,1536]{1,0:T(2,128)(2,1)S(1)} %get-tuple-element.115), channel_id=1, source_target_pairs={{4,0},{8,4},{12,8},{16,12},{20,16},{24,20},{28,24},{32,28},{36,32}... | collective-permute-start | bytes 18440 | tf_op jit(solution)/shard_map/ppermute | solution.py:562
  14.8 3.0 %collective-permute-done.1.high_ref = bf16[2,1536]{1,0:T(2,128)(2,1)S(1)} collective-permute-done((bf16[2,1536]{1,0:T(2,128)(2,1)S(1)}, bf16[2,1536]{1,0:T(2,128)(2,1)S(1)}, u32[]{:S(2)}, u32[]{:S(2)}) %collective-permute-start.1) | collective-permute-done | bytes 6176 | tf_op jit(solution)/shard_map/ppermute | solution.py:562
  17.8 0.6 copy-done.12
  18.4 3.4 %shard_map.160 = (bf16[8,160,128]{2,1,0:T(8,128)(2,1)}, bf16[64,1536]{1,0:T(8,128)(2,1)}, f32[64,1536]{1,0:T(8,128)}, bf16[64,1536]{1,0:T(8,128)(2,1)}, bf16[64,1536]{1,0:T(8,128)(2,1)}) custom-call(s32[1]{0:T(128)} %bitcast.1.first_ref, bf16[128,1536]{1,0:T(8,128)(2,1)} %bitcast.23, bf16[2,1536]{1,0:T(2,128)(2,1)} %copy-done.11, ...), custom_call_target="tpu_custom_call" | custom-call | flops 62914560 | bytes 9437184 | tf_op jit(solution)/shard_map/pallas_call | solution.py:567
  21.8 10.4 %all-to-all-start = ((bf16[8,160,128]{2,1,0:T(8,128)(2,1)}), bf16[8,160,128]{2,1,0:T(8,128)(2,1)S(1)}, u32[]{:S(2)}, u32[]{:S(2)}) async-start(bf16[8,160,128]{2,1,0:T(8,128)(2,1)} %get-tuple-element.62), calls=%async_computation | async-start | bytes 655360 | tf_op jit(solution)/shard_map/all_to_all | solution.py:41
  32.2 4.7 %convolution_convert_fusion.g_ref = bf16[64,1536]{1,0:T(8,128)(2,1)} fusion(bf16[64,1536]{1,0:T(8,128)(2,1)} %bitcast.29, bf16[1536,1536]{1,0:T(8,128)(2,1)} %param.16), kind=kOutput, calls=%fused_computation.2 | convolution fusion | flops 302088192 | bytes 5111808 | tf_op jit(solution)/shard_map/dot_general | solution.py:24
  37.0 1.3 convolution_convert_fusion.1.q_ref
  38.3 1.7 pad_maximum_fusion
  40.0 5.9 %all-to-all-done.refs_0_ = bf16[8,160,128]{2,1,0:T(8,128)(2,1)S(1)} async-done(((bf16[8,160,128]{2,1,0:T(8,128)(2,1)}), bf16[8,160,128]{2,1,0:T(8,128)(2,1)S(1)}, u32[]{:S(2)}, u32[]{:S(2)}) %all-to-all-start) | async-done | bytes 327712 | tf_op jit(solution)/shard_map/all_to_all | solution.py:41
  46.0 0.0 all-gather.5.cloned.1.call-start
  46.0 1.9 collective-permute-start.3
  47.9 7.0 %collective-permute-done.3.refs_1_ = bf16[8,160,128]{2,1,0:T(8,128)(2,1)} collective-permute-done((bf16[8,160,128]{2,1,0:T(8,128)(2,1)S(1)}, bf16[8,160,128]{2,1,0:T(8,128)(2,1)}, u32[]{:S(2)}, u32[]{:S(2)}) %collective-permute-start.3) | collective-permute-done | bytes 327712 | tf_op jit(solution)/shard_map/ppermute | solution.py:608
  54.9 1.8 collective-permute-start.5
  56.8 0.9 collective-permute-start.6
  57.6 0.1 collective-permute-done.4.refs_2_
  57.8 0.4 collective-permute-start.8
  58.1 3.3 %collective-permute-done.5.refs_3_ = bf16[8,160,128]{2,1,0:T(8,128)(2,1)} collective-permute-done((bf16[8,160,128]{2,1,0:T(8,128)(2,1)}, bf16[8,160,128]{2,1,0:T(8,128)(2,1)}, u32[]{:S(2)}, u32[]{:S(2)}) %collective-permute-start.5) | collective-permute-done | bytes 327712 | tf_op jit(solution)/shard_map/ppermute | solution.py:608
  61.5 4.8 %collective-permute-start.9 = (bf16[8,160,128]{2,1,0:T(8,128)(2,1)}, bf16[8,160,128]{2,1,0:T(8,128)(2,1)}, u32[]{:S(2)}, u32[]{:S(2)}) collective-permute-start(bf16[8,160,128]{2,1,0:T(8,128)(2,1)} %collective-permute-done.5.refs_3_), channel_id=1, source_target_pairs={{0,4},{4,0},{1,5},{5,1},{2,6},{6,2},{3,7},{7,3},{8,12},{12,8},{9,1... | collective-permute-start | bytes 983048 | tf_op jit(solution)/shard_map/ppermute | solution.py:32
  66.2 0.6 pad_add_fusion.place_ref
  66.8 1.0 collective-permute-done.9.refs_7_
  67.8 11.8 %shard_map.161 = (bf16[64,1536]{1,0:T(8,128)(2,1)}, bf16[64,1024]{1,0:T(8,128)(2,1)}, bf16[64,1536]{1,0:T(8,128)(2,1)}, bf16[64,1536]{1,0:T(8,128)(2,1)}, bf16[4...) custom-call(s32[2]{0:T(128)} %pad_add_fusion.place_ref, bf16[64,1024]{1,0:T(8,128)(2,1)} %convolution_convert_fusion.1.q_ref, ...), custom_call_target="tpu_custom_call" | custom-call | flops 4026531840 | bytes 5242880 | tf_op jit(solution)/shard_map/pallas_call | solution.py:262
  79.6 0.4 collective-permute-start.11
  80.1 0.2 collective-permute-start.10
  80.2 1.1 collective-permute-done.11
  81.4 1.7 pad_maximum_fusion.1
  83.1 0.3 collective-permute-done.10
  83.4 2.7 %shard_map.162 = bf16[32,160,128]{2,1,0:T(8,128)(2,1)} custom-call(bf16[32,160,128]{2,1,0:T(8,128)(2,1)} %bitcast.31, bf16[32,160,128]{2,1,0:T(8,128)(2,1)} %bitcast.8.refs_1_), custom_call_target="tpu_custom_call" | custom-call | flops 1310720 | bytes 3932160 | tf_op jit(solution)/shard_map/pallas_call | solution.py:324
  86.2 4.3 %all-to-all-start.1 = ((bf16[4,8,160,128]{3,2,1,0:T(8,128)(2,1)}), bf16[4,8,160,128]{3,2,1,0:T(8,128)(2,1)}, u32[]{:S(2)}, u32[]{:S(2)}) async-start(bf16[4,8,160,128]{3,2,1,0:T(8,128)(2,1)} %bitcast.22), calls=%async_computation.1 | async-start | bytes 2621440 | tf_op jit(solution)/shard_map/all_to_all | solution.py:41
  90.5 3.7 %shard_map.163 = (f32[5,64,1536]{2,1,0:T(8,128)}, f32[64,1536]{1,0:T(8,128)}) custom-call(bf16[128,1536]{1,0:T(8,128)(2,1)} %bitcast.24, bf16[2,1536]{1,0:T(2,128)(2,1)} %copy-done.11, bf16[2,1536]{1,0:T(2,128)(2,1)} %copy-done.12, f32[1536]{0:T(1024)} %gain_ref.3, f32[5,1536]{1,0:T(8,128)} %taps_ref.5), custom_call_target="tpu_custom_call" | custom-call | flops 7864320 | bytes 2801664 | tf_op jit(solution)/shard_map/pallas_call | solution.py:47
  94.3 4.1 %fusion = bf16[64,1536]{1,0:T(8,128)(2,1)} fusion(f32[64,1536]{1,0:T(8,128)S(1)} %copy-done.1, bf16[64,1536]{1,0:T(8,128)(2,1)} %get-tuple-element.76, bf16[1536,1536]{1,0:T(8,128)(2,1)} %param.16), kind=kOutput, calls=%fused_computation.1 | convolution fusion | flops 302186496 | bytes 5505024 | tf_op jit(solution)/shard_map/dot_general | solution.py:28
  98.4 10.0 %all-to-all-done.1.refs_0_ = bf16[4,8,160,128]{3,2,1,0:T(8,128)(2,1)} async-done(((bf16[4,8,160,128]{3,2,1,0:T(8,128)(2,1)}), bf16[4,8,160,128]{3,2,1,0:T(8,128)(2,1)}, u32[]{:S(2)}, u32[]{:S(2)}) %all-to-all-start.1) | async-done | bytes 1310752 | tf_op jit(solution)/shard_map/all_to_all | solution.py:41
  108.3 2.2 %shard_map.165 = bf16[8,160,128]{2,1,0:T(8,128)(2,1)} custom-call(bf16[4,8,160,128]{3,2,1,0:T(8,128)(2,1)} %all-to-all-done.1.refs_0_), custom_call_target="tpu_custom_call" | custom-call | flops 655360 | bytes 1638400 | tf_op jit(solution)/shard_map/pallas_call | solution.py:324
  110.6 3.4 %all-to-all-start.2 = ((bf16[8,160,128]{2,1,0:T(8,128)(2,1)}), bf16[8,160,128]{2,1,0:T(8,128)(2,1)S(1)}, u32[]{:S(2)}, u32[]{:S(2)}) async-start(bf16[8,160,128]{2,1,0:T(8,128)(2,1)} %shard_map.165), calls=%async_computation.2 | async-start | bytes 655360 | tf_op jit(solution)/shard_map/all_to_all | solution.py:41
  114.0 0.7 compare_select_fusion.8.target_ref
  114.7 5.1 %shard_map.164 = (bf16[384,512]{1,0:T(8,128)(2,1)}, bf16[1152,128]{1,0:T(8,128)(2,1)}, bf16[1152,128]{1,0:T(8,128)(2,1)}, bf16[1152,128]{1,0:T(8,128)(2,1)}, bf16[1152,128]{1,0:T(8,128)(2,1)}) custom-call(s32[1]{0:T(128)} %bitcast.1.first_ref, s32[1,1536]{1,0:T(1,128)} %compare_select_fusion.8.target_ref, ...), custom_call_target="tpu_custom_call" | custom-call | flops 1207959552 | bytes 9437184 | tf_op jit(solution)/shard_map/pallas_call | solution.py:567
  119.8 0.3 collective-permute-start.12
  120.1 2.4 %collective-permute-start.13 = (bf16[1152,128]{1,0:T(8,128)(2,1)}, bf16[1152,128]{1,0:T(8,128)(2,1)}, u32[]{:S(2)}, u32[]{:S(2)}) collective-permute-start(bf16[1152,128]{1,0:T(8,128)(2,1)} %get-tuple-element.93), channel_id=1, source_target_pairs={{0,24},{8,0},{16,8},{24,16},{1,25},{9,1},{17,9},{25,17},{2,26},{10... | collective-permute-start | bytes 884744 | tf_op jit(solution)/shard_map/ppermute | solution.py:37
  122.5 1.8 fusion.14.part_ref
  124.4 1.3 all-to-all-done.2.parts_ref
  125.6 0.7 copy-done.2
  126.4 4.3 %shard_map.166 = (bf16[64,1536]{1,0:T(8,128)(2,1)}, bf16[1,1536]{1,0:T(2,128)(2,1)}, bf16[1,1536]{1,0:T(2,128)(2,1)}, bf16[8,208,128]{2,1,0:T(8,128)(2,1)}) custom-call(bf16[8,160,128]{2,1,0:T(8,128)(2,1)} %copy-done.2, f32[64,1536]{1,0:T(8,128)} %fusion.14.part_ref, bf16[1536,128]{1,0:T(8,128)(2,1)} %kw_ref.3, bf16[192,1536]{1,0:T(8,128)(2,1)} %bitcast.27, ...), custom_call_target="tpu_custom_call" | custom-call | flops 62914560 | bytes 9437184 | tf_op jit(solution)/shard_map/pallas_call | solution.py:657
  130.8 6.8 %all-to-all-start.3 = ((bf16[8,208,128]{2,1,0:T(8,128)(2,1)}), bf16[8,208,128]{2,1,0:T(8,128)(2,1)}, u32[]{:S(2)}, u32[]{:S(2)}) async-start(bf16[8,208,128]{2,1,0:T(8,128)(2,1)} %get-tuple-element.98), calls=%async_computation.3 | async-start | bytes 851968 | tf_op jit(solution)/shard_map/all_to_all | solution.py:41
  137.6 0.4 collective-permute-start.14
  138.0 8.1 %all-to-all-done.3.got_ref = bf16[8,208,128]{2,1,0:T(8,128)(2,1)} async-done(((bf16[8,208,128]{2,1,0:T(8,128)(2,1)}), bf16[8,208,128]{2,1,0:T(8,128)(2,1)}, u32[]{:S(2)}, u32[]{:S(2)}) %all-to-all-start.3) | async-done | bytes 426016 | tf_op jit(solution)/shard_map/all_to_all | solution.py:41
  146.1 2.3 %shard_map.167 = (bf16[288,128]{1,0:T(8,128)(2,1)}, bf16[288,128]{1,0:T(8,128)(2,1)}, bf16[288,128]{1,0:T(8,128)(2,1)}, bf16[288,128]{1,0:T(8,128)(2,1)}) custom-call(bf16[384,512]{1,0:T(8,128)(2,1)} %get-tuple-element.97.left_ref, bf16[8,208,128]{2,1,0:T(8,128)(2,1)} %all-to-all-done.3.got_ref), custom_call_target="tpu_custom_call" | custom-call | flops 125829120 | bytes 1114112 | tf_op jit(solution)/shard_map/pallas_call | solution.py:47
  148.4 0.3 collective-permute-start.15
  148.7 1.8 collective-permute-start.16
  150.5 0.6 collective-permute-start.17
  151.1 2.3 %collective-permute-done.15.refs_5_ = bf16[288,128]{1,0:T(8,128)(2,1)S(1)} collective-permute-done((bf16[288,128]{1,0:T(8,128)(2,1)}, bf16[288,128]{1,0:T(8,128)(2,1)S(1)}, u32[]{:S(2)}, u32[]{:S(2)}) %collective-permute-start.15) | collective-permute-done | bytes 73760 | tf_op jit(solution)/shard_map/ppermute | solution.py:37
  153.4 0.9 collective-permute-done.16.refs_6_
  154.2 0.4 collective-permute-done.17.refs_7_
  154.7 0.2 copy-done.9
  154.9 0.4 copy-done.10
  155.3 2.5 %shard_map.168 = bf16[16,128,128]{2,1,0:T(8,128)(2,1)} custom-call(s32[1]{0:T(128)} %bitcast.1.first_ref, bf16[1152,128]{1,0:T(8,128)(2,1)} %get-tuple-element.81.refs_0_, bf16[1152,128]{1,0:T(8,128)(2,1)} %collective-permute-done.12.refs_1_, bf16[1152,128]{1,0:T(8,128)(2,1)} %copy-done.4, bf16[1152,128]{1,0:T(8,128)(2,1)} %collective-permute-done.13.refs_3_, ...), custom_call_target="tpu_custom_call" | custom-call | bytes 9437184 | tf_op jit(solution)/shard_map/pallas_call | solution.py:567
  157.8 7.9 %all-to-all-start.4 = ((bf16[16,128,128]{2,1,0:T(8,128)(2,1)}), bf16[16,128,128]{2,1,0:T(8,128)(2,1)}, u32[]{:S(2)}, u32[]{:S(2)}) async-start(bf16[16,128,128]{2,1,0:T(8,128)(2,1)} %shard_map.168), calls=%async_computation.4 | async-start | bytes 1048576 | tf_op jit(solution)/shard_map/all_to_all | solution.py:41
  165.7 2.0 %collective-permute-start.18 = (bf16[1,1536]{1,0:T(2,128)(2,1)S(1)}, bf16[1,1536]{1,0:T(2,128)(2,1)S(1)}, u32[]{:S(2)}, u32[]{:S(2)}) collective-permute-start(bf16[1,1536]{1,0:T(2,128)(2,1)S(1)} %copy-done.16), channel_id=1, source_target_pairs={{0,4},{4,8},{8,12},{12,16},{16,20},{20,24},{24,28},{28,32},{32,36}... | collective-permute-start | bytes 9224 | tf_op jit(solution)/shard_map/ppermute | solution.py:673
  167.7 2.3 %collective-permute-start.19 = (bf16[1,1536]{1,0:T(2,128)(2,1)S(1)}, bf16[1,1536]{1,0:T(2,128)(2,1)S(1)}, u32[]{:S(2)}, u32[]{:S(2)}) collective-permute-start(bf16[1,1536]{1,0:T(2,128)(2,1)S(1)} %copy-done.15), channel_id=1, source_target_pairs={{4,0},{8,4},{12,8},{16,12},{20,16},{24,20},{28,24},{32,28},{36,32}... | collective-permute-start | bytes 9224 | tf_op jit(solution)/shard_map/ppermute | solution.py:673
  170.0 3.0 %collective-permute-done.19.after_ref = bf16[1,1536]{1,0:T(2,128)(2,1)S(1)} collective-permute-done((bf16[1,1536]{1,0:T(2,128)(2,1)S(1)}, bf16[1,1536]{1,0:T(2,128)(2,1)S(1)}, u32[]{:S(2)}, u32[]{:S(2)}) %collective-permute-start.19) | collective-permute-done | bytes 3104 | tf_op jit(solution)/shard_map/ppermute | solution.py:673
  173.0 0.6 copy-done.14
  173.6 3.3 %shard_map.169 = bf16[128,1536]{1,0:T(8,128)(2,1)} custom-call(bf16[128,1536]{1,0:T(8,128)(2,1)} %bitcast.25, f32[1536]{0:T(1024)} %gain_ref.3, f32[5,1536]{1,0:T(8,128)} %taps_ref.5, bf16[64,1536]{1,0:T(8,128)(2,1)} %get-tuple-element.103.half_ref, bf16[1,1536]{1,0:T(2,128)(2,1)} %copy-done.13, bf16[1,1536]{1,0:T(2,128)(2,1)} %copy-done.14), custom_call_target="tpu_custom_call" | custom-call | flops 7864320 | bytes 1026048 | tf_op jit(solution)/shard_map/pallas_call | solution.py:47
  176.9 6.2 %all-to-all-done.4.got_ref = bf16[16,128,128]{2,1,0:T(8,128)(2,1)} async-done(((bf16[16,128,128]{2,1,0:T(8,128)(2,1)}), bf16[16,128,128]{2,1,0:T(8,128)(2,1)}, u32[]{:S(2)}, u32[]{:S(2)}) %all-to-all-start.4) | async-done | bytes 524320 | tf_op jit(solution)/shard_map/all_to_all | solution.py:41
  183.1 1.7 shard_map.170
  (46 shorter events, 0.2 us)
Async XLA Ops:
  7.2 29.8 %copy-start = (bf16[1536,1024]{1,0:T(8,128)(2,1)S(1)}, bf16[1536,1024]{1,0:T(8,128)(2,1)}, u32[]{:S(2)}) copy-start(bf16[1536,1024]{1,0:T(8,128)(2,1)} %param.13) | copy-start | bytes 9437188
  8.1 6.7 %collective-permute-start = (bf16[2,1536]{1,0:T(2,128)(2,1)S(1)}, bf16[2,1536]{1,0:T(2,128)(2,1)S(1)}, u32[]{:S(2)}, u32[]{:S(2)}) collective-permute-start(bf16[2,1536]{1,0:T(2,128)(2,1)S(1)} %get-tuple-element.116), channel_id=1, source_target_pairs={{0,4},{4,8},{8,12},{12,16},{16,20},{20,24},{24,28},{28,32},{32,36}... | collective-permute-start | bytes 18440 | tf_op jit(solution)/shard_map/ppermute | solution.py:561
  12.8 4.9 %collective-permute-start.1 = (bf16[2,1536]{1,0:T(2,128)(2,1)S(1)}, bf16[2,1536]{1,0:T(2,128)(2,1)S(1)}, u32[]{:S(2)}, u32[]{:S(2)}) collective-permute-start(bf16[2,1536]{1,0:T(2,128)(2,1)S(1)} %get-tuple-element.115), channel_id=1, source_target_pairs={{4,0},{8,4},{12,8},{16,12},{20,16},{24,20},{28,24},{32,28},{36,32}... | collective-permute-start | bytes 18440 | tf_op jit(solution)/shard_map/ppermute | solution.py:562
  14.8 3.0 %copy-start.11 = (bf16[2,1536]{1,0:T(2,128)(2,1)}, bf16[2,1536]{1,0:T(2,128)(2,1)S(1)}, u32[]{:S(2)}) copy-start(bf16[2,1536]{1,0:T(2,128)(2,1)S(1)} %collective-permute-done.low_ref) | copy-start | bytes 18436
  17.8 0.6 copy-start.12
  21.8 16.5 %collective-permute-start.2 = (bf16[64,1536]{1,0:T(8,128)(2,1)}, bf16[64,1536]{1,0:T(8,128)(2,1)}, u32[]{:S(2)}, u32[]{:S(2)}) collective-permute-start(bf16[64,1536]{1,0:T(8,128)(2,1)} %get-tuple-element.67), channel_id=1, source_target_pairs={{0,4},{4,0},{1,5},{5,1},{2,6},{6,2},{3,7},{7,3},{8,12},{12,8},{9,1... | collective-permute-start | bytes 589832 | tf_op jit(solution)/shard_map/ppermute | solution.py:32
  21.8 24.1 %all-to-all-start = ((bf16[8,160,128]{2,1,0:T(8,128)(2,1)}), bf16[8,160,128]{2,1,0:T(8,128)(2,1)S(1)}, u32[]{:S(2)}, u32[]{:S(2)}) async-start(bf16[8,160,128]{2,1,0:T(8,128)(2,1)} %get-tuple-element.62), calls=%async_computation | async-start | bytes 655360 | tf_op jit(solution)/shard_map/all_to_all | solution.py:41
  32.2 82.5 %all-gather.3.cloned.1.call-start = ((), (), s32[]{:S(2)}) async-start(), calls=%async_computation.5 | async-start | bytes 1966080 | tf_op jit(solution)/shard_map/all_gather | solution.py:601
  32.2 4.7 %copy-start.6 = (bf16[64,1536]{1,0:T(8,128)(2,1)S(1)}, bf16[64,1536]{1,0:T(8,128)(2,1)}, u32[]{:S(2)}) copy-start(bf16[64,1536]{1,0:T(8,128)(2,1)} %get-tuple-element.64) | copy-start | bytes 589828
  32.2 6.1 %copy-start.5 = (bf16[64,1536]{1,0:T(8,128)(2,1)S(1)}, bf16[64,1536]{1,0:T(8,128)(2,1)}, u32[]{:S(2)}) copy-start(bf16[64,1536]{1,0:T(8,128)(2,1)} %get-tuple-element.66) | copy-start | bytes 589828
  45.9 21.9 %copy-start.3 = (bf16[8,160,128]{2,1,0:T(8,128)(2,1)}, bf16[8,160,128]{2,1,0:T(8,128)(2,1)S(1)}, u32[]{:S(2)}) copy-start(bf16[8,160,128]{2,1,0:T(8,128)(2,1)S(1)} %all-to-all-done.refs_0_) | copy-start | bytes 983044
  46.0 68.8 %all-gather.5.cloned.1.call-start = ((), (), s32[]{:S(2)}) async-start(), calls=%async_computation.6 | async-start | bytes 1966080 | tf_op jit(solution)/shard_map/all_gather | solution.py:618
  46.0 8.9 %collective-permute-start.3 = (bf16[8,160,128]{2,1,0:T(8,128)(2,1)S(1)}, bf16[8,160,128]{2,1,0:T(8,128)(2,1)}, u32[]{:S(2)}, u32[]{:S(2)}) collective-permute-start(bf16[8,160,128]{2,1,0:T(8,128)(2,1)S(1)} %all-to-all-done.refs_0_), channel_id=1, source_target_pairs={{0,8},{4,28},{8,16},{12,4},{16,24},{20,12},{24,0},{28,20},{1,9},{5... | collective-permute-start | bytes 983048 | tf_op jit(solution)/shard_map/ppermute | solution.py:608
  47.9 9.9 %collective-permute-start.4 = (bf16[8,160,128]{2,1,0:T(8,128)(2,1)S(1)}, bf16[8,160,128]{2,1,0:T(8,128)(2,1)}, u32[]{:S(2)}, u32[]{:S(2)}) collective-permute-start(bf16[8,160,128]{2,1,0:T(8,128)(2,1)S(1)} %all-to-all-done.refs_0_), channel_id=1, source_target_pairs={{0,24},{4,12},{8,0},{12,20},{16,8},{20,28},{24,16},{28,4},{1,25},{... | collective-permute-start | bytes 983048 | tf_op jit(solution)/shard_map/ppermute | solution.py:608
  54.9 6.5 %collective-permute-start.5 = (bf16[8,160,128]{2,1,0:T(8,128)(2,1)}, bf16[8,160,128]{2,1,0:T(8,128)(2,1)}, u32[]{:S(2)}, u32[]{:S(2)}) collective-permute-start(bf16[8,160,128]{2,1,0:T(8,128)(2,1)} %collective-permute-done.3.refs_1_), channel_id=1, source_target_pairs={{0,8},{4,28},{8,16},{12,4},{16,24},{20,12},{24,0},{28,20},{1,9},{5... | collective-permute-start | bytes 983048 | tf_op jit(solution)/shard_map/ppermute | solution.py:608
  56.8 10.1 %collective-permute-start.6 = (bf16[8,160,128]{2,1,0:T(8,128)(2,1)S(1)}, bf16[8,160,128]{2,1,0:T(8,128)(2,1)}, u32[]{:S(2)}, u32[]{:S(2)}) collective-permute-start(bf16[8,160,128]{2,1,0:T(8,128)(2,1)S(1)} %all-to-all-done.refs_0_), channel_id=1, source_target_pairs={{0,4},{4,0},{1,5},{5,1},{2,6},{6,2},{3,7},{7,3},{8,12},{12,8},{9,1... | collective-permute-start | bytes 983048 | tf_op jit(solution)/shard_map/ppermute | solution.py:32
  57.6 9.2 %collective-permute-start.7 = (bf16[8,160,128]{2,1,0:T(8,128)(2,1)}, bf16[8,160,128]{2,1,0:T(8,128)(2,1)}, u32[]{:S(2)}, u32[]{:S(2)}) collective-permute-start(bf16[8,160,128]{2,1,0:T(8,128)(2,1)} %collective-permute-done.3.refs_1_), channel_id=1, source_target_pairs={{0,4},{4,0},{1,5},{5,1},{2,6},{6,2},{3,7},{7,3},{8,12},{12,8},{9,1... | collective-permute-start | bytes 983048 | tf_op jit(solution)/shard_map/ppermute | solution.py:32
  57.8 9.0 %collective-permute-start.8 = (bf16[8,160,128]{2,1,0:T(8,128)(2,1)}, bf16[8,160,128]{2,1,0:T(8,128)(2,1)}, u32[]{:S(2)}, u32[]{:S(2)}) collective-permute-start(bf16[8,160,128]{2,1,0:T(8,128)(2,1)} %collective-permute-done.4.refs_2_), channel_id=1, source_target_pairs={{0,4},{4,0},{1,5},{5,1},{2,6},{6,2},{3,7},{7,3},{8,12},{12,8},{9,1... | collective-permute-start | bytes 983048 | tf_op jit(solution)/shard_map/ppermute | solution.py:32
  61.5 6.4 %collective-permute-start.9 = (bf16[8,160,128]{2,1,0:T(8,128)(2,1)}, bf16[8,160,128]{2,1,0:T(8,128)(2,1)}, u32[]{:S(2)}, u32[]{:S(2)}) collective-permute-start(bf16[8,160,128]{2,1,0:T(8,128)(2,1)} %collective-permute-done.5.refs_3_), channel_id=1, source_target_pairs={{0,4},{4,0},{1,5},{5,1},{2,6},{6,2},{3,7},{7,3},{8,12},{12,8},{9,1... | collective-permute-start | bytes 983048 | tf_op jit(solution)/shard_map/ppermute | solution.py:32
  79.6 1.7 collective-permute-start.11
  80.1 3.4 %collective-permute-start.10 = (bf16[4,8,160,128]{3,2,1,0:T(8,128)(2,1)}, bf16[4,8,160,128]{3,2,1,0:T(8,128)(2,1)}, u32[]{:S(2)}, u32[]{:S(2)}) collective-permute-start(bf16[4,8,160,128]{3,2,1,0:T(8,128)(2,1)} %get-tuple-element.72), channel_id=1, source_target_pairs={{0,4},{4,0},{1,5},{5,1},{2,6},{6,2},{3,7},{7,3},{8,12},{12,8},{9,1... | collective-permute-start | bytes 3932168 | tf_op jit(solution)/shard_map/ppermute | solution.py:32
  83.4 10.8 %copy-start.1 = (f32[64,1536]{1,0:T(8,128)S(1)}, f32[64,1536]{1,0:T(8,128)}, u32[]{:S(2)}) copy-start(f32[64,1536]{1,0:T(8,128)} %get-tuple-element.75.pooled_ref) | copy-start | bytes 1179652
  86.2 22.2 %all-to-all-start.1 = ((bf16[4,8,160,128]{3,2,1,0:T(8,128)(2,1)}), bf16[4,8,160,128]{3,2,1,0:T(8,128)(2,1)}, u32[]{:S(2)}, u32[]{:S(2)}) async-start(bf16[4,8,160,128]{3,2,1,0:T(8,128)(2,1)} %bitcast.22), calls=%async_computation.1 | async-start | bytes 2621440 | tf_op jit(solution)/shard_map/all_to_all | solution.py:41
  110.6 15.1 %all-to-all-start.2 = ((bf16[8,160,128]{2,1,0:T(8,128)(2,1)}), bf16[8,160,128]{2,1,0:T(8,128)(2,1)S(1)}, u32[]{:S(2)}, u32[]{:S(2)}) async-start(bf16[8,160,128]{2,1,0:T(8,128)(2,1)} %shard_map.165), calls=%async_computation.2 | async-start | bytes 655360 | tf_op jit(solution)/shard_map/all_to_all | solution.py:41
  114.7 7.8 %copy-start.7 = (bf16[64,1024]{1,0:T(8,128)(2,1)S(1)}, bf16[64,1024]{1,0:T(8,128)(2,1)}, u32[]{:S(2)}) copy-start(bf16[64,1024]{1,0:T(8,128)(2,1)} %get-tuple-element.86) | copy-start | bytes 393220
  119.8 10.9 %collective-permute-start.12 = (bf16[1152,128]{1,0:T(8,128)(2,1)}, bf16[1152,128]{1,0:T(8,128)(2,1)}, u32[]{:S(2)}, u32[]{:S(2)}) collective-permute-start(bf16[1152,128]{1,0:T(8,128)(2,1)} %get-tuple-element.92), channel_id=1, source_target_pairs={{0,8},{8,16},{16,24},{24,0},{1,9},{9,17},{17,25},{25,1},{2,10},{10... | collective-permute-start | bytes 884744 | tf_op jit(solution)/shard_map/ppermute | solution.py:37
  120.1 10.6 %collective-permute-start.13 = (bf16[1152,128]{1,0:T(8,128)(2,1)}, bf16[1152,128]{1,0:T(8,128)(2,1)}, u32[]{:S(2)}, u32[]{:S(2)}) collective-permute-start(bf16[1152,128]{1,0:T(8,128)(2,1)} %get-tuple-element.93), channel_id=1, source_target_pairs={{0,24},{8,0},{16,8},{24,16},{1,25},{9,1},{17,9},{25,17},{2,26},{10... | collective-permute-start | bytes 884744 | tf_op jit(solution)/shard_map/ppermute | solution.py:37
  125.6 0.7 copy-start.2
  130.7 35.0 %copy-start.16 = (bf16[1,1536]{1,0:T(2,128)(2,1)S(1)}, bf16[1,1536]{1,0:T(2,128)(2,1)}, u32[]{:S(2)}) copy-start(bf16[1,1536]{1,0:T(2,128)(2,1)} %get-tuple-element.104) | copy-start | bytes 9220
  130.7 37.0 %copy-start.15 = (bf16[1,1536]{1,0:T(2,128)(2,1)S(1)}, bf16[1,1536]{1,0:T(2,128)(2,1)}, u32[]{:S(2)}) copy-start(bf16[1,1536]{1,0:T(2,128)(2,1)} %get-tuple-element.105) | copy-start | bytes 9220
  130.8 15.4 %all-to-all-start.3 = ((bf16[8,208,128]{2,1,0:T(8,128)(2,1)}), bf16[8,208,128]{2,1,0:T(8,128)(2,1)}, u32[]{:S(2)}, u32[]{:S(2)}) async-start(bf16[8,208,128]{2,1,0:T(8,128)(2,1)} %get-tuple-element.98), calls=%async_computation.3 | async-start | bytes 851968 | tf_op jit(solution)/shard_map/all_to_all | solution.py:41
  137.6 13.5 %collective-permute-start.14 = (bf16[1152,128]{1,0:T(8,128)(2,1)}, bf16[1152,128]{1,0:T(8,128)(2,1)S(1)}, u32[]{:S(2)}, u32[]{:S(2)}) collective-permute-start(bf16[1152,128]{1,0:T(8,128)(2,1)} %get-tuple-element.95), channel_id=1, source_target_pairs={{0,16},{8,24},{16,0},{24,8},{1,17},{9,25},{17,1},{25,9},{2,18},{10... | collective-permute-start | bytes 884744 | tf_op jit(solution)/shard_map/ppermute | solution.py:37
  148.4 5.0 %collective-permute-start.15 = (bf16[288,128]{1,0:T(8,128)(2,1)}, bf16[288,128]{1,0:T(8,128)(2,1)S(1)}, u32[]{:S(2)}, u32[]{:S(2)}) collective-permute-start(bf16[288,128]{1,0:T(8,128)(2,1)} %get-tuple-element.100), channel_id=1, source_target_pairs={{0,8},{8,16},{16,24},{24,0},{1,9},{9,17},{17,25},{25,1},{2,10},{10... | collective-permute-start | bytes 221192 | tf_op jit(solution)/shard_map/ppermute | solution.py:37
  148.7 5.6 %collective-permute-start.16 = (bf16[288,128]{1,0:T(8,128)(2,1)}, bf16[288,128]{1,0:T(8,128)(2,1)S(1)}, u32[]{:S(2)}, u32[]{:S(2)}) collective-permute-start(bf16[288,128]{1,0:T(8,128)(2,1)} %get-tuple-element.101), channel_id=1, source_target_pairs={{0,16},{8,24},{16,0},{24,8},{1,17},{9,25},{17,1},{25,9},{2,18},{10... | collective-permute-start | bytes 221192 | tf_op jit(solution)/shard_map/ppermute | solution.py:37
  150.5 4.2 %collective-permute-start.17 = (bf16[288,128]{1,0:T(8,128)(2,1)}, bf16[288,128]{1,0:T(8,128)(2,1)S(1)}, u32[]{:S(2)}, u32[]{:S(2)}) collective-permute-start(bf16[288,128]{1,0:T(8,128)(2,1)} %get-tuple-element.102), channel_id=1, source_target_pairs={{0,24},{8,0},{16,8},{24,16},{1,25},{9,1},{17,9},{25,17},{2,26},{10... | collective-permute-start | bytes 221192 | tf_op jit(solution)/shard_map/ppermute | solution.py:37
  151.1 3.6 %copy-start.4 = (bf16[1152,128]{1,0:T(8,128)(2,1)}, bf16[1152,128]{1,0:T(8,128)(2,1)S(1)}, u32[]{:S(2)}) copy-start(bf16[1152,128]{1,0:T(8,128)(2,1)S(1)} %collective-permute-done.14.refs_2_) | copy-start | bytes 884740
  153.4 1.3 copy-start.8
  154.2 0.6 copy-start.9
  154.7 0.6 copy-start.10
  157.8 25.3 %all-to-all-start.4 = ((bf16[16,128,128]{2,1,0:T(8,128)(2,1)}), bf16[16,128,128]{2,1,0:T(8,128)(2,1)}, u32[]{:S(2)}, u32[]{:S(2)}) async-start(bf16[16,128,128]{2,1,0:T(8,128)(2,1)} %shard_map.168), calls=%async_computation.4 | async-start | bytes 1048576 | tf_op jit(solution)/shard_map/all_to_all | solution.py:41
  165.7 4.4 %collective-permute-start.18 = (bf16[1,1536]{1,0:T(2,128)(2,1)S(1)}, bf16[1,1536]{1,0:T(2,128)(2,1)S(1)}, u32[]{:S(2)}, u32[]{:S(2)}) collective-permute-start(bf16[1,1536]{1,0:T(2,128)(2,1)S(1)} %copy-done.16), channel_id=1, source_target_pairs={{0,4},{4,8},{8,12},{12,16},{16,20},{20,24},{24,28},{28,32},{32,36}... | collective-permute-start | bytes 9224 | tf_op jit(solution)/shard_map/ppermute | solution.py:673
  167.7 5.3 %collective-permute-start.19 = (bf16[1,1536]{1,0:T(2,128)(2,1)S(1)}, bf16[1,1536]{1,0:T(2,128)(2,1)S(1)}, u32[]{:S(2)}, u32[]{:S(2)}) collective-permute-start(bf16[1,1536]{1,0:T(2,128)(2,1)S(1)} %copy-done.15), channel_id=1, source_target_pairs={{4,0},{8,4},{12,8},{16,12},{20,16},{24,20},{28,24},{32,28},{36,32}... | collective-permute-start | bytes 9224 | tf_op jit(solution)/shard_map/ppermute | solution.py:673
  170.0 3.0 %copy-start.13 = (bf16[1,1536]{1,0:T(2,128)(2,1)}, bf16[1,1536]{1,0:T(2,128)(2,1)S(1)}, u32[]{:S(2)}) copy-start(bf16[1,1536]{1,0:T(2,128)(2,1)S(1)} %collective-permute-done.18.before_ref) | copy-start | bytes 9220
  173.0 0.6 copy-start.14
Sparse Core Ops, SparseCore 0:
  46.1 24.8 all-gather.2
  83.2 23.1 all-gather.4
